TPU v7x, 32 devices: a whole 2x2x4 slice. The times are simulated.
32 devices in a mesh: groups: 2 (over x), mesh: 16 (over z, y, core).
Axes of the slice: x: 2, y: 2, z: 4, core: 2. Of those that a mesh axis runs over, the one named last changes fastest.
Arguments:
- tracers: float32 [2, 16, 32768], P(None, None, ('groups', 'mesh')), parts along dimension 2, may hold values from -6 to 6
- potential: float32 [16, 32768], P(None, ('groups', 'mesh')), parts along dimension 1, may hold values from -4 to 4
- surface_current: float32 [2, 32768], P(None, ('groups', 'mesh')), parts along dimension 1, may hold values from -4 to 4
- cell_neighbors: int32 [6, 16384], P(None, 'mesh'), may hold values from 0 to 16383, as said below
- cell_normal: float32 [6, 16384], P(None, 'mesh'), may hold values from -3.140625 to 3.140625
- cell_weight: float32 [6, 16384], P(None, 'mesh'), may hold values from 0.02 to 0.06
- spectra: float32 [50, 36, 4096], P(None, None, ('groups', 'mesh')), parts along dimension 2, may hold values from 0 to 10, as said below
- wind_velocity: float32 [2, 4096], P(None, ('groups', 'mesh')), parts along dimension 1, may hold values from -6 to 6
- node_neighbors: int32 [6, 2048], P(None, 'mesh'), may hold values from 0 to 2047, as said below
- node_normal: float32 [6, 2048], P(None, 'mesh'), may hold values from -3.140625 to 3.140625
- node_weight: float32 [6, 2048], P(None, 'mesh'), may hold values from 0.02 to 0.1
- send_rows: int32 [16, 16, 16], replicated, may hold values from 0 to 1023
- node_slot: int32 [2048], P('mesh'), may hold values from 0 to 255, as said below
Outputs:
- tracers_new: float32 [2, 16, 32768], P(None, None, ('groups', 'mesh')), parts along dimension 2
- spectra_new: float32 [50, 36, 4096], P(None, None, ('groups', 'mesh')), parts along dimension 2
There are 2 independent parts, one for each index of `groups`. A program takes and returns all parts, laid end to end along the dimension named above; an argument that names none is the same for every part. Nothing has to cross between parts.
Inputs may be any that keep to these rules, and one draw needn't show every extreme that they name: `cell_neighbors`: entry [s, c] is a cell at most 128 places from c in the numbering; c itself marks a padded slot. `node_neighbors`: entry [s, n] is a node at most 64 places from n in the numbering; n itself marks a padded slot. `node_slot`: the nodes of one block use distinct slots; at most 16 nodes of one block take a given cell block, and in every draw one cell block serves exactly 16 nodes of every node block. `spectra`: positive spectral densities.
All inputs are finite; a program needn't handle non-finite values.
Results may differ from a plain program's by a relative error of at most 0.0003.
Values sent between devices are 32-bit elements; how exact they have to be, the bound alone decides.
No kernel may reach another device: no remote copies, remote signals or barrier semaphores. Data moves between devices by JAX's collectives and lax.ppermute only.
A program may use at most 128 MiB of HBM per device.

v0:
```python
import math

import jax
import jax.numpy as jnp
from jax import lax
from jax.sharding import PartitionSpec as P

CELL_HALO = 128
NODE_HALO = 64


fct_floor = 0.001


def extended(x, sides, width):
    for axis, dim in sides:
        devices, length = (lax.axis_size(axis), x.shape[dim])
        up = [(i, (i + 1) % devices) for i in range(devices - 1)]
        down = [(j, i) for i, j in up]
        last = lax.slice_in_dim(x, length - width, length, axis=dim)
        initial = lax.slice_in_dim(x, 0, width, axis=dim)
        before = lax.ppermute(last, axis, up)
        after = lax.ppermute(initial, axis, down)
        x = jnp.concatenate([before, x, after], axis=dim)
    return x


def wave_tables(freq_count, dir_count):
    freq_index = jnp.arange(freq_count, dtype=jnp.float32)
    angles = 2.0 * math.pi * jnp.arange(dir_count, dtype=jnp.float32) / dir_count
    group_speed = jnp.exp(-math.log(1.1) * freq_index)
    stokes_factor = (freq_index + 1.0) / freq_count
    return (angles, group_speed, stokes_factor)


def advect(energy, energy_ext, current, current_ext, neighbors, normal, weight):
    angles, group_speed, stokes_factor = wave_tables(energy.shape[0], energy.shape[1])
    speed_x = group_speed[:, None, None] * jnp.cos(angles)[None, :, None]
    speed_y = group_speed[:, None, None] * jnp.sin(angles)[None, :, None]
    outflow = jnp.zeros(energy.shape, jnp.float32)
    for edge_slot in range(neighbors.shape[0]):
        target = neighbors[edge_slot]
        beside = jnp.take(energy_ext, target, axis=2)
        beside_current = jnp.take(current_ext, target, axis=1)
        current_x = 0.5 * (current[0] + beside_current[0])
        current_y = 0.5 * (current[1] + beside_current[1])
        normal_speed = (speed_x + current_x) * jnp.cos(normal[edge_slot]) + (
            speed_y + current_y
        ) * jnp.sin(normal[edge_slot])
        edge_flux = weight[edge_slot] * (
            jnp.maximum(normal_speed, 0.0) * energy + jnp.minimum(normal_speed, 0.0) * beside
        )
        outflow = outflow + edge_flux
    return energy - outflow


def source(advected, wind_velocity):
    angles, group_speed, stokes_factor = wave_tables(advected.shape[0], advected.shape[1])
    cosine = jnp.cos(angles)[:, None]
    sine = jnp.sin(angles)[:, None]
    forcing = jnp.maximum(
        wind_velocity[0][None, :] * cosine + wind_velocity[1][None, :] * sine, 0.0
    )
    growth = 0.25 * stokes_factor[:, None, None] * forcing[None]
    mean_energy = jnp.mean(advected, axis=(0, 1))
    damping = 2.0 * stokes_factor[:, None, None] * mean_energy[None, None, :]
    evolved = advected * jnp.exp(growth - damping)
    stokes_table = (
        jnp.stack(
            [
                stokes_factor[:, None] * jnp.cos(angles)[None, :],
                stokes_factor[:, None] * jnp.sin(angles)[None, :],
            ]
        )
        / advected.shape[1]
    )
    stokes = jnp.einsum("fdn,cfd->cn", evolved, stokes_table, precision=lax.Precision.HIGHEST)
    return (evolved, stokes)


def antidiffusion(
    tracers, tracers_ext, potential, potential_ext, cell_stokes, neighbors, normal, weight
):
    layer_count = tracers.shape[1]
    beside = jnp.take(tracers_ext, neighbors, axis=2)
    beside_potential = jnp.take(potential_ext, neighbors, axis=1)
    layer_index = jnp.arange(layer_count, dtype=jnp.float32)
    depth_decay = jnp.exp(-3.0 * layer_index / layer_count)
    drift_normal = cell_stokes[0][None, :] * jnp.cos(normal) + cell_stokes[1][None, :] * jnp.sin(
        normal
    )
    velocity = (
        beside_potential - potential[:, None, :] + depth_decay[:, None, None] * drift_normal[None]
    )
    own_value = tracers[:, :, None, :]
    low_flux = weight * (
        jnp.maximum(velocity, 0.0) * own_value + jnp.minimum(velocity, 0.0) * beside
    )
    high_flux = weight * velocity * 0.5 * (own_value + beside)
    antiflux = high_flux - low_flux
    lowered = tracers - jnp.sum(low_flux, axis=2)
    upper_bound = jnp.maximum(tracers, jnp.max(beside, axis=2))
    lower_bound = jnp.minimum(tracers, jnp.min(beside, axis=2))
    inflow_sum = jnp.sum(jnp.maximum(-antiflux, 0.0), axis=2)
    outflow_sum = jnp.sum(jnp.maximum(antiflux, 0.0), axis=2)
    room_up = jnp.maximum(upper_bound - lowered, 0.0)
    room_down = jnp.maximum(lowered - lower_bound, 0.0)
    ratio_plus = jnp.minimum(1.0, room_up / (inflow_sum + fct_floor))
    ratio_minus = jnp.minimum(1.0, room_down / (outflow_sum + fct_floor))
    return (antiflux, lowered, ratio_plus, ratio_minus)


def limited(antiflux, lowered, ratio_plus, ratio_minus, plus_ext, minus_ext, neighbors):
    plus_beside = jnp.take(plus_ext, neighbors, axis=2)
    minus_beside = jnp.take(minus_ext, neighbors, axis=2)
    factor = jnp.where(
        antiflux >= 0.0,
        jnp.minimum(ratio_minus[:, :, None, :], plus_beside),
        jnp.minimum(ratio_plus[:, :, None, :], minus_beside),
    )
    return lowered - jnp.sum(factor * antiflux, axis=2)


def local(
    tracers,
    potential,
    surface_current,
    cell_neighbors,
    cell_normal,
    cell_weight,
    spectra,
    wind_velocity,
    node_neighbors,
    node_normal,
    node_weight,
    send_rows,
    node_slot,
):
    device_index = lax.axis_index("mesh")
    cell_count = tracers.shape[2]
    node_count = spectra.shape[2]
    peer_count = send_rows.shape[0]
    capacity = send_rows.shape[2]
    fields = jnp.concatenate([tracers, potential[None]], axis=0)
    fields_ext = extended(fields, (("mesh", 2),), CELL_HALO)
    cell_local = cell_neighbors - (device_index * cell_count - CELL_HALO)
    node_local = node_neighbors - (device_index * node_count - NODE_HALO)
    surface_all = lax.all_gather(surface_current, "mesh", axis=1, tiled=True)
    column = lax.dynamic_index_in_dim(send_rows, device_index, 1, keepdims=False)
    cell_ids = node_slot // capacity * cell_count + jnp.take(column.reshape(-1), node_slot)
    node_current = jnp.take(surface_all, cell_ids, axis=1)
    joined = jnp.concatenate([spectra.reshape(-1, node_count), node_current], axis=0)
    joined_ext = extended(joined, (("mesh", 1),), NODE_HALO)
    energy_ext = joined_ext[:-2].reshape(spectra.shape[0], spectra.shape[1], -1)
    current_ext = joined_ext[-2:]
    advected = advect(
        spectra, energy_ext, node_current, current_ext, node_local, node_normal, node_weight
    )
    spectra_new, stokes = source(advected, wind_velocity)
    stokes_term = jnp.zeros((2, cell_count * peer_count), jnp.float32).at[:, cell_ids].add(stokes)
    cell_stokes = lax.psum_scatter(stokes_term, "mesh", scatter_dimension=1, tiled=True)
    antiflux, lowered, ratio_plus, ratio_minus = antidiffusion(
        tracers,
        fields_ext[:-1],
        potential,
        fields_ext[-1],
        cell_stokes,
        cell_local,
        cell_normal,
        cell_weight,
    )
    ratios_ext = extended(jnp.stack([ratio_plus, ratio_minus]), (("mesh", 3),), CELL_HALO)
    tracers_new = limited(
        antiflux, lowered, ratio_plus, ratio_minus, ratios_ext[0], ratios_ext[1], cell_local
    )
    return (tracers_new, spectra_new)


def solution(mesh):
    return jax.shard_map(
        local,
        mesh=mesh,
        in_specs=(
            P(None, None, ("groups", "mesh")),
            P(None, ("groups", "mesh")),
            P(None, ("groups", "mesh")),
            P(None, "mesh"),
            P(None, "mesh"),
            P(None, "mesh"),
            P(None, None, ("groups", "mesh")),
            P(None, ("groups", "mesh")),
            P(None, "mesh"),
            P(None, "mesh"),
            P(None, "mesh"),
            P(),
            P("mesh"),
        ),
        out_specs=(P(None, None, ("groups", "mesh")), P(None, None, ("groups", "mesh"))),
        check_vma=False,
    )
```

profile of v0, /device:TPU:0, one launch (start us, length us, event | category | flops | bytes accessed | tf_op | source)
XLA Modules:
  0.0 467.2 jit_solution(11156537173841517532)
XLA Ops:
  11.8 93.8 %all_gather.3 = f32[2,16384]{0,1:T(8,128)} all-gather(f32[2,1024]{0,1:T(8,128)S(1)} %copy.125), channel_id=1, replica_groups=mesh['groups'=2,'mesh'=16] {'mesh'}, dimensions={1}, use_global_device_ids=true | all-gather | bytes 139264 | tf_op jit(solution)/shard_map/all_gather | solution.py:148
  106.0 4.0 gather_fusion.2
  111.1 2.3 collective-permute-start.2
  114.8 3.0 collective-permute-start
  124.3 21.1 %gather_fusion = f32[6144,16]{1,0:T(8,128)} fusion(f32[16,1280]{0,1:T(8,128)S(1)} %bitcast.189, s32[6144]{0:T(1024)S(1)} %broadcast_clamp_fusion), kind=kCustom, calls=%fused_computation.15 | custom fusion | bytes 811008 | tf_op jit(solution)/shard_map/jit(_take)/gather | solution.py:86
  145.3 3.0 copy.124
  155.6 5.2 %copy.128 = f32[50,36,256]{0,1,2:T(8,128)} copy(f32[50,36,256]{2,1,0:T(8,128)S(1)} %reshape.591) | data formatting | bytes 3686400 | tf_op jit(solution)/shard_map/reshape | solution.py:154
  160.7 3.2 gather_fusion.4
  164.0 4.8 %gather_fusion.6 = f32[128,50,36]{1,2,0:T(8,128)} fusion(f32[50,36,256]{0,1,2:T(8,128)} %copy.128, s32[1024]{0:T(1024)S(1)} %pad_clamp_fusion.4), kind=kCustom, calls=%fused_computation.8.clone | custom fusion | bytes 1843712 | tf_op jit(solution)/shard_map/jit(_take)/gather | solution.py:43
  169.9 4.7 %gather_fusion.8 = f32[128,50,36]{1,2,0:T(8,128)} fusion(f32[50,36,256]{0,1,2:T(8,128)} %copy.128, s32[1024]{0:T(1024)S(1)} %pad_clamp_fusion.3), kind=kCustom, calls=%fused_computation.9.clone | custom fusion | bytes 1843712 | tf_op jit(solution)/shard_map/jit(_take)/gather | solution.py:43
  175.9 4.7 %gather_fusion.10 = f32[128,50,36]{1,2,0:T(8,128)} fusion(f32[50,36,256]{0,1,2:T(8,128)} %copy.128, s32[1024]{0:T(1024)S(1)} %pad_clamp_fusion.2), kind=kCustom, calls=%fused_computation.10.clone | custom fusion | bytes 1843712 | tf_op jit(solution)/shard_map/jit(_take)/gather | solution.py:43
  181.8 4.7 %gather_fusion.12 = f32[128,50,36]{1,2,0:T(8,128)} fusion(f32[50,36,256]{0,1,2:T(8,128)} %copy.128, s32[1024]{0:T(1024)S(1)} %pad_clamp_fusion.1), kind=kCustom, calls=%fused_computation.11.clone | custom fusion | bytes 1843712 | tf_op jit(solution)/shard_map/jit(_take)/gather | solution.py:43
  187.7 4.7 %gather_fusion.14 = f32[128,50,36]{1,2,0:T(8,128)} fusion(f32[50,36,256]{0,1,2:T(8,128)} %copy.128, s32[1024]{0:T(1024)S(1)} %pad_clamp_fusion), kind=kCustom, calls=%fused_computation.12.clone | custom fusion | bytes 1843712 | tf_op jit(solution)/shard_map/jit(_take)/gather | solution.py:43
  192.5 2.0 copy.129
  194.4 3.4 copy.131
  197.8 2.0 copy.133
  199.8 3.4 copy.135
  203.2 2.0 copy.137
  205.2 3.3 copy.139
  212.1 5.0 %fusion.69 = (f32[128]{0:T(128)S(1)}, f32[50,36,128]{2,1,0:T(8,128)S(1)}) fusion(f32[50,36,128]{2,1,0:T(8,128)} %param.25, f32[128,50,36]{0,2,1:T(8,128)} %copy.139, pred[128]{0:T(512)(128)(4,1)S(1)} %copy-done.33, f32[128]{0:T(128)} %get-tuple-element.87, f32[128]{0:T(128)S(1)} %get-tuple-element.72, f32[128]{0:T(128)} %get-tuple-element.91, ...), kind=kLoop, calls=%fused_computation.211 | loop fusion | flops 18201472 | bytes 7403840 | tf_op jit(solution)/shard_map/reduce_sum | solution.py:65
  218.4 5.2 %convolution_bitcast_fusion = f32[128,2]{1,0:T(8,128)S(1)} fusion(f32[50,36,128]{2,1,0:T(8,128)S(1)} %exponential_multiply_fusion, f32[1,50,36]{2,0,1:T(1,128)S(1)} %copy-done.31, f32[1,50,36]{2,0,1:T(1,128)S(1)} %copy-done.30), kind=kOutput, calls=%fused_computation.26 | convolution fusion | flops 5536800 | bytes 937024 | tf_op jit(solution)/shard_map/fdn,cfd->cn/dot_general | solution.py:77
  223.7 4.8 %scatter_custom_fusion = f32[2,16384]{0,1:T(8,128)} fusion(s32[128]{0:T(128)} %copy-done.43, f32[128,2]{1,0:T(8,128)S(1)} %convolution_bitcast_fusion, f32[]{:T(128)} %constant.82.clone.1), kind=kCustom, calls=%fused_computation.19 | custom fusion | flops 256 | bytes 131584 | tf_op jit(solution)/shard_map/scatter-add | solution.py:160
  229.9 42.5 %gather_fusion.15 = f32[6144,2,16]{2,1,0:T(2,128)} fusion(f32[2,16,1280]{1,0,2:T(2,128)S(1)} %copy.143, s32[6144]{0:T(1024)S(1)} %broadcast_clamp_fusion), kind=kCustom, calls=%fused_computation.2.clone | custom fusion | bytes 1597440 | tf_op jit(solution)/shard_map/jit(_take)/gather | solution.py:85
  272.4 6.7 %copy.144 = f32[6,1024,2,16]{1,0,3,2:T(8,128)S(1)} copy(f32[6,1024,2,16]{3,2,1,0:T(2,128)} %bitcast.191) | data formatting | bytes 1572864 | tf_op jit(solution)/shard_map/jit(_take)/gather | solution.py:85
  279.1 67.3 %reduce-scatter.2.cloned.1.call-done = f32[2,1024]{0,1:T(8,128)} async-done(((f32[2,16384]{0,1:T(8,128)}), f32[2,1024]{0,1:T(8,128)}) %reduce-scatter.2.cloned.1.call-update) | async-done | bytes 8208 | tf_op jit(solution)/shard_map/reduce_scatter | solution.py:161
  349.3 1.8 bitcast_reduce_fusion
  351.3 1.8 collective-permute-start.4
  354.4 3.0 collective-permute-done.5
  358.8 42.5 %gather_fusion.16 = f32[6144,2,16]{2,1,0:T(2,128)} fusion(f32[2,16,1280]{1,0,2:T(2,128)S(1)} %bitcast.195, s32[6144]{0:T(1024)S(1)} %broadcast_clamp_fusion), kind=kCustom, calls=%fused_computation.13.clone | custom fusion | bytes 1597440 | tf_op jit(solution)/shard_map/jit(_take)/gather | solution.py:114
  401.3 6.3 %copy.154 = f32[6,1024,2,16]{1,0,3,2:T(8,128)S(1)} copy(f32[6,1024,2,16]{3,2,1,0:T(2,128)} %bitcast.192) | data formatting | bytes 1572864 | tf_op jit(solution)/shard_map/jit(_take)/gather | solution.py:114
  409.1 42.5 %gather_fusion.17 = f32[6144,2,16]{2,1,0:T(2,128)} fusion(f32[2,16,1280]{1,0,2:T(2,128)S(1)} %bitcast.194, s32[6144]{0:T(1024)S(1)} %copy-done.20), kind=kCustom, calls=%fused_computation.14.clone | custom fusion | bytes 1597440 | tf_op jit(solution)/shard_map/jit(_take)/gather | solution.py:115
  451.7 6.3 %copy.155 = f32[6,1024,2,16]{1,0,3,2:T(8,128)S(1)} copy(f32[6,1024,2,16]{3,2,1,0:T(2,128)} %bitcast.190) | data formatting | bytes 1572864 | tf_op jit(solution)/shard_map/jit(_take)/gather | solution.py:115
  (178 shorter events, 41.3 us)
Async XLA Ops:
  7.2 339.3 %reduce-scatter.2.cloned.1.call-start = ((), (), s32[]{:S(2)}) async-start(), calls=%async_computation.1 | async-start | bytes 8912896 | tf_op jit(solution)/shard_map/reduce_scatter | solution.py:161
  10.8 94.7 %copy-start.43 = (s32[128]{0:T(128)}, s32[128]{0:T(128)S(1)}, u32[]{:S(2)}) copy-start(s32[128]{0:T(128)S(1)} %get-tuple-element.54) | copy-start | bytes 1540
  11.7 93.8 %copy-start.8 = (f32[50,36,128]{2,1,0:T(8,128)S(1)}, f32[50,36,128]{2,1,0:T(8,128)}, u32[]{:S(2)}) copy-start(f32[50,36,128]{2,1,0:T(8,128)} %param.25) | copy-start | bytes 2764804
  105.5 9.2 %copy-start.4 = (f32[2,16,1024]{2,1,0:T(8,128)S(1)}, f32[2,16,1024]{2,1,0:T(8,128)}, u32[]{:S(2)}) copy-start(f32[2,16,1024]{2,1,0:T(8,128)} %param.19) | copy-start | bytes 393220
  105.5 9.2 %copy-start.17 = (f32[16,1024]{1,0:T(8,128)S(1)}, f32[16,1024]{1,0:T(8,128)}, u32[]{:S(2)}) copy-start(f32[16,1024]{1,0:T(8,128)} %param.20) | copy-start | bytes 196612
  105.6 14.3 %copy-start.38 = (s32[6,128]{1,0:T(8,128)S(1)}, s32[6,128]{1,0:T(8,128)}, u32[]{:S(2)}) copy-start(s32[6,128]{1,0:T(8,128)} %param.27) | copy-start | bytes 9220
  105.6 15.0 %copy-start.44 = (f32[2,128]{1,0:T(2,128)S(1)}, f32[2,128]{1,0:T(2,128)}, u32[]{:S(2)}) copy-start(f32[2,128]{1,0:T(2,128)} %param.26) | copy-start | bytes 3076
  105.6 16.4 %copy-start.28 = (s32[6,1024]{1,0:T(8,128)S(1)}, s32[6,1024]{1,0:T(8,128)}, u32[]{:S(2)}) copy-start(s32[6,1024]{1,0:T(8,128)} %param.22) | copy-start | bytes 73732
  105.6 16.4 %copy-start.39 = (f32[6,128]{1,0:T(8,128)S(1)}, f32[6,128]{1,0:T(8,128)}, u32[]{:S(2)}) copy-start(f32[6,128]{1,0:T(8,128)} %param.28) | copy-start | bytes 9220
  105.7 16.4 %copy-start.40 = (f32[6,128]{1,0:T(8,128)S(1)}, f32[6,128]{1,0:T(8,128)}, u32[]{:S(2)}) copy-start(f32[6,128]{1,0:T(8,128)} %param.29) | copy-start | bytes 9220
  111.1 37.2 %collective-permute-start.2 = (f32[1802,64]{0,1:T(8,128)}, f32[1802,64]{0,1:T(8,128)S(1)}, u32[]{:S(2)}, u32[]{:S(2)}) collective-permute-start(f32[1802,64]{0,1:T(8,128)} %get-tuple-element.60), channel_id=1, source_target_pairs={{0,1},{1,2},{2,3},{3,4},{4,5},{5,6},{6,7},{7,8},{8,9},{9,10},{10,1... | collective-permute-start | bytes 1383944 | tf_op jit(solution)/shard_map/ppermute | solution.py:22
  113.5 34.9 %collective-permute-start.3 = (f32[1802,64]{0,1:T(8,128)}, f32[1802,64]{0,1:T(8,128)S(1)}, u32[]{:S(2)}, u32[]{:S(2)}) collective-permute-start(f32[1802,64]{0,1:T(8,128)} %get-tuple-element.61), channel_id=1, source_target_pairs={{1,0},{2,1},{3,2},{4,3},{5,4},{6,5},{7,6},{8,7},{9,8},{10,9},{11,1... | collective-permute-start | bytes 1383944 | tf_op jit(solution)/shard_map/ppermute | solution.py:23
  114.8 9.2 %collective-permute-start = (f32[3,16,128]{2,1,0:T(8,128)S(1)}, f32[3,16,128]{2,1,0:T(8,128)S(1)}, u32[]{:S(2)}, u32[]{:S(2)}) collective-permute-start(f32[3,16,128]{2,1,0:T(8,128)S(1)} %get-tuple-element.69), channel_id=1, source_target_pairs={{0,1},{1,2},{2,3},{3,4},{4,5},{5,6},{6,7},{7,8},{8,9},{9,10},{10,1... | collective-permute-start | bytes 73736 | tf_op jit(solution)/shard_map/ppermute | solution.py:22
  117.8 6.2 %collective-permute-start.1 = (f32[3,16,128]{2,1,0:T(8,128)S(1)}, f32[3,16,128]{2,1,0:T(8,128)S(1)}, u32[]{:S(2)}, u32[]{:S(2)}) collective-permute-start(f32[3,16,128]{2,1,0:T(8,128)S(1)} %get-tuple-element.70), channel_id=1, source_target_pairs={{1,0},{2,1},{3,2},{4,3},{5,4},{6,5},{7,6},{8,7},{9,8},{10,9},{11,1... | collective-permute-start | bytes 73736 | tf_op jit(solution)/shard_map/ppermute | solution.py:23
  122.1 236.7 %copy-start.19 = (s32[6144]{0:T(1024)}, s32[6144]{0:T(1024)S(1)}, u32[]{:S(2)}) copy-start(s32[6144]{0:T(1024)S(1)} %broadcast_clamp_fusion) | copy-start | bytes 73732
  124.0 24.3 %copy-start.23 = (f32[3,16,128]{2,1,0:T(8,128)}, f32[3,16,128]{2,1,0:T(8,128)S(1)}, u32[]{:S(2)}) copy-start(f32[3,16,128]{2,1,0:T(8,128)S(1)} %collective-permute-done) | copy-start | bytes 73732
  124.0 24.3 %copy-start.25 = (f32[3,16,128]{2,1,0:T(8,128)}, f32[3,16,128]{2,1,0:T(8,128)S(1)}, u32[]{:S(2)}) copy-start(f32[3,16,128]{2,1,0:T(8,128)S(1)} %collective-permute-done.1) | copy-start | bytes 73732
  203.2 7.4 %copy-start.27 = (f32[128,2]{1,0:T(8,128)S(1)}, f32[128,2]{1,0:T(8,128)}, u32[]{:S(2)}) copy-start(f32[128,2]{1,0:T(8,128)} %gather_fusion.3) | copy-start | bytes 3076
  203.2 7.4 %copy-start.36 = (pred[128]{0:T(512)(128)(4,1)S(1)}, pred[128]{0:T(512)(128)(4,1)}, u32[]{:S(2)}) copy-start(pred[128]{0:T(512)(128)(4,1)} %get-tuple-element.99) | copy-start | bytes 388
  203.2 7.4 %copy-start.37 = (pred[128]{0:T(512)(128)(4,1)S(1)}, pred[128]{0:T(512)(128)(4,1)}, u32[]{:S(2)}) copy-start(pred[128]{0:T(512)(128)(4,1)} %get-tuple-element.101) | copy-start | bytes 388
  203.2 8.8 %copy-start.22 = (f32[50,36]{1,0:T(8,128)S(1)}, f32[50,36]{1,0:T(8,128)}, u32[]{:S(2)}) copy-start(f32[50,36]{1,0:T(8,128)} %get-tuple-element.108) | copy-start | bytes 21604
  203.2 8.8 %copy-start.41 = (f32[128]{0:T(128)S(1)}, f32[128]{0:T(128)}, u32[]{:S(2)}) copy-start(f32[128]{0:T(128)} %get-tuple-element.81) | copy-start | bytes 1540
  203.2 8.8 %copy-start.42 = (f32[128]{0:T(128)S(1)}, f32[128]{0:T(128)}, u32[]{:S(2)}) copy-start(f32[128]{0:T(128)} %get-tuple-element.82) | copy-start | bytes 1540
  272.4 75.8 %copy-start.29 = (f32[6,1024]{1,0:T(8,128)S(1)}, f32[6,1024]{1,0:T(8,128)}, u32[]{:S(2)}) copy-start(f32[6,1024]{1,0:T(8,128)} %param.23) | copy-start | bytes 73732
  272.4 75.9 %copy-start.15 = (f32[6,1024,16]{1,2,0:T(8,128)S(1)}, f32[6,1024,16]{1,2,0:T(8,128)}, u32[]{:S(2)}) copy-start(f32[6,1024,16]{1,2,0:T(8,128)} %copy.124) | copy-start | bytes 1179652
  272.4 75.9 %copy-start.21 = (f32[6,1024]{1,0:T(8,128)S(1)}, f32[6,1024]{1,0:T(8,128)}, u32[]{:S(2)}) copy-start(f32[6,1024]{1,0:T(8,128)} %param.24) | copy-start | bytes 73732
  272.4 75.9 %copy-start.45 = (f32[16]{0:T(128)S(1)}, f32[16]{0:T(128)}, u32[]{:S(2)}) copy-start(f32[16]{0:T(128)} %multiply_exponential_fusion.1) | copy-start | bytes 196
  351.2 6.9 %copy-start.11 = (f32[2,16,1024]{2,1,0:T(8,128)}, f32[2,16,1024]{2,1,0:T(8,128)S(1)}, u32[]{:S(2)}) copy-start(f32[2,16,1024]{2,1,0:T(8,128)S(1)} %get-tuple-element.36) | copy-start | bytes 393220
  351.3 3.1 collective-permute-start.4
  353.1 4.3 collective-permute-start.5
  401.3 7.8 %copy-start.20 = (s32[6144]{0:T(1024)S(1)}, s32[6144]{0:T(1024)}, u32[]{:S(2)}) copy-start(s32[6144]{0:T(1024)} %copy-done.19) | copy-start | bytes 73732
  451.7 8.8 %copy-start.1 = (s32[16,16,16]{2,1,0:T(8,128)S(1)}, s32[16,16,16]{2,1,0:T(8,128)}, u32[]{:S(2)}) copy-start(s32[16,16,16]{2,1,0:T(8,128)} %param.30) | copy-start | bytes 49156
  (23 other events, 102.4 us)
Sparse Core Ops, SparseCore 0:
  228.7 117.7 reduce-scatter.1
where the time goes:
time: 471 us; the launch traced here: 467 us
  local copies, waits for them, and re-layouts  246 us (52%)
  blocking collectives  93.8 us (20%)
  waiting for transfers between devices  70.4 us (15%)
  other arithmetic  26.1 us (6%)
  between operations  14.9 us (3%)
  starting transfers between devices  11 us (2%)
  matrix products  5.24 us (1%)
    all_gather x1, blocking collectives, local(): surface_all = lax.all_gather(surface_current, 'mesh', axis=1, tiled=True)  93.8 us
    reduce_scatter x1, waiting for transfers between devices, local(): lax.psum_scatter(stokes_term, 'mesh', scatter_dimension=1, tiled=True)  67.3 us
    gather x2, local copies, waits for them, and re-layouts, antidiffusion(): beside = jnp.take(tracers_ext, neighbors, axis=2)  49.2 us
    gather x2, local copies, waits for them, and re-layouts, limited(): minus_beside = jnp.take(minus_ext, neighbors, axis=2)  48.9 us
    gather x2, local copies, waits for them, and re-layouts, limited(): plus_beside = jnp.take(plus_ext, neighbors, axis=2)  48.8 us
    gather x12, local copies, waits for them, and re-layouts, advect(): beside = jnp.take(energy_ext, target, axis=2)  42.8 us
    gather x2, local copies, waits for them, and re-layouts, antidiffusion(): beside_potential = jnp.take(potential_ext, neighbors, axis=1)  24.1 us
  transfers between devices with their start and end apart: 7, of which 2 were waited for; matrix products, arithmetic and copies ran while one was open for 17% of the time, Pallas kernels for 0%

commit v1 on v0

v1 whole, which is shorter than its diff:
```python
import math

import jax
import jax.numpy as jnp
from jax import lax
from jax.experimental import pallas as pl
from jax.experimental.pallas import tpu as pltpu
from jax.sharding import PartitionSpec as P

LANES = 128
FCT_FLOOR = 0.001
TABLE_ROWS = 24
VMEM_LIMIT = 48 * 1024 * 1024


def lane_gather(values, index):
    return jnp.take_along_axis(values, index, axis=1, mode="promise_in_bounds")


def spread(row, count):
    return jnp.broadcast_to(row, (count, LANES))


def lane_iota(rows):
    return lax.broadcasted_iota(jnp.int32, (rows, LANES), 1)


def row_iota(rows):
    return lax.broadcasted_iota(jnp.int32, (rows, LANES), 0)


def slot_rows(send_rows, block):
    peers, capacity = send_rows.shape[1:]
    entry = send_rows[block]
    wide = jnp.concatenate([entry, jnp.zeros((peers, LANES - capacity), jnp.int32)], axis=1)
    wide = lane_gather(wide, lane_iota(peers) % capacity)
    owner = row_iota(peers)
    out = []
    for half in range(peers * capacity // LANES):
        wanted = (lane_iota(peers) + half * LANES) // capacity
        picked = jnp.where(owner == wanted, wide, 0).astype(jnp.float32)
        out.append(jnp.sum(picked, axis=0, keepdims=True).astype(jnp.int32))
    return out


def pack_kernel(
    spectra, tracers, potential, neighbors, normal, weight, current, send_rows, node_slot,
    tile, ahead, behind,
):
    me = lax.axis_index("mesh")
    freqs, dirs = spectra.shape[:2]
    layers, cells = potential.shape
    blocks = cells // LANES
    field_rows = (tracers.shape[0] + 1) * layers
    stacked = jnp.concatenate(
        [current[:, b * LANES : (b + 1) * LANES] for b in range(blocks)], axis=0
    )
    place = row_iota(2 * blocks)
    halves = slot_rows(send_rows, me)
    tile[...] = jnp.zeros(tile.shape, jnp.float32)
    for half, cell in enumerate(halves):
        found = lane_gather(stacked, spread(cell % LANES, 2 * blocks))
        for part in range(2):
            picked = jnp.where(place == 2 * (cell // LANES) + part, found, 0.0)
            row = part * len(halves) + half
            tile[row : row + 1, :] = jnp.sum(picked, axis=0, keepdims=True)
    row = 2 * len(halves)
    tile[row : row + 1, :] = node_slot[...].astype(jnp.float32)
    for out, first in ((ahead, blocks - 2), (behind, 0)):
        for b in range(2):
            lanes = slice((first + b) * LANES, (first + b + 1) * LANES)
            base = b * field_rows
            for t in range(tracers.shape[0]):
                out[base + t * layers : base + (t + 1) * layers, :] = tracers[t, :, lanes]
            out[base + field_rows - layers : base + field_rows, :] = potential[:, lanes]
    for out, b in ((ahead, blocks - 1), (behind, 0)):
        lanes = slice(b * LANES, (b + 1) * LANES)
        base = 2 * field_rows
        out[base : base + TABLE_ROWS, :] = jnp.zeros((TABLE_ROWS, LANES), jnp.float32)
        edges = neighbors.shape[0]
        out[base : base + edges, :] = neighbors[:, lanes].astype(jnp.float32)
        out[base + 8 : base + 8 + edges, :] = normal[:, lanes]
        out[base + 16 : base + 16 + edges, :] = weight[:, lanes]
    base = 2 * field_rows + TABLE_ROWS
    pairs = freqs // 2
    whole = dirs // 8 * 8
    rest = dirs - whole
    low = lane_iota(dirs) < LANES // 2
    for g in range(pairs):
        natural = spectra[g]
        turned = pltpu.roll(spectra[g + pairs], LANES // 2, 1)
        for out, mixed in (
            (ahead, jnp.where(low, turned, natural)),
            (behind, jnp.where(low, natural, turned)),
        ):
            at = base + g * whole
            out[at : at + whole, :] = mixed[:whole]
            at = base + pairs * whole + g * rest
            out[at : at + rest, :] = mixed[whole:]
    at = base + pairs * dirs
    if at < ahead.shape[0]:
        for out in (ahead, behind):
            out[at:, :] = jnp.zeros((ahead.shape[0] - at, LANES), jnp.float32)


def node_currents(table, slot, block, capacity):
    peers = table.shape[0]
    halves = peers * capacity // LANES
    owner = slot // capacity
    entry = block * capacity + slot % capacity
    lane = spread(entry % LANES, 8)
    owner8 = spread(owner, 8)
    found = jnp.zeros((8, LANES), jnp.float32)
    for p in range(peers):
        found = jnp.where(owner8 == p, lane_gather(table[p], lane), found)
    half = entry // LANES
    out = []
    for part in range(2):
        value = found[part * halves : part * halves + 1]
        for h in range(1, halves):
            row = part * halves + h
            value = jnp.where(half == h, found[row : row + 1], value)
        out.append(value)
    return out


def wave_kernel(
    spectra, before, after, table, node_slot, neighbors, normal, weight, wind, send_rows,
    spectra_new, tile, project, drift,
):
    me = lax.axis_index("mesh")
    freqs, dirs = spectra.shape[:2]
    edges = neighbors.shape[0]
    peers, _, capacity = send_rows.shape
    halves = peers * capacity // LANES
    pairs = freqs // 2
    whole = dirs // 8 * 8
    rest = dirs - whole
    base = before.shape[0] - (pairs * dirs + 7) // 8 * 8
    low1 = lane_iota(1) < LANES // 2

    slot = node_slot[...]
    row = 2 * halves
    previous = jnp.maximum(me - 1, 0)
    following = jnp.minimum(me + 1, peers - 1)
    beside_slot = jnp.where(
        low1, table[following][row : row + 1], table[previous][row : row + 1]
    ).astype(jnp.int32)
    beside_block = jnp.where(low1, following, previous)
    own_block = jnp.full((1, LANES), me, jnp.int32)
    own_x, own_y = node_currents(table, slot, own_block, capacity)
    halo_x, halo_y = node_currents(table, beside_slot, beside_block, capacity)

    target = neighbors[...]
    lane = target % LANES
    inside = target // LANES == me
    angle = normal[...]
    w = weight[...]
    cosine = w * jnp.cos(angle)
    sine = w * jnp.sin(angle)

    def beside(own, halo):
        a = lane_gather(spread(own, edges), lane)
        b = lane_gather(spread(halo, edges), lane)
        return jnp.where(inside, a, b)

    drift[0:edges, :] = (
        0.5 * (own_x + beside(own_x, halo_x)) * cosine
        + 0.5 * (own_y + beside(own_y, halo_y)) * sine
    )
    turn = 2.0 * math.pi / dirs * lax.broadcasted_iota(jnp.int32, (dirs, LANES), 0).astype(
        jnp.float32
    )
    cos_dir = jnp.cos(turn)
    sin_dir = jnp.sin(turn)
    for s in range(edges):
        project[s] = cos_dir * cosine[s : s + 1] + sin_dir * sine[s : s + 1]

    low = lane_iota(dirs) < LANES // 2
    straight = [spread(lane[s : s + 1], dirs) for s in range(edges)]
    swapped = [spread((lane[s : s + 1] + LANES // 2) % LANES, dirs) for s in range(edges)]
    within = [spread(target[s : s + 1] // LANES, dirs) == me for s in range(edges)]
    ratio = 1.0 / 1.1
    jump = ratio**pairs

    def pair(g, carry):
        speed, total = carry
        halo_parts = []
        for message in (before, after):
            at = pl.multiple_of(base + g * whole, 8)
            upper = message[pl.ds(at, whole), :]
            lower = message[pl.ds(base + pairs * whole + g * rest, rest), :]
            halo_parts.append(jnp.concatenate([upper, lower], axis=0))
        b, a = halo_parts
        for f, group_speed, halo, halo_lane in (
            (g, speed, jnp.where(low, a, b), straight),
            (g + pairs, speed * jump, jnp.where(low, b, a), swapped),
        ):
            own = spectra[f]
            out_speed = jnp.zeros((dirs, LANES), jnp.float32)
            inflow = jnp.zeros((dirs, LANES), jnp.float32)
            for s in range(edges):
                normal_speed = group_speed * project[s] + drift[s : s + 1]
                near = jnp.where(
                    within[s], lane_gather(own, straight[s]), lane_gather(halo, halo_lane[s])
                )
                out_speed = out_speed + jnp.maximum(normal_speed, 0.0)
                inflow = inflow + jnp.minimum(normal_speed, 0.0) * near
            advected = own - (out_speed * own + inflow)
            spectra_new[f] = advected
            total = total + advected
        return speed * ratio, total

    zero = jnp.zeros((dirs, LANES), jnp.float32)
    _, total = lax.fori_loop(0, pairs, pair, (jnp.float32(1.0), zero))
    mean = jnp.sum(total, axis=0, keepdims=True) * (1.0 / (freqs * dirs))
    forcing = jnp.maximum(wind[0:1, :] * cos_dir + wind[1:2, :] * sin_dir, 0.0)
    step = jnp.exp((0.25 * forcing - 2.0 * mean) * (1.0 / freqs))

    def grow(f, carry):
        factor, weighted = carry
        factor = factor * step
        evolved = spectra_new[f] * factor
        spectra_new[f] = evolved
        kappa = (f + 1).astype(jnp.float32) * (1.0 / freqs)
        return factor, weighted + kappa * evolved

    _, weighted = lax.fori_loop(0, freqs, grow, (zero + 1.0, zero))
    stokes = jnp.concatenate(
        [
            jnp.sum(weighted * cos_dir, axis=0, keepdims=True),
            jnp.sum(weighted * sin_dir, axis=0, keepdims=True),
        ],
        axis=0,
    ) * (1.0 / dirs)
    in_order = exact_dot(
        stokes, lax.broadcasted_iota(jnp.int32, (halves * LANES, LANES), 0) == slot
    )
    tile[...] = jnp.zeros(tile.shape, jnp.float32)
    for part in range(2):
        for half in range(halves):
            row = part * halves + half
            tile[row : row + 1, :] = in_order[
                part : part + 1, half * LANES : (half + 1) * LANES
            ]


def exact_dot(values, chosen):
    first = values.astype(jnp.bfloat16).astype(jnp.float32)
    left = values - first
    second = left.astype(jnp.bfloat16).astype(jnp.float32)
    third = left - second
    pad = jnp.zeros((10, values.shape[1]), jnp.float32)
    parts = jnp.concatenate([first, second, third, pad], axis=0).astype(jnp.bfloat16)
    picks = jnp.where(chosen, 1.0, 0.0).astype(jnp.bfloat16)
    out = lax.dot_general(
        parts, picks, (((1,), (1,)), ((), ())), preferred_element_type=jnp.float32
    )
    return out[0:2] + (out[2:4] + out[4:6])


def tracer_kernel(
    tracers, potential, before, after, table, neighbors, normal, weight, send_rows,
    tracers_new, fields, target, cosine, sine, scale, stokes, antiflux, lowered, ratios,
):
    me = lax.axis_index("mesh")
    peers, _, capacity = send_rows.shape
    halves = peers * capacity // LANES
    tracer_count, layers, cells = tracers.shape
    blocks = cells // LANES
    edges = neighbors.shape[0]
    field_rows = (tracer_count + 1) * layers
    groups = field_rows // 8
    layer_groups = layers // 8
    tracer_groups = tracer_count * layer_groups

    for b in range(2):
        fields[b] = before[b * field_rows : (b + 1) * field_rows, :]
        fields[blocks + 2 + b] = after[b * field_rows : (b + 1) * field_rows, :]
    for b in range(blocks):
        lanes = slice(b * LANES, (b + 1) * LANES)
        for t in range(tracer_count):
            fields[b + 2, t * layers : (t + 1) * layers, :] = tracers[t, :, lanes]
        fields[b + 2, field_rows - layers : field_rows, :] = potential[:, lanes]
    at = 2 * field_rows
    for b in range(blocks + 2):
        if b == 0 or b == blocks + 1:
            message = before if b == 0 else after
            near = message[at : at + edges, :].astype(jnp.int32)
            angle = message[at + 8 : at + 8 + edges, :]
            w = message[at + 16 : at + 16 + edges, :]
        else:
            lanes = slice((b - 1) * LANES, b * LANES)
            near = neighbors[:, lanes]
            angle = normal[:, lanes]
            w = weight[:, lanes]
        target[b, 0:edges, :] = near
        scale[b, 0:edges, :] = w
        cosine[b, 0:edges, :] = w * jnp.cos(angle)
        sine[b, 0:edges, :] = w * jnp.sin(angle)

    lane1 = lane_iota(1)
    lane8 = lane_iota(8)
    per_row = LANES // capacity
    for which in range(3):
        block = jnp.clip(me + which - 1, 0, peers - 1)
        cell = slot_rows(send_rows, block)
        first = block * capacity
        pick = (first % LANES) + lane8 % capacity
        found = [jnp.zeros((8, LANES), jnp.float32) for _ in range(halves)]
        for d in range(peers):
            half = d // per_row
            found[half] = jnp.where(
                lane8 // capacity == d % per_row, lane_gather(table[d], pick), found[half]
            )
        source_half = first // LANES
        values = []
        for part in range(2):
            row = []
            for half in range(halves):
                value = found[half][part * halves : part * halves + 1]
                for h in range(1, halves):
                    at_row = part * halves + h
                    value = jnp.where(source_half == h, found[half][at_row : at_row + 1], value)
                row.append(value)
            values.append(jnp.concatenate(row, axis=1))
        values = jnp.concatenate(values, axis=0)
        names = jnp.concatenate(cell, axis=1)
        count = cells if which == 1 else LANES
        start = cells - LANES if which == 0 else 0
        number = lax.broadcasted_iota(jnp.int32, (count, halves * LANES), 0) + start
        sums = exact_dot(values, number == names)
        if which == 1:
            for b in range(blocks):
                stokes[b + 1, 0:2, :] = sums[:, b * LANES : (b + 1) * LANES]
        else:
            stokes[0 if which == 0 else blocks + 1, 0:2, :] = sums

    decay = [
        jnp.exp(-3.0 / layers * (row_iota(8) + 8 * g).astype(jnp.float32))
        for g in range(layer_groups)
    ]

    def neighbour_of(near, b, s):
        row = spread(near[s : s + 1, :], 8)
        side = row // LANES - (me * blocks + b - 1)
        return row % LANES, side

    def low_order(b, carry):
        near = target[b]
        w = scale[b]
        slope = cosine[b] * stokes[b, 0:1, :] + sine[b] * stokes[b, 1:2, :]
        own = [fields[b + 1, 8 * g : 8 * g + 8, :] for g in range(groups)]
        zero = jnp.zeros((8, LANES), jnp.float32)
        out_speed = [zero] * layer_groups
        inflow = [zero] * tracer_groups
        upper = own[:tracer_groups]
        lower = own[:tracer_groups]
        positive = [zero] * tracer_groups
        negative = [zero] * tracer_groups
        for s in range(edges):
            lane, side = neighbour_of(near, b, s)
            w8 = spread(w[s : s + 1, :], 8)
            slope8 = spread(slope[s : s + 1, :], 8)
            beside = []
            for g in range(groups):
                rows = slice(8 * g, 8 * g + 8)
                middle = lane_gather(own[g], lane)
                left = lane_gather(fields[b, rows, :], lane)
                right = lane_gather(fields[b + 2, rows, :], lane)
                beside.append(jnp.where(side == 0, middle, jnp.where(side < 0, left, right)))
            for lg in range(layer_groups):
                k = tracer_groups + lg
                speed = w8 * (beside[k] - own[k]) + decay[lg] * slope8
                up = jnp.maximum(speed, 0.0)
                down = jnp.minimum(speed, 0.0)
                half = 0.5 * (up - down)
                out_speed[lg] = out_speed[lg] + up
                for t in range(tracer_count):
                    g = t * layer_groups + lg
                    q = beside[g]
                    flux = half * (q - own[g])
                    antiflux[b, s, 8 * g : 8 * g + 8, :] = flux
                    inflow[g] = inflow[g] + down * q
                    upper[g] = jnp.maximum(upper[g], q)
                    lower[g] = jnp.minimum(lower[g], q)
                    positive[g] = positive[g] + jnp.maximum(flux, 0.0)
                    negative[g] = negative[g] - jnp.minimum(flux, 0.0)
        for g in range(tracer_groups):
            rows = slice(8 * g, 8 * g + 8)
            value = own[g] - (out_speed[g % layer_groups] * own[g] + inflow[g])
            lowered[b, rows, :] = value
            plus = jnp.maximum(upper[g] - value, 0.0) / (negative[g] + FCT_FLOOR)
            minus = jnp.maximum(value - lower[g], 0.0) / (positive[g] + FCT_FLOOR)
            ratios[b, rows, :] = jnp.minimum(1.0, plus)
            at = 8 * (tracer_groups + g)
            ratios[b, at : at + 8, :] = jnp.minimum(1.0, minus)
        return carry

    lax.fori_loop(0, blocks + 2, low_order, 0)

    def limit(i, carry):
        b = i + 1
        near = target[b]
        out = [lowered[b, 8 * g : 8 * g + 8, :] for g in range(tracer_groups)]
        own = [ratios[b, 8 * g : 8 * g + 8, :] for g in range(2 * tracer_groups)]
        for s in range(edges):
            lane, side = neighbour_of(near, b, s)
            beside = []
            for g in range(2 * tracer_groups):
                rows = slice(8 * g, 8 * g + 8)
                middle = lane_gather(own[g], lane)
                left = lane_gather(ratios[b - 1, rows, :], lane)
                right = lane_gather(ratios[b + 1, rows, :], lane)
                beside.append(jnp.where(side == 0, middle, jnp.where(side < 0, left, right)))
            for g in range(tracer_groups):
                flux = antiflux[b, s, 8 * g : 8 * g + 8, :]
                m = g + tracer_groups
                factor = jnp.where(
                    flux >= 0.0,
                    jnp.minimum(own[m], beside[g]),
                    jnp.minimum(own[g], beside[m]),
                )
                out[g] = out[g] - factor * flux
        lanes = pl.ds(pl.multiple_of(i * LANES, LANES), LANES)
        for g in range(tracer_groups):
            t, lg = g // layer_groups, g % layer_groups
            tracers_new[t, 8 * lg : 8 * lg + 8, lanes] = out[g]
        return carry

    lax.fori_loop(0, blocks, limit, 0)


def whole_spec():
    return pl.BlockSpec(memory_space=pltpu.VMEM)


def local(
    tracers,
    potential,
    surface_current,
    cell_neighbors,
    cell_normal,
    cell_weight,
    spectra,
    wind_velocity,
    node_neighbors,
    node_normal,
    node_weight,
    send_rows,
    node_slot,
):
    peers = send_rows.shape[0]
    freqs, dirs, nodes = spectra.shape
    tracer_count, layers, cells = tracers.shape
    edges = cell_neighbors.shape[0]
    blocks = cells // LANES
    field_rows = (tracer_count + 1) * layers
    head_rows = 2 * field_rows + TABLE_ROWS
    message_rows = head_rows + (freqs // 2 * dirs + 7) // 8 * 8
    slots = node_slot.reshape(1, nodes)
    params = pltpu.CompilerParams(vmem_limit_bytes=VMEM_LIMIT)
    f32 = jnp.float32

    tile, ahead, behind = pl.pallas_call(
        pack_kernel,
        out_shape=(
            jax.ShapeDtypeStruct((8, LANES), f32),
            jax.ShapeDtypeStruct((message_rows, LANES), f32),
            jax.ShapeDtypeStruct((message_rows, LANES), f32),
        ),
        in_specs=[whole_spec()] * 9,
        out_specs=(whole_spec(),) * 3,
        compiler_params=params,
        name="pack",
    )(
        spectra, tracers, potential, cell_neighbors, cell_normal, cell_weight, surface_current,
        send_rows, slots,
    )
    up = [(i, i + 1) for i in range(peers - 1)]
    down = [(j, i) for i, j in up]
    before = lax.ppermute(ahead, "mesh", up)
    after = lax.ppermute(behind, "mesh", down)

    def everywhere(one):
        copies = jnp.broadcast_to(one[None], (peers,) + one.shape)
        return lax.all_to_all(copies, "mesh", 0, 0, tiled=True)

    currents = everywhere(tile)

    spectra_new, stokes_tile = pl.pallas_call(
        wave_kernel,
        out_shape=(
            jax.ShapeDtypeStruct(spectra.shape, f32),
            jax.ShapeDtypeStruct((8, LANES), f32),
        ),
        in_specs=[whole_spec()] * 10,
        out_specs=(whole_spec(),) * 2,
        scratch_shapes=[
            pltpu.VMEM((edges, dirs, LANES), f32),
            pltpu.VMEM((8, LANES), f32),
        ],
        compiler_params=params,
        name="wave",
    )(
        spectra, before, after, currents, slots, node_neighbors, node_normal, node_weight,
        wind_velocity, send_rows,
    )

    stokes_all = everywhere(stokes_tile)

    def head_spec():
        return pl.BlockSpec((head_rows, LANES), lambda i: (0, 0))

    def full_spec(x):
        zeros = (0,) * x.ndim
        return pl.BlockSpec(x.shape, lambda i: zeros)

    rows = tracer_count * layers
    tracers_new = pl.pallas_call(
        tracer_kernel,
        grid=(1,),
        out_shape=jax.ShapeDtypeStruct(tracers.shape, f32),
        in_specs=[
            full_spec(tracers),
            full_spec(potential),
            head_spec(),
            head_spec(),
            full_spec(stokes_all),
            full_spec(cell_neighbors),
            full_spec(cell_normal),
            full_spec(cell_weight),
            full_spec(send_rows),
        ],
        out_specs=full_spec(tracers),
        scratch_shapes=[
            pltpu.VMEM((blocks + 4, field_rows, LANES), f32),
            pltpu.VMEM((blocks + 2, 8, LANES), jnp.int32),
            pltpu.VMEM((blocks + 2, 8, LANES), f32),
            pltpu.VMEM((blocks + 2, 8, LANES), f32),
            pltpu.VMEM((blocks + 2, 8, LANES), f32),
            pltpu.VMEM((blocks + 2, 8, LANES), f32),
            pltpu.VMEM((blocks + 2, edges, rows, LANES), f32),
            pltpu.VMEM((blocks + 2, rows, LANES), f32),
            pltpu.VMEM((blocks + 2, 2 * rows, LANES), f32),
        ],
        compiler_params=params,
        name="tracer",
    )(
        tracers, potential, before, after, stokes_all, cell_neighbors, cell_normal, cell_weight,
        send_rows,
    )
    return tracers_new, spectra_new


def solution(mesh):
    return jax.shard_map(
        local,
        mesh=mesh,
        in_specs=(
            P(None, None, ("groups", "mesh")),
            P(None, ("groups", "mesh")),
            P(None, ("groups", "mesh")),
            P(None, "mesh"),
            P(None, "mesh"),
            P(None, "mesh"),
            P(None, None, ("groups", "mesh")),
            P(None, ("groups", "mesh")),
            P(None, "mesh"),
            P(None, "mesh"),
            P(None, "mesh"),
            P(),
            P("mesh"),
        ),
        out_specs=(P(None, None, ("groups", "mesh")), P(None, None, ("groups", "mesh"))),
        check_vma=False,
    )
```

time: 471 us -> 53.4 us (0.11)
  local copies, waits for them, and re-layouts: 246 us -> 7.52 us
  waiting for transfers between devices: 70.4 us -> 0.01 us
  blocking collectives: 93.8 us -> 27.2 us
  other arithmetic: 26.1 us -> 0 us
  between operations: 14.9 us -> 0.75 us
  Pallas kernels: 0 us -> 13.6 us
  starting transfers between devices: 11 us -> 3.68 us
  matrix products: 5.24 us -> 0 us
    gather x28 -> x0, local copies, waits for them, and re-layouts: 226 us -> none  [the longest x2 49.2 us: antidiffusion(): beside = jnp.take(tracers_ext, neighbors, axis=2)]
    all_gather x1 -> x0, blocking collectives: 93.8 us -> none  [local(): surface_all = lax.all_gather(surface_current, 'mesh', axis=1, tiled=True)]
    reduce_scatter x1 -> x0, waiting for transfers between devices: 67.3 us -> none  [local(): lax.psum_scatter(stokes_term, 'mesh', scatter_dimension=1, tiled=True)]
    all_to_all x0 -> x2, blocking collectives: none -> 27.2 us  [everywhere(): return lax.all_to_all(copies, 'mesh', 0, 0, tiled=True)]
    pallas_call x0 -> x3, Pallas kernels: none -> 13.6 us  [the longest x1 7.99 us: local(): pl.pallas_call(wave_kernel, out_shape=(jax.ShapeDtypeStruct(spectra.shape...]
    ppermute x6 -> x2, starting transfers between devices: 11 us -> 3.68 us  [the longest x1 2.39 us: local(): before = lax.ppermute(ahead, 'mesh', up)]
    reshape x5 -> x0, local copies, waits for them, and re-layouts: 7.2 us -> none  [the longest x2 6.72 us: local(): energy_ext = joined_ext[:-2].reshape(spectra.shape[0], spectra.shape[1], -1)]
    reduce_sum x2 -> x0, other arithmetic: 5.8 us -> none  [the longest x1 5.01 us: source(): mean_energy = jnp.mean(advected, axis=(0, 1))]
  transfers between devices with their start and end apart: 7 -> 2, of which waited for: 2 -> 0; matrix products, arithmetic and copies ran while one was open for 17% -> 0% of each run, Pallas kernels for 0% -> 0%
where the time goes in v1:
time: 53.4 us; the launch traced here: 52.7 us
  blocking collectives  27.2 us (51%)
  Pallas kernels  13.6 us (25%)
  local copies, waits for them, and re-layouts  7.52 us (14%)
  starting transfers between devices  3.68 us (7%)
  between operations  0.75 us (1%)
    all_to_all x2, blocking collectives, everywhere(): return lax.all_to_all(copies, 'mesh', 0, 0, tiled=True)  27.2 us
    pallas_call x1, Pallas kernels, local(): pl.pallas_call(wave_kernel, out_shape=(jax.ShapeDtypeStruct(spectra.shape...  7.99 us
    unnamed x30, local copies, waits for them, and re-layouts  7.51 us
    pallas_call x1, Pallas kernels, local(): pl.pallas_call(tracer_kernel, grid=(1,), out_shape=jax.ShapeDtypeStruct(t...  5.4 us
    ppermute x1, starting transfers between devices, local(): before = lax.ppermute(ahead, 'mesh', up)  2.39 us
    ppermute x1, starting transfers between devices, local(): after = lax.ppermute(behind, 'mesh', down)  1.29 us
  transfers between devices with their start and end apart: 2, of which 0 were waited for; matrix products, arithmetic and copies ran while one was open for 0% of the time, Pallas kernels for 0%

profile of v1, /device:TPU:0, one launch (start us, length us, event | category | flops | bytes accessed | tf_op | source)
XLA Modules:
  0.0 52.7 jit_solution(8809112862451497131)
XLA Ops:
  0.6 0.0 copy-start.13
  0.6 0.6 %copy-done.13 = s32[128]{0:T(128)S(1)} copy-done((s32[128]{0:T(128)S(1)}, s32[128]{0:T(128)}, u32[]{:S(2)}) %copy-start.13) | copy-done | bytes 536
  1.3 0.0 copy-start
  1.3 1.2 %copy-done = f32[50,36,128]{2,1,0:T(8,128)S(1)} copy-done((f32[50,36,128]{2,1,0:T(8,128)S(1)}, f32[50,36,128]{2,1,0:T(8,128)}, u32[]{:S(2)}) %copy-start) | copy-done | bytes 921624
  2.5 0.0 copy-start.1
  2.5 0.9 %copy-done.1 = s32[16,16,16]{2,1,0:T(8,128)S(1)} copy-done((s32[16,16,16]{2,1,0:T(8,128)S(1)}, s32[16,16,16]{2,1,0:T(8,128)}, u32[]{:S(2)}) %copy-start.1) | copy-done | bytes 16408
  3.4 0.0 copy-start.2
  3.4 0.9 %copy-done.2 = f32[2,16,1024]{2,1,0:T(8,128)S(1)} copy-done((f32[2,16,1024]{2,1,0:T(8,128)S(1)}, f32[2,16,1024]{2,1,0:T(8,128)}, u32[]{:S(2)}) %copy-start.2) | copy-done | bytes 131096
  4.3 0.8 %copy-done.3 = f32[16,1024]{1,0:T(8,128)S(1)} copy-done((f32[16,1024]{1,0:T(8,128)S(1)}, f32[16,1024]{1,0:T(8,128)}, u32[]{:S(2)}) %copy-start.3) | copy-done | bytes 65560
  5.2 0.8 %copy-done.5 = s32[6,1024]{1,0:T(8,128)S(1)} copy-done((s32[6,1024]{1,0:T(8,128)S(1)}, s32[6,1024]{1,0:T(8,128)}, u32[]{:S(2)}) %copy-start.5) | copy-done | bytes 24600
  5.9 0.8 %copy-done.7 = f32[6,1024]{1,0:T(8,128)S(1)} copy-done((f32[6,1024]{1,0:T(8,128)S(1)}, f32[6,1024]{1,0:T(8,128)}, u32[]{:S(2)}) %copy-start.7) | copy-done | bytes 24600
  6.7 0.8 %copy-done.8 = f32[6,1024]{1,0:T(8,128)S(1)} copy-done((f32[6,1024]{1,0:T(8,128)S(1)}, f32[6,1024]{1,0:T(8,128)}, u32[]{:S(2)}) %copy-start.8) | copy-done | bytes 24600
  7.4 0.7 %copy-done.9 = f32[2,1024]{1,0:T(2,128)S(1)} copy-done((f32[2,1024]{1,0:T(2,128)S(1)}, f32[2,1024]{1,0:T(2,128)}, u32[]{:S(2)}) %copy-start.9) | copy-done | bytes 8216
  8.1 0.2 pack.1
  8.3 2.4 %collective-permute-start = (f32[1024,128]{1,0:T(8,128)S(1)}, f32[1024,128]{1,0:T(8,128)S(1)}, u32[]{:S(2)}, u32[]{:S(2)}) collective-permute-start(f32[1024,128]{1,0:T(8,128)S(1)} %get-tuple-element.7), channel_id=1, source_target_pairs={{0,1},{1,2},{2,3},{3,4},{4,5},{5,6},{6,7},{7,8},{8,9},{9,10},{10,1... | collective-permute-start | bytes 1572872 | tf_op jit(solution)/shard_map/ppermute | solution.py:482
  10.7 1.3 %collective-permute-start.1 = (f32[1024,128]{1,0:T(8,128)S(1)}, f32[1024,128]{1,0:T(8,128)S(1)}, u32[]{:S(2)}, u32[]{:S(2)}) collective-permute-start(f32[1024,128]{1,0:T(8,128)S(1)} %get-tuple-element.8), channel_id=1, source_target_pairs={{1,0},{2,1},{3,2},{4,3},{5,4},{6,5},{7,6},{8,7},{9,8},{10,9},{11,1... | collective-permute-start | bytes 1572872 | tf_op jit(solution)/shard_map/ppermute | solution.py:483
  12.1 0.0 copy-start.10
  12.1 0.0 copy-start.11
  12.1 0.0 copy-start.12
  12.1 0.0 copy-start.14
  12.1 16.1 %all_to_all.10.table = f32[16,8,128]{2,1,0:T(8,128)S(1)} all-to-all(f32[16,8,128]{2,1,0:T(8,128)S(1)} %broadcast_in_dim.4), channel_id=1, replica_groups=mesh['groups'=2,'mesh'=16] {'mesh'}, dimensions={0} | all-to-all | bytes 131072 | tf_op jit(solution)/shard_map/all_to_all | solution.py:487
  28.2 0.0 collective-permute-done.before
  28.2 0.0 collective-permute-done.1.after
  28.2 0.0 copy-done.10
  28.2 0.0 copy-done.11
  28.2 0.0 copy-done.12
  28.2 0.0 copy-done.14
  28.2 8.0 %wave.1 = (f32[50,36,128]{2,1,0:T(8,128)}, f32[8,128]{1,0:T(8,128)S(1)}) custom-call(f32[50,36,128]{2,1,0:T(8,128)S(1)} %copy-done, f32[1024,128]{1,0:T(8,128)S(1)} %collective-permute-done.before, f32[1024,128]{1,0:T(8,128)S(1)} %collective-permute-done.1.after, f32[16,8,128]{2,1,0:T(8,128)S(1)} %all_to_all.10.table, s32[1,128]{1,0:T(1,128)S(1)} %bitcast.2, ...), custom_call_target="tpu_custom_call" | custom-call | tf_op jit(solution)/shard_map/wave/pallas_call | solution.py:491
  36.3 11.1 %all_to_all.11.table = f32[16,8,128]{2,1,0:T(8,128)S(1)} all-to-all(f32[16,8,128]{2,1,0:T(8,128)S(1)} %broadcast_in_dim.5), channel_id=1, replica_groups=mesh['groups'=2,'mesh'=16] {'mesh'}, dimensions={0} | all-to-all | bytes 131072 | tf_op jit(solution)/shard_map/all_to_all | solution.py:487
  47.3 0.0 copy-done.4
  47.3 0.0 copy-done.6
  47.3 5.4 %tracer.1 = f32[2,16,1024]{2,1,0:T(8,128)} custom-call(f32[2,16,1024]{2,1,0:T(8,128)S(1)} %copy-done.2, f32[16,1024]{1,0:T(8,128)S(1)} %copy-done.4, f32[1024,128]{1,0:T(8,128)S(1)} %collective-permute-done.before, f32[1024,128]{1,0:T(8,128)S(1)} %collective-permute-done.1.after, f32[16,8,128]{2,1,0:T(8,128)S(1)} %all_to_all.11.table, ...), custom_call_target="tpu_custom_call" | custom-call | tf_op jit(solution)/shard_map/tracer/pallas_call | solution.py:520
  (9 shorter events, 0.0 us)
Async XLA Ops:
  0.6 0.7 %copy-start.13 = (s32[128]{0:T(128)S(1)}, s32[128]{0:T(128)}, u32[]{:S(2)}) copy-start(s32[128]{0:T(128)} %param.25) | copy-start | bytes 1540
  1.3 1.2 %copy-start = (f32[50,36,128]{2,1,0:T(8,128)S(1)}, f32[50,36,128]{2,1,0:T(8,128)}, u32[]{:S(2)}) copy-start(f32[50,36,128]{2,1,0:T(8,128)} %spectra.3) | copy-start | bytes 2764804
  2.5 0.9 %copy-start.1 = (s32[16,16,16]{2,1,0:T(8,128)S(1)}, s32[16,16,16]{2,1,0:T(8,128)}, u32[]{:S(2)}) copy-start(s32[16,16,16]{2,1,0:T(8,128)} %send_rows.5) | copy-start | bytes 49156
  3.4 0.9 %copy-start.2 = (f32[2,16,1024]{2,1,0:T(8,128)S(1)}, f32[2,16,1024]{2,1,0:T(8,128)}, u32[]{:S(2)}) copy-start(f32[2,16,1024]{2,1,0:T(8,128)} %tracers.3) | copy-start | bytes 393220
  4.3 0.8 %copy-start.3 = (f32[16,1024]{1,0:T(8,128)S(1)}, f32[16,1024]{1,0:T(8,128)}, u32[]{:S(2)}) copy-start(f32[16,1024]{1,0:T(8,128)} %potential.3) | copy-start | bytes 196612
  5.2 0.8 %copy-start.5 = (s32[6,1024]{1,0:T(8,128)S(1)}, s32[6,1024]{1,0:T(8,128)}, u32[]{:S(2)}) copy-start(s32[6,1024]{1,0:T(8,128)} %neighbors.5) | copy-start | bytes 73732
  5.9 0.8 %copy-start.7 = (f32[6,1024]{1,0:T(8,128)S(1)}, f32[6,1024]{1,0:T(8,128)}, u32[]{:S(2)}) copy-start(f32[6,1024]{1,0:T(8,128)} %normal.5) | copy-start | bytes 73732
  6.7 0.8 %copy-start.8 = (f32[6,1024]{1,0:T(8,128)S(1)}, f32[6,1024]{1,0:T(8,128)}, u32[]{:S(2)}) copy-start(f32[6,1024]{1,0:T(8,128)} %weight.5) | copy-start | bytes 73732
  7.4 0.7 %copy-start.9 = (f32[2,1024]{1,0:T(2,128)S(1)}, f32[2,1024]{1,0:T(2,128)}, u32[]{:S(2)}) copy-start(f32[2,1024]{1,0:T(2,128)} %current.1) | copy-start | bytes 24580
  8.3 19.9 %collective-permute-start = (f32[1024,128]{1,0:T(8,128)S(1)}, f32[1024,128]{1,0:T(8,128)S(1)}, u32[]{:S(2)}, u32[]{:S(2)}) collective-permute-start(f32[1024,128]{1,0:T(8,128)S(1)} %get-tuple-element.7), channel_id=1, source_target_pairs={{0,1},{1,2},{2,3},{3,4},{4,5},{5,6},{6,7},{7,8},{8,9},{9,10},{10,1... | collective-permute-start | bytes 1572872 | tf_op jit(solution)/shard_map/ppermute | solution.py:482
  10.7 17.5 %collective-permute-start.1 = (f32[1024,128]{1,0:T(8,128)S(1)}, f32[1024,128]{1,0:T(8,128)S(1)}, u32[]{:S(2)}, u32[]{:S(2)}) collective-permute-start(f32[1024,128]{1,0:T(8,128)S(1)} %get-tuple-element.8), channel_id=1, source_target_pairs={{1,0},{2,1},{3,2},{4,3},{5,4},{6,5},{7,6},{8,7},{9,8},{10,9},{11,1... | collective-permute-start | bytes 1572872 | tf_op jit(solution)/shard_map/ppermute | solution.py:483
  12.1 16.2 %copy-start.10 = (s32[6,128]{1,0:T(8,128)S(1)}, s32[6,128]{1,0:T(8,128)}, u32[]{:S(2)}) copy-start(s32[6,128]{1,0:T(8,128)} %neighbors.4) | copy-start | bytes 9220
  12.1 16.1 %copy-start.11 = (f32[6,128]{1,0:T(8,128)S(1)}, f32[6,128]{1,0:T(8,128)}, u32[]{:S(2)}) copy-start(f32[6,128]{1,0:T(8,128)} %normal.4) | copy-start | bytes 9220
  12.1 16.1 %copy-start.12 = (f32[6,128]{1,0:T(8,128)S(1)}, f32[6,128]{1,0:T(8,128)}, u32[]{:S(2)}) copy-start(f32[6,128]{1,0:T(8,128)} %weight.4) | copy-start | bytes 9220
  12.1 16.1 %copy-start.14 = (f32[2,128]{1,0:T(2,128)S(1)}, f32[2,128]{1,0:T(2,128)}, u32[]{:S(2)}) copy-start(f32[2,128]{1,0:T(2,128)} %wind.1) | copy-start | bytes 3076
  36.2 11.1 %copy-start.4 = (f32[16,1024]{1,0:T(8,128)S(1)}, f32[16,1024]{1,0:T(8,128)}, u32[]{:S(2)}) copy-start(f32[16,1024]{1,0:T(8,128)} %potential.3) | copy-start | bytes 196612
  36.2 11.1 %copy-start.6 = (s32[6,1024]{1,0:T(8,128)S(1)}, s32[6,1024]{1,0:T(8,128)}, u32[]{:S(2)}) copy-start(s32[6,1024]{1,0:T(8,128)} %neighbors.5) | copy-start | bytes 73732

commit v2 on v1

--- a/solution.py
+++ b/solution.py
@@ -29,9 +29,8 @@
     return lax.broadcasted_iota(jnp.int32, (rows, LANES), 0)
 
 
-def slot_rows(send_rows, block):
-    peers, capacity = send_rows.shape[1:]
-    entry = send_rows[block]
+def slot_rows(entry):
+    peers, capacity = entry.shape
     wide = jnp.concatenate([entry, jnp.zeros((peers, LANES - capacity), jnp.int32)], axis=1)
     wide = lane_gather(wide, lane_iota(peers) % capacity)
     owner = row_iota(peers)
@@ -43,11 +42,35 @@
     return out
 
 
+def half_mask(rows, lower):
+    half = lane_iota(rows) // (LANES // 2)
+    return half == jnp.where(lower, 0, 1)
+
+
 def pack_kernel(
-    spectra, tracers, potential, neighbors, normal, weight, current, send_rows, node_slot,
-    tile, ahead, behind,
+    spectra_in, tracers_in, potential_in, neighbors_in, normal_in, weight_in, current_in,
+    send_rows, slot_in,
+    tile, outer, inner, spectra,
+    tracers, potential, neighbors, normal, weight, current, own_rows, node_slot, sems,
 ):
     me = lax.axis_index("mesh")
+    copies = []
+    for source, target in (
+        (send_rows.at[me], own_rows),
+        (current_in, current),
+        (slot_in, node_slot),
+        (spectra_in, spectra),
+        (tracers_in, tracers),
+        (potential_in, potential),
+        (neighbors_in, neighbors),
+        (normal_in, normal),
+        (weight_in, weight),
+    ):
+        copy = pltpu.make_async_copy(source, target, sems.at[len(copies)])
+        copy.start()
+        copies.append(copy)
+    for copy in copies[:3]:
+        copy.wait()
     freqs, dirs = spectra.shape[:2]
     layers, cells = potential.shape
     blocks = cells // LANES
@@ -56,7 +79,7 @@
         [current[:, b * LANES : (b + 1) * LANES] for b in range(blocks)], axis=0
     )
     place = row_iota(2 * blocks)
-    halves = slot_rows(send_rows, me)
+    halves = slot_rows(own_rows[...])
     tile[...] = jnp.zeros(tile.shape, jnp.float32)
     for half, cell in enumerate(halves):
         found = lane_gather(stacked, spread(cell % LANES, 2 * blocks))
@@ -66,41 +89,50 @@
             tile[row : row + 1, :] = jnp.sum(picked, axis=0, keepdims=True)
     row = 2 * len(halves)
     tile[row : row + 1, :] = node_slot[...].astype(jnp.float32)
-    for out, first in ((ahead, blocks - 2), (behind, 0)):
+    for copy in copies[3:]:
+        copy.wait()
+    odd = me % 2 == 1
+    for out, upward in ((outer, odd), (inner, jnp.logical_not(odd))):
         for b in range(2):
-            lanes = slice((first + b) * LANES, (first + b + 1) * LANES)
+            high = slice((blocks - 2 + b) * LANES, (blocks - 1 + b) * LANES)
+            low = slice(b * LANES, (b + 1) * LANES)
             base = b * field_rows
             for t in range(tracers.shape[0]):
-                out[base + t * layers : base + (t + 1) * layers, :] = tracers[t, :, lanes]
-            out[base + field_rows - layers : base + field_rows, :] = potential[:, lanes]
-    for out, b in ((ahead, blocks - 1), (behind, 0)):
-        lanes = slice(b * LANES, (b + 1) * LANES)
+                out[base + t * layers : base + (t + 1) * layers, :] = jnp.where(
+                    upward, tracers[t, :, high], tracers[t, :, low]
+                )
+            out[base + field_rows - layers : base + field_rows, :] = jnp.where(
+                upward, potential[:, high], potential[:, low]
+            )
+        high = slice((blocks - 1) * LANES, blocks * LANES)
+        low = slice(0, LANES)
         base = 2 * field_rows
         out[base : base + TABLE_ROWS, :] = jnp.zeros((TABLE_ROWS, LANES), jnp.float32)
         edges = neighbors.shape[0]
-        out[base : base + edges, :] = neighbors[:, lanes].astype(jnp.float32)
-        out[base + 8 : base + 8 + edges, :] = normal[:, lanes]
-        out[base + 16 : base + 16 + edges, :] = weight[:, lanes]
+        near = jnp.where(upward, neighbors[:, high], neighbors[:, low])
+        out[base : base + edges, :] = near.astype(jnp.float32)
+        out[base + 8 : base + 8 + edges, :] = jnp.where(upward, normal[:, high], normal[:, low])
+        out[base + 16 : base + 16 + edges, :] = jnp.where(upward, weight[:, high], weight[:, low])
     base = 2 * field_rows + TABLE_ROWS
     pairs = freqs // 2
     whole = dirs // 8 * 8
     rest = dirs - whole
-    low = lane_iota(dirs) < LANES // 2
+    turns = half_mask(dirs, odd)
     for g in range(pairs):
         natural = spectra[g]
         turned = pltpu.roll(spectra[g + pairs], LANES // 2, 1)
         for out, mixed in (
-            (ahead, jnp.where(low, turned, natural)),
-            (behind, jnp.where(low, natural, turned)),
+            (outer, jnp.where(turns, turned, natural)),
+            (inner, jnp.where(turns, natural, turned)),
         ):
             at = base + g * whole
             out[at : at + whole, :] = mixed[:whole]
             at = base + pairs * whole + g * rest
             out[at : at + rest, :] = mixed[whole:]
     at = base + pairs * dirs
-    if at < ahead.shape[0]:
-        for out in (ahead, behind):
-            out[at:, :] = jnp.zeros((ahead.shape[0] - at, LANES), jnp.float32)
+    if at < outer.shape[0]:
+        for out in (outer, inner):
+            out[at:, :] = jnp.zeros((outer.shape[0] - at, LANES), jnp.float32)
 
 
 def node_currents(table, slot, block, capacity):
@@ -125,7 +157,7 @@
 
 
 def wave_kernel(
-    spectra, before, after, table, node_slot, neighbors, normal, weight, wind, send_rows,
+    spectra, outer, inner, table, node_slot, neighbors, normal, weight, wind, send_rows,
     spectra_new, tile, project, drift,
 ):
     me = lax.axis_index("mesh")
@@ -136,7 +168,7 @@
     pairs = freqs // 2
     whole = dirs // 8 * 8
     rest = dirs - whole
-    base = before.shape[0] - (pairs * dirs + 7) // 8 * 8
+    base = outer.shape[0] - (pairs * dirs + 7) // 8 * 8
     low1 = lane_iota(1) < LANES // 2
 
     slot = node_slot[...]
@@ -176,7 +208,7 @@
     for s in range(edges):
         project[s] = cos_dir * cosine[s : s + 1] + sin_dir * sine[s : s + 1]
 
-    low = lane_iota(dirs) < LANES // 2
+    from_outer = half_mask(dirs, me % 2 == 1)
     straight = [spread(lane[s : s + 1], dirs) for s in range(edges)]
     swapped = [spread((lane[s : s + 1] + LANES // 2) % LANES, dirs) for s in range(edges)]
     within = [spread(target[s : s + 1] // LANES, dirs) == me for s in range(edges)]
@@ -186,15 +218,15 @@
     def pair(g, carry):
         speed, total = carry
         halo_parts = []
-        for message in (before, after):
+        for message in (outer, inner):
             at = pl.multiple_of(base + g * whole, 8)
             upper = message[pl.ds(at, whole), :]
             lower = message[pl.ds(base + pairs * whole + g * rest, rest), :]
             halo_parts.append(jnp.concatenate([upper, lower], axis=0))
-        b, a = halo_parts
+        x, y = halo_parts
         for f, group_speed, halo, halo_lane in (
-            (g, speed, jnp.where(low, a, b), straight),
-            (g + pairs, speed * jump, jnp.where(low, b, a), swapped),
+            (g, speed, jnp.where(from_outer, x, y), straight),
+            (g + pairs, speed * jump, jnp.where(from_outer, y, x), swapped),
         ):
             own = spectra[f]
             out_speed = jnp.zeros((dirs, LANES), jnp.float32)
@@ -260,7 +292,7 @@
 
 
 def tracer_kernel(
-    tracers, potential, before, after, table, neighbors, normal, weight, send_rows,
+    tracers, potential, outer, inner, table, neighbors, normal, weight, send_rows,
     tracers_new, fields, target, cosine, sine, scale, stokes, antiflux, lowered, ratios,
 ):
     me = lax.axis_index("mesh")
@@ -274,9 +306,12 @@
     layer_groups = layers // 8
     tracer_groups = tracer_count * layer_groups
 
+    odd = me % 2 == 1
     for b in range(2):
-        fields[b] = before[b * field_rows : (b + 1) * field_rows, :]
-        fields[blocks + 2 + b] = after[b * field_rows : (b + 1) * field_rows, :]
+        x = outer[b * field_rows : (b + 1) * field_rows, :]
+        y = inner[b * field_rows : (b + 1) * field_rows, :]
+        fields[b] = jnp.where(odd, y, x)
+        fields[blocks + 2 + b] = jnp.where(odd, x, y)
     for b in range(blocks):
         lanes = slice(b * LANES, (b + 1) * LANES)
         for t in range(tracer_count):
@@ -285,10 +320,12 @@
     at = 2 * field_rows
     for b in range(blocks + 2):
         if b == 0 or b == blocks + 1:
-            message = before if b == 0 else after
-            near = message[at : at + edges, :].astype(jnp.int32)
-            angle = message[at + 8 : at + 8 + edges, :]
-            w = message[at + 16 : at + 16 + edges, :]
+            x = outer[at : at + TABLE_ROWS, :]
+            y = inner[at : at + TABLE_ROWS, :]
+            table_rows = jnp.where(odd, y, x) if b == 0 else jnp.where(odd, x, y)
+            near = table_rows[0:edges].astype(jnp.int32)
+            angle = table_rows[8 : 8 + edges]
+            w = table_rows[16 : 16 + edges]
         else:
             lanes = slice((b - 1) * LANES, b * LANES)
             near = neighbors[:, lanes]
@@ -304,7 +341,7 @@
     per_row = LANES // capacity
     for which in range(3):
         block = jnp.clip(me + which - 1, 0, peers - 1)
-        cell = slot_rows(send_rows, block)
+        cell = slot_rows(send_rows[block])
         first = block * capacity
         pick = (first % LANES) + lane8 % capacity
         found = [jnp.zeros((8, LANES), jnp.float32) for _ in range(halves)]
@@ -431,6 +468,13 @@
     lax.fori_loop(0, blocks, limit, 0)
 
 
+def swap(message, first, peers):
+    pairs = []
+    for i in range(first, peers - 1, 2):
+        pairs += [(i, i + 1), (i + 1, i)]
+    return lax.ppermute(message, "mesh", pairs)
+
+
 def whole_spec():
     return pl.BlockSpec(memory_space=pltpu.VMEM)
 
@@ -462,25 +506,41 @@
     params = pltpu.CompilerParams(vmem_limit_bytes=VMEM_LIMIT)
     f32 = jnp.float32
 
-    tile, ahead, behind = pl.pallas_call(
+    stored = pl.BlockSpec(memory_space=pltpu.HBM)
+    tile, outer, inner, own_spectra = pl.pallas_call(
         pack_kernel,
         out_shape=(
             jax.ShapeDtypeStruct((8, LANES), f32),
             jax.ShapeDtypeStruct((message_rows, LANES), f32),
             jax.ShapeDtypeStruct((message_rows, LANES), f32),
+            jax.ShapeDtypeStruct(spectra.shape, f32),
         ),
-        in_specs=[whole_spec()] * 9,
-        out_specs=(whole_spec(),) * 3,
+        in_specs=[stored] * 9,
+        out_specs=(whole_spec(),) * 4,
+        scratch_shapes=[
+            pltpu.VMEM(tracers.shape, f32),
+            pltpu.VMEM(potential.shape, f32),
+            pltpu.VMEM(cell_neighbors.shape, jnp.int32),
+            pltpu.VMEM(cell_normal.shape, f32),
+            pltpu.VMEM(cell_weight.shape, f32),
+            pltpu.VMEM(surface_current.shape, f32),
+            pltpu.VMEM(send_rows.shape[1:], jnp.int32),
+            pltpu.VMEM(slots.shape, jnp.int32),
+            pltpu.SemaphoreType.DMA((9,)),
+        ],
         compiler_params=params,
         name="pack",
     )(
-        spectra, tracers, potential, cell_neighbors, cell_normal, cell_weight, surface_current,
-        send_rows, slots,
-    )
-    up = [(i, i + 1) for i in range(peers - 1)]
-    down = [(j, i) for i, j in up]
-    before = lax.ppermute(ahead, "mesh", up)
-    after = lax.ppermute(behind, "mesh", down)
+        *(
+            pltpu.with_memory_space_constraint(x, pltpu.HBM)
+            for x in (
+                spectra, tracers, potential, cell_neighbors, cell_normal, cell_weight,
+                surface_current, send_rows, slots,
+            )
+        )
+    )
+    outer = swap(outer, 1, peers)
+    inner = swap(inner, 0, peers)
 
     def everywhere(one):
         copies = jnp.broadcast_to(one[None], (peers,) + one.shape)
@@ -503,7 +563,7 @@
         compiler_params=params,
         name="wave",
     )(
-        spectra, before, after, currents, slots, node_neighbors, node_normal, node_weight,
+        own_spectra, outer, inner, currents, slots, node_neighbors, node_normal, node_weight,
         wind_velocity, send_rows,
     )
 
@@ -547,7 +607,7 @@
         compiler_params=params,
         name="tracer",
     )(
-        tracers, potential, before, after, stokes_all, cell_neighbors, cell_normal, cell_weight,
+        tracers, potential, outer, inner, stokes_all, cell_neighbors, cell_normal, cell_weight,
         send_rows,
     )
     return tracers_new, spectra_new

time: 53.4 us -> 46.9 us (0.88)
  local copies, waits for them, and re-layouts: 7.52 us -> 0.69 us
  blocking collectives: 27.2 us -> 25 us
  starting transfers between devices: 3.68 us -> 5.19 us
  Pallas kernels: 13.6 us -> 14.9 us
    unnamed x30 -> x22, local copies, waits for them, and re-layouts: 7.51 us -> 0.68 us
    all_to_all x2, blocking collectives: 27.2 us -> 25 us  [everywhere(): return lax.all_to_all(copies, 'mesh', 0, 0, tiled=True)]
    ppermute x2, starting transfers between devices: 3.68 us -> 5.19 us  [swap(): return lax.ppermute(message, 'mesh', pairs)]
    pallas_call x1, Pallas kernels: 0.21 us -> 1.53 us  [local(): pl.pallas_call(pack_kernel, out_shape=(jax.ShapeDtypeStruct((8, LANES), f...]
where the time goes in v2:
time: 46.9 us; the launch traced here: 46.6 us
  blocking collectives  25 us (53%)
  Pallas kernels  14.9 us (32%)
  starting transfers between devices  5.19 us (11%)
  between operations  0.74 us (2%)
  local copies, waits for them, and re-layouts  0.69 us (1%)
    all_to_all x2, blocking collectives, everywhere(): return lax.all_to_all(copies, 'mesh', 0, 0, tiled=True)  25 us
    pallas_call x1, Pallas kernels, local(): pl.pallas_call(wave_kernel, out_shape=(jax.ShapeDtypeStruct(spectra.shape...  8.01 us
    pallas_call x1, Pallas kernels, local(): pl.pallas_call(tracer_kernel, grid=(1,), out_shape=jax.ShapeDtypeStruct(t...  5.41 us
    ppermute x2, starting transfers between devices, swap(): return lax.ppermute(message, 'mesh', pairs)  5.19 us
    pallas_call x1, Pallas kernels, local(): pl.pallas_call(pack_kernel, out_shape=(jax.ShapeDtypeStruct((8, LANES), f...  1.53 us
  transfers between devices with their start and end apart: 2, of which 0 were waited for; matrix products, arithmetic and copies ran while one was open for 0% of the time, Pallas kernels for 0%

profile of v2, /device:TPU:0, one launch (start us, length us, event | category | flops | bytes accessed | tf_op | source)
XLA Modules:
  0.0 46.6 jit_solution(15015721376366406411)
XLA Ops:
  0.6 1.5 %pack.1 = (f32[8,128]{1,0:T(8,128)S(1)}, f32[1024,128]{1,0:T(8,128)S(1)}, f32[1024,128]{1,0:T(8,128)S(1)}, f32[50,36,128]{2,1,0:T(8,128)S(1)}) custom-call(f32[50,36,128]{2,1,0:T(8,128)} %spectra_in.1, f32[2,16,1024]{2,1,0:T(8,128)} %tracers.1, f32[16,1024]{1,0:T(8,128)} %potential.1, s32[6,1024]{1,0:T(8,128)} %neighbors.3, f32[6,1024]{1,0:T(8,128)} %normal.3, ...), custom_call_target="tpu_custom_call" | custom-call | tf_op jit(solution)/shard_map/pack/pallas_call | solution.py:510
  2.2 0.0 copy-start
  2.2 0.8 %collective-permute-start = (f32[1024,128]{1,0:T(8,128)S(1)}, f32[1024,128]{1,0:T(8,128)S(1)}, u32[]{:S(2)}, u32[]{:S(2)}) collective-permute-start(f32[1024,128]{1,0:T(8,128)S(1)} %get-tuple-element.8), channel_id=1, source_target_pairs={{1,2},{2,1},{3,4},{4,3},{5,6},{6,5},{7,8},{8,7},{9,10},{10,9},{11,... | collective-permute-start | bytes 1572872 | tf_op jit(solution)/shard_map/ppermute | solution.py:475
  3.0 4.4 %collective-permute-start.1 = (f32[1024,128]{1,0:T(8,128)S(1)}, f32[1024,128]{1,0:T(8,128)S(1)}, u32[]{:S(2)}, u32[]{:S(2)}) collective-permute-start(f32[1024,128]{1,0:T(8,128)S(1)} %get-tuple-element.9), channel_id=1, source_target_pairs={{0,1},{1,0},{2,3},{3,2},{4,5},{5,4},{6,7},{7,6},{8,9},{9,8},{10,11... | collective-permute-start | bytes 1572872 | tf_op jit(solution)/shard_map/ppermute | solution.py:475
  7.4 0.0 copy-start.6
  7.4 0.0 copy-start.7
  7.4 0.0 copy-start.8
  7.4 11.8 %all_to_all.10.table = f32[16,8,128]{2,1,0:T(8,128)S(1)} all-to-all(f32[16,8,128]{2,1,0:T(8,128)S(1)} %broadcast_in_dim.4), channel_id=1, replica_groups=mesh['groups'=2,'mesh'=16] {'mesh'}, dimensions={0} | all-to-all | bytes 131072 | tf_op jit(solution)/shard_map/all_to_all | solution.py:547
  19.2 0.0 copy-start.9
  19.2 0.0 copy-start.10
  19.2 0.0 collective-permute-done.outer
  19.2 0.0 collective-permute-done.1.inner
  19.2 0.0 copy-done
  19.2 0.0 copy-done.6
  19.2 0.0 copy-done.7
  19.3 0.0 copy-done.8
  19.3 0.6 %copy-done.9 = s32[128]{0:T(128)S(1)} copy-done((s32[128]{0:T(128)S(1)}, s32[128]{0:T(128)}, u32[]{:S(2)}) %copy-start.9) | copy-done | bytes 536
  19.9 0.0 copy-done.10
  19.9 0.0 copy-start.3
  19.9 0.0 copy-start.4
  19.9 0.0 copy-start.5
  19.9 8.0 %wave.1 = (f32[50,36,128]{2,1,0:T(8,128)}, f32[8,128]{1,0:T(8,128)S(1)}) custom-call(f32[50,36,128]{2,1,0:T(8,128)S(1)} %get-tuple-element.10.spectra, f32[1024,128]{1,0:T(8,128)S(1)} %collective-permute-done.outer, f32[1024,128]{1,0:T(8,128)S(1)} %collective-permute-done.1.inner, f32[16,8,128]{2,1,0:T(8,128)S(1)} %all_to_all.10.table, ...), custom_call_target="tpu_custom_call" | custom-call | tf_op jit(solution)/shard_map/wave/pallas_call | solution.py:551
  27.9 0.0 copy-start.1
  27.9 0.0 copy-start.2
  27.9 13.2 %all_to_all.11.table = f32[16,8,128]{2,1,0:T(8,128)S(1)} all-to-all(f32[16,8,128]{2,1,0:T(8,128)S(1)} %broadcast_in_dim.5), channel_id=1, replica_groups=mesh['groups'=2,'mesh'=16] {'mesh'}, dimensions={0} | all-to-all | bytes 131072 | tf_op jit(solution)/shard_map/all_to_all | solution.py:547
  41.2 0.0 copy-done.3
  41.2 0.0 copy-done.4
  41.2 0.0 copy-done.5
  41.2 0.0 copy-done.1
  41.2 0.0 copy-done.2
  41.2 5.4 %tracer.1 = f32[2,16,1024]{2,1,0:T(8,128)} custom-call(f32[2,16,1024]{2,1,0:T(8,128)S(1)} %copy-done.1, f32[16,1024]{1,0:T(8,128)S(1)} %copy-done.2, f32[1024,128]{1,0:T(8,128)S(1)} %collective-permute-done.outer, f32[1024,128]{1,0:T(8,128)S(1)} %collective-permute-done.1.inner, f32[16,8,128]{2,1,0:T(8,128)S(1)} %all_to_all.11.table, ...), custom_call_target="tpu_custom_call" | custom-call | tf_op jit(solution)/shard_map/tracer/pallas_call | solution.py:580
  (2 shorter events, 0.0 us)
Async XLA Ops:
  2.2 17.1 %copy-start = (s32[16,16,16]{2,1,0:T(8,128)S(1)}, s32[16,16,16]{2,1,0:T(8,128)}, u32[]{:S(2)}) copy-start(s32[16,16,16]{2,1,0:T(8,128)} %send_rows.5) | copy-start | bytes 49156
  2.2 17.0 %collective-permute-start = (f32[1024,128]{1,0:T(8,128)S(1)}, f32[1024,128]{1,0:T(8,128)S(1)}, u32[]{:S(2)}, u32[]{:S(2)}) collective-permute-start(f32[1024,128]{1,0:T(8,128)S(1)} %get-tuple-element.8), channel_id=1, source_target_pairs={{1,2},{2,1},{3,4},{4,3},{5,6},{6,5},{7,8},{8,7},{9,10},{10,9},{11,... | collective-permute-start | bytes 1572872 | tf_op jit(solution)/shard_map/ppermute | solution.py:475
  3.0 16.2 %collective-permute-start.1 = (f32[1024,128]{1,0:T(8,128)S(1)}, f32[1024,128]{1,0:T(8,128)S(1)}, u32[]{:S(2)}, u32[]{:S(2)}) collective-permute-start(f32[1024,128]{1,0:T(8,128)S(1)} %get-tuple-element.9), channel_id=1, source_target_pairs={{0,1},{1,0},{2,3},{3,2},{4,5},{5,4},{6,7},{7,6},{8,9},{9,8},{10,11... | collective-permute-start | bytes 1572872 | tf_op jit(solution)/shard_map/ppermute | solution.py:475
  7.4 11.9 %copy-start.6 = (s32[6,128]{1,0:T(8,128)S(1)}, s32[6,128]{1,0:T(8,128)}, u32[]{:S(2)}) copy-start(s32[6,128]{1,0:T(8,128)} %neighbors.2) | copy-start | bytes 9220
  7.4 11.9 %copy-start.7 = (f32[6,128]{1,0:T(8,128)S(1)}, f32[6,128]{1,0:T(8,128)}, u32[]{:S(2)}) copy-start(f32[6,128]{1,0:T(8,128)} %normal.2) | copy-start | bytes 9220
  7.4 11.9 %copy-start.8 = (f32[6,128]{1,0:T(8,128)S(1)}, f32[6,128]{1,0:T(8,128)}, u32[]{:S(2)}) copy-start(f32[6,128]{1,0:T(8,128)} %weight.2) | copy-start | bytes 9220
  19.2 0.7 %copy-start.9 = (s32[128]{0:T(128)S(1)}, s32[128]{0:T(128)}, u32[]{:S(2)}) copy-start(s32[128]{0:T(128)} %param.25) | copy-start | bytes 1540
  19.2 0.7 %copy-start.10 = (f32[2,128]{1,0:T(2,128)S(1)}, f32[2,128]{1,0:T(2,128)}, u32[]{:S(2)}) copy-start(f32[2,128]{1,0:T(2,128)} %wind.1) | copy-start | bytes 3076
  19.9 21.2 %copy-start.3 = (s32[6,1024]{1,0:T(8,128)S(1)}, s32[6,1024]{1,0:T(8,128)}, u32[]{:S(2)}) copy-start(s32[6,1024]{1,0:T(8,128)} %neighbors.3) | copy-start | bytes 73732
  19.9 21.2 %copy-start.4 = (f32[6,1024]{1,0:T(8,128)S(1)}, f32[6,1024]{1,0:T(8,128)}, u32[]{:S(2)}) copy-start(f32[6,1024]{1,0:T(8,128)} %normal.3) | copy-start | bytes 73732
  19.9 21.2 %copy-start.5 = (f32[6,1024]{1,0:T(8,128)S(1)}, f32[6,1024]{1,0:T(8,128)}, u32[]{:S(2)}) copy-start(f32[6,1024]{1,0:T(8,128)} %weight.3) | copy-start | bytes 73732
  27.9 13.2 %copy-start.1 = (f32[2,16,1024]{2,1,0:T(8,128)S(1)}, f32[2,16,1024]{2,1,0:T(8,128)}, u32[]{:S(2)}) copy-start(f32[2,16,1024]{2,1,0:T(8,128)} %tracers.1) | copy-start | bytes 393220
  27.9 13.2 %copy-start.2 = (f32[16,1024]{1,0:T(8,128)S(1)}, f32[16,1024]{1,0:T(8,128)}, u32[]{:S(2)}) copy-start(f32[16,1024]{1,0:T(8,128)} %potential.1) | copy-start | bytes 196612

commit v3 on v2

--- a/solution.py
+++ b/solution.py
@@ -543,8 +543,7 @@
     inner = swap(inner, 0, peers)
 
     def everywhere(one):
-        copies = jnp.broadcast_to(one[None], (peers,) + one.shape)
-        return lax.all_to_all(copies, "mesh", 0, 0, tiled=True)
+        return lax.all_gather(one, "mesh")
 
     currents = everywhere(tile)
 

time: 46.9 us -> 65.5 us (1.40)
  blocking collectives: 25 us -> 43.8 us
    all_gather x0 -> x2, blocking collectives: none -> 43.8 us  [everywhere(): return lax.all_gather(one, 'mesh')]
    all_to_all x2 -> x0, blocking collectives: 25 us -> none  [everywhere(): return lax.all_to_all(copies, 'mesh', 0, 0, tiled=True)]
where the time goes in v3:
time: 65.5 us; the launch traced here: 65.3 us
  blocking collectives  43.8 us (67%)
  Pallas kernels  15 us (23%)
  starting transfers between devices  5.06 us (8%)
  between operations  0.72 us (1%)
  local copies, waits for them, and re-layouts  0.68 us (1%)
    all_gather x2, blocking collectives, everywhere(): return lax.all_gather(one, 'mesh')  43.8 us
    pallas_call x1, Pallas kernels, local(): pl.pallas_call(wave_kernel, out_shape=(jax.ShapeDtypeStruct(spectra.shape...  8.01 us
    pallas_call x1, Pallas kernels, local(): pl.pallas_call(tracer_kernel, grid=(1,), out_shape=jax.ShapeDtypeStruct(t...  5.42 us
    ppermute x2, starting transfers between devices, swap(): return lax.ppermute(message, 'mesh', pairs)  5.06 us
    pallas_call x1, Pallas kernels, local(): pl.pallas_call(pack_kernel, out_shape=(jax.ShapeDtypeStruct((8, LANES), f...  1.56 us
  transfers between devices with their start and end apart: 2, of which 0 were waited for; matrix products, arithmetic and copies ran while one was open for 0% of the time, Pallas kernels for 0%

profile of v3, /device:TPU:0, one launch (start us, length us, event | category | flops | bytes accessed | tf_op | source)
XLA Modules:
  0.0 65.3 jit_solution(14888057103140008649)
XLA Ops:
  0.6 0.0 copy-start
  0.6 1.6 %pack.1 = (f32[8,128]{1,0:T(8,128)S(1)}, f32[1024,128]{1,0:T(8,128)S(1)}, f32[1024,128]{1,0:T(8,128)S(1)}, f32[50,36,128]{2,1,0:T(8,128)S(1)}) custom-call(f32[50,36,128]{2,1,0:T(8,128)} %spectra_in.1, f32[2,16,1024]{2,1,0:T(8,128)} %tracers.1, f32[16,1024]{1,0:T(8,128)} %potential.1, s32[6,1024]{1,0:T(8,128)} %neighbors.3, f32[6,1024]{1,0:T(8,128)} %normal.3, ...), custom_call_target="tpu_custom_call" | custom-call | tf_op jit(solution)/shard_map/pack/pallas_call | solution.py:510
  2.2 0.7 %collective-permute-start = (f32[1024,128]{1,0:T(8,128)S(1)}, f32[1024,128]{1,0:T(8,128)S(1)}, u32[]{:S(2)}, u32[]{:S(2)}) collective-permute-start(f32[1024,128]{1,0:T(8,128)S(1)} %get-tuple-element.8), channel_id=1, source_target_pairs={{1,2},{2,1},{3,4},{4,3},{5,6},{6,5},{7,8},{8,7},{9,10},{10,9},{11,... | collective-permute-start | bytes 1572872 | tf_op jit(solution)/shard_map/ppermute | solution.py:475
  2.9 4.4 %collective-permute-start.1 = (f32[1024,128]{1,0:T(8,128)S(1)}, f32[1024,128]{1,0:T(8,128)S(1)}, u32[]{:S(2)}, u32[]{:S(2)}) collective-permute-start(f32[1024,128]{1,0:T(8,128)S(1)} %get-tuple-element.9), channel_id=1, source_target_pairs={{0,1},{1,0},{2,3},{3,2},{4,5},{5,4},{6,7},{7,6},{8,9},{9,8},{10,11... | collective-permute-start | bytes 1572872 | tf_op jit(solution)/shard_map/ppermute | solution.py:475
  7.3 0.0 copy-start.6
  7.3 0.0 copy-start.7
  7.3 0.0 copy-start.8
  7.3 22.9 %all-gather = f32[128,128]{1,0:T(8,128)S(1)} all-gather(f32[8,128]{1,0:T(8,128)S(1)} %get-tuple-element.11), channel_id=2, replica_groups=mesh['groups'=2,'mesh'=16] {'mesh'}, dimensions={0}, use_global_device_ids=true | all-gather | bytes 69632 | tf_op jit(solution)/shard_map/all_gather | solution.py:546
  30.2 0.0 collective-permute-done.outer
  30.2 0.0 collective-permute-done.1.inner
  30.2 0.0 copy-start.9
  30.2 0.0 copy-start.10
  30.3 0.0 copy-done
  30.3 0.0 copy-done.6
  30.3 0.0 copy-done.7
  30.3 0.0 copy-done.8
  30.3 0.6 copy-done.9
  30.9 0.0 copy-done.10
  30.9 0.0 copy-start.1
  30.9 0.0 copy-start.3
  30.9 0.0 copy-start.4
  30.9 0.0 copy-start.5
  30.9 8.0 %wave.1 = (f32[50,36,128]{2,1,0:T(8,128)}, f32[8,128]{1,0:T(8,128)S(1)}) custom-call(f32[50,36,128]{2,1,0:T(8,128)S(1)} %get-tuple-element.10.spectra, f32[1024,128]{1,0:T(8,128)S(1)} %collective-permute-done.outer, f32[1024,128]{1,0:T(8,128)S(1)} %collective-permute-done.1.inner, f32[16,8,128]{2,1,0:T(8,128)S(1)} %bitcast.3, s32[1,128]{1,0:T(1,128)S(1)} %bitcast.6, ...), custom_call_target="tpu_custom_call" | custom-call | tf_op jit(solution)/shard_map/wave/pallas_call | solution.py:550
  39.0 0.0 copy-start.2
  39.0 20.9 %all-gather.1 = f32[128,128]{1,0:T(8,128)S(1)} all-gather(f32[8,128]{1,0:T(8,128)S(1)} %get-tuple-element.12), channel_id=3, replica_groups=mesh['groups'=2,'mesh'=16] {'mesh'}, dimensions={0}, use_global_device_ids=true | all-gather | bytes 69632 | tf_op jit(solution)/shard_map/all_gather | solution.py:546
  59.8 0.0 copy-done.1
  59.8 0.0 copy-done.3
  59.8 0.0 copy-done.4
  59.8 0.0 copy-done.5
  59.8 0.0 copy-done.2
  59.9 5.4 %tracer.1 = f32[2,16,1024]{2,1,0:T(8,128)} custom-call(f32[2,16,1024]{2,1,0:T(8,128)S(1)} %copy-done.1, f32[16,1024]{1,0:T(8,128)S(1)} %copy-done.2, f32[1024,128]{1,0:T(8,128)S(1)} %collective-permute-done.outer, f32[1024,128]{1,0:T(8,128)S(1)} %collective-permute-done.1.inner, f32[16,8,128]{2,1,0:T(8,128)S(1)} %bitcast.4, s32[6,1024]{1,0:T(8,128)S(1)} %copy-done.3, ...), custom_call_target="tpu_custom_call" | custom-call | tf_op jit(solution)/shard_map/tracer/pallas_call | solution.py:579
Async XLA Ops:
  0.6 29.6 %copy-start = (s32[16,16,16]{2,1,0:T(8,128)S(1)}, s32[16,16,16]{2,1,0:T(8,128)}, u32[]{:S(2)}) copy-start(s32[16,16,16]{2,1,0:T(8,128)} %send_rows.5) | copy-start | bytes 49156
  2.2 28.0 %collective-permute-start = (f32[1024,128]{1,0:T(8,128)S(1)}, f32[1024,128]{1,0:T(8,128)S(1)}, u32[]{:S(2)}, u32[]{:S(2)}) collective-permute-start(f32[1024,128]{1,0:T(8,128)S(1)} %get-tuple-element.8), channel_id=1, source_target_pairs={{1,2},{2,1},{3,4},{4,3},{5,6},{6,5},{7,8},{8,7},{9,10},{10,9},{11,... | collective-permute-start | bytes 1572872 | tf_op jit(solution)/shard_map/ppermute | solution.py:475
  2.9 27.3 %collective-permute-start.1 = (f32[1024,128]{1,0:T(8,128)S(1)}, f32[1024,128]{1,0:T(8,128)S(1)}, u32[]{:S(2)}, u32[]{:S(2)}) collective-permute-start(f32[1024,128]{1,0:T(8,128)S(1)} %get-tuple-element.9), channel_id=1, source_target_pairs={{0,1},{1,0},{2,3},{3,2},{4,5},{5,4},{6,7},{7,6},{8,9},{9,8},{10,11... | collective-permute-start | bytes 1572872 | tf_op jit(solution)/shard_map/ppermute | solution.py:475
  7.3 23.0 %copy-start.6 = (s32[6,128]{1,0:T(8,128)S(1)}, s32[6,128]{1,0:T(8,128)}, u32[]{:S(2)}) copy-start(s32[6,128]{1,0:T(8,128)} %neighbors.2) | copy-start | bytes 9220
  7.3 23.0 %copy-start.7 = (f32[6,128]{1,0:T(8,128)S(1)}, f32[6,128]{1,0:T(8,128)}, u32[]{:S(2)}) copy-start(f32[6,128]{1,0:T(8,128)} %normal.2) | copy-start | bytes 9220
  7.3 23.0 %copy-start.8 = (f32[6,128]{1,0:T(8,128)S(1)}, f32[6,128]{1,0:T(8,128)}, u32[]{:S(2)}) copy-start(f32[6,128]{1,0:T(8,128)} %weight.2) | copy-start | bytes 9220
  30.2 0.7 %copy-start.9 = (s32[128]{0:T(128)S(1)}, s32[128]{0:T(128)}, u32[]{:S(2)}) copy-start(s32[128]{0:T(128)} %param.25) | copy-start | bytes 1540
  30.2 0.7 %copy-start.10 = (f32[2,128]{1,0:T(2,128)S(1)}, f32[2,128]{1,0:T(2,128)}, u32[]{:S(2)}) copy-start(f32[2,128]{1,0:T(2,128)} %wind.1) | copy-start | bytes 3076
  30.9 28.9 %copy-start.1 = (f32[2,16,1024]{2,1,0:T(8,128)S(1)}, f32[2,16,1024]{2,1,0:T(8,128)}, u32[]{:S(2)}) copy-start(f32[2,16,1024]{2,1,0:T(8,128)} %tracers.1) | copy-start | bytes 393220
  30.9 28.9 %copy-start.3 = (s32[6,1024]{1,0:T(8,128)S(1)}, s32[6,1024]{1,0:T(8,128)}, u32[]{:S(2)}) copy-start(s32[6,1024]{1,0:T(8,128)} %neighbors.3) | copy-start | bytes 73732
  30.9 28.9 %copy-start.4 = (f32[6,1024]{1,0:T(8,128)S(1)}, f32[6,1024]{1,0:T(8,128)}, u32[]{:S(2)}) copy-start(f32[6,1024]{1,0:T(8,128)} %normal.3) | copy-start | bytes 73732
  30.9 28.9 %copy-start.5 = (f32[6,1024]{1,0:T(8,128)S(1)}, f32[6,1024]{1,0:T(8,128)}, u32[]{:S(2)}) copy-start(f32[6,1024]{1,0:T(8,128)} %weight.3) | copy-start | bytes 73732
  39.0 20.9 %copy-start.2 = (f32[16,1024]{1,0:T(8,128)S(1)}, f32[16,1024]{1,0:T(8,128)}, u32[]{:S(2)}) copy-start(f32[16,1024]{1,0:T(8,128)} %potential.1) | copy-start | bytes 196612

commit v4 on v3

--- a/solution.py
+++ b/solution.py
@@ -1,3 +1,4 @@
+import functools
 import math
 
 import jax
@@ -47,12 +48,27 @@
     return half == jnp.where(lower, 0, 1)
 
 
+def peer_rows(values, peers, capacity):
+    lane = lane_iota(peers)
+    group = lane // capacity
+    block = jnp.clip(row_iota(peers) - 1 + group // 2, 0, peers - 1)
+    entry = block * capacity + lane % capacity
+    out = jnp.zeros((peers, LANES), jnp.float32)
+    for part in range(2):
+        for half, row in enumerate(values[part]):
+            found = lane_gather(spread(row, peers), entry % LANES)
+            wanted = (group < 6) & (group % 2 == part) & (entry // LANES == half)
+            out = jnp.where(wanted, found, out)
+    return out
+
+
 def pack_kernel(
     spectra_in, tracers_in, potential_in, neighbors_in, normal_in, weight_in, current_in,
-    send_rows, slot_in,
-    tile, outer, inner, spectra,
-    tracers, potential, neighbors, normal, weight, current, own_rows, node_slot, sems,
+    send_rows, slot_in, near_in, angle_in, face_in, wind_in,
+    rows_out, outer, inner, spectra, node_slot, near, angle, face, wind,
+    tracers, potential, neighbors, normal, weight, current, own_rows, sems,
 ):
+    peers, _, capacity = send_rows.shape
     me = lax.axis_index("mesh")
     copies = []
     for source, target in (
@@ -65,6 +81,10 @@
         (neighbors_in, neighbors),
         (normal_in, normal),
         (weight_in, weight),
+        (near_in, near),
+        (angle_in, angle),
+        (face_in, face),
+        (wind_in, wind),
     ):
         copy = pltpu.make_async_copy(source, target, sems.at[len(copies)])
         copy.start()
@@ -80,15 +100,13 @@
     )
     place = row_iota(2 * blocks)
     halves = slot_rows(own_rows[...])
-    tile[...] = jnp.zeros(tile.shape, jnp.float32)
-    for half, cell in enumerate(halves):
+    values = [[], []]
+    for cell in halves:
         found = lane_gather(stacked, spread(cell % LANES, 2 * blocks))
         for part in range(2):
             picked = jnp.where(place == 2 * (cell // LANES) + part, found, 0.0)
-            row = part * len(halves) + half
-            tile[row : row + 1, :] = jnp.sum(picked, axis=0, keepdims=True)
-    row = 2 * len(halves)
-    tile[row : row + 1, :] = node_slot[...].astype(jnp.float32)
+            values[part].append(jnp.sum(picked, axis=0, keepdims=True))
+    rows_out[...] = peer_rows(values, peers, capacity)
     for copy in copies[3:]:
         copy.wait()
     odd = me % 2 == 1
@@ -111,6 +129,7 @@
         edges = neighbors.shape[0]
         near = jnp.where(upward, neighbors[:, high], neighbors[:, low])
         out[base : base + edges, :] = near.astype(jnp.float32)
+        out[base + edges : base + edges + 1, :] = node_slot[...].astype(jnp.float32)
         out[base + 8 : base + 8 + edges, :] = jnp.where(upward, normal[:, high], normal[:, low])
         out[base + 16 : base + 16 + edges, :] = jnp.where(upward, weight[:, high], weight[:, low])
     base = 2 * field_rows + TABLE_ROWS
@@ -135,53 +154,40 @@
             out[at:, :] = jnp.zeros((outer.shape[0] - at, LANES), jnp.float32)
 
 
-def node_currents(table, slot, block, capacity):
+def node_currents(table, slot, which, capacity):
     peers = table.shape[0]
-    halves = peers * capacity // LANES
-    owner = slot // capacity
-    entry = block * capacity + slot % capacity
-    lane = spread(entry % LANES, 8)
-    owner8 = spread(owner, 8)
-    found = jnp.zeros((8, LANES), jnp.float32)
-    for p in range(peers):
-        found = jnp.where(owner8 == p, lane_gather(table[p], lane), found)
-    half = entry // LANES
+    owner = row_iota(peers) == slot // capacity
     out = []
     for part in range(2):
-        value = found[part * halves : part * halves + 1]
-        for h in range(1, halves):
-            row = part * halves + h
-            value = jnp.where(half == h, found[row : row + 1], value)
-        out.append(value)
+        lane = (2 * which + part) * capacity + slot % capacity
+        found = jnp.where(owner, lane_gather(table, spread(lane, peers)), 0.0)
+        out.append(jnp.sum(found, axis=0, keepdims=True))
     return out
 
 
 def wave_kernel(
-    spectra, outer, inner, table, node_slot, neighbors, normal, weight, wind, send_rows,
-    spectra_new, tile, project, drift,
+    capacity,
+    spectra, outer, inner, table, node_slot, neighbors, normal, weight, wind,
+    spectra_new, rows_out, project, drift,
 ):
     me = lax.axis_index("mesh")
     freqs, dirs = spectra.shape[:2]
     edges = neighbors.shape[0]
-    peers, _, capacity = send_rows.shape
+    peers = table.shape[0]
     halves = peers * capacity // LANES
     pairs = freqs // 2
     whole = dirs // 8 * 8
     rest = dirs - whole
     base = outer.shape[0] - (pairs * dirs + 7) // 8 * 8
-    low1 = lane_iota(1) < LANES // 2
-
     slot = node_slot[...]
-    row = 2 * halves
-    previous = jnp.maximum(me - 1, 0)
-    following = jnp.minimum(me + 1, peers - 1)
-    beside_slot = jnp.where(
-        low1, table[following][row : row + 1], table[previous][row : row + 1]
+    row = base - TABLE_ROWS + edges
+    halo_slot = jnp.where(
+        half_mask(1, me % 2 == 1), outer[row : row + 1, :], inner[row : row + 1, :]
     ).astype(jnp.int32)
-    beside_block = jnp.where(low1, following, previous)
-    own_block = jnp.full((1, LANES), me, jnp.int32)
-    own_x, own_y = node_currents(table, slot, own_block, capacity)
-    halo_x, halo_y = node_currents(table, beside_slot, beside_block, capacity)
+    lower = lane_iota(1) < LANES // 2
+    currents = table[...]
+    own_x, own_y = node_currents(currents, slot, jnp.ones((1, LANES), jnp.int32), capacity)
+    halo_x, halo_y = node_currents(currents, halo_slot, jnp.where(lower, 2, 0), capacity)
 
     target = neighbors[...]
     lane = target % LANES
@@ -268,13 +274,11 @@
     in_order = exact_dot(
         stokes, lax.broadcasted_iota(jnp.int32, (halves * LANES, LANES), 0) == slot
     )
-    tile[...] = jnp.zeros(tile.shape, jnp.float32)
-    for part in range(2):
-        for half in range(halves):
-            row = part * halves + half
-            tile[row : row + 1, :] = in_order[
-                part : part + 1, half * LANES : (half + 1) * LANES
-            ]
+    values = [
+        [in_order[part : part + 1, h * LANES : (h + 1) * LANES] for h in range(halves)]
+        for part in range(2)
+    ]
+    rows_out[...] = peer_rows(values, peers, capacity)
 
 
 def exact_dot(values, chosen):
@@ -336,30 +340,18 @@
         cosine[b, 0:edges, :] = w * jnp.cos(angle)
         sine[b, 0:edges, :] = w * jnp.sin(angle)
 
-    lane1 = lane_iota(1)
-    lane8 = lane_iota(8)
-    per_row = LANES // capacity
+    received = table[...]
+    lane_of = lane_iota(peers)
     for which in range(3):
-        block = jnp.clip(me + which - 1, 0, peers - 1)
-        cell = slot_rows(send_rows[block])
-        first = block * capacity
-        pick = (first % LANES) + lane8 % capacity
-        found = [jnp.zeros((8, LANES), jnp.float32) for _ in range(halves)]
-        for d in range(peers):
-            half = d // per_row
-            found[half] = jnp.where(
-                lane8 // capacity == d % per_row, lane_gather(table[d], pick), found[half]
-            )
-        source_half = first // LANES
+        cell = slot_rows(send_rows[jnp.clip(me + which - 1, 0, peers - 1)])
         values = []
         for part in range(2):
+            lane = (2 * which + part) * capacity + lane_of % capacity
+            found = lane_gather(received, lane)
             row = []
             for half in range(halves):
-                value = found[half][part * halves : part * halves + 1]
-                for h in range(1, halves):
-                    at_row = part * halves + h
-                    value = jnp.where(source_half == h, found[half][at_row : at_row + 1], value)
-                row.append(value)
+                mine = row_iota(peers) == (lane_of + half * LANES) // capacity
+                row.append(jnp.sum(jnp.where(mine, found, 0.0), axis=0, keepdims=True))
             values.append(jnp.concatenate(row, axis=1))
         values = jnp.concatenate(values, axis=0)
         names = jnp.concatenate(cell, axis=1)
@@ -494,7 +486,7 @@
     send_rows,
     node_slot,
 ):
-    peers = send_rows.shape[0]
+    peers, _, capacity = send_rows.shape
     freqs, dirs, nodes = spectra.shape
     tracer_count, layers, cells = tracers.shape
     edges = cell_neighbors.shape[0]
@@ -507,16 +499,21 @@
     f32 = jnp.float32
 
     stored = pl.BlockSpec(memory_space=pltpu.HBM)
-    tile, outer, inner, own_spectra = pl.pallas_call(
+    currents, outer, inner, own_spectra, *node_tables = pl.pallas_call(
         pack_kernel,
         out_shape=(
-            jax.ShapeDtypeStruct((8, LANES), f32),
+            jax.ShapeDtypeStruct((peers, LANES), f32),
             jax.ShapeDtypeStruct((message_rows, LANES), f32),
             jax.ShapeDtypeStruct((message_rows, LANES), f32),
             jax.ShapeDtypeStruct(spectra.shape, f32),
+            jax.ShapeDtypeStruct(slots.shape, jnp.int32),
+            jax.ShapeDtypeStruct(node_neighbors.shape, jnp.int32),
+            jax.ShapeDtypeStruct(node_normal.shape, f32),
+            jax.ShapeDtypeStruct(node_weight.shape, f32),
+            jax.ShapeDtypeStruct(wind_velocity.shape, f32),
         ),
-        in_specs=[stored] * 9,
-        out_specs=(whole_spec(),) * 4,
+        in_specs=[stored] * 13,
+        out_specs=(whole_spec(),) * 9,
         scratch_shapes=[
             pltpu.VMEM(tracers.shape, f32),
             pltpu.VMEM(potential.shape, f32),
@@ -525,8 +522,7 @@
             pltpu.VMEM(cell_weight.shape, f32),
             pltpu.VMEM(surface_current.shape, f32),
             pltpu.VMEM(send_rows.shape[1:], jnp.int32),
-            pltpu.VMEM(slots.shape, jnp.int32),
-            pltpu.SemaphoreType.DMA((9,)),
+            pltpu.SemaphoreType.DMA((13,)),
         ],
         compiler_params=params,
         name="pack",
@@ -535,25 +531,23 @@
             pltpu.with_memory_space_constraint(x, pltpu.HBM)
             for x in (
                 spectra, tracers, potential, cell_neighbors, cell_normal, cell_weight,
-                surface_current, send_rows, slots,
+                surface_current, send_rows, slots, node_neighbors, node_normal, node_weight,
+                wind_velocity,
             )
         )
     )
     outer = swap(outer, 1, peers)
     inner = swap(inner, 0, peers)
 
-    def everywhere(one):
-        return lax.all_gather(one, "mesh")
-
-    currents = everywhere(tile)
-
-    spectra_new, stokes_tile = pl.pallas_call(
-        wave_kernel,
+    currents = lax.all_to_all(currents, "mesh", 0, 0, tiled=True)
+
+    spectra_new, stokes_rows = pl.pallas_call(
+        functools.partial(wave_kernel, capacity),
         out_shape=(
             jax.ShapeDtypeStruct(spectra.shape, f32),
-            jax.ShapeDtypeStruct((8, LANES), f32),
+            jax.ShapeDtypeStruct((peers, LANES), f32),
         ),
-        in_specs=[whole_spec()] * 10,
+        in_specs=[whole_spec()] * 9,
         out_specs=(whole_spec(),) * 2,
         scratch_shapes=[
             pltpu.VMEM((edges, dirs, LANES), f32),
@@ -562,11 +556,10 @@
         compiler_params=params,
         name="wave",
     )(
-        own_spectra, outer, inner, currents, slots, node_neighbors, node_normal, node_weight,
-        wind_velocity, send_rows,
-    )
-
-    stokes_all = everywhere(stokes_tile)
+        own_spectra, outer, inner, currents, *node_tables,
+    )
+
+    stokes_all = lax.all_to_all(stokes_rows, "mesh", 0, 0, tiled=True)
 
     def head_spec():
         return pl.BlockSpec((head_rows, LANES), lambda i: (0, 0))

time: 65.5 us -> 44.9 us (0.69)
  blocking collectives: 43.8 us -> 23.8 us
    all_gather x2 -> x0, blocking collectives: 43.8 us -> none  [everywhere(): return lax.all_gather(one, 'mesh')]
    all_to_all x0 -> x2, blocking collectives: none -> 23.8 us  [the longest x1 12.6 us: local(): stokes_all = lax.all_to_all(stokes_rows, 'mesh', 0, 0, tiled=True)]
where the time goes in v4:
time: 44.9 us; the launch traced here: 44.6 us
  blocking collectives  23.8 us (53%)
  Pallas kernels  15 us (33%)
  starting transfers between devices  5.06 us (11%)
  between operations  0.72 us (2%)
    all_to_all x1, blocking collectives, local(): stokes_all = lax.all_to_all(stokes_rows, 'mesh', 0, 0, tiled=True)  12.6 us
    all_to_all x1, blocking collectives, local(): currents = lax.all_to_all(currents, 'mesh', 0, 0, tiled=True)  11.2 us
    pallas_call x1, Pallas kernels, local(): pl.pallas_call(functools.partial(wave_kernel, capacity), out_shape=(jax.S...  7.99 us
    pallas_call x1, Pallas kernels, local(): pl.pallas_call(tracer_kernel, grid=(1,), out_shape=jax.ShapeDtypeStruct(t...  5.41 us
    ppermute x2, starting transfers between devices, swap(): return lax.ppermute(message, 'mesh', pairs)  5.06 us
    pallas_call x1, Pallas kernels, local(): pl.pallas_call(pack_kernel, out_shape=(jax.ShapeDtypeStruct((peers, LANES...  1.58 us
  transfers between devices with their start and end apart: 2, of which 0 were waited for; matrix products, arithmetic and copies ran while one was open for 0% of the time, Pallas kernels for 0%

profile of v4, /device:TPU:0, one launch (start us, length us, event | category | flops | bytes accessed | tf_op | source)
XLA Modules:
  0.0 44.6 jit_solution(9907175072478977183)
XLA Ops:
  0.6 1.6 %pack.1 = (f32[16,128]{1,0:T(8,128)S(1)}, f32[1024,128]{1,0:T(8,128)S(1)}, f32[1024,128]{1,0:T(8,128)S(1)}, f32[50,36,128]{2,1,0:T(8,128)S(1)}, s32[1,128]{1,0:T...) custom-call(f32[50,36,128]{2,1,0:T(8,128)} %spectra_in.1, ...), custom_call_target="tpu_custom_call" | custom-call | tf_op jit(solution)/shard_map/pack/pallas_call | solution.py:502
  2.2 0.7 %collective-permute-start = (f32[1024,128]{1,0:T(8,128)S(1)}, f32[1024,128]{1,0:T(8,128)S(1)}, u32[]{:S(2)}, u32[]{:S(2)}) collective-permute-start(f32[1024,128]{1,0:T(8,128)S(1)} %get-tuple-element.13), channel_id=1, source_target_pairs={{1,2},{2,1},{3,4},{4,3},{5,6},{6,5},{7,8},{8,7},{9,10},{10,9},{11,... | collective-permute-start | bytes 1572872 | tf_op jit(solution)/shard_map/ppermute | solution.py:467
  2.9 4.4 %collective-permute-start.1 = (f32[1024,128]{1,0:T(8,128)S(1)}, f32[1024,128]{1,0:T(8,128)S(1)}, u32[]{:S(2)}, u32[]{:S(2)}) collective-permute-start(f32[1024,128]{1,0:T(8,128)S(1)} %get-tuple-element.14), channel_id=1, source_target_pairs={{0,1},{1,0},{2,3},{3,2},{4,5},{5,4},{6,7},{7,6},{8,9},{9,8},{10,11... | collective-permute-start | bytes 1572872 | tf_op jit(solution)/shard_map/ppermute | solution.py:467
  7.3 11.2 %all_to_all.22 = f32[16,1,128]{2,1,0:T(1,128)S(1)} all-to-all(f32[16,1,128]{2,1,0:T(1,128)S(1)} %bitcast.11), channel_id=1, replica_groups=mesh['groups'=2,'mesh'=16] {'mesh'}, dimensions={0} | all-to-all | bytes 16384 | tf_op jit(solution)/shard_map/all_to_all | solution.py:542
  18.5 0.0 collective-permute-done.outer
  18.5 0.0 collective-permute-done.1.inner
  18.5 0.0 copy-start
  18.5 0.0 copy-start.1
  18.5 0.0 copy-start.2
  18.5 0.0 copy-start.3
  18.5 0.0 copy-start.4
  18.5 0.0 copy-start.5
  18.5 8.0 %wave.1 = (f32[50,36,128]{2,1,0:T(8,128)}, f32[16,128]{1,0:T(8,128)S(1)}) custom-call(f32[50,36,128]{2,1,0:T(8,128)S(1)} %get-tuple-element.15.spectra, f32[1024,128]{1,0:T(8,128)S(1)} %collective-permute-done.outer, f32[1024,128]{1,0:T(8,128)S(1)} %collective-permute-done.1.inner, f32[16,128]{1,0:T(8,128)S(1)} %bitcast.9, ...), custom_call_target="tpu_custom_call" | custom-call | tf_op jit(solution)/shard_map/wave/pallas_call | solution.py:544
  26.5 12.6 %all_to_all.23 = f32[16,1,128]{2,1,0:T(1,128)S(1)} all-to-all(f32[16,1,128]{2,1,0:T(1,128)S(1)} %bitcast.12), channel_id=1, replica_groups=mesh['groups'=2,'mesh'=16] {'mesh'}, dimensions={0} | all-to-all | bytes 16384 | tf_op jit(solution)/shard_map/all_to_all | solution.py:562
  39.2 0.0 copy-done
  39.2 0.0 copy-done.1
  39.2 0.0 copy-done.2
  39.2 0.0 copy-done.3
  39.2 0.0 copy-done.4
  39.2 0.0 copy-done.5
  39.2 5.4 %tracer.1 = f32[2,16,1024]{2,1,0:T(8,128)} custom-call(f32[2,16,1024]{2,1,0:T(8,128)S(1)} %copy-done, f32[16,1024]{1,0:T(8,128)S(1)} %copy-done.2, f32[1024,128]{1,0:T(8,128)S(1)} %collective-permute-done.outer, f32[1024,128]{1,0:T(8,128)S(1)} %collective-permute-done.1.inner, f32[16,128]{1,0:T(8,128)S(1)} %bitcast.10, s32[6,1024]{1,0:T(8,128)S(1)} %copy-done.3, ...), custom_call_target="tpu_custom_call" | custom-call | tf_op jit(solution)/shard_map/tracer/pallas_call | solution.py:572
Async XLA Ops:
  2.2 16.2 %collective-permute-start = (f32[1024,128]{1,0:T(8,128)S(1)}, f32[1024,128]{1,0:T(8,128)S(1)}, u32[]{:S(2)}, u32[]{:S(2)}) collective-permute-start(f32[1024,128]{1,0:T(8,128)S(1)} %get-tuple-element.13), channel_id=1, source_target_pairs={{1,2},{2,1},{3,4},{4,3},{5,6},{6,5},{7,8},{8,7},{9,10},{10,9},{11,... | collective-permute-start | bytes 1572872 | tf_op jit(solution)/shard_map/ppermute | solution.py:467
  2.9 15.5 %collective-permute-start.1 = (f32[1024,128]{1,0:T(8,128)S(1)}, f32[1024,128]{1,0:T(8,128)S(1)}, u32[]{:S(2)}, u32[]{:S(2)}) collective-permute-start(f32[1024,128]{1,0:T(8,128)S(1)} %get-tuple-element.14), channel_id=1, source_target_pairs={{0,1},{1,0},{2,3},{3,2},{4,5},{5,4},{6,7},{7,6},{8,9},{9,8},{10,11... | collective-permute-start | bytes 1572872 | tf_op jit(solution)/shard_map/ppermute | solution.py:467
  18.5 20.7 %copy-start = (f32[2,16,1024]{2,1,0:T(8,128)S(1)}, f32[2,16,1024]{2,1,0:T(8,128)}, u32[]{:S(2)}) copy-start(f32[2,16,1024]{2,1,0:T(8,128)} %tracers.1) | copy-start | bytes 393220
  18.5 20.7 %copy-start.1 = (s32[16,16,16]{2,1,0:T(8,128)S(1)}, s32[16,16,16]{2,1,0:T(8,128)}, u32[]{:S(2)}) copy-start(s32[16,16,16]{2,1,0:T(8,128)} %send_rows.3) | copy-start | bytes 49156
  18.5 20.7 %copy-start.2 = (f32[16,1024]{1,0:T(8,128)S(1)}, f32[16,1024]{1,0:T(8,128)}, u32[]{:S(2)}) copy-start(f32[16,1024]{1,0:T(8,128)} %potential.1) | copy-start | bytes 196612
  18.5 20.7 %copy-start.3 = (s32[6,1024]{1,0:T(8,128)S(1)}, s32[6,1024]{1,0:T(8,128)}, u32[]{:S(2)}) copy-start(s32[6,1024]{1,0:T(8,128)} %neighbors.1) | copy-start | bytes 73732
  18.5 20.7 %copy-start.4 = (f32[6,1024]{1,0:T(8,128)S(1)}, f32[6,1024]{1,0:T(8,128)}, u32[]{:S(2)}) copy-start(f32[6,1024]{1,0:T(8,128)} %normal.1) | copy-start | bytes 73732
  18.5 20.7 %copy-start.5 = (f32[6,1024]{1,0:T(8,128)S(1)}, f32[6,1024]{1,0:T(8,128)}, u32[]{:S(2)}) copy-start(f32[6,1024]{1,0:T(8,128)} %weight.1) | copy-start | bytes 73732

commit v5 on v4

--- a/solution.py
+++ b/solution.py
@@ -11,7 +11,7 @@
 LANES = 128
 FCT_FLOOR = 0.001
 TABLE_ROWS = 24
-VMEM_LIMIT = 48 * 1024 * 1024
+VMEM_LIMIT = 40 * 1024 * 1024
 
 
 def lane_gather(values, index):
@@ -62,11 +62,40 @@
     return out
 
 
+def direction(dirs):
+    turn = row_iota(dirs).astype(jnp.float32) * (2.0 * math.pi / dirs)
+    return jnp.cos(turn), jnp.sin(turn)
+
+
+def node_tables(me, near, angle, face, cosine, sine, project, choice):
+    edges, dirs = project.shape[:2]
+    cosine[...] = face[...] * jnp.cos(angle[...])
+    sine[...] = face[...] * jnp.sin(angle[...])
+    cos_dir, sin_dir = direction(dirs)
+    source = row_iota(LANES)
+    minus = jnp.where(source == lane_iota(LANES), -1.0, 0.0)
+    for s in range(edges):
+        project[s] = cos_dir * cosine[s : s + 1, :] + sin_dir * sine[s : s + 1, :]
+        target = near[s : s + 1, :]
+        inside = target // LANES == me
+        lane = target % LANES
+        own = jnp.where(source == jnp.where(inside, lane, LANES), 1.0, 0.0) + minus
+        halo = jnp.where(source == jnp.where(inside, LANES, lane), 1.0, 0.0)
+        lanes = slice(s * LANES, (s + 1) * LANES)
+        for k, part in enumerate((own, own, halo, halo)):
+            choice[k * LANES : (k + 1) * LANES, lanes] = part.astype(jnp.bfloat16)
+
+
+def split(x):
+    first = x.astype(jnp.bfloat16)
+    return first, (x - first.astype(jnp.float32)).astype(jnp.bfloat16)
+
+
 def pack_kernel(
     spectra_in, tracers_in, potential_in, neighbors_in, normal_in, weight_in, current_in,
     send_rows, slot_in, near_in, angle_in, face_in, wind_in,
-    rows_out, outer, inner, spectra, node_slot, near, angle, face, wind,
-    tracers, potential, neighbors, normal, weight, current, own_rows, sems,
+    rows_out, outer, inner, spectra, node_slot, near, wind, cosine, sine, project, choice,
+    angle, face, tracers, potential, neighbors, normal, weight, current, own_rows, sems,
 ):
     peers, _, capacity = send_rows.shape
     me = lax.axis_index("mesh")
@@ -89,7 +118,7 @@
         copy = pltpu.make_async_copy(source, target, sems.at[len(copies)])
         copy.start()
         copies.append(copy)
-    for copy in copies[:3]:
+    for copy in copies[:3] + copies[9:]:
         copy.wait()
     freqs, dirs = spectra.shape[:2]
     layers, cells = potential.shape
@@ -107,7 +136,8 @@
             picked = jnp.where(place == 2 * (cell // LANES) + part, found, 0.0)
             values[part].append(jnp.sum(picked, axis=0, keepdims=True))
     rows_out[...] = peer_rows(values, peers, capacity)
-    for copy in copies[3:]:
+    node_tables(me, near, angle, face, cosine, sine, project, choice)
+    for copy in copies[3:9]:
         copy.wait()
     odd = me % 2 == 1
     for out, upward in ((outer, odd), (inner, jnp.logical_not(odd))):
@@ -166,9 +196,9 @@
 
 
 def wave_kernel(
-    capacity,
-    spectra, outer, inner, table, node_slot, neighbors, normal, weight, wind,
-    spectra_new, rows_out, project, drift,
+    capacity, step_pairs,
+    spectra, outer, inner, table, node_slot, neighbors, wind, cosine, sine, project, choice,
+    spectra_new, rows_out, drift, both, change,
 ):
     me = lax.axis_index("mesh")
     freqs, dirs = spectra.shape[:2]
@@ -178,11 +208,14 @@
     pairs = freqs // 2
     whole = dirs // 8 * 8
     rest = dirs - whole
+    stride = (dirs + 7) // 8 * 8
     base = outer.shape[0] - (pairs * dirs + 7) // 8 * 8
+
+    odd = me % 2 == 1
     slot = node_slot[...]
     row = base - TABLE_ROWS + edges
     halo_slot = jnp.where(
-        half_mask(1, me % 2 == 1), outer[row : row + 1, :], inner[row : row + 1, :]
+        half_mask(1, odd), outer[row : row + 1, :], inner[row : row + 1, :]
     ).astype(jnp.int32)
     lower = lane_iota(1) < LANES // 2
     currents = table[...]
@@ -192,10 +225,6 @@
     target = neighbors[...]
     lane = target % LANES
     inside = target // LANES == me
-    angle = normal[...]
-    w = weight[...]
-    cosine = w * jnp.cos(angle)
-    sine = w * jnp.sin(angle)
 
     def beside(own, halo):
         a = lane_gather(spread(own, edges), lane)
@@ -203,54 +232,63 @@
         return jnp.where(inside, a, b)
 
     drift[0:edges, :] = (
-        0.5 * (own_x + beside(own_x, halo_x)) * cosine
-        + 0.5 * (own_y + beside(own_y, halo_y)) * sine
-    )
-    turn = 2.0 * math.pi / dirs * lax.broadcasted_iota(jnp.int32, (dirs, LANES), 0).astype(
-        jnp.float32
-    )
-    cos_dir = jnp.cos(turn)
-    sin_dir = jnp.sin(turn)
-    for s in range(edges):
-        project[s] = cos_dir * cosine[s : s + 1] + sin_dir * sine[s : s + 1]
-
-    from_outer = half_mask(dirs, me % 2 == 1)
-    straight = [spread(lane[s : s + 1], dirs) for s in range(edges)]
-    swapped = [spread((lane[s : s + 1] + LANES // 2) % LANES, dirs) for s in range(edges)]
-    within = [spread(target[s : s + 1] // LANES, dirs) == me for s in range(edges)]
+        0.5 * (own_x + beside(own_x, halo_x)) * cosine[...]
+        + 0.5 * (own_y + beside(own_y, halo_y)) * sine[...]
+    )
+    drifts = [spread(drift[s : s + 1, :], 8) for s in range(edges)]
+    drift_sum = sum(drifts[1:], drifts[0])
+    from_outer = half_mask(dirs, odd)
+    both[...] = jnp.zeros(both.shape, jnp.float32)
     ratio = 1.0 / 1.1
-    jump = ratio**pairs
-
-    def pair(g, carry):
-        speed, total = carry
-        halo_parts = []
-        for message in (outer, inner):
-            at = pl.multiple_of(base + g * whole, 8)
-            upper = message[pl.ds(at, whole), :]
-            lower = message[pl.ds(base + pairs * whole + g * rest, rest), :]
-            halo_parts.append(jnp.concatenate([upper, lower], axis=0))
-        x, y = halo_parts
-        for f, group_speed, halo, halo_lane in (
-            (g, speed, jnp.where(from_outer, x, y), straight),
-            (g + pairs, speed * jump, jnp.where(from_outer, y, x), swapped),
-        ):
-            own = spectra[f]
-            out_speed = jnp.zeros((dirs, LANES), jnp.float32)
-            inflow = jnp.zeros((dirs, LANES), jnp.float32)
-            for s in range(edges):
-                normal_speed = group_speed * project[s] + drift[s : s + 1]
-                near = jnp.where(
-                    within[s], lane_gather(own, straight[s]), lane_gather(halo, halo_lane[s])
-                )
-                out_speed = out_speed + jnp.maximum(normal_speed, 0.0)
-                inflow = inflow + jnp.minimum(normal_speed, 0.0) * near
-            advected = own - (out_speed * own + inflow)
-            spectra_new[f] = advected
-            total = total + advected
-        return speed * ratio, total
-
+    bands = [slice(r, min(r + 8, dirs)) for r in range(0, dirs, 8)]
+
+    def chunk(c, carry):
+        first_speed, total = carry
+        total = list(total)
+        for i in range(step_pairs):
+            g = c * step_pairs + i
+            parts = []
+            for message in (outer, inner):
+                at = pl.multiple_of(base + g * whole, 8)
+                upper = message[pl.ds(at, whole), :]
+                left = message[pl.ds(base + pairs * whole + g * rest, rest), :]
+                parts.append(jnp.concatenate([upper, left], axis=0))
+            x, y = parts
+            natural = jnp.where(from_outer, x, y)
+            turned = pltpu.roll(jnp.where(from_outer, y, x), LANES // 2, 1)
+            for j, f, halo in ((2 * i, g, natural), (2 * i + 1, g + pairs, turned)):
+                both[j * stride : j * stride + dirs, 0:LANES] = spectra[f]
+                both[j * stride : j * stride + dirs, LANES:] = halo
+        own_first, own_second = split(both[:, 0:LANES])
+        halo_first, halo_second = split(both[:, LANES:])
+        mixed = jnp.concatenate([own_first, own_second, halo_first, halo_second], axis=1)
+        change[...] = jnp.dot(mixed, choice[...], preferred_element_type=jnp.float32)
+        for k, band in enumerate(bands):
+            count = band.stop - band.start
+            along = [project[s, band, :] for s in range(edges)]
+            along_sum = sum(along[1:], along[0])
+            for i in range(step_pairs):
+                for j, f, speed in (
+                    (2 * i, c * step_pairs + i, first_speed * ratio**i),
+                    (2 * i + 1, c * step_pairs + i + pairs, first_speed * ratio ** (i + pairs)),
+                ):
+                    own = spectra[f, band, :]
+                    at = j * stride + band.start
+                    left = 1.0 - (speed * along_sum + drift_sum[:count])
+                    value = left * own
+                    for s in range(edges):
+                        down = jnp.minimum(speed * along[s] + drifts[s][:count], 0.0)
+                        lanes = slice(s * LANES, (s + 1) * LANES)
+                        value = value - down * change[at : at + count, lanes]
+                    spectra_new[f, band, :] = value
+                    total[k] = total[k] + value
+        return first_speed * ratio**step_pairs, tuple(total)
+
+    zeros = tuple(jnp.zeros((band.stop - band.start, LANES), jnp.float32) for band in bands)
+    _, total = lax.fori_loop(0, pairs // step_pairs, chunk, (jnp.float32(1.0), zeros))
+    total = jnp.concatenate(total, axis=0)
     zero = jnp.zeros((dirs, LANES), jnp.float32)
-    _, total = lax.fori_loop(0, pairs, pair, (jnp.float32(1.0), zero))
+    cos_dir, sin_dir = direction(dirs)
     mean = jnp.sum(total, axis=0, keepdims=True) * (1.0 / (freqs * dirs))
     forcing = jnp.maximum(wind[0:1, :] * cos_dir + wind[1:2, :] * sin_dir, 0.0)
     step = jnp.exp((0.25 * forcing - 2.0 * mean) * (1.0 / freqs))
@@ -296,9 +334,11 @@
 
 
 def tracer_kernel(
-    tracers, potential, outer, inner, table, neighbors, normal, weight, send_rows,
-    tracers_new, fields, target, cosine, sine, scale, stokes, antiflux, lowered, ratios,
+    tracers, potential, outer, inner, table, neighbors, normal, weight, send_rows, spectra,
+    tracers_new, spectra_out, fields, target, cosine, sine, scale, stokes, antiflux, lowered, ratios, sem,
 ):
+    write = pltpu.make_async_copy(spectra, spectra_out, sem)
+    write.start()
     me = lax.axis_index("mesh")
     peers, _, capacity = send_rows.shape
     halves = peers * capacity // LANES
@@ -458,6 +498,7 @@
         return carry
 
     lax.fori_loop(0, blocks, limit, 0)
+    write.wait()
 
 
 def swap(message, first, peers):
@@ -499,7 +540,7 @@
     f32 = jnp.float32
 
     stored = pl.BlockSpec(memory_space=pltpu.HBM)
-    currents, outer, inner, own_spectra, *node_tables = pl.pallas_call(
+    currents, outer, inner, *node_parts = pl.pallas_call(
         pack_kernel,
         out_shape=(
             jax.ShapeDtypeStruct((peers, LANES), f32),
@@ -508,13 +549,17 @@
             jax.ShapeDtypeStruct(spectra.shape, f32),
             jax.ShapeDtypeStruct(slots.shape, jnp.int32),
             jax.ShapeDtypeStruct(node_neighbors.shape, jnp.int32),
+            jax.ShapeDtypeStruct(wind_velocity.shape, f32),
             jax.ShapeDtypeStruct(node_normal.shape, f32),
-            jax.ShapeDtypeStruct(node_weight.shape, f32),
-            jax.ShapeDtypeStruct(wind_velocity.shape, f32),
+            jax.ShapeDtypeStruct(node_normal.shape, f32),
+            jax.ShapeDtypeStruct((edges, dirs, LANES), f32),
+            jax.ShapeDtypeStruct((4 * LANES, edges * LANES), jnp.bfloat16),
         ),
         in_specs=[stored] * 13,
-        out_specs=(whole_spec(),) * 9,
+        out_specs=(whole_spec(),) * 11,
         scratch_shapes=[
+            pltpu.VMEM(node_normal.shape, f32),
+            pltpu.VMEM(node_weight.shape, f32),
             pltpu.VMEM(tracers.shape, f32),
             pltpu.VMEM(potential.shape, f32),
             pltpu.VMEM(cell_neighbors.shape, jnp.int32),
@@ -541,22 +586,25 @@
 
     currents = lax.all_to_all(currents, "mesh", 0, 0, tiled=True)
 
+    step_pairs = 5 if freqs % 10 == 0 else 1
+    stride = (dirs + 7) // 8 * 8
     spectra_new, stokes_rows = pl.pallas_call(
-        functools.partial(wave_kernel, capacity),
+        functools.partial(wave_kernel, capacity, step_pairs),
         out_shape=(
             jax.ShapeDtypeStruct(spectra.shape, f32),
             jax.ShapeDtypeStruct((peers, LANES), f32),
         ),
-        in_specs=[whole_spec()] * 9,
+        in_specs=[whole_spec()] * 11,
         out_specs=(whole_spec(),) * 2,
         scratch_shapes=[
-            pltpu.VMEM((edges, dirs, LANES), f32),
             pltpu.VMEM((8, LANES), f32),
+            pltpu.VMEM((2 * step_pairs * stride, 2 * LANES), f32),
+            pltpu.VMEM((2 * step_pairs * stride, edges * LANES), f32),
         ],
         compiler_params=params,
         name="wave",
     )(
-        own_spectra, outer, inner, currents, *node_tables,
+        node_parts[0], outer, inner, currents, *node_parts[1:],
     )
 
     stokes_all = lax.all_to_all(stokes_rows, "mesh", 0, 0, tiled=True)
@@ -569,10 +617,13 @@
         return pl.BlockSpec(x.shape, lambda i: zeros)
 
     rows = tracer_count * layers
-    tracers_new = pl.pallas_call(
+    tracers_new, spectra_new = pl.pallas_call(
         tracer_kernel,
         grid=(1,),
-        out_shape=jax.ShapeDtypeStruct(tracers.shape, f32),
+        out_shape=(
+            jax.ShapeDtypeStruct(tracers.shape, f32),
+            jax.ShapeDtypeStruct(spectra.shape, f32),
+        ),
         in_specs=[
             full_spec(tracers),
             full_spec(potential),
@@ -583,8 +634,9 @@
             full_spec(cell_normal),
             full_spec(cell_weight),
             full_spec(send_rows),
+            pl.BlockSpec(memory_space=pl.ANY),
         ],
-        out_specs=full_spec(tracers),
+        out_specs=(full_spec(tracers), stored),
         scratch_shapes=[
             pltpu.VMEM((blocks + 4, field_rows, LANES), f32),
             pltpu.VMEM((blocks + 2, 8, LANES), jnp.int32),
@@ -595,12 +647,13 @@
             pltpu.VMEM((blocks + 2, edges, rows, LANES), f32),
             pltpu.VMEM((blocks + 2, rows, LANES), f32),
             pltpu.VMEM((blocks + 2, 2 * rows, LANES), f32),
+            pltpu.SemaphoreType.DMA(()),
         ],
         compiler_params=params,
         name="tracer",
     )(
         tracers, potential, outer, inner, stokes_all, cell_neighbors, cell_normal, cell_weight,
-        send_rows,
+        send_rows, pltpu.with_memory_space_constraint(spectra_new, pltpu.VMEM),
     )
     return tracers_new, spectra_new
 

time: 44.9 us -> 41.1 us (0.915)
  Pallas kernels: 15 us -> 11.2 us
    pallas_call x2, Pallas kernels: 13.4 us -> 9.2 us  [the longest x1 5.42 us: local(): pl.pallas_call(tracer_kernel, grid=(1,), out_shape=(jax.ShapeDtypeStruct(...]
where the time goes in v5:
time: 41.1 us; the launch traced here: 40.8 us
  blocking collectives  23.8 us (58%)
  Pallas kernels  11.2 us (27%)
  starting transfers between devices  5.06 us (12%)
  between operations  0.73 us (2%)
    all_to_all x1, blocking collectives, local(): stokes_all = lax.all_to_all(stokes_rows, 'mesh', 0, 0, tiled=True)  12.6 us
    all_to_all x1, blocking collectives, local(): currents = lax.all_to_all(currents, 'mesh', 0, 0, tiled=True)  11.2 us
    pallas_call x1, Pallas kernels, local(): pl.pallas_call(tracer_kernel, grid=(1,), out_shape=(jax.ShapeDtypeStruct(...  5.42 us
    ppermute x2, starting transfers between devices, swap(): return lax.ppermute(message, 'mesh', pairs)  5.06 us
    pallas_call x1, Pallas kernels, local(): pl.pallas_call(functools.partial(wave_kernel, capacity, step_pairs), out_...  3.78 us
    pallas_call x1, Pallas kernels, local(): pl.pallas_call(pack_kernel, out_shape=(jax.ShapeDtypeStruct((peers, LANES...  1.95 us
  transfers between devices with their start and end apart: 2, of which 0 were waited for; matrix products, arithmetic and copies ran while one was open for 0% of the time, Pallas kernels for 0%

profile of v5, /device:TPU:0, one launch (start us, length us, event | category | flops | bytes accessed | tf_op | source)
XLA Modules:
  0.0 40.8 jit_solution(12823572155886105859)
XLA Ops:
  0.6 2.0 %pack.1 = (f32[16,128]{1,0:T(8,128)S(1)}, f32[1024,128]{1,0:T(8,128)S(1)}, f32[1024,128]{1,0:T(8,128)S(1)}, f32[50,36,128]{2,1,0:T(8,128)S(1)}, s32[1,128]{1,0:T...) custom-call(f32[50,36,128]{2,1,0:T(8,128)} %spectra_in.1, ...), custom_call_target="tpu_custom_call" | custom-call | tf_op jit(solution)/shard_map/pack/pallas_call | solution.py:543
  2.6 0.7 %collective-permute-start = (f32[1024,128]{1,0:T(8,128)S(1)}, f32[1024,128]{1,0:T(8,128)S(1)}, u32[]{:S(2)}, u32[]{:S(2)}) collective-permute-start(f32[1024,128]{1,0:T(8,128)S(1)} %get-tuple-element.15), channel_id=1, source_target_pairs={{1,2},{2,1},{3,4},{4,3},{5,6},{6,5},{7,8},{8,7},{9,10},{10,9},{11,... | collective-permute-start | bytes 1572872 | tf_op jit(solution)/shard_map/ppermute | solution.py:508
  3.3 4.4 %collective-permute-start.1 = (f32[1024,128]{1,0:T(8,128)S(1)}, f32[1024,128]{1,0:T(8,128)S(1)}, u32[]{:S(2)}, u32[]{:S(2)}) collective-permute-start(f32[1024,128]{1,0:T(8,128)S(1)} %get-tuple-element.16), channel_id=1, source_target_pairs={{0,1},{1,0},{2,3},{3,2},{4,5},{5,4},{6,7},{7,6},{8,9},{9,8},{10,11... | collective-permute-start | bytes 1572872 | tf_op jit(solution)/shard_map/ppermute | solution.py:508
  7.7 11.2 %all_to_all.22 = f32[16,1,128]{2,1,0:T(1,128)S(1)} all-to-all(f32[16,1,128]{2,1,0:T(1,128)S(1)} %bitcast.11), channel_id=1, replica_groups=mesh['groups'=2,'mesh'=16] {'mesh'}, dimensions={0} | all-to-all | bytes 16384 | tf_op jit(solution)/shard_map/all_to_all | solution.py:587
  18.8 0.0 collective-permute-done.outer
  18.8 0.0 collective-permute-done.1.inner
  18.8 0.0 copy-start
  18.8 0.0 copy-start.1
  18.9 0.0 copy-start.2
  18.9 0.0 copy-start.3
  18.9 0.0 copy-start.4
  18.9 0.0 copy-start.5
  18.9 3.8 %wave.1 = (f32[50,36,128]{2,1,0:T(8,128)S(1)}, f32[16,128]{1,0:T(8,128)S(1)}) custom-call(f32[50,36,128]{2,1,0:T(8,128)S(1)} %get-tuple-element.17.spectra, f32[1024,128]{1,0:T(8,128)S(1)} %collective-permute-done.outer, f32[1024,128]{1,0:T(8,128)S(1)} %collective-permute-done.1.inner, f32[16,128]{1,0:T(8,128)S(1)} %bitcast.9, ...), custom_call_target="tpu_custom_call" | custom-call | tf_op jit(solution)/shard_map/wave/pallas_call | solution.py:591
  22.7 12.6 %all_to_all.23 = f32[16,1,128]{2,1,0:T(1,128)S(1)} all-to-all(f32[16,1,128]{2,1,0:T(1,128)S(1)} %bitcast.12), channel_id=1, replica_groups=mesh['groups'=2,'mesh'=16] {'mesh'}, dimensions={0} | all-to-all | bytes 16384 | tf_op jit(solution)/shard_map/all_to_all | solution.py:610
  35.3 0.0 copy-done
  35.3 0.0 copy-done.1
  35.3 0.0 copy-done.2
  35.4 0.0 copy-done.3
  35.4 0.0 copy-done.4
  35.4 0.0 copy-done.5
  35.4 5.4 %tracer.1 = (f32[2,16,1024]{2,1,0:T(8,128)}, f32[50,36,128]{2,1,0:T(8,128)}) custom-call(f32[2,16,1024]{2,1,0:T(8,128)S(1)} %copy-done, f32[16,1024]{1,0:T(8,128)S(1)} %copy-done.2, f32[1024,128]{1,0:T(8,128)S(1)} %collective-permute-done.outer, f32[1024,128]{1,0:T(8,128)S(1)} %collective-permute-done.1.inner, f32[16,128]{1,0:T(8,128)S(1)} %bitcast.10, ...), custom_call_target="tpu_custom_call" | custom-call | tf_op jit(solution)/shard_map/tracer/pallas_call | solution.py:620
Async XLA Ops:
  2.6 16.2 %collective-permute-start = (f32[1024,128]{1,0:T(8,128)S(1)}, f32[1024,128]{1,0:T(8,128)S(1)}, u32[]{:S(2)}, u32[]{:S(2)}) collective-permute-start(f32[1024,128]{1,0:T(8,128)S(1)} %get-tuple-element.15), channel_id=1, source_target_pairs={{1,2},{2,1},{3,4},{4,3},{5,6},{6,5},{7,8},{8,7},{9,10},{10,9},{11,... | collective-permute-start | bytes 1572872 | tf_op jit(solution)/shard_map/ppermute | solution.py:508
  3.3 15.5 %collective-permute-start.1 = (f32[1024,128]{1,0:T(8,128)S(1)}, f32[1024,128]{1,0:T(8,128)S(1)}, u32[]{:S(2)}, u32[]{:S(2)}) collective-permute-start(f32[1024,128]{1,0:T(8,128)S(1)} %get-tuple-element.16), channel_id=1, source_target_pairs={{0,1},{1,0},{2,3},{3,2},{4,5},{5,4},{6,7},{7,6},{8,9},{9,8},{10,11... | collective-permute-start | bytes 1572872 | tf_op jit(solution)/shard_map/ppermute | solution.py:508
  18.8 16.5 %copy-start = (f32[2,16,1024]{2,1,0:T(8,128)S(1)}, f32[2,16,1024]{2,1,0:T(8,128)}, u32[]{:S(2)}) copy-start(f32[2,16,1024]{2,1,0:T(8,128)} %tracers.1) | copy-start | bytes 393220
  18.8 16.5 %copy-start.1 = (s32[16,16,16]{2,1,0:T(8,128)S(1)}, s32[16,16,16]{2,1,0:T(8,128)}, u32[]{:S(2)}) copy-start(s32[16,16,16]{2,1,0:T(8,128)} %send_rows.3) | copy-start | bytes 49156
  18.9 16.5 %copy-start.2 = (f32[16,1024]{1,0:T(8,128)S(1)}, f32[16,1024]{1,0:T(8,128)}, u32[]{:S(2)}) copy-start(f32[16,1024]{1,0:T(8,128)} %potential.1) | copy-start | bytes 196612
  18.9 16.5 %copy-start.3 = (s32[6,1024]{1,0:T(8,128)S(1)}, s32[6,1024]{1,0:T(8,128)}, u32[]{:S(2)}) copy-start(s32[6,1024]{1,0:T(8,128)} %neighbors.1) | copy-start | bytes 73732
  18.9 16.5 %copy-start.4 = (f32[6,1024]{1,0:T(8,128)S(1)}, f32[6,1024]{1,0:T(8,128)}, u32[]{:S(2)}) copy-start(f32[6,1024]{1,0:T(8,128)} %normal.1) | copy-start | bytes 73732
  18.9 16.5 %copy-start.5 = (f32[6,1024]{1,0:T(8,128)S(1)}, f32[6,1024]{1,0:T(8,128)}, u32[]{:S(2)}) copy-start(f32[6,1024]{1,0:T(8,128)} %weight.1) | copy-start | bytes 73732

commit v6 on v5

--- a/solution.py
+++ b/solution.py
@@ -11,7 +11,7 @@
 LANES = 128
 FCT_FLOOR = 0.001
 TABLE_ROWS = 24
-VMEM_LIMIT = 40 * 1024 * 1024
+VMEM_LIMIT = 32 * 1024 * 1024
 
 
 def lane_gather(values, index):
@@ -94,14 +94,15 @@
 def pack_kernel(
     spectra_in, tracers_in, potential_in, neighbors_in, normal_in, weight_in, current_in,
     send_rows, slot_in, near_in, angle_in, face_in, wind_in,
-    rows_out, outer, inner, spectra, node_slot, near, wind, cosine, sine, project, choice,
-    angle, face, tracers, potential, neighbors, normal, weight, current, own_rows, sems,
+    rows_out, outer, inner, spectra, node_slot, near, angle, face, wind,
+    tracers, potential, neighbors, normal, weight, coupled,
+    current, sems,
 ):
     peers, _, capacity = send_rows.shape
     me = lax.axis_index("mesh")
     copies = []
     for source, target in (
-        (send_rows.at[me], own_rows),
+        (send_rows.at[me], coupled.at[1]),
         (current_in, current),
         (slot_in, node_slot),
         (spectra_in, spectra),
@@ -110,6 +111,8 @@
         (neighbors_in, neighbors),
         (normal_in, normal),
         (weight_in, weight),
+        (send_rows.at[jnp.maximum(me - 1, 0)], coupled.at[0]),
+        (send_rows.at[jnp.minimum(me + 1, peers - 1)], coupled.at[2]),
         (near_in, near),
         (angle_in, angle),
         (face_in, face),
@@ -118,7 +121,7 @@
         copy = pltpu.make_async_copy(source, target, sems.at[len(copies)])
         copy.start()
         copies.append(copy)
-    for copy in copies[:3] + copies[9:]:
+    for copy in copies[:3]:
         copy.wait()
     freqs, dirs = spectra.shape[:2]
     layers, cells = potential.shape
@@ -128,7 +131,7 @@
         [current[:, b * LANES : (b + 1) * LANES] for b in range(blocks)], axis=0
     )
     place = row_iota(2 * blocks)
-    halves = slot_rows(own_rows[...])
+    halves = slot_rows(coupled[1])
     values = [[], []]
     for cell in halves:
         found = lane_gather(stacked, spread(cell % LANES, 2 * blocks))
@@ -136,8 +139,7 @@
             picked = jnp.where(place == 2 * (cell // LANES) + part, found, 0.0)
             values[part].append(jnp.sum(picked, axis=0, keepdims=True))
     rows_out[...] = peer_rows(values, peers, capacity)
-    node_tables(me, near, angle, face, cosine, sine, project, choice)
-    for copy in copies[3:9]:
+    for copy in copies[3:]:
         copy.wait()
     odd = me % 2 == 1
     for out, upward in ((outer, odd), (inner, jnp.logical_not(odd))):
@@ -184,6 +186,73 @@
             out[at:, :] = jnp.zeros((outer.shape[0] - at, LANES), jnp.float32)
 
 
+def choose(cells, first, lanes, matrix):
+    place = cells - first
+    for k in range(3):
+        source = row_iota(LANES) + k * LANES
+        part = jnp.where(source == place, 1.0, 0.0)
+        if k == 1:
+            part = part - jnp.where(row_iota(LANES) == lane_iota(LANES), 1.0, 0.0)
+        matrix[k * LANES : (k + 1) * LANES, lanes] = part.astype(jnp.bfloat16)
+
+
+def stack_split(x):
+    first, second = split(x)
+    return jnp.concatenate([first, second], axis=0)
+
+
+def differences(parts, matrix):
+    mixed = jnp.concatenate(parts, axis=1)
+    out = jnp.dot(mixed, matrix, preferred_element_type=jnp.float32)
+    rows = out.shape[0] // 2
+    return out[:rows] + out[rows:]
+
+
+def prepare_kernel(
+    near, angle, face, tracers, potential, neighbors, normal, weight, coupled,
+    cosine, sine, project, choice,
+    fields, pieces, matrices, inside, cell_cosine, cell_sine, cell_scale, sums,
+):
+    me = lax.axis_index("mesh")
+    node_tables(me, near, angle, face, cosine, sine, project, choice)
+    tracer_count, layers, cells = tracers.shape
+    blocks = cells // LANES
+    edges = neighbors.shape[0]
+    field_rows = (tracer_count + 1) * layers
+    for b in range(blocks):
+        lanes = slice(b * LANES, (b + 1) * LANES)
+        for t in range(tracer_count):
+            fields[b, t * layers : (t + 1) * layers, :] = tracers[t, :, lanes]
+        fields[b, field_rows - layers : field_rows, :] = potential[:, lanes]
+        pieces[b] = stack_split(fields[b])
+        w = weight[:, lanes]
+        cell_scale[b, 0:edges, :] = w
+        cell_cosine[b, 0:edges, :] = w * jnp.cos(normal[:, lanes])
+        cell_sine[b, 0:edges, :] = w * jnp.sin(normal[:, lanes])
+        for s in range(edges):
+            choose(
+                neighbors[s : s + 1, lanes],
+                (me * blocks + b - 1) * LANES,
+                slice(s * LANES, (s + 1) * LANES),
+                matrices.at[b],
+            )
+    for b in range(1, blocks - 1):
+        inside[b - 1] = differences(
+            [pieces[b - 1], pieces[b], pieces[b + 1]], matrices[b]
+        )
+    for which in range(3):
+        first = 0 if which != 0 else cells - LANES
+        count = blocks if which == 1 else 1
+        start = (0, 1, blocks + 1)[which]
+        for half, names in enumerate(slot_rows(coupled[which])):
+            named = jnp.transpose(spread(names, LANES).astype(jnp.float32))
+            for b in range(count):
+                cell = (lane_iota(LANES) + (first + b * LANES)).astype(jnp.float32)
+                picked = jnp.where(named == cell, 1.0, 0.0).astype(jnp.bfloat16)
+                lanes = slice((start + b) * LANES, (start + b + 1) * LANES)
+                sums[half * LANES : (half + 1) * LANES, lanes] = picked
+
+
 def node_currents(table, slot, which, capacity):
     peers = table.shape[0]
     owner = row_iota(peers) == slot // capacity
@@ -309,9 +378,14 @@
         ],
         axis=0,
     ) * (1.0 / dirs)
-    in_order = exact_dot(
-        stokes, lax.broadcasted_iota(jnp.int32, (halves * LANES, LANES), 0) == slot
-    )
+    named = lax.broadcasted_iota(jnp.int32, (halves * LANES, LANES), 0) == slot
+    in_order = lax.dot_general(
+        three_parts(stokes),
+        jnp.where(named, 1.0, 0.0).astype(jnp.bfloat16),
+        (((1,), (1,)), ((), ())),
+        preferred_element_type=jnp.float32,
+    )
+    in_order = in_order[0:2] + (in_order[2:4] + in_order[4:6])
     values = [
         [in_order[part : part + 1, h * LANES : (h + 1) * LANES] for h in range(halves)]
         for part in range(2)
@@ -319,71 +393,66 @@
     rows_out[...] = peer_rows(values, peers, capacity)
 
 
-def exact_dot(values, chosen):
+def three_parts(values):
     first = values.astype(jnp.bfloat16).astype(jnp.float32)
     left = values - first
     second = left.astype(jnp.bfloat16).astype(jnp.float32)
     third = left - second
     pad = jnp.zeros((10, values.shape[1]), jnp.float32)
-    parts = jnp.concatenate([first, second, third, pad], axis=0).astype(jnp.bfloat16)
-    picks = jnp.where(chosen, 1.0, 0.0).astype(jnp.bfloat16)
-    out = lax.dot_general(
-        parts, picks, (((1,), (1,)), ((), ())), preferred_element_type=jnp.float32
-    )
-    return out[0:2] + (out[2:4] + out[4:6])
+    return jnp.concatenate([first, second, third, pad], axis=0).astype(jnp.bfloat16)
 
 
 def tracer_kernel(
-    tracers, potential, outer, inner, table, neighbors, normal, weight, send_rows, spectra,
-    tracers_new, spectra_out, fields, target, cosine, sine, scale, stokes, antiflux, lowered, ratios, sem,
+    capacity, shape,
+    outer, inner, table, fields, pieces, matrices, inside, cosine, sine, scale, sums, spectra,
+    tracers_new, spectra_out,
+    halo, halo_pieces, halo_matrices, halo_tables, beside, stokes, antiflux, lowered, ratios,
+    ratio_pieces, sem,
 ):
     write = pltpu.make_async_copy(spectra, spectra_out, sem)
     write.start()
     me = lax.axis_index("mesh")
-    peers, _, capacity = send_rows.shape
+    tracer_count, layers, edges = shape
+    peers = table.shape[0]
     halves = peers * capacity // LANES
-    tracer_count, layers, cells = tracers.shape
-    blocks = cells // LANES
-    edges = neighbors.shape[0]
-    field_rows = (tracer_count + 1) * layers
-    groups = field_rows // 8
+    blocks, field_rows, _ = fields.shape
     layer_groups = layers // 8
     tracer_groups = tracer_count * layer_groups
-
     odd = me % 2 == 1
+
     for b in range(2):
         x = outer[b * field_rows : (b + 1) * field_rows, :]
         y = inner[b * field_rows : (b + 1) * field_rows, :]
-        fields[b] = jnp.where(odd, y, x)
-        fields[blocks + 2 + b] = jnp.where(odd, x, y)
-    for b in range(blocks):
-        lanes = slice(b * LANES, (b + 1) * LANES)
-        for t in range(tracer_count):
-            fields[b + 2, t * layers : (t + 1) * layers, :] = tracers[t, :, lanes]
-        fields[b + 2, field_rows - layers : field_rows, :] = potential[:, lanes]
+        for side, value in ((0, jnp.where(odd, y, x)), (1, jnp.where(odd, x, y))):
+            halo[2 * side + b] = value
+            halo_pieces[2 * side + b] = stack_split(value)
     at = 2 * field_rows
-    for b in range(blocks + 2):
-        if b == 0 or b == blocks + 1:
-            x = outer[at : at + TABLE_ROWS, :]
-            y = inner[at : at + TABLE_ROWS, :]
-            table_rows = jnp.where(odd, y, x) if b == 0 else jnp.where(odd, x, y)
-            near = table_rows[0:edges].astype(jnp.int32)
-            angle = table_rows[8 : 8 + edges]
-            w = table_rows[16 : 16 + edges]
-        else:
-            lanes = slice((b - 1) * LANES, b * LANES)
-            near = neighbors[:, lanes]
-            angle = normal[:, lanes]
-            w = weight[:, lanes]
-        target[b, 0:edges, :] = near
-        scale[b, 0:edges, :] = w
-        cosine[b, 0:edges, :] = w * jnp.cos(angle)
-        sine[b, 0:edges, :] = w * jnp.sin(angle)
+    x = outer[at : at + TABLE_ROWS, :]
+    y = inner[at : at + TABLE_ROWS, :]
+    for side, rows in ((0, jnp.where(odd, y, x)), (1, jnp.where(odd, x, y))):
+        w = rows[16 : 16 + edges]
+        halo_tables[side, 0, 0:edges, :] = w
+        halo_tables[side, 1, 0:edges, :] = w * jnp.cos(rows[8 : 8 + edges])
+        halo_tables[side, 2, 0:edges, :] = w * jnp.sin(rows[8 : 8 + edges])
+        near = rows[0:edges].astype(jnp.int32)
+        first = (me * blocks - 2 if side == 0 else me * blocks + blocks - 1) * LANES
+        for s in range(edges):
+            choose(
+                near[s : s + 1, :],
+                first,
+                slice(s * LANES, (s + 1) * LANES),
+                halo_matrices.at[side],
+            )
+    beside[0] = differences([halo_pieces[0], halo_pieces[1], pieces[0]], halo_matrices[0])
+    beside[1] = differences([halo_pieces[1], pieces[0], pieces[1]], matrices[0])
+    beside[2] = differences(
+        [pieces[blocks - 2], pieces[blocks - 1], halo_pieces[2]], matrices[blocks - 1]
+    )
+    beside[3] = differences([pieces[blocks - 1], halo_pieces[2], halo_pieces[3]], halo_matrices[1])
 
     received = table[...]
     lane_of = lane_iota(peers)
     for which in range(3):
-        cell = slot_rows(send_rows[jnp.clip(me + which - 1, 0, peers - 1)])
         values = []
         for part in range(2):
             lane = (2 * which + part) * capacity + lane_of % capacity
@@ -393,102 +462,103 @@
                 mine = row_iota(peers) == (lane_of + half * LANES) // capacity
                 row.append(jnp.sum(jnp.where(mine, found, 0.0), axis=0, keepdims=True))
             values.append(jnp.concatenate(row, axis=1))
-        values = jnp.concatenate(values, axis=0)
-        names = jnp.concatenate(cell, axis=1)
-        count = cells if which == 1 else LANES
-        start = cells - LANES if which == 0 else 0
-        number = lax.broadcasted_iota(jnp.int32, (count, halves * LANES), 0) + start
-        sums = exact_dot(values, number == names)
-        if which == 1:
-            for b in range(blocks):
-                stokes[b + 1, 0:2, :] = sums[:, b * LANES : (b + 1) * LANES]
-        else:
-            stokes[0 if which == 0 else blocks + 1, 0:2, :] = sums
+        parts = three_parts(jnp.concatenate(values, axis=0))
+        start = (0, 1, blocks + 1)[which]
+        count = blocks if which == 1 else 1
+        total = jnp.dot(
+            parts,
+            sums[:, start * LANES : (start + count) * LANES],
+            preferred_element_type=jnp.float32,
+        )
+        total = total[0:2] + (total[2:4] + total[4:6])
+        for b in range(count):
+            stokes[start + b, 0:2, :] = total[:, b * LANES : (b + 1) * LANES]
 
     decay = [
         jnp.exp(-3.0 / layers * (row_iota(8) + 8 * g).astype(jnp.float32))
         for g in range(layer_groups)
     ]
 
-    def neighbour_of(near, b, s):
-        row = spread(near[s : s + 1, :], 8)
-        side = row // LANES - (me * blocks + b - 1)
-        return row % LANES, side
-
-    def low_order(b, carry):
-        near = target[b]
-        w = scale[b]
-        slope = cosine[b] * stokes[b, 0:1, :] + sine[b] * stokes[b, 1:2, :]
-        own = [fields[b + 1, 8 * g : 8 * g + 8, :] for g in range(groups)]
+    def low_order(b, value, change, w, wx, wy, keep):
+        slope = wx * stokes[b, 0:1, :] + wy * stokes[b, 1:2, :]
+        own = [value(8 * g) for g in range(tracer_groups)]
         zero = jnp.zeros((8, LANES), jnp.float32)
-        out_speed = [zero] * layer_groups
+        speed_sum = [zero] * layer_groups
         inflow = [zero] * tracer_groups
-        upper = own[:tracer_groups]
-        lower = own[:tracer_groups]
+        highest = [zero] * tracer_groups
+        lowest = [zero] * tracer_groups
         positive = [zero] * tracer_groups
         negative = [zero] * tracer_groups
         for s in range(edges):
-            lane, side = neighbour_of(near, b, s)
             w8 = spread(w[s : s + 1, :], 8)
             slope8 = spread(slope[s : s + 1, :], 8)
-            beside = []
-            for g in range(groups):
-                rows = slice(8 * g, 8 * g + 8)
-                middle = lane_gather(own[g], lane)
-                left = lane_gather(fields[b, rows, :], lane)
-                right = lane_gather(fields[b + 2, rows, :], lane)
-                beside.append(jnp.where(side == 0, middle, jnp.where(side < 0, left, right)))
             for lg in range(layer_groups):
-                k = tracer_groups + lg
-                speed = w8 * (beside[k] - own[k]) + decay[lg] * slope8
-                up = jnp.maximum(speed, 0.0)
+                speed = w8 * change(8 * (tracer_groups + lg), s) + decay[lg] * slope8
                 down = jnp.minimum(speed, 0.0)
-                half = 0.5 * (up - down)
-                out_speed[lg] = out_speed[lg] + up
+                half = 0.5 * speed - down
+                speed_sum[lg] = speed_sum[lg] + speed
                 for t in range(tracer_count):
                     g = t * layer_groups + lg
-                    q = beside[g]
-                    flux = half * (q - own[g])
-                    antiflux[b, s, 8 * g : 8 * g + 8, :] = flux
-                    inflow[g] = inflow[g] + down * q
-                    upper[g] = jnp.maximum(upper[g], q)
-                    lower[g] = jnp.minimum(lower[g], q)
+                    step = change(8 * g, s)
+                    flux = half * step
+                    if keep:
+                        antiflux[b - 1, s, 8 * g : 8 * g + 8, :] = flux
+                    inflow[g] = inflow[g] + down * step
+                    highest[g] = jnp.maximum(highest[g], step)
+                    lowest[g] = jnp.minimum(lowest[g], step)
                     positive[g] = positive[g] + jnp.maximum(flux, 0.0)
                     negative[g] = negative[g] - jnp.minimum(flux, 0.0)
+        plus, minus = [], []
         for g in range(tracer_groups):
-            rows = slice(8 * g, 8 * g + 8)
-            value = own[g] - (out_speed[g % layer_groups] * own[g] + inflow[g])
-            lowered[b, rows, :] = value
-            plus = jnp.maximum(upper[g] - value, 0.0) / (negative[g] + FCT_FLOOR)
-            minus = jnp.maximum(value - lower[g], 0.0) / (positive[g] + FCT_FLOOR)
-            ratios[b, rows, :] = jnp.minimum(1.0, plus)
-            at = 8 * (tracer_groups + g)
-            ratios[b, at : at + 8, :] = jnp.minimum(1.0, minus)
+            loss = speed_sum[g % layer_groups] * own[g] + inflow[g]
+            if keep:
+                lowered[b - 1, 8 * g : 8 * g + 8, :] = own[g] - loss
+            up = jnp.maximum(highest[g] + loss, 0.0) / (negative[g] + FCT_FLOOR)
+            down = jnp.maximum(-loss - lowest[g], 0.0) / (positive[g] + FCT_FLOOR)
+            plus.append(jnp.minimum(1.0, up))
+            minus.append(jnp.minimum(1.0, down))
+        both = jnp.concatenate(plus + minus, axis=0)
+        ratios[b] = both
+        ratio_pieces[b] = stack_split(both)
+
+    def band(ref, *index):
+        return lambda row: ref[(*index, slice(row, row + 8), slice(None))]
+
+    def column(ref, index):
+        return lambda row, s: ref[index, row : row + 8, s * LANES : (s + 1) * LANES]
+
+    def own_tables(i):
+        return scale[i], cosine[i], sine[i]
+
+    def inner_block(i, carry):
+        low_order(i + 2, band(fields, i + 1), column(inside, i), *own_tables(i + 1), True)
         return carry
 
-    lax.fori_loop(0, blocks + 2, low_order, 0)
+    for side in range(2):
+        b = side * (blocks + 1)
+        tables = tuple(halo_tables[side, k] for k in range(3))
+        near = 1 + side
+        low_order(b, band(halo, near), column(beside, 3 * side), *tables, False)
+        i = side * (blocks - 1)
+        low_order(i + 1, band(fields, i), column(beside, 1 + side), *own_tables(i), True)
+    lax.fori_loop(0, blocks - 2, inner_block, 0)
 
     def limit(i, carry):
         b = i + 1
-        near = target[b]
-        out = [lowered[b, 8 * g : 8 * g + 8, :] for g in range(tracer_groups)]
+        step = differences(
+            [ratio_pieces[b - 1], ratio_pieces[b], ratio_pieces[b + 1]], matrices[i]
+        )
+        out = [lowered[i, 8 * g : 8 * g + 8, :] for g in range(tracer_groups)]
         own = [ratios[b, 8 * g : 8 * g + 8, :] for g in range(2 * tracer_groups)]
         for s in range(edges):
-            lane, side = neighbour_of(near, b, s)
-            beside = []
-            for g in range(2 * tracer_groups):
-                rows = slice(8 * g, 8 * g + 8)
-                middle = lane_gather(own[g], lane)
-                left = lane_gather(ratios[b - 1, rows, :], lane)
-                right = lane_gather(ratios[b + 1, rows, :], lane)
-                beside.append(jnp.where(side == 0, middle, jnp.where(side < 0, left, right)))
+            lanes = slice(s * LANES, (s + 1) * LANES)
             for g in range(tracer_groups):
-                flux = antiflux[b, s, 8 * g : 8 * g + 8, :]
                 m = g + tracer_groups
+                flux = antiflux[i, s, 8 * g : 8 * g + 8, :]
+                plus = own[g] + step[8 * g : 8 * g + 8, lanes]
+                minus = own[m] + step[8 * m : 8 * m + 8, lanes]
                 factor = jnp.where(
-                    flux >= 0.0,
-                    jnp.minimum(own[m], beside[g]),
-                    jnp.minimum(own[g], beside[m]),
+                    flux >= 0.0, jnp.minimum(own[m], plus), jnp.minimum(own[g], minus)
                 )
                 out[g] = out[g] - factor * flux
         lanes = pl.ds(pl.multiple_of(i * LANES, LANES), LANES)
@@ -540,122 +610,132 @@
     f32 = jnp.float32
 
     stored = pl.BlockSpec(memory_space=pltpu.HBM)
-    currents, outer, inner, *node_parts = pl.pallas_call(
+    rows = tracer_count * layers
+
+    def like(x):
+        return jax.ShapeDtypeStruct(x.shape, x.dtype)
+
+    def shaped(*shape, dtype=f32):
+        return jax.ShapeDtypeStruct(shape, dtype)
+
+    def call(kernel, name, inputs, outputs, scratch, out_specs=None):
+        return pl.pallas_call(
+            kernel,
+            out_shape=outputs,
+            in_specs=[whole_spec()] * len(inputs),
+            out_specs=out_specs or (whole_spec(),) * len(outputs),
+            scratch_shapes=scratch,
+            compiler_params=params,
+            name=name,
+        )(*inputs)
+
+    inputs = (
+        spectra, tracers, potential, cell_neighbors, cell_normal, cell_weight, surface_current,
+        send_rows, slots, node_neighbors, node_normal, node_weight, wind_velocity,
+    )
+    (
+        currents, outer, inner, own_spectra, own_slots, near, angle, face, wind,
+        own_tracers, own_potential, neighbors, normal, weight, coupled,
+    ) = pl.pallas_call(
         pack_kernel,
         out_shape=(
-            jax.ShapeDtypeStruct((peers, LANES), f32),
-            jax.ShapeDtypeStruct((message_rows, LANES), f32),
-            jax.ShapeDtypeStruct((message_rows, LANES), f32),
-            jax.ShapeDtypeStruct(spectra.shape, f32),
-            jax.ShapeDtypeStruct(slots.shape, jnp.int32),
-            jax.ShapeDtypeStruct(node_neighbors.shape, jnp.int32),
-            jax.ShapeDtypeStruct(wind_velocity.shape, f32),
-            jax.ShapeDtypeStruct(node_normal.shape, f32),
-            jax.ShapeDtypeStruct(node_normal.shape, f32),
-            jax.ShapeDtypeStruct((edges, dirs, LANES), f32),
-            jax.ShapeDtypeStruct((4 * LANES, edges * LANES), jnp.bfloat16),
+            shaped(peers, LANES),
+            shaped(message_rows, LANES),
+            shaped(message_rows, LANES),
+            like(spectra),
+            like(slots),
+            like(node_neighbors),
+            like(node_normal),
+            like(node_weight),
+            like(wind_velocity),
+            like(tracers),
+            like(potential),
+            like(cell_neighbors),
+            like(cell_normal),
+            like(cell_weight),
+            shaped(3, peers, capacity, dtype=jnp.int32),
         ),
-        in_specs=[stored] * 13,
-        out_specs=(whole_spec(),) * 11,
+        in_specs=[stored] * len(inputs),
+        out_specs=(whole_spec(),) * 15,
         scratch_shapes=[
-            pltpu.VMEM(node_normal.shape, f32),
-            pltpu.VMEM(node_weight.shape, f32),
-            pltpu.VMEM(tracers.shape, f32),
-            pltpu.VMEM(potential.shape, f32),
-            pltpu.VMEM(cell_neighbors.shape, jnp.int32),
-            pltpu.VMEM(cell_normal.shape, f32),
-            pltpu.VMEM(cell_weight.shape, f32),
             pltpu.VMEM(surface_current.shape, f32),
-            pltpu.VMEM(send_rows.shape[1:], jnp.int32),
-            pltpu.SemaphoreType.DMA((13,)),
+            pltpu.SemaphoreType.DMA((15,)),
         ],
         compiler_params=params,
         name="pack",
-    )(
-        *(
-            pltpu.with_memory_space_constraint(x, pltpu.HBM)
-            for x in (
-                spectra, tracers, potential, cell_neighbors, cell_normal, cell_weight,
-                surface_current, send_rows, slots, node_neighbors, node_normal, node_weight,
-                wind_velocity,
-            )
-        )
-    )
+    )(*(pltpu.with_memory_space_constraint(x, pltpu.HBM) for x in inputs))
     outer = swap(outer, 1, peers)
     inner = swap(inner, 0, peers)
 
+    (
+        cosine, sine, project, choice,
+        fields, pieces, matrices, inside, cell_cosine, cell_sine, cell_scale, sums,
+    ) = call(
+        prepare_kernel,
+        "prepare",
+        (
+            near, angle, face, own_tracers, own_potential, neighbors, normal, weight, coupled,
+        ),
+        (
+            like(node_normal),
+            like(node_normal),
+            shaped(edges, dirs, LANES),
+            shaped(4 * LANES, edges * LANES, dtype=jnp.bfloat16),
+            shaped(blocks, field_rows, LANES),
+            shaped(blocks, 2 * field_rows, LANES, dtype=jnp.bfloat16),
+            shaped(blocks, 3 * LANES, edges * LANES, dtype=jnp.bfloat16),
+            shaped(blocks - 2, field_rows, edges * LANES),
+            shaped(blocks, 8, LANES),
+            shaped(blocks, 8, LANES),
+            shaped(blocks, 8, LANES),
+            shaped(peers * capacity, (blocks + 2) * LANES, dtype=jnp.bfloat16),
+        ),
+        [],
+    )
+    currents, cosine = lax.optimization_barrier((currents, cosine))
     currents = lax.all_to_all(currents, "mesh", 0, 0, tiled=True)
 
     step_pairs = 5 if freqs % 10 == 0 else 1
     stride = (dirs + 7) // 8 * 8
-    spectra_new, stokes_rows = pl.pallas_call(
+    spectra_new, stokes_rows = call(
         functools.partial(wave_kernel, capacity, step_pairs),
-        out_shape=(
-            jax.ShapeDtypeStruct(spectra.shape, f32),
-            jax.ShapeDtypeStruct((peers, LANES), f32),
+        "wave",
+        (
+            own_spectra, outer, inner, currents, own_slots, near, wind,
+            cosine, sine, project, choice,
         ),
-        in_specs=[whole_spec()] * 11,
-        out_specs=(whole_spec(),) * 2,
-        scratch_shapes=[
+        (like(spectra), shaped(peers, LANES)),
+        [
             pltpu.VMEM((8, LANES), f32),
             pltpu.VMEM((2 * step_pairs * stride, 2 * LANES), f32),
             pltpu.VMEM((2 * step_pairs * stride, edges * LANES), f32),
         ],
-        compiler_params=params,
-        name="wave",
-    )(
-        node_parts[0], outer, inner, currents, *node_parts[1:],
-    )
-
+    )
     stokes_all = lax.all_to_all(stokes_rows, "mesh", 0, 0, tiled=True)
 
-    def head_spec():
-        return pl.BlockSpec((head_rows, LANES), lambda i: (0, 0))
-
-    def full_spec(x):
-        zeros = (0,) * x.ndim
-        return pl.BlockSpec(x.shape, lambda i: zeros)
-
-    rows = tracer_count * layers
-    tracers_new, spectra_new = pl.pallas_call(
-        tracer_kernel,
-        grid=(1,),
-        out_shape=(
-            jax.ShapeDtypeStruct(tracers.shape, f32),
-            jax.ShapeDtypeStruct(spectra.shape, f32),
+    return call(
+        functools.partial(tracer_kernel, capacity, (tracer_count, layers, edges)),
+        "tracer",
+        (
+            outer, inner, stokes_all, fields, pieces, matrices, inside, cell_cosine, cell_sine,
+            cell_scale, sums, pltpu.with_memory_space_constraint(spectra_new, pltpu.VMEM),
         ),
-        in_specs=[
-            full_spec(tracers),
-            full_spec(potential),
-            head_spec(),
-            head_spec(),
-            full_spec(stokes_all),
-            full_spec(cell_neighbors),
-            full_spec(cell_normal),
-            full_spec(cell_weight),
-            full_spec(send_rows),
-            pl.BlockSpec(memory_space=pl.ANY),
-        ],
-        out_specs=(full_spec(tracers), stored),
-        scratch_shapes=[
-            pltpu.VMEM((blocks + 4, field_rows, LANES), f32),
-            pltpu.VMEM((blocks + 2, 8, LANES), jnp.int32),
+        (like(tracers), like(spectra)),
+        [
+            pltpu.VMEM((4, field_rows, LANES), f32),
+            pltpu.VMEM((4, 2 * field_rows, LANES), jnp.bfloat16),
+            pltpu.VMEM((2, 3 * LANES, edges * LANES), jnp.bfloat16),
+            pltpu.VMEM((2, 3, 8, LANES), f32),
+            pltpu.VMEM((4, field_rows, edges * LANES), f32),
             pltpu.VMEM((blocks + 2, 8, LANES), f32),
-            pltpu.VMEM((blocks + 2, 8, LANES), f32),
-            pltpu.VMEM((blocks + 2, 8, LANES), f32),
-            pltpu.VMEM((blocks + 2, 8, LANES), f32),
-            pltpu.VMEM((blocks + 2, edges, rows, LANES), f32),
-            pltpu.VMEM((blocks + 2, rows, LANES), f32),
+            pltpu.VMEM((blocks, edges, rows, LANES), f32),
+            pltpu.VMEM((blocks, rows, LANES), f32),
             pltpu.VMEM((blocks + 2, 2 * rows, LANES), f32),
+            pltpu.VMEM((blocks + 2, 4 * rows, LANES), jnp.bfloat16),
             pltpu.SemaphoreType.DMA(()),
         ],
-        compiler_params=params,
-        name="tracer",
-    )(
-        tracers, potential, outer, inner, stokes_all, cell_neighbors, cell_normal, cell_weight,
-        send_rows, pltpu.with_memory_space_constraint(spectra_new, pltpu.VMEM),
-    )
-    return tracers_new, spectra_new
+        out_specs=(whole_spec(), stored),
+    )
 
 
 def solution(mesh):

time: 41.1 us -> 39.3 us (0.956)
  blocking collectives: 23.8 us -> 21.7 us
    all_to_all x1, blocking collectives: 12.6 us -> 10.5 us  [local(): stokes_all = lax.all_to_all(stokes_rows, 'mesh', 0, 0, tiled=True)]
    pallas_call x3 -> x4, Pallas kernels: 11.2 us -> 11.6 us  [the longest x3 10 us: call(): pl.pallas_call(kernel, out_shape=outputs, in_specs=[whole_spec()] * len(i...]
  transfers between devices with their start and end apart: 2 -> 2, of which waited for: 0 -> 0; matrix products, arithmetic and copies ran while one was open for 0% -> 0% of each run, Pallas kernels for 0% -> 5%
where the time goes in v6:
time: 39.3 us; the launch traced here: 39 us
  blocking collectives  21.7 us (55%)
  Pallas kernels  11.6 us (30%)
  starting transfers between devices  5.06 us (13%)
  between operations  0.67 us (2%)
    all_to_all x1, blocking collectives, local(): currents = lax.all_to_all(currents, 'mesh', 0, 0, tiled=True)  11.2 us
    all_to_all x1, blocking collectives, local(): stokes_all = lax.all_to_all(stokes_rows, 'mesh', 0, 0, tiled=True)  10.5 us
    pallas_call x3, Pallas kernels, call(): pl.pallas_call(kernel, out_shape=outputs, in_specs=[whole_spec()] * len(i...  10 us
    ppermute x2, starting transfers between devices, swap(): return lax.ppermute(message, 'mesh', pairs)  5.06 us
    pallas_call x1, Pallas kernels, local(): pl.pallas_call(pack_kernel, out_shape=(shaped(peers, LANES), shaped(messa...  1.6 us
  transfers between devices with their start and end apart: 2, of which 0 were waited for; matrix products, arithmetic and copies ran while one was open for 0% of the time, Pallas kernels for 5%

profile of v6, /device:TPU:0, one launch (start us, length us, event | category | flops | bytes accessed | tf_op | source)
XLA Modules:
  0.0 39.0 jit_solution(16594943482953385064)
XLA Ops:
  0.6 1.6 %pack.1 = (f32[16,128]{1,0:T(8,128)S(1)}, f32[1024,128]{1,0:T(8,128)S(1)}, f32[1024,128]{1,0:T(8,128)S(1)}, f32[50,36,128]{2,1,0:T(8,128)S(1)}, s32[1,128]{1,0:T...) custom-call(f32[50,36,128]{2,1,0:T(8,128)} %spectra_in.1, ...), custom_call_target="tpu_custom_call" | custom-call | tf_op jit(solution)/shard_map/pack/pallas_call | solution.py:639
  2.2 0.7 %collective-permute-start = (f32[1024,128]{1,0:T(8,128)S(1)}, f32[1024,128]{1,0:T(8,128)S(1)}, u32[]{:S(2)}, u32[]{:S(2)}) collective-permute-start(f32[1024,128]{1,0:T(8,128)S(1)} %get-tuple-element.33), channel_id=1, source_target_pairs={{1,2},{2,1},{3,4},{4,3},{5,6},{6,5},{7,8},{8,7},{9,10},{10,9},{11,... | collective-permute-start | bytes 1572872 | tf_op jit(solution)/shard_map/ppermute | solution.py:578
  2.9 4.4 %collective-permute-start.1 = (f32[1024,128]{1,0:T(8,128)S(1)}, f32[1024,128]{1,0:T(8,128)S(1)}, u32[]{:S(2)}, u32[]{:S(2)}) collective-permute-start(f32[1024,128]{1,0:T(8,128)S(1)} %get-tuple-element.34), channel_id=1, source_target_pairs={{0,1},{1,0},{2,3},{3,2},{4,5},{5,4},{6,7},{7,6},{8,9},{9,8},{10,11... | collective-permute-start | bytes 1572872 | tf_op jit(solution)/shard_map/ppermute | solution.py:578
  7.3 2.1 %prepare.1 = (f32[6,128]{1,0:T(8,128)S(1)}, f32[6,128]{1,0:T(8,128)S(1)}, f32[6,36,128]{2,1,0:T(8,128)S(1)}, bf16[512,768]{1,0:T(8,128)(2,1)S(1)}, f32[8,48,128]...) custom-call(s32[6,128]{1,0:T(8,128)S(1)} %get-tuple-element.37.near., ...), custom_call_target="tpu_custom_call" | custom-call | tf_op jit(solution)/shard_map/prepare/pallas_call | solution.py:622
  9.5 11.2 %all_to_all.22 = f32[16,1,128]{2,1,0:T(1,128)S(1)} all-to-all(f32[16,1,128]{2,1,0:T(1,128)S(1)} %bitcast.11), channel_id=1, replica_groups=mesh['groups'=2,'mesh'=16] {'mesh'}, dimensions={0} | all-to-all | bytes 16384 | tf_op jit(solution)/shard_map/all_to_all | solution.py:696
  20.6 0.0 collective-permute-done.outer
  20.7 0.0 collective-permute-done.1.inner
  20.7 3.8 %wave.1 = (f32[50,36,128]{2,1,0:T(8,128)S(1)}, f32[16,128]{1,0:T(8,128)S(1)}) custom-call(f32[50,36,128]{2,1,0:T(8,128)S(1)} %get-tuple-element.35.spectra, f32[1024,128]{1,0:T(8,128)S(1)} %collective-permute-done.outer, f32[1024,128]{1,0:T(8,128)S(1)} %collective-permute-done.1.inner, f32[16,128]{1,0:T(8,128)S(1)} %bitcast.9, ...), custom_call_target="tpu_custom_call" | custom-call | tf_op jit(solution)/shard_map/wave/pallas_call | solution.py:622
  24.4 10.5 %all_to_all.23 = f32[16,1,128]{2,1,0:T(1,128)S(1)} all-to-all(f32[16,1,128]{2,1,0:T(1,128)S(1)} %bitcast.12), channel_id=1, replica_groups=mesh['groups'=2,'mesh'=16] {'mesh'}, dimensions={0} | all-to-all | bytes 16384 | tf_op jit(solution)/shard_map/all_to_all | solution.py:714
  34.9 4.1 %tracer.1 = (f32[2,16,1024]{2,1,0:T(8,128)}, f32[50,36,128]{2,1,0:T(8,128)}) custom-call(f32[1024,128]{1,0:T(8,128)S(1)} %collective-permute-done.outer, f32[1024,128]{1,0:T(8,128)S(1)} %collective-permute-done.1.inner, f32[16,128]{1,0:T(8,128)S(1)} %bitcast.10, f32[8,48,128]{2,1,0:T(8,128)S(1)} %get-tuple-element.55.fields, ...), custom_call_target="tpu_custom_call" | custom-call | tf_op jit(solution)/shard_map/tracer/pallas_call | solution.py:622
Async XLA Ops:
  2.2 18.4 %collective-permute-start = (f32[1024,128]{1,0:T(8,128)S(1)}, f32[1024,128]{1,0:T(8,128)S(1)}, u32[]{:S(2)}, u32[]{:S(2)}) collective-permute-start(f32[1024,128]{1,0:T(8,128)S(1)} %get-tuple-element.33), channel_id=1, source_target_pairs={{1,2},{2,1},{3,4},{4,3},{5,6},{6,5},{7,8},{8,7},{9,10},{10,9},{11,... | collective-permute-start | bytes 1572872 | tf_op jit(solution)/shard_map/ppermute | solution.py:578
  2.9 17.7 %collective-permute-start.1 = (f32[1024,128]{1,0:T(8,128)S(1)}, f32[1024,128]{1,0:T(8,128)S(1)}, u32[]{:S(2)}, u32[]{:S(2)}) collective-permute-start(f32[1024,128]{1,0:T(8,128)S(1)} %get-tuple-element.34), channel_id=1, source_target_pairs={{0,1},{1,0},{2,3},{3,2},{4,5},{5,4},{6,7},{7,6},{8,9},{9,8},{10,11... | collective-permute-start | bytes 1572872 | tf_op jit(solution)/shard_map/ppermute | solution.py:578

commit v7 on v6

--- a/solution.py
+++ b/solution.py
@@ -62,16 +62,16 @@
     return out
 
 
-def direction(dirs):
-    turn = row_iota(dirs).astype(jnp.float32) * (2.0 * math.pi / dirs)
+def direction(dirs, padded):
+    turn = row_iota(padded).astype(jnp.float32) * (2.0 * math.pi / dirs)
     return jnp.cos(turn), jnp.sin(turn)
 
 
-def node_tables(me, near, angle, face, cosine, sine, project, choice):
-    edges, dirs = project.shape[:2]
+def node_tables(me, dirs, near, angle, face, cosine, sine, project, choice):
+    edges, padded = project.shape[:2]
     cosine[...] = face[...] * jnp.cos(angle[...])
     sine[...] = face[...] * jnp.sin(angle[...])
-    cos_dir, sin_dir = direction(dirs)
+    cos_dir, sin_dir = direction(dirs, padded)
     source = row_iota(LANES)
     minus = jnp.where(source == lane_iota(LANES), -1.0, 0.0)
     for s in range(edges):
@@ -100,12 +100,16 @@
 ):
     peers, _, capacity = send_rows.shape
     me = lax.axis_index("mesh")
+    freqs, dirs = spectra_in.shape[:2]
+    if dirs < spectra.shape[1]:
+        for f in range(freqs):
+            spectra[f, dirs // 8 * 8 :, :] = jnp.zeros((8, LANES), jnp.float32)
     copies = []
     for source, target in (
         (send_rows.at[me], coupled.at[1]),
         (current_in, current),
         (slot_in, node_slot),
-        (spectra_in, spectra),
+        (spectra_in, spectra.at[:, 0:dirs, :]),
         (tracers_in, tracers),
         (potential_in, potential),
         (neighbors_in, neighbors),
@@ -123,7 +127,6 @@
         copies.append(copy)
     for copy in copies[:3]:
         copy.wait()
-    freqs, dirs = spectra.shape[:2]
     layers, cells = potential.shape
     blocks = cells // LANES
     field_rows = (tracers.shape[0] + 1) * layers
@@ -170,8 +173,8 @@
     rest = dirs - whole
     turns = half_mask(dirs, odd)
     for g in range(pairs):
-        natural = spectra[g]
-        turned = pltpu.roll(spectra[g + pairs], LANES // 2, 1)
+        natural = spectra[g, 0:dirs, :]
+        turned = pltpu.roll(spectra[g + pairs, 0:dirs, :], LANES // 2, 1)
         for out, mixed in (
             (outer, jnp.where(turns, turned, natural)),
             (inner, jnp.where(turns, natural, turned)),
@@ -209,12 +212,26 @@
 
 
 def prepare_kernel(
-    near, angle, face, tracers, potential, neighbors, normal, weight, coupled,
-    cosine, sine, project, choice,
+    dirs, step_rows,
+    spectra, near, angle, face, tracers, potential, neighbors, normal, weight, coupled,
+    cosine, sine, project, choice, own_change,
     fields, pieces, matrices, inside, cell_cosine, cell_sine, cell_scale, sums,
 ):
     me = lax.axis_index("mesh")
-    node_tables(me, near, angle, face, cosine, sine, project, choice)
+    node_tables(me, dirs, near, angle, face, cosine, sine, project, choice)
+    freqs, padded, _ = spectra.shape
+    step = step_rows // padded
+
+    def own_part(c, carry):
+        own = spectra[pl.ds(c * step, step)].reshape(step_rows, LANES)
+        own_change[pl.ds(pl.multiple_of(c * step_rows, 8), step_rows), :] = jnp.dot(
+            jnp.concatenate(split(own), axis=1),
+            choice[0 : 2 * LANES, :],
+            preferred_element_type=jnp.float32,
+        )
+        return carry
+
+    lax.fori_loop(0, freqs // step, own_part, 0)
     tracer_count, layers, cells = tracers.shape
     blocks = cells // LANES
     edges = neighbors.shape[0]
@@ -265,19 +282,19 @@
 
 
 def wave_kernel(
-    capacity, step_pairs,
+    capacity, step_pairs, dirs,
     spectra, outer, inner, table, node_slot, neighbors, wind, cosine, sine, project, choice,
-    spectra_new, rows_out, drift, both, change,
+    own_change,
+    spectra_new, rows_out, drift, halos, change_a, change_b,
 ):
     me = lax.axis_index("mesh")
-    freqs, dirs = spectra.shape[:2]
+    freqs, stride = spectra.shape[:2]
     edges = neighbors.shape[0]
     peers = table.shape[0]
     halves = peers * capacity // LANES
     pairs = freqs // 2
     whole = dirs // 8 * 8
     rest = dirs - whole
-    stride = (dirs + 7) // 8 * 8
     base = outer.shape[0] - (pairs * dirs + 7) // 8 * 8
 
     odd = me % 2 == 1
@@ -307,13 +324,11 @@
     drifts = [spread(drift[s : s + 1, :], 8) for s in range(edges)]
     drift_sum = sum(drifts[1:], drifts[0])
     from_outer = half_mask(dirs, odd)
-    both[...] = jnp.zeros(both.shape, jnp.float32)
+    halos[...] = jnp.zeros(halos.shape, jnp.float32)
     ratio = 1.0 / 1.1
-    bands = [slice(r, min(r + 8, dirs)) for r in range(0, dirs, 8)]
-
-    def chunk(c, carry):
-        first_speed, total = carry
-        total = list(total)
+    bands = [slice(r, r + 8) for r in range(0, stride, 8)]
+
+    def gather(c, change):
         for i in range(step_pairs):
             g = c * step_pairs + i
             parts = []
@@ -323,41 +338,59 @@
                 left = message[pl.ds(base + pairs * whole + g * rest, rest), :]
                 parts.append(jnp.concatenate([upper, left], axis=0))
             x, y = parts
-            natural = jnp.where(from_outer, x, y)
-            turned = pltpu.roll(jnp.where(from_outer, y, x), LANES // 2, 1)
-            for j, f, halo in ((2 * i, g, natural), (2 * i + 1, g + pairs, turned)):
-                both[j * stride : j * stride + dirs, 0:LANES] = spectra[f]
-                both[j * stride : j * stride + dirs, LANES:] = halo
-        own_first, own_second = split(both[:, 0:LANES])
-        halo_first, halo_second = split(both[:, LANES:])
-        mixed = jnp.concatenate([own_first, own_second, halo_first, halo_second], axis=1)
-        change[...] = jnp.dot(mixed, choice[...], preferred_element_type=jnp.float32)
+            at = 2 * i * stride
+            halos[at : at + dirs, :] = jnp.where(from_outer, x, y)
+            at += stride
+            halos[at : at + dirs, :] = pltpu.roll(jnp.where(from_outer, y, x), LANES // 2, 1)
+        mixed = jnp.concatenate(split(halos[...]), axis=1)
+        change[...] = jnp.dot(
+            mixed, choice[2 * LANES : 4 * LANES, :], preferred_element_type=jnp.float32
+        )
+
+    def advect(c, change, first_speed, total):
+        total = list(total)
         for k, band in enumerate(bands):
-            count = band.stop - band.start
             along = [project[s, band, :] for s in range(edges)]
             along_sum = sum(along[1:], along[0])
             for i in range(step_pairs):
+                g = c * step_pairs + i
                 for j, f, speed in (
-                    (2 * i, c * step_pairs + i, first_speed * ratio**i),
-                    (2 * i + 1, c * step_pairs + i + pairs, first_speed * ratio ** (i + pairs)),
+                    (2 * i, g, first_speed * ratio**i),
+                    (2 * i + 1, g + pairs, first_speed * ratio ** (i + pairs)),
                 ):
                     own = spectra[f, band, :]
                     at = j * stride + band.start
-                    left = 1.0 - (speed * along_sum + drift_sum[:count])
-                    value = left * own
+                    own_at = pl.ds(pl.multiple_of(f * stride + band.start, 8), 8)
+                    value = own - (speed * along_sum + drift_sum) * own
                     for s in range(edges):
-                        down = jnp.minimum(speed * along[s] + drifts[s][:count], 0.0)
+                        down = jnp.minimum(speed * along[s] + drifts[s], 0.0)
                         lanes = slice(s * LANES, (s + 1) * LANES)
-                        value = value - down * change[at : at + count, lanes]
+                        step = change[at : at + 8, lanes] + own_change[own_at, lanes]
+                        value = value - down * step
                     spectra_new[f, band, :] = value
                     total[k] = total[k] + value
         return first_speed * ratio**step_pairs, tuple(total)
 
-    zeros = tuple(jnp.zeros((band.stop - band.start, LANES), jnp.float32) for band in bands)
-    _, total = lax.fori_loop(0, pairs // step_pairs, chunk, (jnp.float32(1.0), zeros))
+    zeros = tuple(jnp.zeros((8, LANES), jnp.float32) for _ in bands)
+    chunks = pairs // step_pairs
+    gather(0, change_a)
+
+    def two_chunks(h, carry):
+        gather(2 * h + 1, change_b)
+        carry = advect(2 * h, change_a, *carry)
+        gather(2 * h + 2, change_a)
+        return advect(2 * h + 1, change_b, *carry)
+
+    speed, total = lax.fori_loop(0, (chunks - 1) // 2, two_chunks, (jnp.float32(1.0), zeros))
+    if chunks % 2 == 0:
+        gather(chunks - 1, change_b)
+        speed, total = advect(chunks - 2, change_a, speed, total)
+        _, total = advect(chunks - 1, change_b, speed, total)
+    else:
+        _, total = advect(chunks - 1, change_a, speed, total)
     total = jnp.concatenate(total, axis=0)
-    zero = jnp.zeros((dirs, LANES), jnp.float32)
-    cos_dir, sin_dir = direction(dirs)
+    zero = jnp.zeros((stride, LANES), jnp.float32)
+    cos_dir, sin_dir = direction(dirs, stride)
     mean = jnp.sum(total, axis=0, keepdims=True) * (1.0 / (freqs * dirs))
     forcing = jnp.maximum(wind[0:1, :] * cos_dir + wind[1:2, :] * sin_dir, 0.0)
     step = jnp.exp((0.25 * forcing - 2.0 * mean) * (1.0 / freqs))
@@ -407,9 +440,10 @@
     outer, inner, table, fields, pieces, matrices, inside, cosine, sine, scale, sums, spectra,
     tracers_new, spectra_out,
     halo, halo_pieces, halo_matrices, halo_tables, beside, stokes, antiflux, lowered, ratios,
-    ratio_pieces, sem,
+    ratio_pieces, steps_a, steps_b, sem,
 ):
-    write = pltpu.make_async_copy(spectra, spectra_out, sem)
+    dirs = spectra_out.shape[1]
+    write = pltpu.make_async_copy(spectra.at[:, 0:dirs, :], spectra_out, sem)
     write.start()
     me = lax.axis_index("mesh")
     tracer_count, layers, edges = shape
@@ -530,10 +564,8 @@
     def own_tables(i):
         return scale[i], cosine[i], sine[i]
 
-    def inner_block(i, carry):
+    for i in range(blocks - 2):
         low_order(i + 2, band(fields, i + 1), column(inside, i), *own_tables(i + 1), True)
-        return carry
-
     for side in range(2):
         b = side * (blocks + 1)
         tables = tuple(halo_tables[side, k] for k in range(3))
@@ -541,33 +573,40 @@
         low_order(b, band(halo, near), column(beside, 3 * side), *tables, False)
         i = side * (blocks - 1)
         low_order(i + 1, band(fields, i), column(beside, 1 + side), *own_tables(i), True)
-    lax.fori_loop(0, blocks - 2, inner_block, 0)
-
-    def limit(i, carry):
-        b = i + 1
-        step = differences(
-            [ratio_pieces[b - 1], ratio_pieces[b], ratio_pieces[b + 1]], matrices[i]
-        )
+
+    def products(i, steps):
+        mixed = jnp.concatenate([ratio_pieces[i], ratio_pieces[i + 1], ratio_pieces[i + 2]], axis=1)
+        steps[...] = jnp.dot(mixed, matrices[i], preferred_element_type=jnp.float32)
+
+    def limit(i, steps):
         out = [lowered[i, 8 * g : 8 * g + 8, :] for g in range(tracer_groups)]
-        own = [ratios[b, 8 * g : 8 * g + 8, :] for g in range(2 * tracer_groups)]
+        own = [ratios[i + 1, 8 * g : 8 * g + 8, :] for g in range(2 * tracer_groups)]
+        low = 16 * tracer_groups
         for s in range(edges):
             lanes = slice(s * LANES, (s + 1) * LANES)
+            beside = [
+                own[g]
+                + (steps[8 * g : 8 * g + 8, lanes] + steps[low + 8 * g : low + 8 * g + 8, lanes])
+                for g in range(2 * tracer_groups)
+            ]
             for g in range(tracer_groups):
                 m = g + tracer_groups
                 flux = antiflux[i, s, 8 * g : 8 * g + 8, :]
-                plus = own[g] + step[8 * g : 8 * g + 8, lanes]
-                minus = own[m] + step[8 * m : 8 * m + 8, lanes]
                 factor = jnp.where(
-                    flux >= 0.0, jnp.minimum(own[m], plus), jnp.minimum(own[g], minus)
+                    flux >= 0.0, jnp.minimum(own[m], beside[g]), jnp.minimum(own[g], beside[m])
                 )
                 out[g] = out[g] - factor * flux
-        lanes = pl.ds(pl.multiple_of(i * LANES, LANES), LANES)
+        lanes = slice(i * LANES, (i + 1) * LANES)
         for g in range(tracer_groups):
             t, lg = g // layer_groups, g % layer_groups
             tracers_new[t, 8 * lg : 8 * lg + 8, lanes] = out[g]
-        return carry
-
-    lax.fori_loop(0, blocks, limit, 0)
+
+    buffers = (steps_a, steps_b)
+    products(0, steps_a)
+    for i in range(blocks):
+        if i + 1 < blocks:
+            products(i + 1, buffers[(i + 1) % 2])
+        limit(i, buffers[i % 2])
     write.wait()
 
 
@@ -611,6 +650,9 @@
 
     stored = pl.BlockSpec(memory_space=pltpu.HBM)
     rows = tracer_count * layers
+    stride = (dirs + 7) // 8 * 8
+    step_pairs = 5 if freqs % 10 == 0 else 1
+    step_rows = 2 * step_pairs * stride
 
     def like(x):
         return jax.ShapeDtypeStruct(x.shape, x.dtype)
@@ -642,7 +684,7 @@
             shaped(peers, LANES),
             shaped(message_rows, LANES),
             shaped(message_rows, LANES),
-            like(spectra),
+            shaped(freqs, stride, LANES),
             like(slots),
             like(node_neighbors),
             like(node_normal),
@@ -668,19 +710,20 @@
     inner = swap(inner, 0, peers)
 
     (
-        cosine, sine, project, choice,
+        cosine, sine, project, choice, own_change,
         fields, pieces, matrices, inside, cell_cosine, cell_sine, cell_scale, sums,
     ) = call(
-        prepare_kernel,
+        functools.partial(prepare_kernel, dirs, step_rows),
         "prepare",
         (
-            near, angle, face, own_tracers, own_potential, neighbors, normal, weight, coupled,
+            own_spectra, near, angle, face, own_tracers, own_potential, neighbors, normal, weight, coupled,
         ),
         (
             like(node_normal),
             like(node_normal),
-            shaped(edges, dirs, LANES),
+            shaped(edges, stride, LANES),
             shaped(4 * LANES, edges * LANES, dtype=jnp.bfloat16),
+            shaped(freqs * stride, edges * LANES),
             shaped(blocks, field_rows, LANES),
             shaped(blocks, 2 * field_rows, LANES, dtype=jnp.bfloat16),
             shaped(blocks, 3 * LANES, edges * LANES, dtype=jnp.bfloat16),
@@ -695,20 +738,19 @@
     currents, cosine = lax.optimization_barrier((currents, cosine))
     currents = lax.all_to_all(currents, "mesh", 0, 0, tiled=True)
 
-    step_pairs = 5 if freqs % 10 == 0 else 1
-    stride = (dirs + 7) // 8 * 8
     spectra_new, stokes_rows = call(
-        functools.partial(wave_kernel, capacity, step_pairs),
+        functools.partial(wave_kernel, capacity, step_pairs, dirs),
         "wave",
         (
             own_spectra, outer, inner, currents, own_slots, near, wind,
-            cosine, sine, project, choice,
+            cosine, sine, project, choice, own_change,
         ),
-        (like(spectra), shaped(peers, LANES)),
+        (shaped(freqs, stride, LANES), shaped(peers, LANES)),
         [
             pltpu.VMEM((8, LANES), f32),
-            pltpu.VMEM((2 * step_pairs * stride, 2 * LANES), f32),
-            pltpu.VMEM((2 * step_pairs * stride, edges * LANES), f32),
+            pltpu.VMEM((step_rows, LANES), f32),
+            pltpu.VMEM((step_rows, edges * LANES), f32),
+            pltpu.VMEM((step_rows, edges * LANES), f32),
         ],
     )
     stokes_all = lax.all_to_all(stokes_rows, "mesh", 0, 0, tiled=True)
@@ -732,6 +774,8 @@
             pltpu.VMEM((blocks, rows, LANES), f32),
             pltpu.VMEM((blocks + 2, 2 * rows, LANES), f32),
             pltpu.VMEM((blocks + 2, 4 * rows, LANES), jnp.bfloat16),
+            pltpu.VMEM((4 * rows, edges * LANES), f32),
+            pltpu.VMEM((4 * rows, edges * LANES), f32),
             pltpu.SemaphoreType.DMA(()),
         ],
         out_specs=(whole_spec(), stored),

time: 39.3 us -> 37.9 us (0.964)
  blocking collectives: 21.7 us -> 20.2 us
    all_to_all x1, blocking collectives: 10.5 us -> 8.98 us  [local(): stokes_all = lax.all_to_all(stokes_rows, 'mesh', 0, 0, tiled=True)]
  transfers between devices with their start and end apart: 2 -> 2, of which waited for: 0 -> 0; matrix products, arithmetic and copies ran while one was open for 0% -> 0% of each run, Pallas kernels for 5% -> 10%
where the time goes in v7:
time: 37.9 us; the launch traced here: 37.6 us
  blocking collectives  20.2 us (53%)
  Pallas kernels  11.7 us (31%)
  starting transfers between devices  5.06 us (13%)
  between operations  0.67 us (2%)
    all_to_all x1, blocking collectives, local(): currents = lax.all_to_all(currents, 'mesh', 0, 0, tiled=True)  11.2 us
    pallas_call x3, Pallas kernels, call(): pl.pallas_call(kernel, out_shape=outputs, in_specs=[whole_spec()] * len(i...  10.1 us
    all_to_all x1, blocking collectives, local(): stokes_all = lax.all_to_all(stokes_rows, 'mesh', 0, 0, tiled=True)  8.98 us
    ppermute x2, starting transfers between devices, swap(): return lax.ppermute(message, 'mesh', pairs)  5.06 us
    pallas_call x1, Pallas kernels, local(): pl.pallas_call(pack_kernel, out_shape=(shaped(peers, LANES), shaped(messa...  1.6 us
  transfers between devices with their start and end apart: 2, of which 0 were waited for; matrix products, arithmetic and copies ran while one was open for 0% of the time, Pallas kernels for 10%

profile of v7, /device:TPU:0, one launch (start us, length us, event | category | flops | bytes accessed | tf_op | source)
XLA Modules:
  0.0 37.6 jit_solution(10359921624631917577)
XLA Ops:
  0.6 1.6 %pack.1 = (f32[16,128]{1,0:T(8,128)S(1)}, f32[1024,128]{1,0:T(8,128)S(1)}, f32[1024,128]{1,0:T(8,128)S(1)}, f32[50,40,128]{2,1,0:T(8,128)S(1)}, s32[1,128]{1,0:T...) custom-call(f32[50,36,128]{2,1,0:T(8,128)} %spectra_in.1, ...), custom_call_target="tpu_custom_call" | custom-call | tf_op jit(solution)/shard_map/pack/pallas_call | solution.py:681
  2.2 0.7 %collective-permute-start = (f32[1024,128]{1,0:T(8,128)S(1)}, f32[1024,128]{1,0:T(8,128)S(1)}, u32[]{:S(2)}, u32[]{:S(2)}) collective-permute-start(f32[1024,128]{1,0:T(8,128)S(1)} %get-tuple-element.34), channel_id=1, source_target_pairs={{1,2},{2,1},{3,4},{4,3},{5,6},{6,5},{7,8},{8,7},{9,10},{10,9},{11,... | collective-permute-start | bytes 1572872 | tf_op jit(solution)/shard_map/ppermute | solution.py:617
  2.9 4.4 %collective-permute-start.1 = (f32[1024,128]{1,0:T(8,128)S(1)}, f32[1024,128]{1,0:T(8,128)S(1)}, u32[]{:S(2)}, u32[]{:S(2)}) collective-permute-start(f32[1024,128]{1,0:T(8,128)S(1)} %get-tuple-element.35), channel_id=1, source_target_pairs={{0,1},{1,0},{2,3},{3,2},{4,5},{5,4},{6,7},{7,6},{8,9},{9,8},{10,11... | collective-permute-start | bytes 1572872 | tf_op jit(solution)/shard_map/ppermute | solution.py:617
  7.3 3.8 %prepare.1 = (f32[6,128]{1,0:T(8,128)S(1)}, f32[6,128]{1,0:T(8,128)S(1)}, f32[6,40,128]{2,1,0:T(8,128)S(1)}, bf16[512,768]{1,0:T(8,128)(2,1)S(1)}, f32[2000,768]...) custom-call(f32[50,40,128]{2,1,0:T(8,128)S(1)} %get-tuple-element.36, ...), custom_call_target="tpu_custom_call" | custom-call | tf_op jit(solution)/shard_map/prepare/pallas_call | solution.py:664
  11.2 11.2 %all_to_all.22 = f32[16,1,128]{2,1,0:T(1,128)S(1)} all-to-all(f32[16,1,128]{2,1,0:T(1,128)S(1)} %bitcast.11), channel_id=1, replica_groups=mesh['groups'=2,'mesh'=16] {'mesh'}, dimensions={0} | all-to-all | bytes 16384 | tf_op jit(solution)/shard_map/all_to_all | solution.py:739
  22.3 0.0 collective-permute-done.outer
  22.3 0.0 collective-permute-done.1.inner
  22.3 3.4 %wave.1 = (f32[50,40,128]{2,1,0:T(8,128)S(1)}, f32[16,128]{1,0:T(8,128)S(1)}) custom-call(f32[50,40,128]{2,1,0:T(8,128)S(1)} %get-tuple-element.36.spectra, f32[1024,128]{1,0:T(8,128)S(1)} %collective-permute-done.outer, f32[1024,128]{1,0:T(8,128)S(1)} %collective-permute-done.1.inner, f32[16,128]{1,0:T(8,128)S(1)} %bitcast.9, ...), custom_call_target="tpu_custom_call" | custom-call | tf_op jit(solution)/shard_map/wave/pallas_call | solution.py:664
  25.8 9.0 %all_to_all.23 = f32[16,1,128]{2,1,0:T(1,128)S(1)} all-to-all(f32[16,1,128]{2,1,0:T(1,128)S(1)} %bitcast.12), channel_id=1, replica_groups=mesh['groups'=2,'mesh'=16] {'mesh'}, dimensions={0} | all-to-all | bytes 16384 | tf_op jit(solution)/shard_map/all_to_all | solution.py:756
  34.8 2.8 %tracer.1 = (f32[2,16,1024]{2,1,0:T(8,128)}, f32[50,36,128]{2,1,0:T(8,128)}) custom-call(f32[1024,128]{1,0:T(8,128)S(1)} %collective-permute-done.outer, f32[1024,128]{1,0:T(8,128)S(1)} %collective-permute-done.1.inner, f32[16,128]{1,0:T(8,128)S(1)} %bitcast.10, f32[8,48,128]{2,1,0:T(8,128)S(1)} %get-tuple-element.57.fields, ...), custom_call_target="tpu_custom_call" | custom-call | tf_op jit(solution)/shard_map/tracer/pallas_call | solution.py:664
Async XLA Ops:
  2.2 20.1 %collective-permute-start = (f32[1024,128]{1,0:T(8,128)S(1)}, f32[1024,128]{1,0:T(8,128)S(1)}, u32[]{:S(2)}, u32[]{:S(2)}) collective-permute-start(f32[1024,128]{1,0:T(8,128)S(1)} %get-tuple-element.34), channel_id=1, source_target_pairs={{1,2},{2,1},{3,4},{4,3},{5,6},{6,5},{7,8},{8,7},{9,10},{10,9},{11,... | collective-permute-start | bytes 1572872 | tf_op jit(solution)/shard_map/ppermute | solution.py:617
  2.9 19.4 %collective-permute-start.1 = (f32[1024,128]{1,0:T(8,128)S(1)}, f32[1024,128]{1,0:T(8,128)S(1)}, u32[]{:S(2)}, u32[]{:S(2)}) collective-permute-start(f32[1024,128]{1,0:T(8,128)S(1)} %get-tuple-element.35), channel_id=1, source_target_pairs={{0,1},{1,0},{2,3},{3,2},{4,5},{5,4},{6,7},{7,6},{8,9},{9,8},{10,11... | collective-permute-start | bytes 1572872 | tf_op jit(solution)/shard_map/ppermute | solution.py:617

commit v8 on v7

--- a/solution.py
+++ b/solution.py
@@ -437,7 +437,7 @@
 
 def tracer_kernel(
     capacity, shape,
-    outer, inner, table, fields, pieces, matrices, inside, cosine, sine, scale, sums, spectra,
+    outer, inner, table, other, fields, pieces, matrices, inside, cosine, sine, scale, sums, spectra,
     tracers_new, spectra_out,
     halo, halo_pieces, halo_matrices, halo_tables, beside, stokes, antiflux, lowered, ratios,
     ratio_pieces, steps_a, steps_b, sem,
@@ -485,16 +485,22 @@
     beside[3] = differences([pieces[blocks - 1], halo_pieces[2], halo_pieces[3]], halo_matrices[1])
 
     received = table[...]
+    swapped = other[...]
     lane_of = lane_iota(peers)
+    held = row_iota(peers) % 2 == me % 2
+    here = jnp.where(held, row_iota(peers), -1)
+    there = jnp.where(held, row_iota(peers) + 1 - 2 * (me % 2), -1)
     for which in range(3):
         values = []
         for part in range(2):
             lane = (2 * which + part) * capacity + lane_of % capacity
-            found = lane_gather(received, lane)
+            near = lane_gather(received, lane)
+            far = lane_gather(swapped, lane)
             row = []
             for half in range(halves):
-                mine = row_iota(peers) == (lane_of + half * LANES) // capacity
-                row.append(jnp.sum(jnp.where(mine, found, 0.0), axis=0, keepdims=True))
+                source = (lane_of + half * LANES) // capacity
+                found = jnp.where(here == source, near, jnp.where(there == source, far, 0.0))
+                row.append(jnp.sum(found, axis=0, keepdims=True))
             values.append(jnp.concatenate(row, axis=1))
         parts = three_parts(jnp.concatenate(values, axis=0))
         start = (0, 1, blocks + 1)[which]
@@ -753,13 +759,17 @@
             pltpu.VMEM((step_rows, edges * LANES), f32),
         ],
     )
-    stokes_all = lax.all_to_all(stokes_rows, "mesh", 0, 0, tiled=True)
+    cores = [list(range(core, peers, 2)) for core in range(2)]
+    stokes_all = lax.all_to_all(
+        stokes_rows, "mesh", 0, 0, axis_index_groups=cores, tiled=True
+    )
+    stokes_other = swap(stokes_all, 0, peers)
 
     return call(
         functools.partial(tracer_kernel, capacity, (tracer_count, layers, edges)),
         "tracer",
         (
-            outer, inner, stokes_all, fields, pieces, matrices, inside, cell_cosine, cell_sine,
+            outer, inner, stokes_all, stokes_other, fields, pieces, matrices, inside, cell_cosine, cell_sine,
             cell_scale, sums, pltpu.with_memory_space_constraint(spectra_new, pltpu.VMEM),
         ),
         (like(tracers), like(spectra)),

time: 37.9 us -> 38.9 us (1.026)
  waiting for transfers between devices: 0.01 us -> 1.17 us
    ppermute x2 -> x3, waiting for transfers between devices: 0.01 us -> 1.17 us  [swap(): return lax.ppermute(message, 'mesh', pairs)]
    ppermute x2 -> x3, starting transfers between devices: 5.06 us -> 5.06 us  [swap(): return lax.ppermute(message, 'mesh', pairs)]
  transfers between devices with their start and end apart: 2 -> 3, of which waited for: 0 -> 1; matrix products, arithmetic and copies ran while one was open for 0% -> 0% of each run, Pallas kernels for 10% -> 10%
where the time goes in v8:
time: 38.9 us; the launch traced here: 38.7 us
  blocking collectives  20.1 us (52%)
  Pallas kernels  11.7 us (30%)
  starting transfers between devices  5.06 us (13%)
  waiting for transfers between devices  1.17 us (3%)
  between operations  0.67 us (2%)
    all_to_all x1, blocking collectives, local(): currents = lax.all_to_all(currents, 'mesh', 0, 0, tiled=True)  11.2 us
    pallas_call x3, Pallas kernels, call(): pl.pallas_call(kernel, out_shape=outputs, in_specs=[whole_spec()] * len(i...  10.1 us
    all_to_all x1, blocking collectives, local(): lax.all_to_all(stokes_rows, 'mesh', 0, 0, axis_index_groups=cores, tiled=...  8.88 us
    ppermute x3, starting transfers between devices, swap(): return lax.ppermute(message, 'mesh', pairs)  5.06 us
    pallas_call x1, Pallas kernels, local(): pl.pallas_call(pack_kernel, out_shape=(shaped(peers, LANES), shaped(messa...  1.6 us
    ppermute x3, waiting for transfers between devices, swap(): return lax.ppermute(message, 'mesh', pairs)  1.17 us
  transfers between devices with their start and end apart: 3, of which 1 were waited for; matrix products, arithmetic and copies ran while one was open for 0% of the time, Pallas kernels for 10%

profile of v8, /device:TPU:0, one launch (start us, length us, event | category | flops | bytes accessed | tf_op | source)
XLA Modules:
  0.0 38.7 jit_solution(5928160341991968260)
XLA Ops:
  0.6 1.6 %pack.1 = (f32[16,128]{1,0:T(8,128)S(1)}, f32[1024,128]{1,0:T(8,128)S(1)}, f32[1024,128]{1,0:T(8,128)S(1)}, f32[50,40,128]{2,1,0:T(8,128)S(1)}, s32[1,128]{1,0:T...) custom-call(f32[50,36,128]{2,1,0:T(8,128)} %spectra_in.1, ...), custom_call_target="tpu_custom_call" | custom-call | tf_op jit(solution)/shard_map/pack/pallas_call | solution.py:687
  2.2 0.7 %collective-permute-start = (f32[1024,128]{1,0:T(8,128)S(1)}, f32[1024,128]{1,0:T(8,128)S(1)}, u32[]{:S(2)}, u32[]{:S(2)}) collective-permute-start(f32[1024,128]{1,0:T(8,128)S(1)} %get-tuple-element.34), channel_id=1, source_target_pairs={{1,2},{2,1},{3,4},{4,3},{5,6},{6,5},{7,8},{8,7},{9,10},{10,9},{11,... | collective-permute-start | bytes 1572872 | tf_op jit(solution)/shard_map/ppermute | solution.py:623
  2.9 4.4 %collective-permute-start.1 = (f32[1024,128]{1,0:T(8,128)S(1)}, f32[1024,128]{1,0:T(8,128)S(1)}, u32[]{:S(2)}, u32[]{:S(2)}) collective-permute-start(f32[1024,128]{1,0:T(8,128)S(1)} %get-tuple-element.35), channel_id=1, source_target_pairs={{0,1},{1,0},{2,3},{3,2},{4,5},{5,4},{6,7},{7,6},{8,9},{9,8},{10,11... | collective-permute-start | bytes 1572872 | tf_op jit(solution)/shard_map/ppermute | solution.py:623
  7.3 3.8 %prepare.1 = (f32[6,128]{1,0:T(8,128)S(1)}, f32[6,128]{1,0:T(8,128)S(1)}, f32[6,40,128]{2,1,0:T(8,128)S(1)}, bf16[512,768]{1,0:T(8,128)(2,1)S(1)}, f32[2000,768]...) custom-call(f32[50,40,128]{2,1,0:T(8,128)S(1)} %get-tuple-element.36, ...), custom_call_target="tpu_custom_call" | custom-call | tf_op jit(solution)/shard_map/prepare/pallas_call | solution.py:670
  11.2 11.2 %all_to_all.22 = f32[16,1,128]{2,1,0:T(1,128)S(1)} all-to-all(f32[16,1,128]{2,1,0:T(1,128)S(1)} %bitcast.10), channel_id=1, replica_groups=mesh['groups'=2,'mesh'=16] {'mesh'}, dimensions={0} | all-to-all | bytes 16384 | tf_op jit(solution)/shard_map/all_to_all | solution.py:745
  22.3 0.0 collective-permute-done.outer
  22.3 0.0 collective-permute-done.1.inner
  22.3 3.4 %wave.1 = (f32[50,40,128]{2,1,0:T(8,128)S(1)}, f32[16,128]{1,0:T(8,128)S(1)}) custom-call(f32[50,40,128]{2,1,0:T(8,128)S(1)} %get-tuple-element.36.spectra, f32[1024,128]{1,0:T(8,128)S(1)} %collective-permute-done.outer, f32[1024,128]{1,0:T(8,128)S(1)} %collective-permute-done.1.inner, f32[16,128]{1,0:T(8,128)S(1)} %bitcast.9, ...), custom_call_target="tpu_custom_call" | custom-call | tf_op jit(solution)/shard_map/wave/pallas_call | solution.py:670
  25.8 8.9 %all_to_all.23 = f32[8,2,128]{2,1,0:T(2,128)S(1)} all-to-all(f32[8,2,128]{2,1,0:T(2,128)S(1)} %bitcast.11), channel_id=1, replica_groups={{0,2,4,6,8,10,12,14},{1,3,5,7,9,11,13,15},{16,18,20,22,24,26,28,30},{17..., dimensions={0} | all-to-all | bytes 16384 | tf_op jit(solution)/shard_map/all_to_all | solution.py:763
  34.7 0.0 collective-permute-start.2
  34.7 1.2 %collective-permute-done.2.other = f32[16,128]{1,0:T(8,128)S(1)} collective-permute-done((f32[16,128]{1,0:T(8,128)S(1)}, f32[16,128]{1,0:T(8,128)S(1)}, u32[]{:S(2)}, u32[]{:S(2)}) %collective-permute-start.2) | collective-permute-done | bytes 8224 | tf_op jit(solution)/shard_map/ppermute | solution.py:623
  35.8 2.8 %tracer.1 = (f32[2,16,1024]{2,1,0:T(8,128)}, f32[50,36,128]{2,1,0:T(8,128)}) custom-call(f32[1024,128]{1,0:T(8,128)S(1)} %collective-permute-done.outer, f32[1024,128]{1,0:T(8,128)S(1)} %collective-permute-done.1.inner, f32[16,128]{1,0:T(8,128)S(1)} %bitcast.8, f32[16,128]{1,0:T(8,128)S(1)} %collective-permute-done.2.other, ...), custom_call_target="tpu_custom_call" | custom-call | tf_op jit(solution)/shard_map/tracer/pallas_call | solution.py:670
Async XLA Ops:
  2.2 20.1 %collective-permute-start = (f32[1024,128]{1,0:T(8,128)S(1)}, f32[1024,128]{1,0:T(8,128)S(1)}, u32[]{:S(2)}, u32[]{:S(2)}) collective-permute-start(f32[1024,128]{1,0:T(8,128)S(1)} %get-tuple-element.34), channel_id=1, source_target_pairs={{1,2},{2,1},{3,4},{4,3},{5,6},{6,5},{7,8},{8,7},{9,10},{10,9},{11,... | collective-permute-start | bytes 1572872 | tf_op jit(solution)/shard_map/ppermute | solution.py:623
  2.9 19.4 %collective-permute-start.1 = (f32[1024,128]{1,0:T(8,128)S(1)}, f32[1024,128]{1,0:T(8,128)S(1)}, u32[]{:S(2)}, u32[]{:S(2)}) collective-permute-start(f32[1024,128]{1,0:T(8,128)S(1)} %get-tuple-element.35), channel_id=1, source_target_pairs={{0,1},{1,0},{2,3},{3,2},{4,5},{5,4},{6,7},{7,6},{8,9},{9,8},{10,11... | collective-permute-start | bytes 1572872 | tf_op jit(solution)/shard_map/ppermute | solution.py:623
  34.7 1.2 %collective-permute-start.2 = (f32[16,128]{1,0:T(8,128)S(1)}, f32[16,128]{1,0:T(8,128)S(1)}, u32[]{:S(2)}, u32[]{:S(2)}) collective-permute-start(f32[16,128]{1,0:T(8,128)S(1)} %bitcast.7), channel_id=1, source_target_pairs={{0,1},{1,0},{2,3},{3,2},{4,5},{5,4},{6,7},{7,6},{8,9},{9,8},{10,11... | collective-permute-start | bytes 24584 | tf_op jit(solution)/shard_map/ppermute | solution.py:623

commit v9 on v7

--- a/solution.py
+++ b/solution.py
@@ -67,11 +67,21 @@
     return jnp.cos(turn), jnp.sin(turn)
 
 
-def node_tables(me, dirs, near, angle, face, cosine, sine, project, choice):
+def node_tables(
+    me, dirs, near, angle, face, wind, slot, cosine, sine, project, choice, ways, slots
+):
     edges, padded = project.shape[:2]
     cosine[...] = face[...] * jnp.cos(angle[...])
     sine[...] = face[...] * jnp.sin(angle[...])
     cos_dir, sin_dir = direction(dirs, padded)
+    ways[0] = cos_dir
+    ways[1] = sin_dir
+    ways[2] = 0.25 * jnp.maximum(wind[0:1, :] * cos_dir + wind[1:2, :] * sin_dir, 0.0)
+    taken = jnp.transpose(spread(slot[...].astype(jnp.float32), LANES))
+    for half in range(slots.shape[1] // LANES):
+        number = (lane_iota(LANES) + half * LANES).astype(jnp.float32)
+        picked = jnp.where(taken == number, 1.0, 0.0).astype(jnp.bfloat16)
+        slots[:, half * LANES : (half + 1) * LANES] = picked
     source = row_iota(LANES)
     minus = jnp.where(source == lane_iota(LANES), -1.0, 0.0)
     for s in range(edges):
@@ -104,17 +114,24 @@
     if dirs < spectra.shape[1]:
         for f in range(freqs):
             spectra[f, dirs // 8 * 8 :, :] = jnp.zeros((8, LANES), jnp.float32)
+    pairs = freqs // 2
+    piece = 5 if pairs % 5 == 0 else pairs
+    pieces = [
+        slice(start + first, start + first + piece)
+        for first in range(0, pairs, piece)
+        for start in (0, pairs)
+    ]
     copies = []
     for source, target in (
         (send_rows.at[me], coupled.at[1]),
         (current_in, current),
         (slot_in, node_slot),
-        (spectra_in, spectra.at[:, 0:dirs, :]),
         (tracers_in, tracers),
         (potential_in, potential),
         (neighbors_in, neighbors),
         (normal_in, normal),
         (weight_in, weight),
+        *((spectra_in.at[part], spectra.at[part, 0:dirs, :]) for part in pieces),
         (send_rows.at[jnp.maximum(me - 1, 0)], coupled.at[0]),
         (send_rows.at[jnp.minimum(me + 1, peers - 1)], coupled.at[2]),
         (near_in, near),
@@ -142,7 +159,7 @@
             picked = jnp.where(place == 2 * (cell // LANES) + part, found, 0.0)
             values[part].append(jnp.sum(picked, axis=0, keepdims=True))
     rows_out[...] = peer_rows(values, peers, capacity)
-    for copy in copies[3:]:
+    for copy in copies[3:8]:
         copy.wait()
     odd = me % 2 == 1
     for out, upward in ((outer, odd), (inner, jnp.logical_not(odd))):
@@ -168,11 +185,14 @@
         out[base + 8 : base + 8 + edges, :] = jnp.where(upward, normal[:, high], normal[:, low])
         out[base + 16 : base + 16 + edges, :] = jnp.where(upward, weight[:, high], weight[:, low])
     base = 2 * field_rows + TABLE_ROWS
-    pairs = freqs // 2
     whole = dirs // 8 * 8
     rest = dirs - whole
     turns = half_mask(dirs, odd)
     for g in range(pairs):
+        if g % piece == 0:
+            at = 8 + 2 * (g // piece)
+            for copy in copies[at : at + 2]:
+                copy.wait()
         natural = spectra[g, 0:dirs, :]
         turned = pltpu.roll(spectra[g + pairs, 0:dirs, :], LANES // 2, 1)
         for out, mixed in (
@@ -187,16 +207,21 @@
     if at < outer.shape[0]:
         for out in (outer, inner):
             out[at:, :] = jnp.zeros((outer.shape[0] - at, LANES), jnp.float32)
+    for copy in copies[8 + len(pieces) :]:
+        copy.wait()
 
 
 def choose(cells, first, lanes, matrix):
-    place = cells - first
+    place = (cells - first - LANES).astype(jnp.float32).astype(jnp.bfloat16)
+    place = spread(place, LANES)
+    one = jnp.ones((LANES, LANES), jnp.bfloat16)
     for k in range(3):
-        source = row_iota(LANES) + k * LANES
-        part = jnp.where(source == place, 1.0, 0.0)
+        source = (row_iota(LANES) + (k - 1) * LANES).astype(jnp.float32).astype(jnp.bfloat16)
+        part = jnp.where(source == place, one, 0 * one)
         if k == 1:
-            part = part - jnp.where(row_iota(LANES) == lane_iota(LANES), 1.0, 0.0)
-        matrix[k * LANES : (k + 1) * LANES, lanes] = part.astype(jnp.bfloat16)
+            own = jnp.where(row_iota(LANES) == lane_iota(LANES), 1.0, 0.0).astype(jnp.bfloat16)
+            part = part - own
+        matrix[k * LANES : (k + 1) * LANES, lanes] = part
 
 
 def stack_split(x):
@@ -213,12 +238,14 @@
 
 def prepare_kernel(
     dirs, step_rows,
-    spectra, near, angle, face, tracers, potential, neighbors, normal, weight, coupled,
-    cosine, sine, project, choice, own_change,
+    spectra, near, angle, face, wind, slot, tracers, potential, neighbors, normal, weight, coupled,
+    cosine, sine, project, choice, ways, slots, own_change,
     fields, pieces, matrices, inside, cell_cosine, cell_sine, cell_scale, sums,
 ):
     me = lax.axis_index("mesh")
-    node_tables(me, dirs, near, angle, face, cosine, sine, project, choice)
+    node_tables(
+        me, dirs, near, angle, face, wind, slot, cosine, sine, project, choice, ways, slots
+    )
     freqs, padded, _ = spectra.shape
     step = step_rows // padded
 
@@ -283,7 +310,7 @@
 
 def wave_kernel(
     capacity, step_pairs, dirs,
-    spectra, outer, inner, table, node_slot, neighbors, wind, cosine, sine, project, choice,
+    spectra, outer, inner, table, node_slot, neighbors, cosine, sine, project, choice, ways, slots,
     own_change,
     spectra_new, rows_out, drift, halos, change_a, change_b,
 ):
@@ -390,20 +417,23 @@
         _, total = advect(chunks - 1, change_a, speed, total)
     total = jnp.concatenate(total, axis=0)
     zero = jnp.zeros((stride, LANES), jnp.float32)
-    cos_dir, sin_dir = direction(dirs, stride)
+    cos_dir, sin_dir = ways[0], ways[1]
     mean = jnp.sum(total, axis=0, keepdims=True) * (1.0 / (freqs * dirs))
-    forcing = jnp.maximum(wind[0:1, :] * cos_dir + wind[1:2, :] * sin_dir, 0.0)
-    step = jnp.exp((0.25 * forcing - 2.0 * mean) * (1.0 / freqs))
-
-    def grow(f, carry):
+    step = jnp.exp((ways[2] - 2.0 * mean) * (1.0 / freqs))
+    run = 10 if freqs % 10 == 0 else 1
+
+    def grow(c, carry):
         factor, weighted = carry
-        factor = factor * step
-        evolved = spectra_new[f] * factor
-        spectra_new[f] = evolved
-        kappa = (f + 1).astype(jnp.float32) * (1.0 / freqs)
-        return factor, weighted + kappa * evolved
-
-    _, weighted = lax.fori_loop(0, freqs, grow, (zero + 1.0, zero))
+        for i in range(run):
+            f = c * run + i
+            factor = factor * step
+            evolved = spectra_new[f] * factor
+            spectra_new[f] = evolved
+            kappa = (f + 1).astype(jnp.float32) * (1.0 / freqs)
+            weighted = weighted + kappa * evolved
+        return factor, weighted
+
+    _, weighted = lax.fori_loop(0, freqs // run, grow, (zero + 1.0, zero))
     stokes = jnp.concatenate(
         [
             jnp.sum(weighted * cos_dir, axis=0, keepdims=True),
@@ -411,12 +441,8 @@
         ],
         axis=0,
     ) * (1.0 / dirs)
-    named = lax.broadcasted_iota(jnp.int32, (halves * LANES, LANES), 0) == slot
-    in_order = lax.dot_general(
-        three_parts(stokes),
-        jnp.where(named, 1.0, 0.0).astype(jnp.bfloat16),
-        (((1,), (1,)), ((), ())),
-        preferred_element_type=jnp.float32,
+    in_order = jnp.dot(
+        three_parts(stokes), slots[...], preferred_element_type=jnp.float32
     )
     in_order = in_order[0:2] + (in_order[2:4] + in_order[4:6])
     values = [
@@ -701,7 +727,7 @@
         out_specs=(whole_spec(),) * 15,
         scratch_shapes=[
             pltpu.VMEM(surface_current.shape, f32),
-            pltpu.SemaphoreType.DMA((15,)),
+            pltpu.SemaphoreType.DMA((64,)),
         ],
         compiler_params=params,
         name="pack",
@@ -710,19 +736,22 @@
     inner = swap(inner, 0, peers)
 
     (
-        cosine, sine, project, choice, own_change,
+        cosine, sine, project, choice, ways, slot_choice, own_change,
         fields, pieces, matrices, inside, cell_cosine, cell_sine, cell_scale, sums,
     ) = call(
         functools.partial(prepare_kernel, dirs, step_rows),
         "prepare",
         (
-            own_spectra, near, angle, face, own_tracers, own_potential, neighbors, normal, weight, coupled,
+            own_spectra, near, angle, face, wind, own_slots, own_tracers, own_potential,
+            neighbors, normal, weight, coupled,
         ),
         (
             like(node_normal),
             like(node_normal),
             shaped(edges, stride, LANES),
             shaped(4 * LANES, edges * LANES, dtype=jnp.bfloat16),
+            shaped(3, stride, LANES),
+            shaped(nodes, peers * capacity, dtype=jnp.bfloat16),
             shaped(freqs * stride, edges * LANES),
             shaped(blocks, field_rows, LANES),
             shaped(blocks, 2 * field_rows, LANES, dtype=jnp.bfloat16),
@@ -742,8 +771,8 @@
         functools.partial(wave_kernel, capacity, step_pairs, dirs),
         "wave",
         (
-            own_spectra, outer, inner, currents, own_slots, near, wind,
-            cosine, sine, project, choice, own_change,
+            own_spectra, outer, inner, currents, own_slots, near,
+            cosine, sine, project, choice, ways, slot_choice, own_change,
         ),
         (shaped(freqs, stride, LANES), shaped(peers, LANES)),
         [

time: 37.9 us -> 37.7 us (level)
  Pallas kernels: 11.7 us -> 11.1 us
    pallas_call x3, Pallas kernels: 10.1 us -> 8.94 us  [call(): pl.pallas_call(kernel, out_shape=outputs, in_specs=[whole_spec()] * len(i...]
    pallas_call x1, Pallas kernels: 1.6 us -> 2.21 us  [local(): pl.pallas_call(pack_kernel, out_shape=(shaped(peers, LANES), shaped(messa...]
  transfers between devices with their start and end apart: 2 -> 2, of which waited for: 0 -> 0; matrix products, arithmetic and copies ran while one was open for 0% -> 0% of each run, Pallas kernels for 10% -> 9%
where the time goes in v9:
time: 37.7 us; the launch traced here: 37.4 us
  blocking collectives  20.5 us (54%)
  Pallas kernels  11.1 us (29%)
  starting transfers between devices  5.06 us (13%)
  between operations  0.67 us (2%)
    all_to_all x1, blocking collectives, local(): currents = lax.all_to_all(currents, 'mesh', 0, 0, tiled=True)  11.2 us
    all_to_all x1, blocking collectives, local(): stokes_all = lax.all_to_all(stokes_rows, 'mesh', 0, 0, tiled=True)  9.3 us
    pallas_call x3, Pallas kernels, call(): pl.pallas_call(kernel, out_shape=outputs, in_specs=[whole_spec()] * len(i...  8.94 us
    ppermute x2, starting transfers between devices, swap(): return lax.ppermute(message, 'mesh', pairs)  5.06 us
    pallas_call x1, Pallas kernels, local(): pl.pallas_call(pack_kernel, out_shape=(shaped(peers, LANES), shaped(messa...  2.21 us
  transfers between devices with their start and end apart: 2, of which 0 were waited for; matrix products, arithmetic and copies ran while one was open for 0% of the time, Pallas kernels for 9%

profile of v9, /device:TPU:0, one launch (start us, length us, event | category | flops | bytes accessed | tf_op | source)
XLA Modules:
  0.0 37.4 jit_solution(6231023487622859399)
XLA Ops:
  0.6 2.2 %pack.1 = (f32[16,128]{1,0:T(8,128)S(1)}, f32[1024,128]{1,0:T(8,128)S(1)}, f32[1024,128]{1,0:T(8,128)S(1)}, f32[50,40,128]{2,1,0:T(8,128)S(1)}, s32[1,128]{1,0:T...) custom-call(f32[50,36,128]{2,1,0:T(8,128)} %spectra_in.1, ...), custom_call_target="tpu_custom_call" | custom-call | tf_op jit(solution)/shard_map/pack/pallas_call | solution.py:707
  2.9 0.7 %collective-permute-start = (f32[1024,128]{1,0:T(8,128)S(1)}, f32[1024,128]{1,0:T(8,128)S(1)}, u32[]{:S(2)}, u32[]{:S(2)}) collective-permute-start(f32[1024,128]{1,0:T(8,128)S(1)} %get-tuple-element.36), channel_id=1, source_target_pairs={{1,2},{2,1},{3,4},{4,3},{5,6},{6,5},{7,8},{8,7},{9,10},{10,9},{11,... | collective-permute-start | bytes 1572872 | tf_op jit(solution)/shard_map/ppermute | solution.py:643
  3.6 4.4 %collective-permute-start.1 = (f32[1024,128]{1,0:T(8,128)S(1)}, f32[1024,128]{1,0:T(8,128)S(1)}, u32[]{:S(2)}, u32[]{:S(2)}) collective-permute-start(f32[1024,128]{1,0:T(8,128)S(1)} %get-tuple-element.37), channel_id=1, source_target_pairs={{0,1},{1,0},{2,3},{3,2},{4,5},{5,4},{6,7},{7,6},{8,9},{9,8},{10,11... | collective-permute-start | bytes 1572872 | tf_op jit(solution)/shard_map/ppermute | solution.py:643
  7.9 3.3 %prepare.1 = (f32[6,128]{1,0:T(8,128)S(1)}, f32[6,128]{1,0:T(8,128)S(1)}, f32[6,40,128]{2,1,0:T(8,128)S(1)}, bf16[512,768]{1,0:T(8,128)(2,1)S(1)}, f32[3,40,128]...) custom-call(f32[50,40,128]{2,1,0:T(8,128)S(1)} %get-tuple-element.38, ...), custom_call_target="tpu_custom_call" | custom-call | tf_op jit(solution)/shard_map/prepare/pallas_call | solution.py:690
  11.2 11.2 %all_to_all.22 = f32[16,1,128]{2,1,0:T(1,128)S(1)} all-to-all(f32[16,1,128]{2,1,0:T(1,128)S(1)} %bitcast.11), channel_id=1, replica_groups=mesh['groups'=2,'mesh'=16] {'mesh'}, dimensions={0} | all-to-all | bytes 16384 | tf_op jit(solution)/shard_map/all_to_all | solution.py:768
  22.4 0.0 collective-permute-done.outer
  22.4 0.0 collective-permute-done.1.inner
  22.4 2.9 %wave.1 = (f32[50,40,128]{2,1,0:T(8,128)S(1)}, f32[16,128]{1,0:T(8,128)S(1)}) custom-call(f32[50,40,128]{2,1,0:T(8,128)S(1)} %get-tuple-element.38.spectra, f32[1024,128]{1,0:T(8,128)S(1)} %collective-permute-done.outer, f32[1024,128]{1,0:T(8,128)S(1)} %collective-permute-done.1.inner, f32[16,128]{1,0:T(8,128)S(1)} %bitcast.9, ...), custom_call_target="tpu_custom_call" | custom-call | tf_op jit(solution)/shard_map/wave/pallas_call | solution.py:690
  25.4 9.3 %all_to_all.23 = f32[16,1,128]{2,1,0:T(1,128)S(1)} all-to-all(f32[16,1,128]{2,1,0:T(1,128)S(1)} %bitcast.12), channel_id=1, replica_groups=mesh['groups'=2,'mesh'=16] {'mesh'}, dimensions={0} | all-to-all | bytes 16384 | tf_op jit(solution)/shard_map/all_to_all | solution.py:785
  34.7 2.7 %tracer.1 = (f32[2,16,1024]{2,1,0:T(8,128)}, f32[50,36,128]{2,1,0:T(8,128)}) custom-call(f32[1024,128]{1,0:T(8,128)S(1)} %collective-permute-done.outer, f32[1024,128]{1,0:T(8,128)S(1)} %collective-permute-done.1.inner, f32[16,128]{1,0:T(8,128)S(1)} %bitcast.10, f32[8,48,128]{2,1,0:T(8,128)S(1)} %get-tuple-element.61.fields, ...), custom_call_target="tpu_custom_call" | custom-call | tf_op jit(solution)/shard_map/tracer/pallas_call | solution.py:690
Async XLA Ops:
  2.9 19.6 %collective-permute-start = (f32[1024,128]{1,0:T(8,128)S(1)}, f32[1024,128]{1,0:T(8,128)S(1)}, u32[]{:S(2)}, u32[]{:S(2)}) collective-permute-start(f32[1024,128]{1,0:T(8,128)S(1)} %get-tuple-element.36), channel_id=1, source_target_pairs={{1,2},{2,1},{3,4},{4,3},{5,6},{6,5},{7,8},{8,7},{9,10},{10,9},{11,... | collective-permute-start | bytes 1572872 | tf_op jit(solution)/shard_map/ppermute | solution.py:643
  3.6 18.9 %collective-permute-start.1 = (f32[1024,128]{1,0:T(8,128)S(1)}, f32[1024,128]{1,0:T(8,128)S(1)}, u32[]{:S(2)}, u32[]{:S(2)}) collective-permute-start(f32[1024,128]{1,0:T(8,128)S(1)} %get-tuple-element.37), channel_id=1, source_target_pairs={{0,1},{1,0},{2,3},{3,2},{4,5},{5,4},{6,7},{7,6},{8,9},{9,8},{10,11... | collective-permute-start | bytes 1572872 | tf_op jit(solution)/shard_map/ppermute | solution.py:643

commit v10 on v9

--- a/solution.py
+++ b/solution.py
@@ -102,64 +102,33 @@
 
 
 def pack_kernel(
-    spectra_in, tracers_in, potential_in, neighbors_in, normal_in, weight_in, current_in,
-    send_rows, slot_in, near_in, angle_in, face_in, wind_in,
-    rows_out, outer, inner, spectra, node_slot, near, angle, face, wind,
-    tracers, potential, neighbors, normal, weight, coupled,
-    current, sems,
+    spectra_in, tracers_in, potential_in, neighbors_in, normal_in, weight_in, slot_in,
+    outer, inner, spectra, tracers, potential, neighbors, normal, weight, node_slot,
+    sems,
 ):
-    peers, _, capacity = send_rows.shape
     me = lax.axis_index("mesh")
     freqs, dirs = spectra_in.shape[:2]
     if dirs < spectra.shape[1]:
         for f in range(freqs):
             spectra[f, dirs // 8 * 8 :, :] = jnp.zeros((8, LANES), jnp.float32)
-    pairs = freqs // 2
-    piece = 5 if pairs % 5 == 0 else pairs
-    pieces = [
-        slice(start + first, start + first + piece)
-        for first in range(0, pairs, piece)
-        for start in (0, pairs)
-    ]
     copies = []
     for source, target in (
-        (send_rows.at[me], coupled.at[1]),
-        (current_in, current),
-        (slot_in, node_slot),
+        (spectra_in, spectra.at[:, 0:dirs, :]),
         (tracers_in, tracers),
         (potential_in, potential),
         (neighbors_in, neighbors),
         (normal_in, normal),
         (weight_in, weight),
-        *((spectra_in.at[part], spectra.at[part, 0:dirs, :]) for part in pieces),
-        (send_rows.at[jnp.maximum(me - 1, 0)], coupled.at[0]),
-        (send_rows.at[jnp.minimum(me + 1, peers - 1)], coupled.at[2]),
-        (near_in, near),
-        (angle_in, angle),
-        (face_in, face),
-        (wind_in, wind),
+        (slot_in, node_slot),
     ):
         copy = pltpu.make_async_copy(source, target, sems.at[len(copies)])
         copy.start()
         copies.append(copy)
-    for copy in copies[:3]:
-        copy.wait()
+    pairs = freqs // 2
     layers, cells = potential.shape
     blocks = cells // LANES
     field_rows = (tracers.shape[0] + 1) * layers
-    stacked = jnp.concatenate(
-        [current[:, b * LANES : (b + 1) * LANES] for b in range(blocks)], axis=0
-    )
-    place = row_iota(2 * blocks)
-    halves = slot_rows(coupled[1])
-    values = [[], []]
-    for cell in halves:
-        found = lane_gather(stacked, spread(cell % LANES, 2 * blocks))
-        for part in range(2):
-            picked = jnp.where(place == 2 * (cell // LANES) + part, found, 0.0)
-            values[part].append(jnp.sum(picked, axis=0, keepdims=True))
-    rows_out[...] = peer_rows(values, peers, capacity)
-    for copy in copies[3:8]:
+    for copy in copies[1:]:
         copy.wait()
     odd = me % 2 == 1
     for out, upward in ((outer, odd), (inner, jnp.logical_not(odd))):
@@ -188,11 +157,8 @@
     whole = dirs // 8 * 8
     rest = dirs - whole
     turns = half_mask(dirs, odd)
+    copies[0].wait()
     for g in range(pairs):
-        if g % piece == 0:
-            at = 8 + 2 * (g // piece)
-            for copy in copies[at : at + 2]:
-                copy.wait()
         natural = spectra[g, 0:dirs, :]
         turned = pltpu.roll(spectra[g + pairs, 0:dirs, :], LANES // 2, 1)
         for out, mixed in (
@@ -207,8 +173,22 @@
     if at < outer.shape[0]:
         for out in (outer, inner):
             out[at:, :] = jnp.zeros((outer.shape[0] - at, LANES), jnp.float32)
-    for copy in copies[8 + len(pieces) :]:
-        copy.wait()
+
+
+def current_rows(current, coupled, rows_out):
+    peers, capacity = coupled.shape[1:]
+    blocks = current.shape[1] // LANES
+    stacked = jnp.concatenate(
+        [current[:, b * LANES : (b + 1) * LANES] for b in range(blocks)], axis=0
+    )
+    place = row_iota(2 * blocks)
+    values = [[], []]
+    for cell in slot_rows(coupled[1]):
+        found = lane_gather(stacked, spread(cell % LANES, 2 * blocks))
+        for part in range(2):
+            picked = jnp.where(place == 2 * (cell // LANES) + part, found, 0.0)
+            values[part].append(jnp.sum(picked, axis=0, keepdims=True))
+    rows_out[...] = peer_rows(values, peers, capacity)
 
 
 def choose(cells, first, lanes, matrix):
@@ -238,27 +218,28 @@
 
 def prepare_kernel(
     dirs, step_rows,
-    spectra, near, angle, face, wind, slot, tracers, potential, neighbors, normal, weight, coupled,
-    cosine, sine, project, choice, ways, slots, own_change,
+    spectra, slot, tracers, potential, neighbors, normal, weight,
+    near_in, angle_in, face_in, wind_in, send_rows, current_in,
+    near, rows_out, cosine, sine, project, choice, ways, slots, own_change,
     fields, pieces, matrices, inside, cell_cosine, cell_sine, cell_scale, sums,
+    angle, face, wind, coupled, current, sems,
 ):
     me = lax.axis_index("mesh")
-    node_tables(
-        me, dirs, near, angle, face, wind, slot, cosine, sine, project, choice, ways, slots
-    )
-    freqs, padded, _ = spectra.shape
-    step = step_rows // padded
-
-    def own_part(c, carry):
-        own = spectra[pl.ds(c * step, step)].reshape(step_rows, LANES)
-        own_change[pl.ds(pl.multiple_of(c * step_rows, 8), step_rows), :] = jnp.dot(
-            jnp.concatenate(split(own), axis=1),
-            choice[0 : 2 * LANES, :],
-            preferred_element_type=jnp.float32,
-        )
-        return carry
-
-    lax.fori_loop(0, freqs // step, own_part, 0)
+    peers = send_rows.shape[0]
+    copies = []
+    for source, target in (
+        (near_in, near),
+        (angle_in, angle),
+        (face_in, face),
+        (wind_in, wind),
+        (current_in, current),
+        (send_rows.at[jnp.maximum(me - 1, 0)], coupled.at[0]),
+        (send_rows.at[me], coupled.at[1]),
+        (send_rows.at[jnp.minimum(me + 1, peers - 1)], coupled.at[2]),
+    ):
+        copy = pltpu.make_async_copy(source, target, sems.at[len(copies)])
+        copy.start()
+        copies.append(copy)
     tracer_count, layers, cells = tracers.shape
     blocks = cells // LANES
     edges = neighbors.shape[0]
@@ -284,6 +265,25 @@
         inside[b - 1] = differences(
             [pieces[b - 1], pieces[b], pieces[b + 1]], matrices[b]
         )
+    for copy in copies:
+        copy.wait()
+    current_rows(current, coupled, rows_out)
+    node_tables(
+        me, dirs, near, angle, face, wind, slot, cosine, sine, project, choice, ways, slots
+    )
+    freqs, padded, _ = spectra.shape
+    step = step_rows // padded
+
+    def own_part(c, carry):
+        own = spectra[pl.ds(c * step, step)].reshape(step_rows, LANES)
+        own_change[pl.ds(pl.multiple_of(c * step_rows, 8), step_rows), :] = jnp.dot(
+            jnp.concatenate(split(own), axis=1),
+            choice[0 : 2 * LANES, :],
+            preferred_element_type=jnp.float32,
+        )
+        return carry
+
+    lax.fori_loop(0, freqs // step, own_part, 0)
     for which in range(3):
         first = 0 if which != 0 else cells - LANES
         count = blocks if which == 1 else 1
@@ -686,11 +686,11 @@
     def shaped(*shape, dtype=f32):
         return jax.ShapeDtypeStruct(shape, dtype)
 
-    def call(kernel, name, inputs, outputs, scratch, out_specs=None):
+    def call(kernel, name, inputs, outputs, scratch, in_specs=None, out_specs=None):
         return pl.pallas_call(
             kernel,
             out_shape=outputs,
-            in_specs=[whole_spec()] * len(inputs),
+            in_specs=in_specs or [whole_spec()] * len(inputs),
             out_specs=out_specs or (whole_spec(),) * len(outputs),
             scratch_shapes=scratch,
             compiler_params=params,
@@ -698,37 +698,21 @@
         )(*inputs)
 
     inputs = (
-        spectra, tracers, potential, cell_neighbors, cell_normal, cell_weight, surface_current,
-        send_rows, slots, node_neighbors, node_normal, node_weight, wind_velocity,
+        spectra, tracers, potential, cell_neighbors, cell_normal, cell_weight, slots,
     )
     (
-        currents, outer, inner, own_spectra, own_slots, near, angle, face, wind,
-        own_tracers, own_potential, neighbors, normal, weight, coupled,
+        outer, inner, own_spectra, own_tracers, own_potential, neighbors, normal, weight, own_slots,
     ) = pl.pallas_call(
         pack_kernel,
         out_shape=(
-            shaped(peers, LANES),
             shaped(message_rows, LANES),
             shaped(message_rows, LANES),
             shaped(freqs, stride, LANES),
-            like(slots),
-            like(node_neighbors),
-            like(node_normal),
-            like(node_weight),
-            like(wind_velocity),
-            like(tracers),
-            like(potential),
-            like(cell_neighbors),
-            like(cell_normal),
-            like(cell_weight),
-            shaped(3, peers, capacity, dtype=jnp.int32),
+            *(like(x) for x in inputs[1:]),
         ),
         in_specs=[stored] * len(inputs),
-        out_specs=(whole_spec(),) * 15,
-        scratch_shapes=[
-            pltpu.VMEM(surface_current.shape, f32),
-            pltpu.SemaphoreType.DMA((64,)),
-        ],
+        out_specs=(whole_spec(),) * 9,
+        scratch_shapes=[pltpu.SemaphoreType.DMA((7,))],
         compiler_params=params,
         name="pack",
     )(*(pltpu.with_memory_space_constraint(x, pltpu.HBM) for x in inputs))
@@ -736,16 +720,24 @@
     inner = swap(inner, 0, peers)
 
     (
-        cosine, sine, project, choice, ways, slot_choice, own_change,
+        near, currents, cosine, sine, project, choice, ways, slot_choice, own_change,
         fields, pieces, matrices, inside, cell_cosine, cell_sine, cell_scale, sums,
     ) = call(
         functools.partial(prepare_kernel, dirs, step_rows),
         "prepare",
         (
-            own_spectra, near, angle, face, wind, own_slots, own_tracers, own_potential,
-            neighbors, normal, weight, coupled,
+            own_spectra, own_slots, own_tracers, own_potential, neighbors, normal, weight,
+            *(
+                pltpu.with_memory_space_constraint(x, pltpu.HBM)
+                for x in (
+                    node_neighbors, node_normal, node_weight, wind_velocity, send_rows,
+                    surface_current,
+                )
+            ),
         ),
         (
+            like(node_neighbors),
+            shaped(peers, LANES),
             like(node_normal),
             like(node_normal),
             shaped(edges, stride, LANES),
@@ -762,9 +754,16 @@
             shaped(blocks, 8, LANES),
             shaped(peers * capacity, (blocks + 2) * LANES, dtype=jnp.bfloat16),
         ),
-        [],
-    )
-    currents, cosine = lax.optimization_barrier((currents, cosine))
+        [
+            pltpu.VMEM(node_normal.shape, f32),
+            pltpu.VMEM(node_weight.shape, f32),
+            pltpu.VMEM(wind_velocity.shape, f32),
+            pltpu.VMEM((3, peers, capacity), jnp.int32),
+            pltpu.VMEM(surface_current.shape, f32),
+            pltpu.SemaphoreType.DMA((8,)),
+        ],
+        in_specs=[whole_spec()] * 7 + [stored] * 6,
+    )
     currents = lax.all_to_all(currents, "mesh", 0, 0, tiled=True)
 
     spectra_new, stokes_rows = call(

time: 37.7 us -> 38 us (level)
  Pallas kernels: 11.1 us -> 11.8 us
    pallas_call x4, Pallas kernels: 11.1 us -> 11.8 us  [the longest x3 10.3 us: call(): pl.pallas_call(kernel, out_shape=outputs, in_specs=in_specs or [whole_spe...]
  transfers between devices with their start and end apart: 2 -> 2, of which waited for: 0 -> 0; matrix products, arithmetic and copies ran while one was open for 0% -> 0% of each run, Pallas kernels for 9% -> 12%
where the time goes in v10:
time: 38 us; the launch traced here: 37.7 us
  blocking collectives  20.2 us (53%)
  Pallas kernels  11.8 us (31%)
  starting transfers between devices  5.06 us (13%)
  between operations  0.67 us (2%)
    all_to_all x1, blocking collectives, local(): currents = lax.all_to_all(currents, 'mesh', 0, 0, tiled=True)  11.2 us
    pallas_call x3, Pallas kernels, call(): pl.pallas_call(kernel, out_shape=outputs, in_specs=in_specs or [whole_spe...  10.3 us
    all_to_all x1, blocking collectives, local(): stokes_all = lax.all_to_all(stokes_rows, 'mesh', 0, 0, tiled=True)  8.98 us
    ppermute x2, starting transfers between devices, swap(): return lax.ppermute(message, 'mesh', pairs)  5.06 us
    pallas_call x1, Pallas kernels, local(): pl.pallas_call(pack_kernel, out_shape=(shaped(message_rows, LANES), shape...  1.48 us
  transfers between devices with their start and end apart: 2, of which 0 were waited for; matrix products, arithmetic and copies ran while one was open for 0% of the time, Pallas kernels for 12%

profile of v10, /device:TPU:0, one launch (start us, length us, event | category | flops | bytes accessed | tf_op | source)
XLA Modules:
  0.0 37.7 jit_solution(14955715890467506898)
XLA Ops:
  0.6 1.5 %pack.1 = (f32[1024,128]{1,0:T(8,128)S(1)}, f32[1024,128]{1,0:T(8,128)S(1)}, f32[50,40,128]{2,1,0:T(8,128)S(1)}, f32[2,16,1024]{2,1,0:T(8,128)S(1)}, f32[16,1024...) custom-call(f32[50,36,128]{2,1,0:T(8,128)} %spectra_in.1, ...), custom_call_target="tpu_custom_call" | custom-call | tf_op jit(solution)/shard_map/pack/pallas_call | solution.py:705
  2.1 0.7 %collective-permute-start = (f32[1024,128]{1,0:T(8,128)S(1)}, f32[1024,128]{1,0:T(8,128)S(1)}, u32[]{:S(2)}, u32[]{:S(2)}) collective-permute-start(f32[1024,128]{1,0:T(8,128)S(1)} %get-tuple-element.30), channel_id=1, source_target_pairs={{1,2},{2,1},{3,4},{4,3},{5,6},{6,5},{7,8},{8,7},{9,10},{10,9},{11,... | collective-permute-start | bytes 1572872 | tf_op jit(solution)/shard_map/ppermute | solution.py:643
  2.8 4.4 %collective-permute-start.1 = (f32[1024,128]{1,0:T(8,128)S(1)}, f32[1024,128]{1,0:T(8,128)S(1)}, u32[]{:S(2)}, u32[]{:S(2)}) collective-permute-start(f32[1024,128]{1,0:T(8,128)S(1)} %get-tuple-element.31), channel_id=1, source_target_pairs={{0,1},{1,0},{2,3},{3,2},{4,5},{5,4},{6,7},{7,6},{8,9},{9,8},{10,11... | collective-permute-start | bytes 1572872 | tf_op jit(solution)/shard_map/ppermute | solution.py:643
  7.2 4.5 %prepare.1 = (s32[6,128]{1,0:T(8,128)S(1)}, f32[16,128]{1,0:T(8,128)S(1)}, f32[6,128]{1,0:T(8,128)S(1)}, f32[6,128]{1,0:T(8,128)S(1)}, f32[6,40,128]{2,1,0:T(8,1...) custom-call(f32[50,40,128]{2,1,0:T(8,128)S(1)} %get-tuple-element.32, ...), custom_call_target="tpu_custom_call" | custom-call | tf_op jit(solution)/shard_map/prepare/pallas_call | solution.py:690
  11.7 11.2 %all_to_all.22 = f32[16,1,128]{2,1,0:T(1,128)S(1)} all-to-all(f32[16,1,128]{2,1,0:T(1,128)S(1)} %bitcast.11), channel_id=1, replica_groups=mesh['groups'=2,'mesh'=16] {'mesh'}, dimensions={0} | all-to-all | bytes 16384 | tf_op jit(solution)/shard_map/all_to_all | solution.py:767
  22.9 0.0 collective-permute-done.outer
  22.9 0.0 collective-permute-done.1.inner
  22.9 3.0 %wave.1 = (f32[50,40,128]{2,1,0:T(8,128)S(1)}, f32[16,128]{1,0:T(8,128)S(1)}) custom-call(f32[50,40,128]{2,1,0:T(8,128)S(1)} %get-tuple-element.32.spectra, f32[1024,128]{1,0:T(8,128)S(1)} %collective-permute-done.outer, f32[1024,128]{1,0:T(8,128)S(1)} %collective-permute-done.1.inner, f32[16,128]{1,0:T(8,128)S(1)} %bitcast.9, ...), custom_call_target="tpu_custom_call" | custom-call | tf_op jit(solution)/shard_map/wave/pallas_call | solution.py:690
  25.9 9.0 %all_to_all.23 = f32[16,1,128]{2,1,0:T(1,128)S(1)} all-to-all(f32[16,1,128]{2,1,0:T(1,128)S(1)} %bitcast.12), channel_id=1, replica_groups=mesh['groups'=2,'mesh'=16] {'mesh'}, dimensions={0} | all-to-all | bytes 16384 | tf_op jit(solution)/shard_map/all_to_all | solution.py:784
  34.9 2.8 %tracer.1 = (f32[2,16,1024]{2,1,0:T(8,128)}, f32[50,36,128]{2,1,0:T(8,128)}) custom-call(f32[1024,128]{1,0:T(8,128)S(1)} %collective-permute-done.outer, f32[1024,128]{1,0:T(8,128)S(1)} %collective-permute-done.1.inner, f32[16,128]{1,0:T(8,128)S(1)} %bitcast.10, f32[8,48,128]{2,1,0:T(8,128)S(1)} %get-tuple-element.49.fields, ...), custom_call_target="tpu_custom_call" | custom-call | tf_op jit(solution)/shard_map/tracer/pallas_call | solution.py:690
Async XLA Ops:
  2.1 20.8 %collective-permute-start = (f32[1024,128]{1,0:T(8,128)S(1)}, f32[1024,128]{1,0:T(8,128)S(1)}, u32[]{:S(2)}, u32[]{:S(2)}) collective-permute-start(f32[1024,128]{1,0:T(8,128)S(1)} %get-tuple-element.30), channel_id=1, source_target_pairs={{1,2},{2,1},{3,4},{4,3},{5,6},{6,5},{7,8},{8,7},{9,10},{10,9},{11,... | collective-permute-start | bytes 1572872 | tf_op jit(solution)/shard_map/ppermute | solution.py:643
  2.8 20.1 %collective-permute-start.1 = (f32[1024,128]{1,0:T(8,128)S(1)}, f32[1024,128]{1,0:T(8,128)S(1)}, u32[]{:S(2)}, u32[]{:S(2)}) collective-permute-start(f32[1024,128]{1,0:T(8,128)S(1)} %get-tuple-element.31), channel_id=1, source_target_pairs={{0,1},{1,0},{2,3},{3,2},{4,5},{5,4},{6,7},{7,6},{8,9},{9,8},{10,11... | collective-permute-start | bytes 1572872 | tf_op jit(solution)/shard_map/ppermute | solution.py:643

commit v11 on v9

--- a/solution.py
+++ b/solution.py
@@ -115,23 +115,17 @@
         for f in range(freqs):
             spectra[f, dirs // 8 * 8 :, :] = jnp.zeros((8, LANES), jnp.float32)
     pairs = freqs // 2
-    piece = 5 if pairs % 5 == 0 else pairs
-    pieces = [
-        slice(start + first, start + first + piece)
-        for first in range(0, pairs, piece)
-        for start in (0, pairs)
-    ]
     copies = []
     for source, target in (
         (send_rows.at[me], coupled.at[1]),
         (current_in, current),
         (slot_in, node_slot),
+        (spectra_in, spectra.at[:, 0:dirs, :]),
         (tracers_in, tracers),
         (potential_in, potential),
         (neighbors_in, neighbors),
         (normal_in, normal),
         (weight_in, weight),
-        *((spectra_in.at[part], spectra.at[part, 0:dirs, :]) for part in pieces),
         (send_rows.at[jnp.maximum(me - 1, 0)], coupled.at[0]),
         (send_rows.at[jnp.minimum(me + 1, peers - 1)], coupled.at[2]),
         (near_in, near),
@@ -159,7 +153,7 @@
             picked = jnp.where(place == 2 * (cell // LANES) + part, found, 0.0)
             values[part].append(jnp.sum(picked, axis=0, keepdims=True))
     rows_out[...] = peer_rows(values, peers, capacity)
-    for copy in copies[3:8]:
+    for copy in copies[4:9]:
         copy.wait()
     odd = me % 2 == 1
     for out, upward in ((outer, odd), (inner, jnp.logical_not(odd))):
@@ -188,11 +182,8 @@
     whole = dirs // 8 * 8
     rest = dirs - whole
     turns = half_mask(dirs, odd)
+    copies[3].wait()
     for g in range(pairs):
-        if g % piece == 0:
-            at = 8 + 2 * (g // piece)
-            for copy in copies[at : at + 2]:
-                copy.wait()
         natural = spectra[g, 0:dirs, :]
         turned = pltpu.roll(spectra[g + pairs, 0:dirs, :], LANES // 2, 1)
         for out, mixed in (
@@ -207,7 +198,7 @@
     if at < outer.shape[0]:
         for out in (outer, inner):
             out[at:, :] = jnp.zeros((outer.shape[0] - at, LANES), jnp.float32)
-    for copy in copies[8 + len(pieces) :]:
+    for copy in copies[9:]:
         copy.wait()
 
 
@@ -240,7 +231,8 @@
     dirs, step_rows,
     spectra, near, angle, face, wind, slot, tracers, potential, neighbors, normal, weight, coupled,
     cosine, sine, project, choice, ways, slots, own_change,
-    fields, pieces, matrices, inside, cell_cosine, cell_sine, cell_scale, sums,
+    fields, matrices, inside, cell_cosine, cell_sine, cell_scale, sums,
+    pieces,
 ):
     me = lax.axis_index("mesh")
     node_tables(
@@ -280,10 +272,11 @@
                 slice(s * LANES, (s + 1) * LANES),
                 matrices.at[b],
             )
-    for b in range(1, blocks - 1):
-        inside[b - 1] = differences(
-            [pieces[b - 1], pieces[b], pieces[b + 1]], matrices[b]
-        )
+    for b in range(blocks):
+        first, last = max(b - 1, 0), min(b + 1, blocks - 1)
+        rows = slice((first - b + 1) * LANES, (last - b + 2) * LANES)
+        parts = [pieces[k] for k in range(first, last + 1)]
+        inside[b] = differences(parts, matrices[b, rows, :])
     for which in range(3):
         first = 0 if which != 0 else cells - LANES
         count = blocks if which == 1 else 1
@@ -349,7 +342,6 @@
         + 0.5 * (own_y + beside(own_y, halo_y)) * sine[...]
     )
     drifts = [spread(drift[s : s + 1, :], 8) for s in range(edges)]
-    drift_sum = sum(drifts[1:], drifts[0])
     from_outer = half_mask(dirs, odd)
     halos[...] = jnp.zeros(halos.shape, jnp.float32)
     ratio = 1.0 / 1.1
@@ -374,29 +366,35 @@
             mixed, choice[2 * LANES : 4 * LANES, :], preferred_element_type=jnp.float32
         )
 
-    def advect(c, change, first_speed, total):
+    def advect(c, change, first_speed, first_slow, total):
         total = list(total)
+        speeds = []
+        for i in range(step_pairs):
+            speeds += [first_speed * ratio**i, first_speed * ratio ** (i + pairs)]
+        slowness = []
+        for i in range(step_pairs):
+            slowness += [first_slow * ratio**-i, first_slow * ratio ** -(i + pairs)]
+        relative = [[drift * slow for drift in drifts] for slow in slowness]
+        relative_sum = [sum(each[1:], each[0]) for each in relative]
         for k, band in enumerate(bands):
             along = [project[s, band, :] for s in range(edges)]
             along_sum = sum(along[1:], along[0])
             for i in range(step_pairs):
                 g = c * step_pairs + i
-                for j, f, speed in (
-                    (2 * i, g, first_speed * ratio**i),
-                    (2 * i + 1, g + pairs, first_speed * ratio ** (i + pairs)),
-                ):
+                for j, f in ((2 * i, g), (2 * i + 1, g + pairs)):
                     own = spectra[f, band, :]
                     at = j * stride + band.start
                     own_at = pl.ds(pl.multiple_of(f * stride + band.start, 8), 8)
-                    value = own - (speed * along_sum + drift_sum) * own
+                    flux = (along_sum + relative_sum[j]) * own
                     for s in range(edges):
-                        down = jnp.minimum(speed * along[s] + drifts[s], 0.0)
+                        down = jnp.minimum(along[s] + relative[j][s], 0.0)
                         lanes = slice(s * LANES, (s + 1) * LANES)
                         step = change[at : at + 8, lanes] + own_change[own_at, lanes]
-                        value = value - down * step
+                        flux = flux + down * step
+                    value = own - speeds[j] * flux
                     spectra_new[f, band, :] = value
                     total[k] = total[k] + value
-        return first_speed * ratio**step_pairs, tuple(total)
+        return first_speed * ratio**step_pairs, first_slow * ratio**-step_pairs, tuple(total)
 
     zeros = tuple(jnp.zeros((8, LANES), jnp.float32) for _ in bands)
     chunks = pairs // step_pairs
@@ -408,13 +406,15 @@
         gather(2 * h + 2, change_a)
         return advect(2 * h + 1, change_b, *carry)
 
-    speed, total = lax.fori_loop(0, (chunks - 1) // 2, two_chunks, (jnp.float32(1.0), zeros))
+    carry = (jnp.float32(1.0), jnp.float32(1.0), zeros)
+    carry = lax.fori_loop(0, (chunks - 1) // 2, two_chunks, carry)
     if chunks % 2 == 0:
         gather(chunks - 1, change_b)
-        speed, total = advect(chunks - 2, change_a, speed, total)
-        _, total = advect(chunks - 1, change_b, speed, total)
+        carry = advect(chunks - 2, change_a, *carry)
+        carry = advect(chunks - 1, change_b, *carry)
     else:
-        _, total = advect(chunks - 1, change_a, speed, total)
+        carry = advect(chunks - 1, change_a, *carry)
+    total = carry[2]
     total = jnp.concatenate(total, axis=0)
     zero = jnp.zeros((stride, LANES), jnp.float32)
     cos_dir, sin_dir = ways[0], ways[1]
@@ -463,9 +463,9 @@
 
 def tracer_kernel(
     capacity, shape,
-    outer, inner, table, fields, pieces, matrices, inside, cosine, sine, scale, sums, spectra,
+    outer, inner, table, fields, neighbors, matrices, inside, cosine, sine, scale, sums, spectra,
     tracers_new, spectra_out,
-    halo, halo_pieces, halo_matrices, halo_tables, beside, stokes, antiflux, lowered, ratios,
+    halo, halo_near, halo_tables, stokes, antiflux, lowered, ratios,
     ratio_pieces, steps_a, steps_b, sem,
 ):
     dirs = spectra_out.shape[1]
@@ -485,7 +485,6 @@
         y = inner[b * field_rows : (b + 1) * field_rows, :]
         for side, value in ((0, jnp.where(odd, y, x)), (1, jnp.where(odd, x, y))):
             halo[2 * side + b] = value
-            halo_pieces[2 * side + b] = stack_split(value)
     at = 2 * field_rows
     x = outer[at : at + TABLE_ROWS, :]
     y = inner[at : at + TABLE_ROWS, :]
@@ -494,21 +493,7 @@
         halo_tables[side, 0, 0:edges, :] = w
         halo_tables[side, 1, 0:edges, :] = w * jnp.cos(rows[8 : 8 + edges])
         halo_tables[side, 2, 0:edges, :] = w * jnp.sin(rows[8 : 8 + edges])
-        near = rows[0:edges].astype(jnp.int32)
-        first = (me * blocks - 2 if side == 0 else me * blocks + blocks - 1) * LANES
-        for s in range(edges):
-            choose(
-                near[s : s + 1, :],
-                first,
-                slice(s * LANES, (s + 1) * LANES),
-                halo_matrices.at[side],
-            )
-    beside[0] = differences([halo_pieces[0], halo_pieces[1], pieces[0]], halo_matrices[0])
-    beside[1] = differences([halo_pieces[1], pieces[0], pieces[1]], matrices[0])
-    beside[2] = differences(
-        [pieces[blocks - 2], pieces[blocks - 1], halo_pieces[2]], matrices[blocks - 1]
-    )
-    beside[3] = differences([pieces[blocks - 1], halo_pieces[2], halo_pieces[3]], halo_matrices[1])
+        halo_near[side, 0:edges, :] = rows[0:edges].astype(jnp.int32)
 
     received = table[...]
     lane_of = lane_iota(peers)
@@ -584,21 +569,52 @@
     def band(ref, *index):
         return lambda row: ref[(*index, slice(row, row + 8), slice(None))]
 
-    def column(ref, index):
-        return lambda row, s: ref[index, row : row + 8, s * LANES : (s + 1) * LANES]
-
     def own_tables(i):
         return scale[i], cosine[i], sine[i]
 
-    for i in range(blocks - 2):
-        low_order(i + 2, band(fields, i + 1), column(inside, i), *own_tables(i + 1), True)
+    def within(i):
+        return lambda row, s: inside[i, row : row + 8, s * LANES : (s + 1) * LANES]
+
+    def edge(i, side):
+        beside = halo.at[1 + side]
+        sign = 2 * side - 1
+
+        def change(row, s):
+            near = spread(neighbors[s : s + 1, i * LANES : (i + 1) * LANES], 8)
+            from_halo = near // LANES - (me * blocks + i) == sign
+            picked = lane_gather(beside[row : row + 8, :], near % LANES)
+            return within(i)(row, s) + jnp.where(from_halo, picked, 0.0)
+
+        return change
+
+    def outside(side):
+        i = side * (blocks - 1)
+        low, own, high = (
+            (halo.at[0], halo.at[1], fields.at[i]),
+            (fields.at[i], halo.at[2], halo.at[3]),
+        )[side]
+
+        def change(row, s):
+            rows = slice(row, row + 8)
+            near = spread(halo_near[side, s : s + 1, :], 8)
+            place = near // LANES - (me * blocks + i + 2 * side - 1)
+            lane = near % LANES
+            mine = own[rows, :]
+            middle = lane_gather(mine, lane)
+            left = lane_gather(low[rows, :], lane)
+            right = lane_gather(high[rows, :], lane)
+            return jnp.where(place == 0, middle, jnp.where(place < 0, left, right)) - mine
+
+        return change
+
+    for i in range(1, blocks - 1):
+        low_order(i + 1, band(fields, i), within(i), *own_tables(i), True)
     for side in range(2):
         b = side * (blocks + 1)
         tables = tuple(halo_tables[side, k] for k in range(3))
-        near = 1 + side
-        low_order(b, band(halo, near), column(beside, 3 * side), *tables, False)
+        low_order(b, band(halo, 1 + side), outside(side), *tables, False)
         i = side * (blocks - 1)
-        low_order(i + 1, band(fields, i), column(beside, 1 + side), *own_tables(i), True)
+        low_order(i + 1, band(fields, i), edge(i, side), *own_tables(i), True)
 
     def products(i, steps):
         mixed = jnp.concatenate([ratio_pieces[i], ratio_pieces[i + 1], ratio_pieces[i + 2]], axis=1)
@@ -727,7 +743,7 @@
         out_specs=(whole_spec(),) * 15,
         scratch_shapes=[
             pltpu.VMEM(surface_current.shape, f32),
-            pltpu.SemaphoreType.DMA((64,)),
+            pltpu.SemaphoreType.DMA((15,)),
         ],
         compiler_params=params,
         name="pack",
@@ -737,7 +753,7 @@
 
     (
         cosine, sine, project, choice, ways, slot_choice, own_change,
-        fields, pieces, matrices, inside, cell_cosine, cell_sine, cell_scale, sums,
+        fields, matrices, inside, cell_cosine, cell_sine, cell_scale, sums,
     ) = call(
         functools.partial(prepare_kernel, dirs, step_rows),
         "prepare",
@@ -754,15 +770,14 @@
             shaped(nodes, peers * capacity, dtype=jnp.bfloat16),
             shaped(freqs * stride, edges * LANES),
             shaped(blocks, field_rows, LANES),
-            shaped(blocks, 2 * field_rows, LANES, dtype=jnp.bfloat16),
             shaped(blocks, 3 * LANES, edges * LANES, dtype=jnp.bfloat16),
-            shaped(blocks - 2, field_rows, edges * LANES),
+            shaped(blocks, field_rows, edges * LANES),
             shaped(blocks, 8, LANES),
             shaped(blocks, 8, LANES),
             shaped(blocks, 8, LANES),
             shaped(peers * capacity, (blocks + 2) * LANES, dtype=jnp.bfloat16),
         ),
-        [],
+        [pltpu.VMEM((blocks, 2 * field_rows, LANES), jnp.bfloat16)],
     )
     currents, cosine = lax.optimization_barrier((currents, cosine))
     currents = lax.all_to_all(currents, "mesh", 0, 0, tiled=True)
@@ -788,16 +803,14 @@
         functools.partial(tracer_kernel, capacity, (tracer_count, layers, edges)),
         "tracer",
         (
-            outer, inner, stokes_all, fields, pieces, matrices, inside, cell_cosine, cell_sine,
+            outer, inner, stokes_all, fields, neighbors, matrices, inside, cell_cosine, cell_sine,
             cell_scale, sums, pltpu.with_memory_space_constraint(spectra_new, pltpu.VMEM),
         ),
         (like(tracers), like(spectra)),
         [
             pltpu.VMEM((4, field_rows, LANES), f32),
-            pltpu.VMEM((4, 2 * field_rows, LANES), jnp.bfloat16),
-            pltpu.VMEM((2, 3 * LANES, edges * LANES), jnp.bfloat16),
+            pltpu.VMEM((2, 8, LANES), jnp.int32),
             pltpu.VMEM((2, 3, 8, LANES), f32),
-            pltpu.VMEM((4, field_rows, edges * LANES), f32),
             pltpu.VMEM((blocks + 2, 8, LANES), f32),
             pltpu.VMEM((blocks, edges, rows, LANES), f32),
             pltpu.VMEM((blocks, rows, LANES), f32),

time: 37.7 us -> 36.8 us (0.976)
  Pallas kernels: 11.1 us -> 10.3 us
    pallas_call x1, Pallas kernels: 2.21 us -> 1.62 us  [local(): pl.pallas_call(pack_kernel, out_shape=(shaped(peers, LANES), shaped(messa...]
where the time goes in v11:
time: 36.8 us; the launch traced here: 36.5 us
  blocking collectives  20.5 us (56%)
  Pallas kernels  10.3 us (28%)
  starting transfers between devices  5.06 us (14%)
  between operations  0.67 us (2%)
    all_to_all x1, blocking collectives, local(): currents = lax.all_to_all(currents, 'mesh', 0, 0, tiled=True)  11.2 us
    all_to_all x1, blocking collectives, local(): stokes_all = lax.all_to_all(stokes_rows, 'mesh', 0, 0, tiled=True)  9.27 us
    pallas_call x3, Pallas kernels, call(): pl.pallas_call(kernel, out_shape=outputs, in_specs=[whole_spec()] * len(i...  8.65 us
    ppermute x2, starting transfers between devices, swap(): return lax.ppermute(message, 'mesh', pairs)  5.06 us
    pallas_call x1, Pallas kernels, local(): pl.pallas_call(pack_kernel, out_shape=(shaped(peers, LANES), shaped(messa...  1.62 us
  transfers between devices with their start and end apart: 2, of which 0 were waited for; matrix products, arithmetic and copies ran while one was open for 0% of the time, Pallas kernels for 9%

profile of v11, /device:TPU:0, one launch (start us, length us, event | category | flops | bytes accessed | tf_op | source)
XLA Modules:
  0.0 36.5 jit_solution(3509844304615069758)
XLA Ops:
  0.6 1.6 %pack.1 = (f32[16,128]{1,0:T(8,128)S(1)}, f32[1024,128]{1,0:T(8,128)S(1)}, f32[1024,128]{1,0:T(8,128)S(1)}, f32[50,40,128]{2,1,0:T(8,128)S(1)}, s32[1,128]{1,0:T...) custom-call(f32[50,36,128]{2,1,0:T(8,128)} %spectra_in.1, ...), custom_call_target="tpu_custom_call" | custom-call | tf_op jit(solution)/shard_map/pack/pallas_call | solution.py:723
  2.3 0.7 %collective-permute-start = (f32[1024,128]{1,0:T(8,128)S(1)}, f32[1024,128]{1,0:T(8,128)S(1)}, u32[]{:S(2)}, u32[]{:S(2)}) collective-permute-start(f32[1024,128]{1,0:T(8,128)S(1)} %get-tuple-element.35), channel_id=1, source_target_pairs={{1,2},{2,1},{3,4},{4,3},{5,6},{6,5},{7,8},{8,7},{9,10},{10,9},{11,... | collective-permute-start | bytes 1572872 | tf_op jit(solution)/shard_map/ppermute | solution.py:659
  3.0 4.4 %collective-permute-start.1 = (f32[1024,128]{1,0:T(8,128)S(1)}, f32[1024,128]{1,0:T(8,128)S(1)}, u32[]{:S(2)}, u32[]{:S(2)}) collective-permute-start(f32[1024,128]{1,0:T(8,128)S(1)} %get-tuple-element.36), channel_id=1, source_target_pairs={{0,1},{1,0},{2,3},{3,2},{4,5},{5,4},{6,7},{7,6},{8,9},{9,8},{10,11... | collective-permute-start | bytes 1572872 | tf_op jit(solution)/shard_map/ppermute | solution.py:659
  7.3 3.4 %prepare.1 = (f32[6,128]{1,0:T(8,128)S(1)}, f32[6,128]{1,0:T(8,128)S(1)}, f32[6,40,128]{2,1,0:T(8,128)S(1)}, bf16[512,768]{1,0:T(8,128)(2,1)S(1)}, f32[3,40,128]...) custom-call(f32[50,40,128]{2,1,0:T(8,128)S(1)} %get-tuple-element.37, ...), custom_call_target="tpu_custom_call" | custom-call | tf_op jit(solution)/shard_map/prepare/pallas_call | solution.py:706
  10.7 11.2 %all_to_all.22 = f32[16,1,128]{2,1,0:T(1,128)S(1)} all-to-all(f32[16,1,128]{2,1,0:T(1,128)S(1)} %bitcast.11), channel_id=1, replica_groups=mesh['groups'=2,'mesh'=16] {'mesh'}, dimensions={0} | all-to-all | bytes 16384 | tf_op jit(solution)/shard_map/all_to_all | solution.py:783
  21.9 0.0 collective-permute-done.outer
  21.9 0.0 collective-permute-done.1.inner
  21.9 2.9 %wave.1 = (f32[50,40,128]{2,1,0:T(8,128)S(1)}, f32[16,128]{1,0:T(8,128)S(1)}) custom-call(f32[50,40,128]{2,1,0:T(8,128)S(1)} %get-tuple-element.37.spectra, f32[1024,128]{1,0:T(8,128)S(1)} %collective-permute-done.outer, f32[1024,128]{1,0:T(8,128)S(1)} %collective-permute-done.1.inner, f32[16,128]{1,0:T(8,128)S(1)} %bitcast.9, ...), custom_call_target="tpu_custom_call" | custom-call | tf_op jit(solution)/shard_map/wave/pallas_call | solution.py:706
  24.7 9.3 %all_to_all.23 = f32[16,1,128]{2,1,0:T(1,128)S(1)} all-to-all(f32[16,1,128]{2,1,0:T(1,128)S(1)} %bitcast.12), channel_id=1, replica_groups=mesh['groups'=2,'mesh'=16] {'mesh'}, dimensions={0} | all-to-all | bytes 16384 | tf_op jit(solution)/shard_map/all_to_all | solution.py:800
  34.0 2.4 %tracer.1 = (f32[2,16,1024]{2,1,0:T(8,128)}, f32[50,36,128]{2,1,0:T(8,128)}) custom-call(f32[1024,128]{1,0:T(8,128)S(1)} %collective-permute-done.outer, f32[1024,128]{1,0:T(8,128)S(1)} %collective-permute-done.1.inner, f32[16,128]{1,0:T(8,128)S(1)} %bitcast.10, f32[8,48,128]{2,1,0:T(8,128)S(1)} %get-tuple-element.60.fields, ...), custom_call_target="tpu_custom_call" | custom-call | tf_op jit(solution)/shard_map/tracer/pallas_call | solution.py:706
Async XLA Ops:
  2.3 19.6 %collective-permute-start = (f32[1024,128]{1,0:T(8,128)S(1)}, f32[1024,128]{1,0:T(8,128)S(1)}, u32[]{:S(2)}, u32[]{:S(2)}) collective-permute-start(f32[1024,128]{1,0:T(8,128)S(1)} %get-tuple-element.35), channel_id=1, source_target_pairs={{1,2},{2,1},{3,4},{4,3},{5,6},{6,5},{7,8},{8,7},{9,10},{10,9},{11,... | collective-permute-start | bytes 1572872 | tf_op jit(solution)/shard_map/ppermute | solution.py:659
  3.0 18.9 %collective-permute-start.1 = (f32[1024,128]{1,0:T(8,128)S(1)}, f32[1024,128]{1,0:T(8,128)S(1)}, u32[]{:S(2)}, u32[]{:S(2)}) collective-permute-start(f32[1024,128]{1,0:T(8,128)S(1)} %get-tuple-element.36), channel_id=1, source_target_pairs={{0,1},{1,0},{2,3},{3,2},{4,5},{5,4},{6,7},{7,6},{8,9},{9,8},{10,11... | collective-permute-start | bytes 1572872 | tf_op jit(solution)/shard_map/ppermute | solution.py:659

commit v12 on v11

--- a/solution.py
+++ b/solution.py
@@ -276,7 +276,12 @@
         first, last = max(b - 1, 0), min(b + 1, blocks - 1)
         rows = slice((first - b + 1) * LANES, (last - b + 2) * LANES)
         parts = [pieces[k] for k in range(first, last + 1)]
-        inside[b] = differences(parts, matrices[b, rows, :])
+        change = differences(parts, matrices[b, rows, :])
+        last_field = field_rows - layers
+        inside[b, 0:last_field, :] = change[:last_field]
+        for s in range(edges):
+            at = slice(s * LANES, (s + 1) * LANES)
+            inside[b, last_field:, at] = change[last_field:, at] * cell_scale[b, s : s + 1, :]
     for which in range(3):
         first = 0 if which != 0 else cells - LANES
         count = blocks if which == 1 else 1
@@ -352,9 +357,10 @@
             g = c * step_pairs + i
             parts = []
             for message in (outer, inner):
-                at = pl.multiple_of(base + g * whole, 8)
-                upper = message[pl.ds(at, whole), :]
-                left = message[pl.ds(base + pairs * whole + g * rest, rest), :]
+                at = base + g * whole
+                upper = message[at : at + whole, :]
+                at = base + pairs * whole + g * rest
+                left = message[at : at + rest, :]
                 parts.append(jnp.concatenate([upper, left], axis=0))
             x, y = parts
             at = 2 * i * stride
@@ -384,7 +390,7 @@
                 for j, f in ((2 * i, g), (2 * i + 1, g + pairs)):
                     own = spectra[f, band, :]
                     at = j * stride + band.start
-                    own_at = pl.ds(pl.multiple_of(f * stride + band.start, 8), 8)
+                    own_at = slice(f * stride + band.start, f * stride + band.stop)
                     flux = (along_sum + relative_sum[j]) * own
                     for s in range(edges):
                         down = jnp.minimum(along[s] + relative[j][s], 0.0)
@@ -398,22 +404,13 @@
 
     zeros = tuple(jnp.zeros((8, LANES), jnp.float32) for _ in bands)
     chunks = pairs // step_pairs
+    buffers = (change_a, change_b)
+    carry = (1.0, 1.0, zeros)
     gather(0, change_a)
-
-    def two_chunks(h, carry):
-        gather(2 * h + 1, change_b)
-        carry = advect(2 * h, change_a, *carry)
-        gather(2 * h + 2, change_a)
-        return advect(2 * h + 1, change_b, *carry)
-
-    carry = (jnp.float32(1.0), jnp.float32(1.0), zeros)
-    carry = lax.fori_loop(0, (chunks - 1) // 2, two_chunks, carry)
-    if chunks % 2 == 0:
-        gather(chunks - 1, change_b)
-        carry = advect(chunks - 2, change_a, *carry)
-        carry = advect(chunks - 1, change_b, *carry)
-    else:
-        carry = advect(chunks - 1, change_a, *carry)
+    for c in range(chunks):
+        if c + 1 < chunks:
+            gather(c + 1, buffers[(c + 1) % 2])
+        carry = advect(c, buffers[c % 2], *carry)
     total = carry[2]
     total = jnp.concatenate(total, axis=0)
     zero = jnp.zeros((stride, LANES), jnp.float32)
@@ -497,6 +494,7 @@
 
     received = table[...]
     lane_of = lane_iota(peers)
+    sections = []
     for which in range(3):
         values = []
         for part in range(2):
@@ -507,24 +505,23 @@
                 mine = row_iota(peers) == (lane_of + half * LANES) // capacity
                 row.append(jnp.sum(jnp.where(mine, found, 0.0), axis=0, keepdims=True))
             values.append(jnp.concatenate(row, axis=1))
-        parts = three_parts(jnp.concatenate(values, axis=0))
-        start = (0, 1, blocks + 1)[which]
-        count = blocks if which == 1 else 1
-        total = jnp.dot(
-            parts,
-            sums[:, start * LANES : (start + count) * LANES],
-            preferred_element_type=jnp.float32,
-        )
-        total = total[0:2] + (total[2:4] + total[4:6])
-        for b in range(count):
-            stokes[start + b, 0:2, :] = total[:, b * LANES : (b + 1) * LANES]
+        sections.append(three_parts(jnp.concatenate(values, axis=0)))
+    total = jnp.dot(
+        jnp.concatenate(sections, axis=0), sums[...], preferred_element_type=jnp.float32
+    )
+    for b in range(blocks + 2):
+        which = 0 if b == 0 else 2 if b == blocks + 1 else 1
+        at = 16 * which
+        lanes = slice(b * LANES, (b + 1) * LANES)
+        first, second, third = (total[at + k : at + k + 2, lanes] for k in (0, 2, 4))
+        stokes[b, 0:2, :] = first + (second + third)
 
     decay = [
         jnp.exp(-3.0 / layers * (row_iota(8) + 8 * g).astype(jnp.float32))
         for g in range(layer_groups)
     ]
 
-    def low_order(b, value, change, w, wx, wy, keep):
+    def low_order(b, value, change, wx, wy, keep):
         slope = wx * stokes[b, 0:1, :] + wy * stokes[b, 1:2, :]
         own = [value(8 * g) for g in range(tracer_groups)]
         zero = jnp.zeros((8, LANES), jnp.float32)
@@ -535,10 +532,9 @@
         positive = [zero] * tracer_groups
         negative = [zero] * tracer_groups
         for s in range(edges):
-            w8 = spread(w[s : s + 1, :], 8)
             slope8 = spread(slope[s : s + 1, :], 8)
             for lg in range(layer_groups):
-                speed = w8 * change(8 * (tracer_groups + lg), s) + decay[lg] * slope8
+                speed = change(8 * (tracer_groups + lg), s) + decay[lg] * slope8
                 down = jnp.minimum(speed, 0.0)
                 half = 0.5 * speed - down
                 speed_sum[lg] = speed_sum[lg] + speed
@@ -569,8 +565,7 @@
     def band(ref, *index):
         return lambda row: ref[(*index, slice(row, row + 8), slice(None))]
 
-    def own_tables(i):
-        return scale[i], cosine[i], sine[i]
+    potential_row = tracer_groups * 8
 
     def within(i):
         return lambda row, s: inside[i, row : row + 8, s * LANES : (s + 1) * LANES]
@@ -583,6 +578,8 @@
             near = spread(neighbors[s : s + 1, i * LANES : (i + 1) * LANES], 8)
             from_halo = near // LANES - (me * blocks + i) == sign
             picked = lane_gather(beside[row : row + 8, :], near % LANES)
+            if row >= potential_row:
+                picked = picked * spread(scale[i, s : s + 1, :], 8)
             return within(i)(row, s) + jnp.where(from_halo, picked, 0.0)
 
         return change
@@ -603,18 +600,21 @@
             middle = lane_gather(mine, lane)
             left = lane_gather(low[rows, :], lane)
             right = lane_gather(high[rows, :], lane)
-            return jnp.where(place == 0, middle, jnp.where(place < 0, left, right)) - mine
+            out = jnp.where(place == 0, middle, jnp.where(place < 0, left, right)) - mine
+            if row >= potential_row:
+                out = out * spread(halo_tables[side, 0, s : s + 1, :], 8)
+            return out
 
         return change
 
     for i in range(1, blocks - 1):
-        low_order(i + 1, band(fields, i), within(i), *own_tables(i), True)
+        low_order(i + 1, band(fields, i), within(i), cosine[i], sine[i], True)
     for side in range(2):
         b = side * (blocks + 1)
-        tables = tuple(halo_tables[side, k] for k in range(3))
+        tables = (halo_tables[side, 1], halo_tables[side, 2])
         low_order(b, band(halo, 1 + side), outside(side), *tables, False)
         i = side * (blocks - 1)
-        low_order(i + 1, band(fields, i), edge(i, side), *own_tables(i), True)
+        low_order(i + 1, band(fields, i), edge(i, side), cosine[i], sine[i], True)
 
     def products(i, steps):
         mixed = jnp.concatenate([ratio_pieces[i], ratio_pieces[i + 1], ratio_pieces[i + 2]], axis=1)

time: 36.8 us -> 36.4 us (0.989)
  no operation moved by 1% of the time
where the time goes in v12:
time: 36.4 us; the launch traced here: 36.2 us
  blocking collectives  20.4 us (56%)
  Pallas kernels  10 us (27%)
  starting transfers between devices  5.06 us (14%)
  between operations  0.67 us (2%)
    all_to_all x1, blocking collectives, local(): currents = lax.all_to_all(currents, 'mesh', 0, 0, tiled=True)  11.2 us
    all_to_all x1, blocking collectives, local(): stokes_all = lax.all_to_all(stokes_rows, 'mesh', 0, 0, tiled=True)  9.23 us
    pallas_call x3, Pallas kernels, call(): pl.pallas_call(kernel, out_shape=outputs, in_specs=[whole_spec()] * len(i...  8.39 us
    ppermute x2, starting transfers between devices, swap(): return lax.ppermute(message, 'mesh', pairs)  5.06 us
    pallas_call x1, Pallas kernels, local(): pl.pallas_call(pack_kernel, out_shape=(shaped(peers, LANES), shaped(messa...  1.62 us
  transfers between devices with their start and end apart: 2, of which 0 were waited for; matrix products, arithmetic and copies ran while one was open for 0% of the time, Pallas kernels for 9%

profile of v12, /device:TPU:0, one launch (start us, length us, event | category | flops | bytes accessed | tf_op | source)
XLA Modules:
  0.0 36.2 jit_solution(6578106529538709363)
XLA Ops:
  0.6 1.6 %pack.1 = (f32[16,128]{1,0:T(8,128)S(1)}, f32[1024,128]{1,0:T(8,128)S(1)}, f32[1024,128]{1,0:T(8,128)S(1)}, f32[50,40,128]{2,1,0:T(8,128)S(1)}, s32[1,128]{1,0:T...) custom-call(f32[50,36,128]{2,1,0:T(8,128)} %spectra_in.1, ...), custom_call_target="tpu_custom_call" | custom-call | tf_op jit(solution)/shard_map/pack/pallas_call | solution.py:723
  2.3 0.7 %collective-permute-start = (f32[1024,128]{1,0:T(8,128)S(1)}, f32[1024,128]{1,0:T(8,128)S(1)}, u32[]{:S(2)}, u32[]{:S(2)}) collective-permute-start(f32[1024,128]{1,0:T(8,128)S(1)} %get-tuple-element.35), channel_id=1, source_target_pairs={{1,2},{2,1},{3,4},{4,3},{5,6},{6,5},{7,8},{8,7},{9,10},{10,9},{11,... | collective-permute-start | bytes 1572872 | tf_op jit(solution)/shard_map/ppermute | solution.py:659
  3.0 4.4 %collective-permute-start.1 = (f32[1024,128]{1,0:T(8,128)S(1)}, f32[1024,128]{1,0:T(8,128)S(1)}, u32[]{:S(2)}, u32[]{:S(2)}) collective-permute-start(f32[1024,128]{1,0:T(8,128)S(1)} %get-tuple-element.36), channel_id=1, source_target_pairs={{0,1},{1,0},{2,3},{3,2},{4,5},{5,4},{6,7},{7,6},{8,9},{9,8},{10,11... | collective-permute-start | bytes 1572872 | tf_op jit(solution)/shard_map/ppermute | solution.py:659
  7.3 3.4 %prepare.1 = (f32[6,128]{1,0:T(8,128)S(1)}, f32[6,128]{1,0:T(8,128)S(1)}, f32[6,40,128]{2,1,0:T(8,128)S(1)}, bf16[512,768]{1,0:T(8,128)(2,1)S(1)}, f32[3,40,128]...) custom-call(f32[50,40,128]{2,1,0:T(8,128)S(1)} %get-tuple-element.37, ...), custom_call_target="tpu_custom_call" | custom-call | tf_op jit(solution)/shard_map/prepare/pallas_call | solution.py:706
  10.7 11.2 %all_to_all.22 = f32[16,1,128]{2,1,0:T(1,128)S(1)} all-to-all(f32[16,1,128]{2,1,0:T(1,128)S(1)} %bitcast.11), channel_id=1, replica_groups=mesh['groups'=2,'mesh'=16] {'mesh'}, dimensions={0} | all-to-all | bytes 16384 | tf_op jit(solution)/shard_map/all_to_all | solution.py:783
  21.9 0.0 collective-permute-done.outer
  21.9 0.0 collective-permute-done.1.inner
  21.9 2.6 %wave.1 = (f32[50,40,128]{2,1,0:T(8,128)S(1)}, f32[16,128]{1,0:T(8,128)S(1)}) custom-call(f32[50,40,128]{2,1,0:T(8,128)S(1)} %get-tuple-element.37.spectra, f32[1024,128]{1,0:T(8,128)S(1)} %collective-permute-done.outer, f32[1024,128]{1,0:T(8,128)S(1)} %collective-permute-done.1.inner, f32[16,128]{1,0:T(8,128)S(1)} %bitcast.9, ...), custom_call_target="tpu_custom_call" | custom-call | tf_op jit(solution)/shard_map/wave/pallas_call | solution.py:706
  24.5 9.2 %all_to_all.23 = f32[16,1,128]{2,1,0:T(1,128)S(1)} all-to-all(f32[16,1,128]{2,1,0:T(1,128)S(1)} %bitcast.12), channel_id=1, replica_groups=mesh['groups'=2,'mesh'=16] {'mesh'}, dimensions={0} | all-to-all | bytes 16384 | tf_op jit(solution)/shard_map/all_to_all | solution.py:800
  33.7 2.4 %tracer.1 = (f32[2,16,1024]{2,1,0:T(8,128)}, f32[50,36,128]{2,1,0:T(8,128)}) custom-call(f32[1024,128]{1,0:T(8,128)S(1)} %collective-permute-done.outer, f32[1024,128]{1,0:T(8,128)S(1)} %collective-permute-done.1.inner, f32[16,128]{1,0:T(8,128)S(1)} %bitcast.10, f32[8,48,128]{2,1,0:T(8,128)S(1)} %get-tuple-element.60.fields, ...), custom_call_target="tpu_custom_call" | custom-call | tf_op jit(solution)/shard_map/tracer/pallas_call | solution.py:706
Async XLA Ops:
  2.3 19.7 %collective-permute-start = (f32[1024,128]{1,0:T(8,128)S(1)}, f32[1024,128]{1,0:T(8,128)S(1)}, u32[]{:S(2)}, u32[]{:S(2)}) collective-permute-start(f32[1024,128]{1,0:T(8,128)S(1)} %get-tuple-element.35), channel_id=1, source_target_pairs={{1,2},{2,1},{3,4},{4,3},{5,6},{6,5},{7,8},{8,7},{9,10},{10,9},{11,... | collective-permute-start | bytes 1572872 | tf_op jit(solution)/shard_map/ppermute | solution.py:659
  3.0 19.0 %collective-permute-start.1 = (f32[1024,128]{1,0:T(8,128)S(1)}, f32[1024,128]{1,0:T(8,128)S(1)}, u32[]{:S(2)}, u32[]{:S(2)}) collective-permute-start(f32[1024,128]{1,0:T(8,128)S(1)} %get-tuple-element.36), channel_id=1, source_target_pairs={{0,1},{1,0},{2,3},{3,2},{4,5},{5,4},{6,7},{7,6},{8,9},{9,8},{10,11... | collective-permute-start | bytes 1572872 | tf_op jit(solution)/shard_map/ppermute | solution.py:659

commit v13 on v12

--- a/solution.py
+++ b/solution.py
@@ -206,25 +206,15 @@
     place = (cells - first - LANES).astype(jnp.float32).astype(jnp.bfloat16)
     place = spread(place, LANES)
     one = jnp.ones((LANES, LANES), jnp.bfloat16)
-    for k in range(3):
-        source = (row_iota(LANES) + (k - 1) * LANES).astype(jnp.float32).astype(jnp.bfloat16)
-        part = jnp.where(source == place, one, 0 * one)
-        if k == 1:
-            own = jnp.where(row_iota(LANES) == lane_iota(LANES), 1.0, 0.0).astype(jnp.bfloat16)
-            part = part - own
+    for k in range(2):
+        source = (row_iota(LANES) + (2 * k - 1) * LANES).astype(jnp.float32)
+        part = jnp.where(source.astype(jnp.bfloat16) == place, one, 0 * one)
         matrix[k * LANES : (k + 1) * LANES, lanes] = part
 
 
 def stack_split(x):
     first, second = split(x)
     return jnp.concatenate([first, second], axis=0)
-
-
-def differences(parts, matrix):
-    mixed = jnp.concatenate(parts, axis=1)
-    out = jnp.dot(mixed, matrix, preferred_element_type=jnp.float32)
-    rows = out.shape[0] // 2
-    return out[:rows] + out[rows:]
 
 
 def prepare_kernel(
@@ -232,7 +222,7 @@
     spectra, near, angle, face, wind, slot, tracers, potential, neighbors, normal, weight, coupled,
     cosine, sine, project, choice, ways, slots, own_change,
     fields, matrices, inside, cell_cosine, cell_sine, cell_scale, sums,
-    pieces,
+    pieces, beside,
 ):
     me = lax.axis_index("mesh")
     node_tables(
@@ -273,15 +263,26 @@
                 matrices.at[b],
             )
     for b in range(blocks):
-        first, last = max(b - 1, 0), min(b + 1, blocks - 1)
-        rows = slice((first - b + 1) * LANES, (last - b + 2) * LANES)
-        parts = [pieces[k] for k in range(first, last + 1)]
-        change = differences(parts, matrices[b, rows, :])
-        last_field = field_rows - layers
-        inside[b, 0:last_field, :] = change[:last_field]
+        parts = [pieces[k] for k in (b - 1, b + 1) if 0 <= k < blocks]
+        rows = slice(LANES if b == 0 else 0, LANES if b == blocks - 1 else 2 * LANES)
+        beside[...] = jnp.dot(
+            jnp.concatenate(parts, axis=1), matrices[b, rows, :], preferred_element_type=jnp.float32
+        )
         for s in range(edges):
             at = slice(s * LANES, (s + 1) * LANES)
-            inside[b, last_field:, at] = change[last_field:, at] * cell_scale[b, s : s + 1, :]
+            near = spread(neighbors[s : s + 1, b * LANES : (b + 1) * LANES], 8)
+            same = near // LANES == me * blocks + b
+            lane = near % LANES
+            for row in range(0, field_rows, 8):
+                own = fields[b, row : row + 8, :]
+                other = (
+                    beside[row : row + 8, at]
+                    + beside[field_rows + row : field_rows + row + 8, at]
+                )
+                change = jnp.where(same, lane_gather(own, lane), other) - own
+                if row >= field_rows - layers:
+                    change = change * cell_scale[b, s : s + 1, :]
+                inside[b, row : row + 8, at] = change
     for which in range(3):
         first = 0 if which != 0 else cells - LANES
         count = blocks if which == 1 else 1
@@ -617,7 +618,7 @@
         low_order(i + 1, band(fields, i), edge(i, side), cosine[i], sine[i], True)
 
     def products(i, steps):
-        mixed = jnp.concatenate([ratio_pieces[i], ratio_pieces[i + 1], ratio_pieces[i + 2]], axis=1)
+        mixed = jnp.concatenate([ratio_pieces[i], ratio_pieces[i + 2]], axis=1)
         steps[...] = jnp.dot(mixed, matrices[i], preferred_element_type=jnp.float32)
 
     def limit(i, steps):
@@ -626,9 +627,15 @@
         low = 16 * tracer_groups
         for s in range(edges):
             lanes = slice(s * LANES, (s + 1) * LANES)
+            near = spread(neighbors[s : s + 1, i * LANES : (i + 1) * LANES], 8)
+            same = near // LANES == me * blocks + i
+            lane = near % LANES
             beside = [
-                own[g]
-                + (steps[8 * g : 8 * g + 8, lanes] + steps[low + 8 * g : low + 8 * g + 8, lanes])
+                jnp.where(
+                    same,
+                    lane_gather(own[g], lane),
+                    steps[8 * g : 8 * g + 8, lanes] + steps[low + 8 * g : low + 8 * g + 8, lanes],
+                )
                 for g in range(2 * tracer_groups)
             ]
             for g in range(tracer_groups):
@@ -770,14 +777,17 @@
             shaped(nodes, peers * capacity, dtype=jnp.bfloat16),
             shaped(freqs * stride, edges * LANES),
             shaped(blocks, field_rows, LANES),
-            shaped(blocks, 3 * LANES, edges * LANES, dtype=jnp.bfloat16),
+            shaped(blocks, 2 * LANES, edges * LANES, dtype=jnp.bfloat16),
             shaped(blocks, field_rows, edges * LANES),
             shaped(blocks, 8, LANES),
             shaped(blocks, 8, LANES),
             shaped(blocks, 8, LANES),
             shaped(peers * capacity, (blocks + 2) * LANES, dtype=jnp.bfloat16),
         ),
-        [pltpu.VMEM((blocks, 2 * field_rows, LANES), jnp.bfloat16)],
+        [
+            pltpu.VMEM((blocks, 2 * field_rows, LANES), jnp.bfloat16),
+            pltpu.VMEM((2 * field_rows, edges * LANES), f32),
+        ],
     )
     currents, cosine = lax.optimization_barrier((currents, cosine))
     currents = lax.all_to_all(currents, "mesh", 0, 0, tiled=True)

time: 36.4 us -> 37 us (1.016)
  Pallas kernels: 10 us -> 10.6 us
    pallas_call x3, Pallas kernels: 8.39 us -> 8.99 us  [call(): pl.pallas_call(kernel, out_shape=outputs, in_specs=[whole_spec()] * len(i...]
where the time goes in v13:
time: 37 us; the launch traced here: 36.8 us
  blocking collectives  20.4 us (55%)
  Pallas kernels  10.6 us (29%)
  starting transfers between devices  5.06 us (14%)
  between operations  0.67 us (2%)
    all_to_all x1, blocking collectives, local(): currents = lax.all_to_all(currents, 'mesh', 0, 0, tiled=True)  11.2 us
    all_to_all x1, blocking collectives, local(): stokes_all = lax.all_to_all(stokes_rows, 'mesh', 0, 0, tiled=True)  9.23 us
    pallas_call x3, Pallas kernels, call(): pl.pallas_call(kernel, out_shape=outputs, in_specs=[whole_spec()] * len(i...  8.99 us
    ppermute x2, starting transfers between devices, swap(): return lax.ppermute(message, 'mesh', pairs)  5.06 us
    pallas_call x1, Pallas kernels, local(): pl.pallas_call(pack_kernel, out_shape=(shaped(peers, LANES), shaped(messa...  1.62 us
  transfers between devices with their start and end apart: 2, of which 0 were waited for; matrix products, arithmetic and copies ran while one was open for 0% of the time, Pallas kernels for 9%

profile of v13, /device:TPU:0, one launch (start us, length us, event | category | flops | bytes accessed | tf_op | source)
XLA Modules:
  0.0 36.8 jit_solution(3983857517873985289)
XLA Ops:
  0.6 1.6 %pack.1 = (f32[16,128]{1,0:T(8,128)S(1)}, f32[1024,128]{1,0:T(8,128)S(1)}, f32[1024,128]{1,0:T(8,128)S(1)}, f32[50,40,128]{2,1,0:T(8,128)S(1)}, s32[1,128]{1,0:T...) custom-call(f32[50,36,128]{2,1,0:T(8,128)} %spectra_in.1, ...), custom_call_target="tpu_custom_call" | custom-call | tf_op jit(solution)/shard_map/pack/pallas_call | solution.py:730
  2.3 0.7 %collective-permute-start = (f32[1024,128]{1,0:T(8,128)S(1)}, f32[1024,128]{1,0:T(8,128)S(1)}, u32[]{:S(2)}, u32[]{:S(2)}) collective-permute-start(f32[1024,128]{1,0:T(8,128)S(1)} %get-tuple-element.35), channel_id=1, source_target_pairs={{1,2},{2,1},{3,4},{4,3},{5,6},{6,5},{7,8},{8,7},{9,10},{10,9},{11,... | collective-permute-start | bytes 1572872 | tf_op jit(solution)/shard_map/ppermute | solution.py:666
  3.0 4.4 %collective-permute-start.1 = (f32[1024,128]{1,0:T(8,128)S(1)}, f32[1024,128]{1,0:T(8,128)S(1)}, u32[]{:S(2)}, u32[]{:S(2)}) collective-permute-start(f32[1024,128]{1,0:T(8,128)S(1)} %get-tuple-element.36), channel_id=1, source_target_pairs={{0,1},{1,0},{2,3},{3,2},{4,5},{5,4},{6,7},{7,6},{8,9},{9,8},{10,11... | collective-permute-start | bytes 1572872 | tf_op jit(solution)/shard_map/ppermute | solution.py:666
  7.3 3.4 %prepare.1 = (f32[6,128]{1,0:T(8,128)S(1)}, f32[6,128]{1,0:T(8,128)S(1)}, f32[6,40,128]{2,1,0:T(8,128)S(1)}, bf16[512,768]{1,0:T(8,128)(2,1)S(1)}, f32[3,40,128]...) custom-call(f32[50,40,128]{2,1,0:T(8,128)S(1)} %get-tuple-element.37, ...), custom_call_target="tpu_custom_call" | custom-call | tf_op jit(solution)/shard_map/prepare/pallas_call | solution.py:713
  10.7 11.2 %all_to_all.22 = f32[16,1,128]{2,1,0:T(1,128)S(1)} all-to-all(f32[16,1,128]{2,1,0:T(1,128)S(1)} %bitcast.11), channel_id=1, replica_groups=mesh['groups'=2,'mesh'=16] {'mesh'}, dimensions={0} | all-to-all | bytes 16384 | tf_op jit(solution)/shard_map/all_to_all | solution.py:793
  21.9 0.0 collective-permute-done.outer
  21.9 0.0 collective-permute-done.1.inner
  21.9 2.6 %wave.1 = (f32[50,40,128]{2,1,0:T(8,128)S(1)}, f32[16,128]{1,0:T(8,128)S(1)}) custom-call(f32[50,40,128]{2,1,0:T(8,128)S(1)} %get-tuple-element.37.spectra, f32[1024,128]{1,0:T(8,128)S(1)} %collective-permute-done.outer, f32[1024,128]{1,0:T(8,128)S(1)} %collective-permute-done.1.inner, f32[16,128]{1,0:T(8,128)S(1)} %bitcast.9, ...), custom_call_target="tpu_custom_call" | custom-call | tf_op jit(solution)/shard_map/wave/pallas_call | solution.py:713
  24.5 9.2 %all_to_all.23 = f32[16,1,128]{2,1,0:T(1,128)S(1)} all-to-all(f32[16,1,128]{2,1,0:T(1,128)S(1)} %bitcast.12), channel_id=1, replica_groups=mesh['groups'=2,'mesh'=16] {'mesh'}, dimensions={0} | all-to-all | bytes 16384 | tf_op jit(solution)/shard_map/all_to_all | solution.py:810
  33.8 3.0 %tracer.1 = (f32[2,16,1024]{2,1,0:T(8,128)}, f32[50,36,128]{2,1,0:T(8,128)}) custom-call(f32[1024,128]{1,0:T(8,128)S(1)} %collective-permute-done.outer, f32[1024,128]{1,0:T(8,128)S(1)} %collective-permute-done.1.inner, f32[16,128]{1,0:T(8,128)S(1)} %bitcast.10, f32[8,48,128]{2,1,0:T(8,128)S(1)} %get-tuple-element.60.fields, ...), custom_call_target="tpu_custom_call" | custom-call | tf_op jit(solution)/shard_map/tracer/pallas_call | solution.py:713
Async XLA Ops:
  2.3 19.7 %collective-permute-start = (f32[1024,128]{1,0:T(8,128)S(1)}, f32[1024,128]{1,0:T(8,128)S(1)}, u32[]{:S(2)}, u32[]{:S(2)}) collective-permute-start(f32[1024,128]{1,0:T(8,128)S(1)} %get-tuple-element.35), channel_id=1, source_target_pairs={{1,2},{2,1},{3,4},{4,3},{5,6},{6,5},{7,8},{8,7},{9,10},{10,9},{11,... | collective-permute-start | bytes 1572872 | tf_op jit(solution)/shard_map/ppermute | solution.py:666
  3.0 19.0 %collective-permute-start.1 = (f32[1024,128]{1,0:T(8,128)S(1)}, f32[1024,128]{1,0:T(8,128)S(1)}, u32[]{:S(2)}, u32[]{:S(2)}) collective-permute-start(f32[1024,128]{1,0:T(8,128)S(1)} %get-tuple-element.36), channel_id=1, source_target_pairs={{0,1},{1,0},{2,3},{3,2},{4,5},{5,4},{6,7},{7,6},{8,9},{9,8},{10,11... | collective-permute-start | bytes 1572872 | tf_op jit(solution)/shard_map/ppermute | solution.py:666

commit v14 on v12

--- a/solution.py
+++ b/solution.py
@@ -306,11 +306,67 @@
     return out
 
 
+def halo_tasks(
+    layers, outer, inner, fields, neighbors, inside, scale,
+    halo, tables, edge_change, halo_change, near_cells,
+):
+    me = lax.axis_index("mesh")
+    odd = me % 2 == 1
+    blocks, field_rows, _ = fields.shape
+    edges = neighbors.shape[0]
+    for b in range(2):
+        x = outer[b * field_rows : (b + 1) * field_rows, :]
+        y = inner[b * field_rows : (b + 1) * field_rows, :]
+        halo[b] = jnp.where(odd, y, x)
+        halo[2 + b] = jnp.where(odd, x, y)
+    at = 2 * field_rows
+    x = outer[at : at + TABLE_ROWS, :]
+    y = inner[at : at + TABLE_ROWS, :]
+    for side, rows in ((0, jnp.where(odd, y, x)), (1, jnp.where(odd, x, y))):
+        w = rows[16 : 16 + edges]
+        tables[side, 0, 0:edges, :] = w
+        tables[side, 1, 0:edges, :] = w * jnp.cos(rows[8 : 8 + edges])
+        tables[side, 2, 0:edges, :] = w * jnp.sin(rows[8 : 8 + edges])
+        near_cells[side, 0:edges, :] = rows[0:edges].astype(jnp.int32)
+
+    def task(side, s):
+        i = side * (blocks - 1)
+        lanes = slice(s * LANES, (s + 1) * LANES)
+        low, own, high = (
+            (halo.at[0], halo.at[1], fields.at[i]),
+            (fields.at[i], halo.at[2], halo.at[3]),
+        )[side]
+        near = spread(neighbors[s : s + 1, i * LANES : (i + 1) * LANES], 8)
+        from_halo = near // LANES - (me * blocks + i) == 2 * side - 1
+        lane = near % LANES
+        far = spread(near_cells[side, s : s + 1, :], 8)
+        place = far // LANES - (me * blocks + i + 2 * side - 1)
+        far_lane = far % LANES
+        for row in range(0, field_rows, 8):
+            rows = slice(row, row + 8)
+            mine = own[rows, :]
+            picked = lane_gather(mine, lane)
+            middle = lane_gather(mine, far_lane)
+            left = lane_gather(low[rows, :], far_lane)
+            right = lane_gather(high[rows, :], far_lane)
+            out = jnp.where(place == 0, middle, jnp.where(place < 0, left, right)) - mine
+            if row >= field_rows - layers:
+                picked = picked * spread(scale[i, s : s + 1, :], 8)
+                out = out * spread(tables[side, 0, s : s + 1, :], 8)
+            halo_change[side, rows, lanes] = out
+            edge_change[side, rows, lanes] = inside[i, rows, lanes] + jnp.where(
+                from_halo, picked, 0.0
+            )
+
+    return [functools.partial(task, side, s) for s in range(edges) for side in range(2)]
+
+
 def wave_kernel(
-    capacity, step_pairs, dirs,
+    capacity, step_pairs, dirs, layers,
     spectra, outer, inner, table, node_slot, neighbors, cosine, sine, project, choice, ways, slots,
-    own_change,
-    spectra_new, rows_out, drift, halos, change_a, change_b,
+    own_change, fields, cell_neighbors, cell_inside, scale,
+    spectra_new, rows_out, halo, tables, edge_change, halo_change,
+    drift, halos, change_a, change_b, near_cells,
 ):
     me = lax.axis_index("mesh")
     freqs, stride = spectra.shape[:2]
@@ -407,9 +463,15 @@
     buffers = (change_a, change_b)
     carry = (1.0, 1.0, zeros)
     gather(0, change_a)
+    tasks = halo_tasks(
+        layers, outer, inner, fields, cell_neighbors, cell_inside, scale,
+        halo, tables, edge_change, halo_change, near_cells,
+    )
     for c in range(chunks):
         if c + 1 < chunks:
             gather(c + 1, buffers[(c + 1) % 2])
+        for task in tasks[c * len(tasks) // chunks : (c + 1) * len(tasks) // chunks]:
+            task()
         carry = advect(c, buffers[c % 2], *carry)
     total = carry[2]
     total = jnp.concatenate(total, axis=0)
@@ -460,37 +522,21 @@
 
 def tracer_kernel(
     capacity, shape,
-    outer, inner, table, fields, neighbors, matrices, inside, cosine, sine, scale, sums, spectra,
+    halo, halo_tables, edge_change, halo_change, table, fields, matrices, inside, cosine, sine,
+    sums, spectra,
     tracers_new, spectra_out,
-    halo, halo_near, halo_tables, stokes, antiflux, lowered, ratios,
+    stokes, antiflux, lowered, ratios,
     ratio_pieces, steps_a, steps_b, sem,
 ):
     dirs = spectra_out.shape[1]
     write = pltpu.make_async_copy(spectra.at[:, 0:dirs, :], spectra_out, sem)
     write.start()
-    me = lax.axis_index("mesh")
     tracer_count, layers, edges = shape
     peers = table.shape[0]
     halves = peers * capacity // LANES
     blocks, field_rows, _ = fields.shape
     layer_groups = layers // 8
     tracer_groups = tracer_count * layer_groups
-    odd = me % 2 == 1
-
-    for b in range(2):
-        x = outer[b * field_rows : (b + 1) * field_rows, :]
-        y = inner[b * field_rows : (b + 1) * field_rows, :]
-        for side, value in ((0, jnp.where(odd, y, x)), (1, jnp.where(odd, x, y))):
-            halo[2 * side + b] = value
-    at = 2 * field_rows
-    x = outer[at : at + TABLE_ROWS, :]
-    y = inner[at : at + TABLE_ROWS, :]
-    for side, rows in ((0, jnp.where(odd, y, x)), (1, jnp.where(odd, x, y))):
-        w = rows[16 : 16 + edges]
-        halo_tables[side, 0, 0:edges, :] = w
-        halo_tables[side, 1, 0:edges, :] = w * jnp.cos(rows[8 : 8 + edges])
-        halo_tables[side, 2, 0:edges, :] = w * jnp.sin(rows[8 : 8 + edges])
-        halo_near[side, 0:edges, :] = rows[0:edges].astype(jnp.int32)
 
     received = table[...]
     lane_of = lane_iota(peers)
@@ -565,56 +611,18 @@
     def band(ref, *index):
         return lambda row: ref[(*index, slice(row, row + 8), slice(None))]
 
-    potential_row = tracer_groups * 8
-
-    def within(i):
-        return lambda row, s: inside[i, row : row + 8, s * LANES : (s + 1) * LANES]
-
-    def edge(i, side):
-        beside = halo.at[1 + side]
-        sign = 2 * side - 1
-
-        def change(row, s):
-            near = spread(neighbors[s : s + 1, i * LANES : (i + 1) * LANES], 8)
-            from_halo = near // LANES - (me * blocks + i) == sign
-            picked = lane_gather(beside[row : row + 8, :], near % LANES)
-            if row >= potential_row:
-                picked = picked * spread(scale[i, s : s + 1, :], 8)
-            return within(i)(row, s) + jnp.where(from_halo, picked, 0.0)
-
-        return change
-
-    def outside(side):
-        i = side * (blocks - 1)
-        low, own, high = (
-            (halo.at[0], halo.at[1], fields.at[i]),
-            (fields.at[i], halo.at[2], halo.at[3]),
-        )[side]
-
-        def change(row, s):
-            rows = slice(row, row + 8)
-            near = spread(halo_near[side, s : s + 1, :], 8)
-            place = near // LANES - (me * blocks + i + 2 * side - 1)
-            lane = near % LANES
-            mine = own[rows, :]
-            middle = lane_gather(mine, lane)
-            left = lane_gather(low[rows, :], lane)
-            right = lane_gather(high[rows, :], lane)
-            out = jnp.where(place == 0, middle, jnp.where(place < 0, left, right)) - mine
-            if row >= potential_row:
-                out = out * spread(halo_tables[side, 0, s : s + 1, :], 8)
-            return out
-
-        return change
-
-    for i in range(1, blocks - 1):
-        low_order(i + 1, band(fields, i), within(i), cosine[i], sine[i], True)
+    def column(ref, index):
+        return lambda row, s: ref[index, row : row + 8, s * LANES : (s + 1) * LANES]
+
     for side in range(2):
         b = side * (blocks + 1)
-        tables = (halo_tables[side, 1], halo_tables[side, 2])
-        low_order(b, band(halo, 1 + side), outside(side), *tables, False)
-        i = side * (blocks - 1)
-        low_order(i + 1, band(fields, i), edge(i, side), cosine[i], sine[i], True)
+        normals = (halo_tables[side, 1], halo_tables[side, 2])
+        low_order(b, band(halo, 1 + side), column(halo_change, side), *normals, False)
+    for i in range(blocks):
+        change = column(inside, i)
+        if i in (0, blocks - 1):
+            change = column(edge_change, min(i, 1))
+        low_order(i + 1, band(fields, i), change, cosine[i], sine[i], True)
 
     def products(i, steps):
         mixed = jnp.concatenate([ratio_pieces[i], ratio_pieces[i + 1], ratio_pieces[i + 2]], axis=1)
@@ -782,19 +790,28 @@
     currents, cosine = lax.optimization_barrier((currents, cosine))
     currents = lax.all_to_all(currents, "mesh", 0, 0, tiled=True)
 
-    spectra_new, stokes_rows = call(
-        functools.partial(wave_kernel, capacity, step_pairs, dirs),
+    spectra_new, stokes_rows, halo, halo_tables, edge_change, halo_change = call(
+        functools.partial(wave_kernel, capacity, step_pairs, dirs, layers),
         "wave",
         (
             own_spectra, outer, inner, currents, own_slots, near,
             cosine, sine, project, choice, ways, slot_choice, own_change,
+            fields, neighbors, inside, cell_scale,
         ),
-        (shaped(freqs, stride, LANES), shaped(peers, LANES)),
+        (
+            shaped(freqs, stride, LANES),
+            shaped(peers, LANES),
+            shaped(4, field_rows, LANES),
+            shaped(2, 3, 8, LANES),
+            shaped(2, field_rows, edges * LANES),
+            shaped(2, field_rows, edges * LANES),
+        ),
         [
             pltpu.VMEM((8, LANES), f32),
             pltpu.VMEM((step_rows, LANES), f32),
             pltpu.VMEM((step_rows, edges * LANES), f32),
             pltpu.VMEM((step_rows, edges * LANES), f32),
+            pltpu.VMEM((2, 8, LANES), jnp.int32),
         ],
     )
     stokes_all = lax.all_to_all(stokes_rows, "mesh", 0, 0, tiled=True)
@@ -803,14 +820,11 @@
         functools.partial(tracer_kernel, capacity, (tracer_count, layers, edges)),
         "tracer",
         (
-            outer, inner, stokes_all, fields, neighbors, matrices, inside, cell_cosine, cell_sine,
-            cell_scale, sums, pltpu.with_memory_space_constraint(spectra_new, pltpu.VMEM),
+            halo, halo_tables, edge_change, halo_change, stokes_all, fields, matrices, inside,
+            cell_cosine, cell_sine, sums, pltpu.with_memory_space_constraint(spectra_new, pltpu.VMEM),
         ),
         (like(tracers), like(spectra)),
         [
-            pltpu.VMEM((4, field_rows, LANES), f32),
-            pltpu.VMEM((2, 8, LANES), jnp.int32),
-            pltpu.VMEM((2, 3, 8, LANES), f32),
             pltpu.VMEM((blocks + 2, 8, LANES), f32),
             pltpu.VMEM((blocks, edges, rows, LANES), f32),
             pltpu.VMEM((blocks, rows, LANES), f32),

time: 36.4 us -> 36.6 us (level)
  no operation moved by 1% of the time
where the time goes in v14:
time: 36.6 us; the launch traced here: 36.3 us
  blocking collectives  20.4 us (56%)
  Pallas kernels  10.1 us (28%)
  starting transfers between devices  5.06 us (14%)
  between operations  0.67 us (2%)
    all_to_all x1, blocking collectives, local(): currents = lax.all_to_all(currents, 'mesh', 0, 0, tiled=True)  11.2 us
    all_to_all x1, blocking collectives, local(): stokes_all = lax.all_to_all(stokes_rows, 'mesh', 0, 0, tiled=True)  9.23 us
    pallas_call x3, Pallas kernels, call(): pl.pallas_call(kernel, out_shape=outputs, in_specs=[whole_spec()] * len(i...  8.5 us
    ppermute x2, starting transfers between devices, swap(): return lax.ppermute(message, 'mesh', pairs)  5.06 us
    pallas_call x1, Pallas kernels, local(): pl.pallas_call(pack_kernel, out_shape=(shaped(peers, LANES), shaped(messa...  1.62 us
  transfers between devices with their start and end apart: 2, of which 0 were waited for; matrix products, arithmetic and copies ran while one was open for 0% of the time, Pallas kernels for 9%

profile of v14, /device:TPU:0, one launch (start us, length us, event | category | flops | bytes accessed | tf_op | source)
XLA Modules:
  0.0 36.3 jit_solution(11145153259922110112)
XLA Ops:
  0.6 1.6 %pack.1 = (f32[16,128]{1,0:T(8,128)S(1)}, f32[1024,128]{1,0:T(8,128)S(1)}, f32[1024,128]{1,0:T(8,128)S(1)}, f32[50,40,128]{2,1,0:T(8,128)S(1)}, s32[1,128]{1,0:T...) custom-call(f32[50,36,128]{2,1,0:T(8,128)} %spectra_in.1, ...), custom_call_target="tpu_custom_call" | custom-call | tf_op jit(solution)/shard_map/pack/pallas_call | solution.py:731
  2.3 0.7 %collective-permute-start = (f32[1024,128]{1,0:T(8,128)S(1)}, f32[1024,128]{1,0:T(8,128)S(1)}, u32[]{:S(2)}, u32[]{:S(2)}) collective-permute-start(f32[1024,128]{1,0:T(8,128)S(1)} %get-tuple-element.40), channel_id=1, source_target_pairs={{1,2},{2,1},{3,4},{4,3},{5,6},{6,5},{7,8},{8,7},{9,10},{10,9},{11,... | collective-permute-start | bytes 1572872 | tf_op jit(solution)/shard_map/ppermute | solution.py:667
  3.0 4.4 %collective-permute-start.1 = (f32[1024,128]{1,0:T(8,128)S(1)}, f32[1024,128]{1,0:T(8,128)S(1)}, u32[]{:S(2)}, u32[]{:S(2)}) collective-permute-start(f32[1024,128]{1,0:T(8,128)S(1)} %get-tuple-element.41), channel_id=1, source_target_pairs={{0,1},{1,0},{2,3},{3,2},{4,5},{5,4},{6,7},{7,6},{8,9},{9,8},{10,11... | collective-permute-start | bytes 1572872 | tf_op jit(solution)/shard_map/ppermute | solution.py:667
  7.3 3.4 %prepare.1 = (f32[6,128]{1,0:T(8,128)S(1)}, f32[6,128]{1,0:T(8,128)S(1)}, f32[6,40,128]{2,1,0:T(8,128)S(1)}, bf16[512,768]{1,0:T(8,128)(2,1)S(1)}, f32[3,40,128]...) custom-call(f32[50,40,128]{2,1,0:T(8,128)S(1)} %get-tuple-element.39, ...), custom_call_target="tpu_custom_call" | custom-call | tf_op jit(solution)/shard_map/prepare/pallas_call | solution.py:714
  10.7 11.2 %all_to_all.22 = f32[16,1,128]{2,1,0:T(1,128)S(1)} all-to-all(f32[16,1,128]{2,1,0:T(1,128)S(1)} %bitcast.11), channel_id=1, replica_groups=mesh['groups'=2,'mesh'=16] {'mesh'}, dimensions={0} | all-to-all | bytes 16384 | tf_op jit(solution)/shard_map/all_to_all | solution.py:791
  21.9 0.0 collective-permute-done.outer
  21.9 0.0 collective-permute-done.1.inner
  21.9 2.8 %wave.1 = (f32[50,40,128]{2,1,0:T(8,128)S(1)}, f32[16,128]{1,0:T(8,128)S(1)}, f32[4,48,128]{2,1,0:T(8,128)S(1)}, f32[2,3,8,128]{3,2,1,0:T(8,128)S(1)}, f32[2,48,...) custom-call(f32[50,40,128]{2,1,0:T(8,128)S(1)} %get-tuple-element.39.spectra, f32[1024,128]{1,0:T(8,128)S(1)} %collective-permute-done.outer, ...), custom_call_target="tpu_custom_call" | custom-call | tf_op jit(solution)/shard_map/wave/pallas_call | solution.py:714
  24.7 9.2 %all_to_all.23 = f32[16,1,128]{2,1,0:T(1,128)S(1)} all-to-all(f32[16,1,128]{2,1,0:T(1,128)S(1)} %bitcast.12), channel_id=1, replica_groups=mesh['groups'=2,'mesh'=16] {'mesh'}, dimensions={0} | all-to-all | bytes 16384 | tf_op jit(solution)/shard_map/all_to_all | solution.py:817
  34.0 2.3 %tracer.1 = (f32[2,16,1024]{2,1,0:T(8,128)}, f32[50,36,128]{2,1,0:T(8,128)}) custom-call(f32[4,48,128]{2,1,0:T(8,128)S(1)} %get-tuple-element.66.halo, f32[2,3,8,128]{3,2,1,0:T(8,128)S(1)} %get-tuple-element.67.halo_tables, f32[2,48,768]{2,1,0:T(8,128)S(1)} %get-tuple-element.68.edge_change, f32[2,48,768]{2,1,0:T(8,128)S(1)} %get-tuple-element.69.halo_change, ...), custom_call_target="tpu_custom_call" | custom-call | tf_op jit(solution)/shard_map/tracer/pallas_call | solution.py:714
Async XLA Ops:
  2.3 19.7 %collective-permute-start = (f32[1024,128]{1,0:T(8,128)S(1)}, f32[1024,128]{1,0:T(8,128)S(1)}, u32[]{:S(2)}, u32[]{:S(2)}) collective-permute-start(f32[1024,128]{1,0:T(8,128)S(1)} %get-tuple-element.40), channel_id=1, source_target_pairs={{1,2},{2,1},{3,4},{4,3},{5,6},{6,5},{7,8},{8,7},{9,10},{10,9},{11,... | collective-permute-start | bytes 1572872 | tf_op jit(solution)/shard_map/ppermute | solution.py:667
  3.0 19.0 %collective-permute-start.1 = (f32[1024,128]{1,0:T(8,128)S(1)}, f32[1024,128]{1,0:T(8,128)S(1)}, u32[]{:S(2)}, u32[]{:S(2)}) collective-permute-start(f32[1024,128]{1,0:T(8,128)S(1)} %get-tuple-element.41), channel_id=1, source_target_pairs={{0,1},{1,0},{2,3},{3,2},{4,5},{5,4},{6,7},{7,6},{8,9},{9,8},{10,11... | collective-permute-start | bytes 1572872 | tf_op jit(solution)/shard_map/ppermute | solution.py:667

commit v15 on v14

--- a/solution.py
+++ b/solution.py
@@ -614,15 +614,17 @@
     def column(ref, index):
         return lambda row, s: ref[index, row : row + 8, s * LANES : (s + 1) * LANES]
 
-    for side in range(2):
-        b = side * (blocks + 1)
-        normals = (halo_tables[side, 1], halo_tables[side, 2])
-        low_order(b, band(halo, 1 + side), column(halo_change, side), *normals, False)
-    for i in range(blocks):
-        change = column(inside, i)
-        if i in (0, blocks - 1):
-            change = column(edge_change, min(i, 1))
-        low_order(i + 1, band(fields, i), change, cosine[i], sine[i], True)
+    def ratios_of(b):
+        if b in (0, blocks + 1):
+            side = min(b, 1)
+            normals = (halo_tables[side, 1], halo_tables[side, 2])
+            low_order(b, band(halo, 1 + side), column(halo_change, side), *normals, False)
+        else:
+            i = b - 1
+            change = column(inside, i)
+            if i in (0, blocks - 1):
+                change = column(edge_change, min(i, 1))
+            low_order(b, band(fields, i), change, cosine[i], sine[i], True)
 
     def products(i, steps):
         mixed = jnp.concatenate([ratio_pieces[i], ratio_pieces[i + 1], ratio_pieces[i + 2]], axis=1)
@@ -652,11 +654,15 @@
             tracers_new[t, 8 * lg : 8 * lg + 8, lanes] = out[g]
 
     buffers = (steps_a, steps_b)
-    products(0, steps_a)
+    for b in range(3):
+        ratios_of(b)
     for i in range(blocks):
-        if i + 1 < blocks:
-            products(i + 1, buffers[(i + 1) % 2])
-        limit(i, buffers[i % 2])
+        products(i, buffers[i % 2])
+        if i + 3 < blocks + 2:
+            ratios_of(i + 3)
+        if i > 0:
+            limit(i - 1, buffers[(i - 1) % 2])
+    limit(blocks - 1, buffers[(blocks - 1) % 2])
     write.wait()
 
 

time: 36.6 us -> 36.6 us (level)
  no operation moved by 1% of the time
where the time goes in v15:
time: 36.6 us; the launch traced here: 36.3 us
  blocking collectives  20.4 us (56%)
  Pallas kernels  10.1 us (28%)
  starting transfers between devices  5.06 us (14%)
  between operations  0.67 us (2%)
    all_to_all x1, blocking collectives, local(): currents = lax.all_to_all(currents, 'mesh', 0, 0, tiled=True)  11.2 us
    all_to_all x1, blocking collectives, local(): stokes_all = lax.all_to_all(stokes_rows, 'mesh', 0, 0, tiled=True)  9.23 us
    pallas_call x3, Pallas kernels, call(): pl.pallas_call(kernel, out_shape=outputs, in_specs=[whole_spec()] * len(i...  8.5 us
    ppermute x2, starting transfers between devices, swap(): return lax.ppermute(message, 'mesh', pairs)  5.06 us
    pallas_call x1, Pallas kernels, local(): pl.pallas_call(pack_kernel, out_shape=(shaped(peers, LANES), shaped(messa...  1.62 us
  transfers between devices with their start and end apart: 2, of which 0 were waited for; matrix products, arithmetic and copies ran while one was open for 0% of the time, Pallas kernels for 9%

profile of v15, /device:TPU:0, one launch (start us, length us, event | category | flops | bytes accessed | tf_op | source)
XLA Modules:
  0.0 36.3 jit_solution(11145153259922110112)
XLA Ops:
  0.6 1.6 %pack.1 = (f32[16,128]{1,0:T(8,128)S(1)}, f32[1024,128]{1,0:T(8,128)S(1)}, f32[1024,128]{1,0:T(8,128)S(1)}, f32[50,40,128]{2,1,0:T(8,128)S(1)}, s32[1,128]{1,0:T...) custom-call(f32[50,36,128]{2,1,0:T(8,128)} %spectra_in.1, ...), custom_call_target="tpu_custom_call" | custom-call | tf_op jit(solution)/shard_map/pack/pallas_call | solution.py:737
  2.3 0.7 %collective-permute-start = (f32[1024,128]{1,0:T(8,128)S(1)}, f32[1024,128]{1,0:T(8,128)S(1)}, u32[]{:S(2)}, u32[]{:S(2)}) collective-permute-start(f32[1024,128]{1,0:T(8,128)S(1)} %get-tuple-element.40), channel_id=1, source_target_pairs={{1,2},{2,1},{3,4},{4,3},{5,6},{6,5},{7,8},{8,7},{9,10},{10,9},{11,... | collective-permute-start | bytes 1572872 | tf_op jit(solution)/shard_map/ppermute | solution.py:673
  3.0 4.4 %collective-permute-start.1 = (f32[1024,128]{1,0:T(8,128)S(1)}, f32[1024,128]{1,0:T(8,128)S(1)}, u32[]{:S(2)}, u32[]{:S(2)}) collective-permute-start(f32[1024,128]{1,0:T(8,128)S(1)} %get-tuple-element.41), channel_id=1, source_target_pairs={{0,1},{1,0},{2,3},{3,2},{4,5},{5,4},{6,7},{7,6},{8,9},{9,8},{10,11... | collective-permute-start | bytes 1572872 | tf_op jit(solution)/shard_map/ppermute | solution.py:673
  7.3 3.4 %prepare.1 = (f32[6,128]{1,0:T(8,128)S(1)}, f32[6,128]{1,0:T(8,128)S(1)}, f32[6,40,128]{2,1,0:T(8,128)S(1)}, bf16[512,768]{1,0:T(8,128)(2,1)S(1)}, f32[3,40,128]...) custom-call(f32[50,40,128]{2,1,0:T(8,128)S(1)} %get-tuple-element.39, ...), custom_call_target="tpu_custom_call" | custom-call | tf_op jit(solution)/shard_map/prepare/pallas_call | solution.py:720
  10.7 11.2 %all_to_all.22 = f32[16,1,128]{2,1,0:T(1,128)S(1)} all-to-all(f32[16,1,128]{2,1,0:T(1,128)S(1)} %bitcast.11), channel_id=1, replica_groups=mesh['groups'=2,'mesh'=16] {'mesh'}, dimensions={0} | all-to-all | bytes 16384 | tf_op jit(solution)/shard_map/all_to_all | solution.py:797
  21.9 0.0 collective-permute-done.outer
  21.9 0.0 collective-permute-done.1.inner
  21.9 2.8 %wave.1 = (f32[50,40,128]{2,1,0:T(8,128)S(1)}, f32[16,128]{1,0:T(8,128)S(1)}, f32[4,48,128]{2,1,0:T(8,128)S(1)}, f32[2,3,8,128]{3,2,1,0:T(8,128)S(1)}, f32[2,48,...) custom-call(f32[50,40,128]{2,1,0:T(8,128)S(1)} %get-tuple-element.39.spectra, f32[1024,128]{1,0:T(8,128)S(1)} %collective-permute-done.outer, ...), custom_call_target="tpu_custom_call" | custom-call | tf_op jit(solution)/shard_map/wave/pallas_call | solution.py:720
  24.7 9.2 %all_to_all.23 = f32[16,1,128]{2,1,0:T(1,128)S(1)} all-to-all(f32[16,1,128]{2,1,0:T(1,128)S(1)} %bitcast.12), channel_id=1, replica_groups=mesh['groups'=2,'mesh'=16] {'mesh'}, dimensions={0} | all-to-all | bytes 16384 | tf_op jit(solution)/shard_map/all_to_all | solution.py:823
  34.0 2.3 %tracer.1 = (f32[2,16,1024]{2,1,0:T(8,128)}, f32[50,36,128]{2,1,0:T(8,128)}) custom-call(f32[4,48,128]{2,1,0:T(8,128)S(1)} %get-tuple-element.66.halo, f32[2,3,8,128]{3,2,1,0:T(8,128)S(1)} %get-tuple-element.67.halo_tables, f32[2,48,768]{2,1,0:T(8,128)S(1)} %get-tuple-element.68.edge_change, f32[2,48,768]{2,1,0:T(8,128)S(1)} %get-tuple-element.69.halo_change, ...), custom_call_target="tpu_custom_call" | custom-call | tf_op jit(solution)/shard_map/tracer/pallas_call | solution.py:720
Async XLA Ops:
  2.3 19.7 %collective-permute-start = (f32[1024,128]{1,0:T(8,128)S(1)}, f32[1024,128]{1,0:T(8,128)S(1)}, u32[]{:S(2)}, u32[]{:S(2)}) collective-permute-start(f32[1024,128]{1,0:T(8,128)S(1)} %get-tuple-element.40), channel_id=1, source_target_pairs={{1,2},{2,1},{3,4},{4,3},{5,6},{6,5},{7,8},{8,7},{9,10},{10,9},{11,... | collective-permute-start | bytes 1572872 | tf_op jit(solution)/shard_map/ppermute | solution.py:673
  3.0 19.0 %collective-permute-start.1 = (f32[1024,128]{1,0:T(8,128)S(1)}, f32[1024,128]{1,0:T(8,128)S(1)}, u32[]{:S(2)}, u32[]{:S(2)}) collective-permute-start(f32[1024,128]{1,0:T(8,128)S(1)} %get-tuple-element.41), channel_id=1, source_target_pairs={{0,1},{1,0},{2,3},{3,2},{4,5},{5,4},{6,7},{7,6},{8,9},{9,8},{10,11... | collective-permute-start | bytes 1572872 | tf_op jit(solution)/shard_map/ppermute | solution.py:673

commit v16 on v15

--- a/solution.py
+++ b/solution.py
@@ -526,7 +526,7 @@
     sums, spectra,
     tracers_new, spectra_out,
     stokes, antiflux, lowered, ratios,
-    ratio_pieces, steps_a, steps_b, sem,
+    ratio_pieces, changes, sem,
 ):
     dirs = spectra_out.shape[1]
     write = pltpu.make_async_copy(spectra.at[:, 0:dirs, :], spectra_out, sem)
@@ -626,11 +626,12 @@
                 change = column(edge_change, min(i, 1))
             low_order(b, band(fields, i), change, cosine[i], sine[i], True)
 
-    def products(i, steps):
+    def products(i):
         mixed = jnp.concatenate([ratio_pieces[i], ratio_pieces[i + 1], ratio_pieces[i + 2]], axis=1)
-        steps[...] = jnp.dot(mixed, matrices[i], preferred_element_type=jnp.float32)
-
-    def limit(i, steps):
+        changes[i % 2] = jnp.dot(mixed, matrices[i], preferred_element_type=jnp.float32)
+
+    def limit(i):
+        steps = changes.at[i % 2]
         out = [lowered[i, 8 * g : 8 * g + 8, :] for g in range(tracer_groups)]
         own = [ratios[i + 1, 8 * g : 8 * g + 8, :] for g in range(2 * tracer_groups)]
         low = 16 * tracer_groups
@@ -648,21 +649,22 @@
                     flux >= 0.0, jnp.minimum(own[m], beside[g]), jnp.minimum(own[g], beside[m])
                 )
                 out[g] = out[g] - factor * flux
-        lanes = slice(i * LANES, (i + 1) * LANES)
+        lanes = pl.ds(pl.multiple_of(i * LANES, LANES), LANES)
         for g in range(tracer_groups):
             t, lg = g // layer_groups, g % layer_groups
             tracers_new[t, 8 * lg : 8 * lg + 8, lanes] = out[g]
 
-    buffers = (steps_a, steps_b)
-    for b in range(3):
+    for b in range(blocks + 2):
         ratios_of(b)
-    for i in range(blocks):
-        products(i, buffers[i % 2])
-        if i + 3 < blocks + 2:
-            ratios_of(i + 3)
-        if i > 0:
-            limit(i - 1, buffers[(i - 1) % 2])
-    limit(blocks - 1, buffers[(blocks - 1) % 2])
+    products(0)
+
+    def next_block(i, carry):
+        products(i + 1)
+        limit(i)
+        return carry
+
+    lax.fori_loop(0, blocks - 1, next_block, 0)
+    limit(jnp.int32(blocks - 1))
     write.wait()
 
 
@@ -836,8 +838,7 @@
             pltpu.VMEM((blocks, rows, LANES), f32),
             pltpu.VMEM((blocks + 2, 2 * rows, LANES), f32),
             pltpu.VMEM((blocks + 2, 4 * rows, LANES), jnp.bfloat16),
-            pltpu.VMEM((4 * rows, edges * LANES), f32),
-            pltpu.VMEM((4 * rows, edges * LANES), f32),
+            pltpu.VMEM((2, 4 * rows, edges * LANES), f32),
             pltpu.SemaphoreType.DMA(()),
         ],
         out_specs=(whole_spec(), stored),

time: 36.6 us -> 38.2 us (1.044)
  Pallas kernels: 10.1 us -> 11.8 us
    pallas_call x3, Pallas kernels: 8.5 us -> 10.2 us  [call(): pl.pallas_call(kernel, out_shape=outputs, in_specs=[whole_spec()] * len(i...]
where the time goes in v16:
time: 38.2 us; the launch traced here: 37.9 us
  blocking collectives  20.4 us (53%)
  Pallas kernels  11.8 us (31%)
  starting transfers between devices  5.06 us (13%)
  between operations  0.67 us (2%)
    all_to_all x1, blocking collectives, local(): currents = lax.all_to_all(currents, 'mesh', 0, 0, tiled=True)  11.2 us
    pallas_call x3, Pallas kernels, call(): pl.pallas_call(kernel, out_shape=outputs, in_specs=[whole_spec()] * len(i...  10.2 us
    all_to_all x1, blocking collectives, local(): stokes_all = lax.all_to_all(stokes_rows, 'mesh', 0, 0, tiled=True)  9.23 us
    ppermute x2, starting transfers between devices, swap(): return lax.ppermute(message, 'mesh', pairs)  5.06 us
    pallas_call x1, Pallas kernels, local(): pl.pallas_call(pack_kernel, out_shape=(shaped(peers, LANES), shaped(messa...  1.62 us
  transfers between devices with their start and end apart: 2, of which 0 were waited for; matrix products, arithmetic and copies ran while one was open for 0% of the time, Pallas kernels for 9%

profile of v16, /device:TPU:0, one launch (start us, length us, event | category | flops | bytes accessed | tf_op | source)
XLA Modules:
  0.0 37.9 jit_solution(6807568740286757534)
XLA Ops:
  0.6 1.6 %pack.1 = (f32[16,128]{1,0:T(8,128)S(1)}, f32[1024,128]{1,0:T(8,128)S(1)}, f32[1024,128]{1,0:T(8,128)S(1)}, f32[50,40,128]{2,1,0:T(8,128)S(1)}, s32[1,128]{1,0:T...) custom-call(f32[50,36,128]{2,1,0:T(8,128)} %spectra_in.1, ...), custom_call_target="tpu_custom_call" | custom-call | tf_op jit(solution)/shard_map/pack/pallas_call | solution.py:739
  2.3 0.7 %collective-permute-start = (f32[1024,128]{1,0:T(8,128)S(1)}, f32[1024,128]{1,0:T(8,128)S(1)}, u32[]{:S(2)}, u32[]{:S(2)}) collective-permute-start(f32[1024,128]{1,0:T(8,128)S(1)} %get-tuple-element.40), channel_id=1, source_target_pairs={{1,2},{2,1},{3,4},{4,3},{5,6},{6,5},{7,8},{8,7},{9,10},{10,9},{11,... | collective-permute-start | bytes 1572872 | tf_op jit(solution)/shard_map/ppermute | solution.py:675
  3.0 4.4 %collective-permute-start.1 = (f32[1024,128]{1,0:T(8,128)S(1)}, f32[1024,128]{1,0:T(8,128)S(1)}, u32[]{:S(2)}, u32[]{:S(2)}) collective-permute-start(f32[1024,128]{1,0:T(8,128)S(1)} %get-tuple-element.41), channel_id=1, source_target_pairs={{0,1},{1,0},{2,3},{3,2},{4,5},{5,4},{6,7},{7,6},{8,9},{9,8},{10,11... | collective-permute-start | bytes 1572872 | tf_op jit(solution)/shard_map/ppermute | solution.py:675
  7.3 3.4 %prepare.1 = (f32[6,128]{1,0:T(8,128)S(1)}, f32[6,128]{1,0:T(8,128)S(1)}, f32[6,40,128]{2,1,0:T(8,128)S(1)}, bf16[512,768]{1,0:T(8,128)(2,1)S(1)}, f32[3,40,128]...) custom-call(f32[50,40,128]{2,1,0:T(8,128)S(1)} %get-tuple-element.39, ...), custom_call_target="tpu_custom_call" | custom-call | tf_op jit(solution)/shard_map/prepare/pallas_call | solution.py:722
  10.7 11.2 %all_to_all.22 = f32[16,1,128]{2,1,0:T(1,128)S(1)} all-to-all(f32[16,1,128]{2,1,0:T(1,128)S(1)} %bitcast.11), channel_id=1, replica_groups=mesh['groups'=2,'mesh'=16] {'mesh'}, dimensions={0} | all-to-all | bytes 16384 | tf_op jit(solution)/shard_map/all_to_all | solution.py:799
  21.9 0.0 collective-permute-done.outer
  21.9 0.0 collective-permute-done.1.inner
  21.9 2.8 %wave.1 = (f32[50,40,128]{2,1,0:T(8,128)S(1)}, f32[16,128]{1,0:T(8,128)S(1)}, f32[4,48,128]{2,1,0:T(8,128)S(1)}, f32[2,3,8,128]{3,2,1,0:T(8,128)S(1)}, f32[2,48,...) custom-call(f32[50,40,128]{2,1,0:T(8,128)S(1)} %get-tuple-element.39.spectra, f32[1024,128]{1,0:T(8,128)S(1)} %collective-permute-done.outer, ...), custom_call_target="tpu_custom_call" | custom-call | tf_op jit(solution)/shard_map/wave/pallas_call | solution.py:722
  24.7 9.2 %all_to_all.23 = f32[16,1,128]{2,1,0:T(1,128)S(1)} all-to-all(f32[16,1,128]{2,1,0:T(1,128)S(1)} %bitcast.12), channel_id=1, replica_groups=mesh['groups'=2,'mesh'=16] {'mesh'}, dimensions={0} | all-to-all | bytes 16384 | tf_op jit(solution)/shard_map/all_to_all | solution.py:825
  34.0 4.0 %tracer.1 = (f32[2,16,1024]{2,1,0:T(8,128)}, f32[50,36,128]{2,1,0:T(8,128)}) custom-call(f32[4,48,128]{2,1,0:T(8,128)S(1)} %get-tuple-element.66.halo, f32[2,3,8,128]{3,2,1,0:T(8,128)S(1)} %get-tuple-element.67.halo_tables, f32[2,48,768]{2,1,0:T(8,128)S(1)} %get-tuple-element.68.edge_change, f32[2,48,768]{2,1,0:T(8,128)S(1)} %get-tuple-element.69.halo_change, ...), custom_call_target="tpu_custom_call" | custom-call | tf_op jit(solution)/shard_map/tracer/pallas_call | solution.py:722
Async XLA Ops:
  2.3 19.7 %collective-permute-start = (f32[1024,128]{1,0:T(8,128)S(1)}, f32[1024,128]{1,0:T(8,128)S(1)}, u32[]{:S(2)}, u32[]{:S(2)}) collective-permute-start(f32[1024,128]{1,0:T(8,128)S(1)} %get-tuple-element.40), channel_id=1, source_target_pairs={{1,2},{2,1},{3,4},{4,3},{5,6},{6,5},{7,8},{8,7},{9,10},{10,9},{11,... | collective-permute-start | bytes 1572872 | tf_op jit(solution)/shard_map/ppermute | solution.py:675
  3.0 19.0 %collective-permute-start.1 = (f32[1024,128]{1,0:T(8,128)S(1)}, f32[1024,128]{1,0:T(8,128)S(1)}, u32[]{:S(2)}, u32[]{:S(2)}) collective-permute-start(f32[1024,128]{1,0:T(8,128)S(1)} %get-tuple-element.41), channel_id=1, source_target_pairs={{0,1},{1,0},{2,3},{3,2},{4,5},{5,4},{6,7},{7,6},{8,9},{9,8},{10,11... | collective-permute-start | bytes 1572872 | tf_op jit(solution)/shard_map/ppermute | solution.py:675

commit v17 on v12

--- a/solution.py
+++ b/solution.py
@@ -68,9 +68,10 @@
 
 
 def node_tables(
-    me, dirs, near, angle, face, wind, slot, cosine, sine, project, choice, ways, slots
+    me, dirs, capacity, near, angle, face, wind, slot, cosine, sine, project, choice, ways, slots
 ):
     edges, padded = project.shape[:2]
+    peers = slots.shape[0]
     cosine[...] = face[...] * jnp.cos(angle[...])
     sine[...] = face[...] * jnp.sin(angle[...])
     cos_dir, sin_dir = direction(dirs, padded)
@@ -78,10 +79,12 @@
     ways[1] = sin_dir
     ways[2] = 0.25 * jnp.maximum(wind[0:1, :] * cos_dir + wind[1:2, :] * sin_dir, 0.0)
     taken = jnp.transpose(spread(slot[...].astype(jnp.float32), LANES))
-    for half in range(slots.shape[1] // LANES):
+    node = (row_iota(LANES) + 1).astype(jnp.float32)
+    holders = []
+    for half in range(peers * capacity // LANES):
         number = (lane_iota(LANES) + half * LANES).astype(jnp.float32)
-        picked = jnp.where(taken == number, 1.0, 0.0).astype(jnp.bfloat16)
-        slots[:, half * LANES : (half + 1) * LANES] = picked
+        holders.append(jnp.sum(jnp.where(taken == number, node, 0.0), axis=0, keepdims=True))
+    slots[...] = peer_rows([holders, holders], peers, capacity).astype(jnp.int32)
     source = row_iota(LANES)
     minus = jnp.where(source == lane_iota(LANES), -1.0, 0.0)
     for s in range(edges):
@@ -236,7 +239,8 @@
 ):
     me = lax.axis_index("mesh")
     node_tables(
-        me, dirs, near, angle, face, wind, slot, cosine, sine, project, choice, ways, slots
+        me, dirs, coupled.shape[2], near, angle, face, wind, slot, cosine, sine, project, choice,
+        ways, slots,
     )
     freqs, padded, _ = spectra.shape
     step = step_rows // padded
@@ -316,7 +320,6 @@
     freqs, stride = spectra.shape[:2]
     edges = neighbors.shape[0]
     peers = table.shape[0]
-    halves = peers * capacity // LANES
     pairs = freqs // 2
     whole = dirs // 8 * 8
     rest = dirs - whole
@@ -417,45 +420,27 @@
     cos_dir, sin_dir = ways[0], ways[1]
     mean = jnp.sum(total, axis=0, keepdims=True) * (1.0 / (freqs * dirs))
     step = jnp.exp((ways[2] - 2.0 * mean) * (1.0 / freqs))
-    run = 10 if freqs % 10 == 0 else 1
-
-    def grow(c, carry):
-        factor, weighted = carry
-        for i in range(run):
-            f = c * run + i
-            factor = factor * step
-            evolved = spectra_new[f] * factor
-            spectra_new[f] = evolved
-            kappa = (f + 1).astype(jnp.float32) * (1.0 / freqs)
-            weighted = weighted + kappa * evolved
-        return factor, weighted
-
-    _, weighted = lax.fori_loop(0, freqs // run, grow, (zero + 1.0, zero))
-    stokes = jnp.concatenate(
-        [
-            jnp.sum(weighted * cos_dir, axis=0, keepdims=True),
-            jnp.sum(weighted * sin_dir, axis=0, keepdims=True),
-        ],
-        axis=0,
-    ) * (1.0 / dirs)
-    in_order = jnp.dot(
-        three_parts(stokes), slots[...], preferred_element_type=jnp.float32
-    )
-    in_order = in_order[0:2] + (in_order[2:4] + in_order[4:6])
-    values = [
-        [in_order[part : part + 1, h * LANES : (h + 1) * LANES] for h in range(halves)]
-        for part in range(2)
-    ]
-    rows_out[...] = peer_rows(values, peers, capacity)
-
-
-def three_parts(values):
+    factor = zero + 1.0
+    weighted = zero
+    for f in range(freqs):
+        factor = factor * step
+        evolved = spectra_new[f] * factor
+        spectra_new[f] = evolved
+        weighted = weighted + ((f + 1) / (freqs * dirs)) * evolved
+    drift_x = jnp.sum(weighted * cos_dir, axis=0, keepdims=True)
+    drift_y = jnp.sum(weighted * sin_dir, axis=0, keepdims=True)
+    node = slots[...] - 1
+    pick = jnp.maximum(node, 0)
+    first = lane_gather(spread(drift_x, peers), pick)
+    second = lane_gather(spread(drift_y, peers), pick)
+    part = lane_iota(peers) // capacity % 2
+    rows_out[...] = jnp.where(node < 0, 0.0, jnp.where(part == 0, first, second))
+
+
+def two_parts(values):
     first = values.astype(jnp.bfloat16).astype(jnp.float32)
-    left = values - first
-    second = left.astype(jnp.bfloat16).astype(jnp.float32)
-    third = left - second
-    pad = jnp.zeros((10, values.shape[1]), jnp.float32)
-    return jnp.concatenate([first, second, third, pad], axis=0).astype(jnp.bfloat16)
+    pad = jnp.zeros((4, values.shape[1]), jnp.float32)
+    return jnp.concatenate([first, values - first, pad], axis=0)
 
 
 def tracer_kernel(
@@ -505,16 +490,18 @@
                 mine = row_iota(peers) == (lane_of + half * LANES) // capacity
                 row.append(jnp.sum(jnp.where(mine, found, 0.0), axis=0, keepdims=True))
             values.append(jnp.concatenate(row, axis=1))
-        sections.append(three_parts(jnp.concatenate(values, axis=0)))
+        sections.append(two_parts(jnp.concatenate(values, axis=0)))
+    sections.append(jnp.zeros_like(sections[0]))
     total = jnp.dot(
-        jnp.concatenate(sections, axis=0), sums[...], preferred_element_type=jnp.float32
+        jnp.concatenate(sections, axis=0).astype(jnp.bfloat16),
+        sums[...],
+        preferred_element_type=jnp.float32,
     )
     for b in range(blocks + 2):
         which = 0 if b == 0 else 2 if b == blocks + 1 else 1
-        at = 16 * which
+        at = 8 * which
         lanes = slice(b * LANES, (b + 1) * LANES)
-        first, second, third = (total[at + k : at + k + 2, lanes] for k in (0, 2, 4))
-        stokes[b, 0:2, :] = first + (second + third)
+        stokes[b, 0:2, :] = total[at : at + 2, lanes] + total[at + 2 : at + 4, lanes]
 
     decay = [
         jnp.exp(-3.0 / layers * (row_iota(8) + 8 * g).astype(jnp.float32))
@@ -767,7 +754,7 @@
             shaped(edges, stride, LANES),
             shaped(4 * LANES, edges * LANES, dtype=jnp.bfloat16),
             shaped(3, stride, LANES),
-            shaped(nodes, peers * capacity, dtype=jnp.bfloat16),
+            shaped(peers, LANES, dtype=jnp.int32),
             shaped(freqs * stride, edges * LANES),
             shaped(blocks, field_rows, LANES),
             shaped(blocks, 3 * LANES, edges * LANES, dtype=jnp.bfloat16),

time: 36.4 us -> 36.6 us (level)
  transfers between devices with their start and end apart: 2 -> 2, of which waited for: 0 -> 0; matrix products, arithmetic and copies ran while one was open for 0% -> 0% of each run, Pallas kernels for 9% -> 10%
where the time goes in v17:
time: 36.6 us; the launch traced here: 36.3 us
  blocking collectives  20.3 us (55%)
  Pallas kernels  10.3 us (28%)
  starting transfers between devices  5.06 us (14%)
  between operations  0.66 us (2%)
    all_to_all x1, blocking collectives, local(): currents = lax.all_to_all(currents, 'mesh', 0, 0, tiled=True)  11.2 us
    all_to_all x1, blocking collectives, local(): stokes_all = lax.all_to_all(stokes_rows, 'mesh', 0, 0, tiled=True)  9.13 us
    pallas_call x3, Pallas kernels, call(): pl.pallas_call(kernel, out_shape=outputs, in_specs=[whole_spec()] * len(i...  8.69 us
    ppermute x2, starting transfers between devices, swap(): return lax.ppermute(message, 'mesh', pairs)  5.06 us
    pallas_call x1, Pallas kernels, local(): pl.pallas_call(pack_kernel, out_shape=(shaped(peers, LANES), shaped(messa...  1.62 us
  transfers between devices with their start and end apart: 2, of which 0 were waited for; matrix products, arithmetic and copies ran while one was open for 0% of the time, Pallas kernels for 10%

profile of v17, /device:TPU:0, one launch (start us, length us, event | category | flops | bytes accessed | tf_op | source)
XLA Modules:
  0.0 36.3 jit_solution(6404356351135190631)
XLA Ops:
  0.6 1.6 %pack.1 = (f32[16,128]{1,0:T(8,128)S(1)}, f32[1024,128]{1,0:T(8,128)S(1)}, f32[1024,128]{1,0:T(8,128)S(1)}, f32[50,40,128]{2,1,0:T(8,128)S(1)}, s32[1,128]{1,0:T...) custom-call(f32[50,36,128]{2,1,0:T(8,128)} %spectra_in.1, ...), custom_call_target="tpu_custom_call" | custom-call | tf_op jit(solution)/shard_map/pack/pallas_call | solution.py:710
  2.3 0.7 %collective-permute-start = (f32[1024,128]{1,0:T(8,128)S(1)}, f32[1024,128]{1,0:T(8,128)S(1)}, u32[]{:S(2)}, u32[]{:S(2)}) collective-permute-start(f32[1024,128]{1,0:T(8,128)S(1)} %get-tuple-element.35), channel_id=1, source_target_pairs={{1,2},{2,1},{3,4},{4,3},{5,6},{6,5},{7,8},{8,7},{9,10},{10,9},{11,... | collective-permute-start | bytes 1572872 | tf_op jit(solution)/shard_map/ppermute | solution.py:646
  3.0 4.4 %collective-permute-start.1 = (f32[1024,128]{1,0:T(8,128)S(1)}, f32[1024,128]{1,0:T(8,128)S(1)}, u32[]{:S(2)}, u32[]{:S(2)}) collective-permute-start(f32[1024,128]{1,0:T(8,128)S(1)} %get-tuple-element.36), channel_id=1, source_target_pairs={{0,1},{1,0},{2,3},{3,2},{4,5},{5,4},{6,7},{7,6},{8,9},{9,8},{10,11... | collective-permute-start | bytes 1572872 | tf_op jit(solution)/shard_map/ppermute | solution.py:646
  7.3 3.5 %prepare.1 = (f32[6,128]{1,0:T(8,128)S(1)}, f32[6,128]{1,0:T(8,128)S(1)}, f32[6,40,128]{2,1,0:T(8,128)S(1)}, bf16[512,768]{1,0:T(8,128)(2,1)S(1)}, f32[3,40,128]...) custom-call(f32[50,40,128]{2,1,0:T(8,128)S(1)} %get-tuple-element.37, ...), custom_call_target="tpu_custom_call" | custom-call | tf_op jit(solution)/shard_map/prepare/pallas_call | solution.py:693
  10.8 11.2 %all_to_all.22 = f32[16,1,128]{2,1,0:T(1,128)S(1)} all-to-all(f32[16,1,128]{2,1,0:T(1,128)S(1)} %bitcast.11), channel_id=1, replica_groups=mesh['groups'=2,'mesh'=16] {'mesh'}, dimensions={0} | all-to-all | bytes 16384 | tf_op jit(solution)/shard_map/all_to_all | solution.py:770
  22.0 0.0 collective-permute-done.outer
  22.0 0.0 collective-permute-done.1.inner
  22.0 2.6 %wave.1 = (f32[50,40,128]{2,1,0:T(8,128)S(1)}, f32[16,128]{1,0:T(8,128)S(1)}) custom-call(f32[50,40,128]{2,1,0:T(8,128)S(1)} %get-tuple-element.37.spectra, f32[1024,128]{1,0:T(8,128)S(1)} %collective-permute-done.outer, f32[1024,128]{1,0:T(8,128)S(1)} %collective-permute-done.1.inner, f32[16,128]{1,0:T(8,128)S(1)} %bitcast.9, ...), custom_call_target="tpu_custom_call" | custom-call | tf_op jit(solution)/shard_map/wave/pallas_call | solution.py:693
  24.6 9.1 %all_to_all.23 = f32[16,1,128]{2,1,0:T(1,128)S(1)} all-to-all(f32[16,1,128]{2,1,0:T(1,128)S(1)} %bitcast.12), channel_id=1, replica_groups=mesh['groups'=2,'mesh'=16] {'mesh'}, dimensions={0} | all-to-all | bytes 16384 | tf_op jit(solution)/shard_map/all_to_all | solution.py:787
  33.8 2.6 %tracer.1 = (f32[2,16,1024]{2,1,0:T(8,128)}, f32[50,36,128]{2,1,0:T(8,128)}) custom-call(f32[1024,128]{1,0:T(8,128)S(1)} %collective-permute-done.outer, f32[1024,128]{1,0:T(8,128)S(1)} %collective-permute-done.1.inner, f32[16,128]{1,0:T(8,128)S(1)} %bitcast.10, f32[8,48,128]{2,1,0:T(8,128)S(1)} %get-tuple-element.60.fields, ...), custom_call_target="tpu_custom_call" | custom-call | tf_op jit(solution)/shard_map/tracer/pallas_call | solution.py:693
Async XLA Ops:
  2.3 19.8 %collective-permute-start = (f32[1024,128]{1,0:T(8,128)S(1)}, f32[1024,128]{1,0:T(8,128)S(1)}, u32[]{:S(2)}, u32[]{:S(2)}) collective-permute-start(f32[1024,128]{1,0:T(8,128)S(1)} %get-tuple-element.35), channel_id=1, source_target_pairs={{1,2},{2,1},{3,4},{4,3},{5,6},{6,5},{7,8},{8,7},{9,10},{10,9},{11,... | collective-permute-start | bytes 1572872 | tf_op jit(solution)/shard_map/ppermute | solution.py:646
  3.0 19.1 %collective-permute-start.1 = (f32[1024,128]{1,0:T(8,128)S(1)}, f32[1024,128]{1,0:T(8,128)S(1)}, u32[]{:S(2)}, u32[]{:S(2)}) collective-permute-start(f32[1024,128]{1,0:T(8,128)S(1)} %get-tuple-element.36), channel_id=1, source_target_pairs={{0,1},{1,0},{2,3},{3,2},{4,5},{5,4},{6,7},{7,6},{8,9},{9,8},{10,11... | collective-permute-start | bytes 1572872 | tf_op jit(solution)/shard_map/ppermute | solution.py:646

commit v18 on v12

--- a/solution.py
+++ b/solution.py
@@ -101,10 +101,18 @@
     return first, (x - first.astype(jnp.float32)).astype(jnp.bfloat16)
 
 
+def spot(refs, counts, head, g, whole, rest):
+    for k, count in enumerate(counts):
+        if g < count:
+            start = head if k == 0 else 0
+            return refs[k], start + g * whole, start + count * whole + g * rest
+        g -= count
+
+
 def pack_kernel(
     spectra_in, tracers_in, potential_in, neighbors_in, normal_in, weight_in, current_in,
     send_rows, slot_in, near_in, angle_in, face_in, wind_in,
-    rows_out, outer, inner, spectra, node_slot, near, angle, face, wind,
+    rows_out, outer, more, inner, spectra, node_slot, near, angle, face, wind,
     tracers, potential, neighbors, normal, weight, coupled,
     current, sems,
 ):
@@ -186,18 +194,13 @@
     for g in range(pairs):
         natural = spectra[g, 0:dirs, :]
         turned = pltpu.roll(spectra[g + pairs, 0:dirs, :], LANES // 2, 1)
-        for out, mixed in (
-            (outer, jnp.where(turns, turned, natural)),
-            (inner, jnp.where(turns, natural, turned)),
+        for refs, counts, mixed in (
+            ((outer, more), (pairs // 2, pairs - pairs // 2), jnp.where(turns, turned, natural)),
+            ((inner,), (pairs,), jnp.where(turns, natural, turned)),
         ):
-            at = base + g * whole
+            out, at, left = spot(refs, counts, base, g, whole, rest)
             out[at : at + whole, :] = mixed[:whole]
-            at = base + pairs * whole + g * rest
-            out[at : at + rest, :] = mixed[whole:]
-    at = base + pairs * dirs
-    if at < outer.shape[0]:
-        for out in (outer, inner):
-            out[at:, :] = jnp.zeros((outer.shape[0] - at, LANES), jnp.float32)
+            out[left : left + rest, :] = mixed[whole:]
     for copy in copies[9:]:
         copy.wait()
 
@@ -241,16 +244,13 @@
     freqs, padded, _ = spectra.shape
     step = step_rows // padded
 
-    def own_part(c, carry):
-        own = spectra[pl.ds(c * step, step)].reshape(step_rows, LANES)
-        own_change[pl.ds(pl.multiple_of(c * step_rows, 8), step_rows), :] = jnp.dot(
+    for c in range(freqs // step):
+        own = spectra[c * step : (c + 1) * step].reshape(step_rows, LANES)
+        own_change[c * step_rows : (c + 1) * step_rows, :] = jnp.dot(
             jnp.concatenate(split(own), axis=1),
             choice[0 : 2 * LANES, :],
             preferred_element_type=jnp.float32,
         )
-        return carry
-
-    lax.fori_loop(0, freqs // step, own_part, 0)
     tracer_count, layers, cells = tracers.shape
     blocks = cells // LANES
     edges = neighbors.shape[0]
@@ -307,8 +307,8 @@
 
 
 def wave_kernel(
-    capacity, step_pairs, dirs,
-    spectra, outer, inner, table, node_slot, neighbors, cosine, sine, project, choice, ways, slots,
+    capacity, step_pairs, dirs, field_rows,
+    spectra, outer, more, inner, table, node_slot, neighbors, cosine, sine, project, choice, ways, slots,
     own_change,
     spectra_new, rows_out, drift, halos, change_a, change_b,
 ):
@@ -320,7 +320,7 @@
     pairs = freqs // 2
     whole = dirs // 8 * 8
     rest = dirs - whole
-    base = outer.shape[0] - (pairs * dirs + 7) // 8 * 8
+    base = 2 * field_rows + TABLE_ROWS
 
     odd = me % 2 == 1
     slot = node_slot[...]
@@ -356,11 +356,13 @@
         for i in range(step_pairs):
             g = c * step_pairs + i
             parts = []
-            for message in (outer, inner):
-                at = base + g * whole
+            for refs, counts in (
+                ((outer, more), (pairs // 2, pairs - pairs // 2)),
+                ((inner,), (pairs,)),
+            ):
+                message, at, low = spot(refs, counts, base, g, whole, rest)
                 upper = message[at : at + whole, :]
-                at = base + pairs * whole + g * rest
-                left = message[at : at + rest, :]
+                left = message[low : low + rest, :]
                 parts.append(jnp.concatenate([upper, left], axis=0))
             x, y = parts
             at = 2 * i * stride
@@ -685,7 +687,7 @@
     blocks = cells // LANES
     field_rows = (tracer_count + 1) * layers
     head_rows = 2 * field_rows + TABLE_ROWS
-    message_rows = head_rows + (freqs // 2 * dirs + 7) // 8 * 8
+    pairs = freqs // 2
     slots = node_slot.reshape(1, nodes)
     params = pltpu.CompilerParams(vmem_limit_bytes=VMEM_LIMIT)
     f32 = jnp.float32
@@ -718,14 +720,15 @@
         send_rows, slots, node_neighbors, node_normal, node_weight, wind_velocity,
     )
     (
-        currents, outer, inner, own_spectra, own_slots, near, angle, face, wind,
+        currents, outer, more, inner, own_spectra, own_slots, near, angle, face, wind,
         own_tracers, own_potential, neighbors, normal, weight, coupled,
     ) = pl.pallas_call(
         pack_kernel,
         out_shape=(
             shaped(peers, LANES),
-            shaped(message_rows, LANES),
-            shaped(message_rows, LANES),
+            shaped(head_rows + (pairs // 2 * dirs + 7) // 8 * 8, LANES),
+            shaped(((pairs - pairs // 2) * dirs + 7) // 8 * 8, LANES),
+            shaped(head_rows + (pairs * dirs + 7) // 8 * 8, LANES),
             shaped(freqs, stride, LANES),
             like(slots),
             like(node_neighbors),
@@ -740,7 +743,7 @@
             shaped(3, peers, capacity, dtype=jnp.int32),
         ),
         in_specs=[stored] * len(inputs),
-        out_specs=(whole_spec(),) * 15,
+        out_specs=(whole_spec(),) * 16,
         scratch_shapes=[
             pltpu.VMEM(surface_current.shape, f32),
             pltpu.SemaphoreType.DMA((15,)),
@@ -749,6 +752,7 @@
         name="pack",
     )(*(pltpu.with_memory_space_constraint(x, pltpu.HBM) for x in inputs))
     outer = swap(outer, 1, peers)
+    more = swap(more, 1, peers)
     inner = swap(inner, 0, peers)
 
     (
@@ -783,10 +787,10 @@
     currents = lax.all_to_all(currents, "mesh", 0, 0, tiled=True)
 
     spectra_new, stokes_rows = call(
-        functools.partial(wave_kernel, capacity, step_pairs, dirs),
+        functools.partial(wave_kernel, capacity, step_pairs, dirs, field_rows),
         "wave",
         (
-            own_spectra, outer, inner, currents, own_slots, near,
+            own_spectra, outer, more, inner, currents, own_slots, near,
             cosine, sine, project, choice, ways, slot_choice, own_change,
         ),
         (shaped(freqs, stride, LANES), shaped(peers, LANES)),

time: 36.4 us -> 38.3 us (1.052)
  blocking collectives: 20.4 us -> 26.4 us
  starting transfers between devices: 5.06 us -> 1.86 us
  Pallas kernels: 10 us -> 9.09 us
    all_to_all x1, blocking collectives: 11.2 us -> 17.4 us  [local(): currents = lax.all_to_all(currents, 'mesh', 0, 0, tiled=True)]
    ppermute x2 -> x3, starting transfers between devices: 5.06 us -> 1.86 us  [swap(): return lax.ppermute(message, 'mesh', pairs)]
    pallas_call x3, Pallas kernels: 8.39 us -> 7.47 us  [call(): pl.pallas_call(kernel, out_shape=outputs, in_specs=[whole_spec()] * len(i...]
  transfers between devices with their start and end apart: 2 -> 3, of which waited for: 0 -> 0; matrix products, arithmetic and copies ran while one was open for 0% -> 0% of each run, Pallas kernels for 9% -> 6%
where the time goes in v18:
time: 38.3 us; the launch traced here: 38 us
  blocking collectives  26.4 us (69%)
  Pallas kernels  9.09 us (24%)
  starting transfers between devices  1.86 us (5%)
  between operations  0.68 us (2%)
    all_to_all x1, blocking collectives, local(): currents = lax.all_to_all(currents, 'mesh', 0, 0, tiled=True)  17.4 us
    all_to_all x1, blocking collectives, local(): stokes_all = lax.all_to_all(stokes_rows, 'mesh', 0, 0, tiled=True)  8.98 us
    pallas_call x3, Pallas kernels, call(): pl.pallas_call(kernel, out_shape=outputs, in_specs=[whole_spec()] * len(i...  7.47 us
    ppermute x3, starting transfers between devices, swap(): return lax.ppermute(message, 'mesh', pairs)  1.86 us
    pallas_call x1, Pallas kernels, local(): pl.pallas_call(pack_kernel, out_shape=(shaped(peers, LANES), shaped(head_...  1.62 us
  transfers between devices with their start and end apart: 3, of which 0 were waited for; matrix products, arithmetic and copies ran while one was open for 0% of the time, Pallas kernels for 6%

profile of v18, /device:TPU:0, one launch (start us, length us, event | category | flops | bytes accessed | tf_op | source)
XLA Modules:
  0.0 38.0 jit_solution(10973214643695838257)
XLA Ops:
  0.6 1.6 %pack.1 = (f32[16,128]{1,0:T(8,128)S(1)}, f32[552,128]{1,0:T(8,128)S(1)}, f32[472,128]{1,0:T(8,128)S(1)}, f32[1024,128]{1,0:T(8,128)S(1)}, f32[50,40,128]{2,1,0:...) custom-call(f32[50,36,128]{2,1,0:T(8,128)} %spectra_in.1, ...), custom_call_target="tpu_custom_call" | custom-call | tf_op jit(solution)/shard_map/pack/pallas_call | solution.py:725
  2.3 0.5 %collective-permute-start.1 = (f32[1024,128]{1,0:T(8,128)S(1)}, f32[1024,128]{1,0:T(8,128)S(1)}, u32[]{:S(2)}, u32[]{:S(2)}) collective-permute-start(f32[1024,128]{1,0:T(8,128)S(1)} %get-tuple-element.37), channel_id=1, source_target_pairs={{0,1},{1,0},{2,3},{3,2},{4,5},{5,4},{6,7},{7,6},{8,9},{9,8},{10,11... | collective-permute-start | bytes 1572872 | tf_op jit(solution)/shard_map/ppermute | solution.py:661
  2.8 0.7 %collective-permute-start = (f32[552,128]{1,0:T(8,128)S(1)}, f32[552,128]{1,0:T(8,128)S(1)}, u32[]{:S(2)}, u32[]{:S(2)}) collective-permute-start(f32[552,128]{1,0:T(8,128)S(1)} %get-tuple-element.36), channel_id=1, source_target_pairs={{1,2},{2,1},{3,4},{4,3},{5,6},{6,5},{7,8},{8,7},{9,10},{10,9},{11,... | collective-permute-start | bytes 847880 | tf_op jit(solution)/shard_map/ppermute | solution.py:661
  3.5 0.7 %collective-permute-start.2 = (f32[472,128]{1,0:T(8,128)S(1)}, f32[472,128]{1,0:T(8,128)S(1)}, u32[]{:S(2)}, u32[]{:S(2)}) collective-permute-start(f32[472,128]{1,0:T(8,128)S(1)} %get-tuple-element.39), channel_id=1, source_target_pairs={{1,2},{2,1},{3,4},{4,3},{5,6},{6,5},{7,8},{8,7},{9,10},{10,9},{11,... | collective-permute-start | bytes 725000 | tf_op jit(solution)/shard_map/ppermute | solution.py:661
  4.1 2.4 %prepare.1 = (f32[6,128]{1,0:T(8,128)S(1)}, f32[6,128]{1,0:T(8,128)S(1)}, f32[6,40,128]{2,1,0:T(8,128)S(1)}, bf16[512,768]{1,0:T(8,128)(2,1)S(1)}, f32[3,40,128]...) custom-call(f32[50,40,128]{2,1,0:T(8,128)S(1)} %get-tuple-element.38, ...), custom_call_target="tpu_custom_call" | custom-call | tf_op jit(solution)/shard_map/prepare/pallas_call | solution.py:708
  6.6 17.4 %all_to_all.22 = f32[16,1,128]{2,1,0:T(1,128)S(1)} all-to-all(f32[16,1,128]{2,1,0:T(1,128)S(1)} %bitcast.11), channel_id=1, replica_groups=mesh['groups'=2,'mesh'=16] {'mesh'}, dimensions={0} | all-to-all | bytes 16384 | tf_op jit(solution)/shard_map/all_to_all | solution.py:787
  23.9 0.0 collective-permute-done.2.more
  24.0 0.0 collective-permute-done.outer
  24.0 0.0 collective-permute-done.1.inner
  24.0 2.6 %wave.1 = (f32[50,40,128]{2,1,0:T(8,128)S(1)}, f32[16,128]{1,0:T(8,128)S(1)}) custom-call(f32[50,40,128]{2,1,0:T(8,128)S(1)} %get-tuple-element.38.spectra, f32[552,128]{1,0:T(8,128)S(1)} %collective-permute-done.outer, f32[472,128]{1,0:T(8,128)S(1)} %collective-permute-done.2.more, f32[1024,128]{1,0:T(8,128)S(1)} %collective-permute-done.1.inner, ...), custom_call_target="tpu_custom_call" | custom-call | tf_op jit(solution)/shard_map/wave/pallas_call | solution.py:708
  26.6 9.0 %all_to_all.23 = f32[16,1,128]{2,1,0:T(1,128)S(1)} all-to-all(f32[16,1,128]{2,1,0:T(1,128)S(1)} %bitcast.12), channel_id=1, replica_groups=mesh['groups'=2,'mesh'=16] {'mesh'}, dimensions={0} | all-to-all | bytes 16384 | tf_op jit(solution)/shard_map/all_to_all | solution.py:804
  35.6 2.4 %tracer.1 = (f32[2,16,1024]{2,1,0:T(8,128)}, f32[50,36,128]{2,1,0:T(8,128)}) custom-call(f32[552,128]{1,0:T(8,128)S(1)} %collective-permute-done.outer, f32[1024,128]{1,0:T(8,128)S(1)} %collective-permute-done.1.inner, f32[16,128]{1,0:T(8,128)S(1)} %bitcast.10, f32[8,48,128]{2,1,0:T(8,128)S(1)} %get-tuple-element.62.fields, ...), custom_call_target="tpu_custom_call" | custom-call | tf_op jit(solution)/shard_map/tracer/pallas_call | solution.py:708
Async XLA Ops:
  2.3 21.7 %collective-permute-start.1 = (f32[1024,128]{1,0:T(8,128)S(1)}, f32[1024,128]{1,0:T(8,128)S(1)}, u32[]{:S(2)}, u32[]{:S(2)}) collective-permute-start(f32[1024,128]{1,0:T(8,128)S(1)} %get-tuple-element.37), channel_id=1, source_target_pairs={{0,1},{1,0},{2,3},{3,2},{4,5},{5,4},{6,7},{7,6},{8,9},{9,8},{10,11... | collective-permute-start | bytes 1572872 | tf_op jit(solution)/shard_map/ppermute | solution.py:661
  2.8 21.2 %collective-permute-start = (f32[552,128]{1,0:T(8,128)S(1)}, f32[552,128]{1,0:T(8,128)S(1)}, u32[]{:S(2)}, u32[]{:S(2)}) collective-permute-start(f32[552,128]{1,0:T(8,128)S(1)} %get-tuple-element.36), channel_id=1, source_target_pairs={{1,2},{2,1},{3,4},{4,3},{5,6},{6,5},{7,8},{8,7},{9,10},{10,9},{11,... | collective-permute-start | bytes 847880 | tf_op jit(solution)/shard_map/ppermute | solution.py:661
  3.5 20.5 %collective-permute-start.2 = (f32[472,128]{1,0:T(8,128)S(1)}, f32[472,128]{1,0:T(8,128)S(1)}, u32[]{:S(2)}, u32[]{:S(2)}) collective-permute-start(f32[472,128]{1,0:T(8,128)S(1)} %get-tuple-element.39), channel_id=1, source_target_pairs={{1,2},{2,1},{3,4},{4,3},{5,6},{6,5},{7,8},{8,7},{9,10},{10,9},{11,... | collective-permute-start | bytes 725000 | tf_op jit(solution)/shard_map/ppermute | solution.py:661

commit v19 on v12

--- a/solution.py
+++ b/solution.py
@@ -230,7 +230,7 @@
 def prepare_kernel(
     dirs, step_rows,
     spectra, near, angle, face, wind, slot, tracers, potential, neighbors, normal, weight, coupled,
-    cosine, sine, project, choice, ways, slots, own_change,
+    cosine, sine, project, choice, ways, slots, own_parts,
     fields, matrices, inside, cell_cosine, cell_sine, cell_scale, sums,
     pieces,
 ):
@@ -239,18 +239,14 @@
         me, dirs, near, angle, face, wind, slot, cosine, sine, project, choice, ways, slots
     )
     freqs, padded, _ = spectra.shape
-    step = step_rows // padded
-
-    def own_part(c, carry):
-        own = spectra[pl.ds(c * step, step)].reshape(step_rows, LANES)
-        own_change[pl.ds(pl.multiple_of(c * step_rows, 8), step_rows), :] = jnp.dot(
-            jnp.concatenate(split(own), axis=1),
-            choice[0 : 2 * LANES, :],
-            preferred_element_type=jnp.float32,
-        )
-        return carry
-
-    lax.fori_loop(0, freqs // step, own_part, 0)
+    step = step_rows // padded // 2
+    pairs = freqs // 2
+    for c in range(pairs // step):
+        rows = []
+        for g in range(c * step, (c + 1) * step):
+            rows += [spectra[g], spectra[g + pairs]]
+        mixed = jnp.concatenate(split(jnp.concatenate(rows, axis=0)), axis=1)
+        own_parts[c * step_rows : (c + 1) * step_rows, :] = mixed
     tracer_count, layers, cells = tracers.shape
     blocks = cells // LANES
     edges = neighbors.shape[0]
@@ -309,7 +305,7 @@
 def wave_kernel(
     capacity, step_pairs, dirs,
     spectra, outer, inner, table, node_slot, neighbors, cosine, sine, project, choice, ways, slots,
-    own_change,
+    own_parts,
     spectra_new, rows_out, drift, halos, change_a, change_b,
 ):
     me = lax.axis_index("mesh")
@@ -348,6 +344,7 @@
     )
     drifts = [spread(drift[s : s + 1, :], 8) for s in range(edges)]
     from_outer = half_mask(dirs, odd)
+    step_rows = halos.shape[0]
     halos[...] = jnp.zeros(halos.shape, jnp.float32)
     ratio = 1.0 / 1.1
     bands = [slice(r, r + 8) for r in range(0, stride, 8)]
@@ -367,10 +364,9 @@
             halos[at : at + dirs, :] = jnp.where(from_outer, x, y)
             at += stride
             halos[at : at + dirs, :] = pltpu.roll(jnp.where(from_outer, y, x), LANES // 2, 1)
-        mixed = jnp.concatenate(split(halos[...]), axis=1)
-        change[...] = jnp.dot(
-            mixed, choice[2 * LANES : 4 * LANES, :], preferred_element_type=jnp.float32
-        )
+        own = own_parts[c * step_rows : (c + 1) * step_rows, :]
+        mixed = jnp.concatenate([own, *split(halos[...])], axis=1)
+        change[...] = jnp.dot(mixed, choice[...], preferred_element_type=jnp.float32)
 
     def advect(c, change, first_speed, first_slow, total):
         total = list(total)
@@ -390,13 +386,11 @@
                 for j, f in ((2 * i, g), (2 * i + 1, g + pairs)):
                     own = spectra[f, band, :]
                     at = j * stride + band.start
-                    own_at = slice(f * stride + band.start, f * stride + band.stop)
                     flux = (along_sum + relative_sum[j]) * own
                     for s in range(edges):
                         down = jnp.minimum(along[s] + relative[j][s], 0.0)
                         lanes = slice(s * LANES, (s + 1) * LANES)
-                        step = change[at : at + 8, lanes] + own_change[own_at, lanes]
-                        flux = flux + down * step
+                        flux = flux + down * change[at : at + 8, lanes]
                     value = own - speeds[j] * flux
                     spectra_new[f, band, :] = value
                     total[k] = total[k] + value
@@ -752,7 +746,7 @@
     inner = swap(inner, 0, peers)
 
     (
-        cosine, sine, project, choice, ways, slot_choice, own_change,
+        cosine, sine, project, choice, ways, slot_choice, own_parts,
         fields, matrices, inside, cell_cosine, cell_sine, cell_scale, sums,
     ) = call(
         functools.partial(prepare_kernel, dirs, step_rows),
@@ -768,7 +762,7 @@
             shaped(4 * LANES, edges * LANES, dtype=jnp.bfloat16),
             shaped(3, stride, LANES),
             shaped(nodes, peers * capacity, dtype=jnp.bfloat16),
-            shaped(freqs * stride, edges * LANES),
+            shaped(freqs * stride, 2 * LANES, dtype=jnp.bfloat16),
             shaped(blocks, field_rows, LANES),
             shaped(blocks, 3 * LANES, edges * LANES, dtype=jnp.bfloat16),
             shaped(blocks, field_rows, edges * LANES),
@@ -787,7 +781,7 @@
         "wave",
         (
             own_spectra, outer, inner, currents, own_slots, near,
-            cosine, sine, project, choice, ways, slot_choice, own_change,
+            cosine, sine, project, choice, ways, slot_choice, own_parts,
         ),
         (shaped(freqs, stride, LANES), shaped(peers, LANES)),
         [

time: 36.4 us -> 36.6 us (level)
  blocking collectives: 20.4 us -> 21.8 us
  Pallas kernels: 10 us -> 8.74 us
    all_to_all x1, blocking collectives: 9.23 us -> 10.6 us  [local(): stokes_all = lax.all_to_all(stokes_rows, 'mesh', 0, 0, tiled=True)]
    pallas_call x3, Pallas kernels: 8.39 us -> 7.13 us  [call(): pl.pallas_call(kernel, out_shape=outputs, in_specs=[whole_spec()] * len(i...]
  transfers between devices with their start and end apart: 2 -> 2, of which waited for: 0 -> 0; matrix products, arithmetic and copies ran while one was open for 0% -> 0% of each run, Pallas kernels for 9% -> 6%
where the time goes in v19:
time: 36.6 us; the launch traced here: 36.3 us
  blocking collectives  21.8 us (60%)
  Pallas kernels  8.74 us (24%)
  starting transfers between devices  5.06 us (14%)
  between operations  0.67 us (2%)
    all_to_all x1, blocking collectives, local(): currents = lax.all_to_all(currents, 'mesh', 0, 0, tiled=True)  11.2 us
    all_to_all x1, blocking collectives, local(): stokes_all = lax.all_to_all(stokes_rows, 'mesh', 0, 0, tiled=True)  10.6 us
    pallas_call x3, Pallas kernels, call(): pl.pallas_call(kernel, out_shape=outputs, in_specs=[whole_spec()] * len(i...  7.13 us
    ppermute x2, starting transfers between devices, swap(): return lax.ppermute(message, 'mesh', pairs)  5.06 us
    pallas_call x1, Pallas kernels, local(): pl.pallas_call(pack_kernel, out_shape=(shaped(peers, LANES), shaped(messa...  1.62 us
  transfers between devices with their start and end apart: 2, of which 0 were waited for; matrix products, arithmetic and copies ran while one was open for 0% of the time, Pallas kernels for 6%

profile of v19, /device:TPU:0, one launch (start us, length us, event | category | flops | bytes accessed | tf_op | source)
XLA Modules:
  0.0 36.3 jit_solution(18415721064449800101)
XLA Ops:
  0.6 1.6 %pack.1 = (f32[16,128]{1,0:T(8,128)S(1)}, f32[1024,128]{1,0:T(8,128)S(1)}, f32[1024,128]{1,0:T(8,128)S(1)}, f32[50,40,128]{2,1,0:T(8,128)S(1)}, s32[1,128]{1,0:T...) custom-call(f32[50,36,128]{2,1,0:T(8,128)} %spectra_in.1, ...), custom_call_target="tpu_custom_call" | custom-call | tf_op jit(solution)/shard_map/pack/pallas_call | solution.py:717
  2.3 0.7 %collective-permute-start = (f32[1024,128]{1,0:T(8,128)S(1)}, f32[1024,128]{1,0:T(8,128)S(1)}, u32[]{:S(2)}, u32[]{:S(2)}) collective-permute-start(f32[1024,128]{1,0:T(8,128)S(1)} %get-tuple-element.35), channel_id=1, source_target_pairs={{1,2},{2,1},{3,4},{4,3},{5,6},{6,5},{7,8},{8,7},{9,10},{10,9},{11,... | collective-permute-start | bytes 1572872 | tf_op jit(solution)/shard_map/ppermute | solution.py:653
  3.0 4.4 %collective-permute-start.1 = (f32[1024,128]{1,0:T(8,128)S(1)}, f32[1024,128]{1,0:T(8,128)S(1)}, u32[]{:S(2)}, u32[]{:S(2)}) collective-permute-start(f32[1024,128]{1,0:T(8,128)S(1)} %get-tuple-element.36), channel_id=1, source_target_pairs={{0,1},{1,0},{2,3},{3,2},{4,5},{5,4},{6,7},{7,6},{8,9},{9,8},{10,11... | collective-permute-start | bytes 1572872 | tf_op jit(solution)/shard_map/ppermute | solution.py:653
  7.3 2.0 %prepare.1 = (f32[6,128]{1,0:T(8,128)S(1)}, f32[6,128]{1,0:T(8,128)S(1)}, f32[6,40,128]{2,1,0:T(8,128)S(1)}, bf16[512,768]{1,0:T(8,128)(2,1)S(1)}, f32[3,40,128]...) custom-call(f32[50,40,128]{2,1,0:T(8,128)S(1)} %get-tuple-element.37, ...), custom_call_target="tpu_custom_call" | custom-call | tf_op jit(solution)/shard_map/prepare/pallas_call | solution.py:700
  9.3 11.2 %all_to_all.22 = f32[16,1,128]{2,1,0:T(1,128)S(1)} all-to-all(f32[16,1,128]{2,1,0:T(1,128)S(1)} %bitcast.11), channel_id=1, replica_groups=mesh['groups'=2,'mesh'=16] {'mesh'}, dimensions={0} | all-to-all | bytes 16384 | tf_op jit(solution)/shard_map/all_to_all | solution.py:777
  20.5 0.0 collective-permute-done.outer
  20.5 0.0 collective-permute-done.1.inner
  20.5 2.5 %wave.1 = (f32[50,40,128]{2,1,0:T(8,128)S(1)}, f32[16,128]{1,0:T(8,128)S(1)}) custom-call(f32[50,40,128]{2,1,0:T(8,128)S(1)} %get-tuple-element.37.spectra, f32[1024,128]{1,0:T(8,128)S(1)} %collective-permute-done.outer, f32[1024,128]{1,0:T(8,128)S(1)} %collective-permute-done.1.inner, f32[16,128]{1,0:T(8,128)S(1)} %bitcast.9, ...), custom_call_target="tpu_custom_call" | custom-call | tf_op jit(solution)/shard_map/wave/pallas_call | solution.py:700
  23.1 10.6 %all_to_all.23 = f32[16,1,128]{2,1,0:T(1,128)S(1)} all-to-all(f32[16,1,128]{2,1,0:T(1,128)S(1)} %bitcast.12), channel_id=1, replica_groups=mesh['groups'=2,'mesh'=16] {'mesh'}, dimensions={0} | all-to-all | bytes 16384 | tf_op jit(solution)/shard_map/all_to_all | solution.py:794
  33.7 2.6 %tracer.1 = (f32[2,16,1024]{2,1,0:T(8,128)}, f32[50,36,128]{2,1,0:T(8,128)}) custom-call(f32[1024,128]{1,0:T(8,128)S(1)} %collective-permute-done.outer, f32[1024,128]{1,0:T(8,128)S(1)} %collective-permute-done.1.inner, f32[16,128]{1,0:T(8,128)S(1)} %bitcast.10, f32[8,48,128]{2,1,0:T(8,128)S(1)} %get-tuple-element.60.fields, ...), custom_call_target="tpu_custom_call" | custom-call | tf_op jit(solution)/shard_map/tracer/pallas_call | solution.py:700
Async XLA Ops:
  2.3 18.3 %collective-permute-start = (f32[1024,128]{1,0:T(8,128)S(1)}, f32[1024,128]{1,0:T(8,128)S(1)}, u32[]{:S(2)}, u32[]{:S(2)}) collective-permute-start(f32[1024,128]{1,0:T(8,128)S(1)} %get-tuple-element.35), channel_id=1, source_target_pairs={{1,2},{2,1},{3,4},{4,3},{5,6},{6,5},{7,8},{8,7},{9,10},{10,9},{11,... | collective-permute-start | bytes 1572872 | tf_op jit(solution)/shard_map/ppermute | solution.py:653
  3.0 17.6 %collective-permute-start.1 = (f32[1024,128]{1,0:T(8,128)S(1)}, f32[1024,128]{1,0:T(8,128)S(1)}, u32[]{:S(2)}, u32[]{:S(2)}) collective-permute-start(f32[1024,128]{1,0:T(8,128)S(1)} %get-tuple-element.36), channel_id=1, source_target_pairs={{0,1},{1,0},{2,3},{3,2},{4,5},{5,4},{6,7},{7,6},{8,9},{9,8},{10,11... | collective-permute-start | bytes 1572872 | tf_op jit(solution)/shard_map/ppermute | solution.py:653

commit v20 on v19

--- a/solution.py
+++ b/solution.py
@@ -102,58 +102,37 @@
 
 
 def pack_kernel(
-    spectra_in, tracers_in, potential_in, neighbors_in, normal_in, weight_in, current_in,
-    send_rows, slot_in, near_in, angle_in, face_in, wind_in,
-    rows_out, outer, inner, spectra, node_slot, near, angle, face, wind,
-    tracers, potential, neighbors, normal, weight, coupled,
-    current, sems,
+    spectra_in, tracers_in, potential_in, neighbors_in, normal_in, weight_in, slot_in,
+    outer, inner, spectra, tracers, potential, neighbors, normal, weight, node_slot,
+    sems,
 ):
-    peers, _, capacity = send_rows.shape
     me = lax.axis_index("mesh")
     freqs, dirs = spectra_in.shape[:2]
     if dirs < spectra.shape[1]:
         for f in range(freqs):
             spectra[f, dirs // 8 * 8 :, :] = jnp.zeros((8, LANES), jnp.float32)
     pairs = freqs // 2
+    early = pairs // 2
     copies = []
     for source, target in (
-        (send_rows.at[me], coupled.at[1]),
-        (current_in, current),
-        (slot_in, node_slot),
-        (spectra_in, spectra.at[:, 0:dirs, :]),
+        (spectra_in.at[0:early], spectra.at[0:early, 0:dirs, :]),
+        (spectra_in.at[pairs : pairs + early], spectra.at[pairs : pairs + early, 0:dirs, :]),
         (tracers_in, tracers),
         (potential_in, potential),
         (neighbors_in, neighbors),
         (normal_in, normal),
         (weight_in, weight),
-        (send_rows.at[jnp.maximum(me - 1, 0)], coupled.at[0]),
-        (send_rows.at[jnp.minimum(me + 1, peers - 1)], coupled.at[2]),
-        (near_in, near),
-        (angle_in, angle),
-        (face_in, face),
-        (wind_in, wind),
+        (slot_in, node_slot),
+        (spectra_in.at[early:pairs], spectra.at[early:pairs, 0:dirs, :]),
+        (spectra_in.at[pairs + early :], spectra.at[pairs + early :, 0:dirs, :]),
     ):
         copy = pltpu.make_async_copy(source, target, sems.at[len(copies)])
         copy.start()
         copies.append(copy)
-    for copy in copies[:3]:
-        copy.wait()
     layers, cells = potential.shape
     blocks = cells // LANES
     field_rows = (tracers.shape[0] + 1) * layers
-    stacked = jnp.concatenate(
-        [current[:, b * LANES : (b + 1) * LANES] for b in range(blocks)], axis=0
-    )
-    place = row_iota(2 * blocks)
-    halves = slot_rows(coupled[1])
-    values = [[], []]
-    for cell in halves:
-        found = lane_gather(stacked, spread(cell % LANES, 2 * blocks))
-        for part in range(2):
-            picked = jnp.where(place == 2 * (cell // LANES) + part, found, 0.0)
-            values[part].append(jnp.sum(picked, axis=0, keepdims=True))
-    rows_out[...] = peer_rows(values, peers, capacity)
-    for copy in copies[4:9]:
+    for copy in copies[2:8]:
         copy.wait()
     odd = me % 2 == 1
     for out, upward in ((outer, odd), (inner, jnp.logical_not(odd))):
@@ -182,8 +161,11 @@
     whole = dirs // 8 * 8
     rest = dirs - whole
     turns = half_mask(dirs, odd)
-    copies[3].wait()
     for g in range(pairs):
+        if g in (0, early):
+            at = 0 if g == 0 else 8
+            copies[at].wait()
+            copies[at + 1].wait()
         natural = spectra[g, 0:dirs, :]
         turned = pltpu.roll(spectra[g + pairs, 0:dirs, :], LANES // 2, 1)
         for out, mixed in (
@@ -198,8 +180,22 @@
     if at < outer.shape[0]:
         for out in (outer, inner):
             out[at:, :] = jnp.zeros((outer.shape[0] - at, LANES), jnp.float32)
-    for copy in copies[9:]:
-        copy.wait()
+
+
+def current_rows(current, coupled, rows_out):
+    peers, capacity = coupled.shape[1:]
+    blocks = current.shape[1] // LANES
+    stacked = jnp.concatenate(
+        [current[:, b * LANES : (b + 1) * LANES] for b in range(blocks)], axis=0
+    )
+    place = row_iota(2 * blocks)
+    values = [[], []]
+    for cell in slot_rows(coupled[1]):
+        found = lane_gather(stacked, spread(cell % LANES, 2 * blocks))
+        for part in range(2):
+            picked = jnp.where(place == 2 * (cell // LANES) + part, found, 0.0)
+            values[part].append(jnp.sum(picked, axis=0, keepdims=True))
+    rows_out[...] = peer_rows(values, peers, capacity)
 
 
 def choose(cells, first, lanes, matrix):
@@ -229,24 +225,28 @@
 
 def prepare_kernel(
     dirs, step_rows,
-    spectra, near, angle, face, wind, slot, tracers, potential, neighbors, normal, weight, coupled,
-    cosine, sine, project, choice, ways, slots, own_parts,
+    spectra, slot, tracers, potential, neighbors, normal, weight,
+    near_in, angle_in, face_in, wind_in, send_rows, current_in,
+    near, rows_out, cosine, sine, project, choice, ways, slots, own_parts,
     fields, matrices, inside, cell_cosine, cell_sine, cell_scale, sums,
-    pieces,
+    pieces, angle, face, wind, coupled, current, sems,
 ):
     me = lax.axis_index("mesh")
-    node_tables(
-        me, dirs, near, angle, face, wind, slot, cosine, sine, project, choice, ways, slots
-    )
-    freqs, padded, _ = spectra.shape
-    step = step_rows // padded // 2
-    pairs = freqs // 2
-    for c in range(pairs // step):
-        rows = []
-        for g in range(c * step, (c + 1) * step):
-            rows += [spectra[g], spectra[g + pairs]]
-        mixed = jnp.concatenate(split(jnp.concatenate(rows, axis=0)), axis=1)
-        own_parts[c * step_rows : (c + 1) * step_rows, :] = mixed
+    peers = send_rows.shape[0]
+    copies = []
+    for source, target in (
+        (near_in, near),
+        (angle_in, angle),
+        (face_in, face),
+        (wind_in, wind),
+        (current_in, current),
+        (send_rows.at[jnp.maximum(me - 1, 0)], coupled.at[0]),
+        (send_rows.at[me], coupled.at[1]),
+        (send_rows.at[jnp.minimum(me + 1, peers - 1)], coupled.at[2]),
+    ):
+        copy = pltpu.make_async_copy(source, target, sems.at[len(copies)])
+        copy.start()
+        copies.append(copy)
     tracer_count, layers, cells = tracers.shape
     blocks = cells // LANES
     edges = neighbors.shape[0]
@@ -278,6 +278,21 @@
         for s in range(edges):
             at = slice(s * LANES, (s + 1) * LANES)
             inside[b, last_field:, at] = change[last_field:, at] * cell_scale[b, s : s + 1, :]
+    for copy in copies:
+        copy.wait()
+    current_rows(current, coupled, rows_out)
+    node_tables(
+        me, dirs, near, angle, face, wind, slot, cosine, sine, project, choice, ways, slots
+    )
+    freqs, padded, _ = spectra.shape
+    step = step_rows // padded // 2
+    pairs = freqs // 2
+    for c in range(pairs // step):
+        rows = []
+        for g in range(c * step, (c + 1) * step):
+            rows += [spectra[g], spectra[g + pairs]]
+        mixed = jnp.concatenate(split(jnp.concatenate(rows, axis=0)), axis=1)
+        own_parts[c * step_rows : (c + 1) * step_rows, :] = mixed
     for which in range(3):
         first = 0 if which != 0 else cells - LANES
         count = blocks if which == 1 else 1
@@ -696,11 +711,11 @@
     def shaped(*shape, dtype=f32):
         return jax.ShapeDtypeStruct(shape, dtype)
 
-    def call(kernel, name, inputs, outputs, scratch, out_specs=None):
+    def call(kernel, name, inputs, outputs, scratch, in_specs=None, out_specs=None):
         return pl.pallas_call(
             kernel,
             out_shape=outputs,
-            in_specs=[whole_spec()] * len(inputs),
+            in_specs=in_specs or [whole_spec()] * len(inputs),
             out_specs=out_specs or (whole_spec(),) * len(outputs),
             scratch_shapes=scratch,
             compiler_params=params,
@@ -708,37 +723,21 @@
         )(*inputs)
 
     inputs = (
-        spectra, tracers, potential, cell_neighbors, cell_normal, cell_weight, surface_current,
-        send_rows, slots, node_neighbors, node_normal, node_weight, wind_velocity,
+        spectra, tracers, potential, cell_neighbors, cell_normal, cell_weight, slots,
     )
     (
-        currents, outer, inner, own_spectra, own_slots, near, angle, face, wind,
-        own_tracers, own_potential, neighbors, normal, weight, coupled,
+        outer, inner, own_spectra, own_tracers, own_potential, neighbors, normal, weight, own_slots,
     ) = pl.pallas_call(
         pack_kernel,
         out_shape=(
-            shaped(peers, LANES),
             shaped(message_rows, LANES),
             shaped(message_rows, LANES),
             shaped(freqs, stride, LANES),
-            like(slots),
-            like(node_neighbors),
-            like(node_normal),
-            like(node_weight),
-            like(wind_velocity),
-            like(tracers),
-            like(potential),
-            like(cell_neighbors),
-            like(cell_normal),
-            like(cell_weight),
-            shaped(3, peers, capacity, dtype=jnp.int32),
+            *(like(x) for x in inputs[1:]),
         ),
         in_specs=[stored] * len(inputs),
-        out_specs=(whole_spec(),) * 15,
-        scratch_shapes=[
-            pltpu.VMEM(surface_current.shape, f32),
-            pltpu.SemaphoreType.DMA((15,)),
-        ],
+        out_specs=(whole_spec(),) * 9,
+        scratch_shapes=[pltpu.SemaphoreType.DMA((10,))],
         compiler_params=params,
         name="pack",
     )(*(pltpu.with_memory_space_constraint(x, pltpu.HBM) for x in inputs))
@@ -746,16 +745,24 @@
     inner = swap(inner, 0, peers)
 
     (
-        cosine, sine, project, choice, ways, slot_choice, own_parts,
+        near, currents, cosine, sine, project, choice, ways, slot_choice, own_parts,
         fields, matrices, inside, cell_cosine, cell_sine, cell_scale, sums,
     ) = call(
         functools.partial(prepare_kernel, dirs, step_rows),
         "prepare",
         (
-            own_spectra, near, angle, face, wind, own_slots, own_tracers, own_potential,
-            neighbors, normal, weight, coupled,
+            own_spectra, own_slots, own_tracers, own_potential, neighbors, normal, weight,
+            *(
+                pltpu.with_memory_space_constraint(x, pltpu.HBM)
+                for x in (
+                    node_neighbors, node_normal, node_weight, wind_velocity, send_rows,
+                    surface_current,
+                )
+            ),
         ),
         (
+            like(node_neighbors),
+            shaped(peers, LANES),
             like(node_normal),
             like(node_normal),
             shaped(edges, stride, LANES),
@@ -771,9 +778,17 @@
             shaped(blocks, 8, LANES),
             shaped(peers * capacity, (blocks + 2) * LANES, dtype=jnp.bfloat16),
         ),
-        [pltpu.VMEM((blocks, 2 * field_rows, LANES), jnp.bfloat16)],
-    )
-    currents, cosine = lax.optimization_barrier((currents, cosine))
+        [
+            pltpu.VMEM((blocks, 2 * field_rows, LANES), jnp.bfloat16),
+            pltpu.VMEM(node_normal.shape, f32),
+            pltpu.VMEM(node_weight.shape, f32),
+            pltpu.VMEM(wind_velocity.shape, f32),
+            pltpu.VMEM((3, peers, capacity), jnp.int32),
+            pltpu.VMEM(surface_current.shape, f32),
+            pltpu.SemaphoreType.DMA((8,)),
+        ],
+        in_specs=[whole_spec()] * 7 + [stored] * 6,
+    )
     currents = lax.all_to_all(currents, "mesh", 0, 0, tiled=True)
 
     spectra_new, stokes_rows = call(

time: 36.6 us -> 36.6 us (level)
  Pallas kernels: 8.74 us -> 9.9 us
  blocking collectives: 21.8 us -> 20.7 us
    pallas_call x4, Pallas kernels: 8.74 us -> 9.9 us  [the longest x3 8.28 us: call(): pl.pallas_call(kernel, out_shape=outputs, in_specs=in_specs or [whole_spe...]
    all_to_all x1, blocking collectives: 10.6 us -> 9.51 us  [local(): stokes_all = lax.all_to_all(stokes_rows, 'mesh', 0, 0, tiled=True)]
  transfers between devices with their start and end apart: 2 -> 2, of which waited for: 0 -> 0; matrix products, arithmetic and copies ran while one was open for 0% -> 0% of each run, Pallas kernels for 6% -> 9%
where the time goes in v20:
time: 36.6 us; the launch traced here: 36.3 us
  blocking collectives  20.7 us (57%)
  Pallas kernels  9.9 us (27%)
  starting transfers between devices  5.06 us (14%)
  between operations  0.67 us (2%)
    all_to_all x1, blocking collectives, local(): currents = lax.all_to_all(currents, 'mesh', 0, 0, tiled=True)  11.2 us
    all_to_all x1, blocking collectives, local(): stokes_all = lax.all_to_all(stokes_rows, 'mesh', 0, 0, tiled=True)  9.51 us
    pallas_call x3, Pallas kernels, call(): pl.pallas_call(kernel, out_shape=outputs, in_specs=in_specs or [whole_spe...  8.28 us
    ppermute x2, starting transfers between devices, swap(): return lax.ppermute(message, 'mesh', pairs)  5.06 us
    pallas_call x1, Pallas kernels, local(): pl.pallas_call(pack_kernel, out_shape=(shaped(message_rows, LANES), shape...  1.62 us
  transfers between devices with their start and end apart: 2, of which 0 were waited for; matrix products, arithmetic and copies ran while one was open for 0% of the time, Pallas kernels for 9%

profile of v20, /device:TPU:0, one launch (start us, length us, event | category | flops | bytes accessed | tf_op | source)
XLA Modules:
  0.0 36.3 jit_solution(9628947329492715949)
XLA Ops:
  0.6 1.6 %pack.1 = (f32[1024,128]{1,0:T(8,128)S(1)}, f32[1024,128]{1,0:T(8,128)S(1)}, f32[50,40,128]{2,1,0:T(8,128)S(1)}, f32[2,16,1024]{2,1,0:T(8,128)S(1)}, f32[16,1024...) custom-call(f32[50,36,128]{2,1,0:T(8,128)} %spectra_in.1, ...), custom_call_target="tpu_custom_call" | custom-call | tf_op jit(solution)/shard_map/pack/pallas_call | solution.py:730
  2.3 0.7 %collective-permute-start = (f32[1024,128]{1,0:T(8,128)S(1)}, f32[1024,128]{1,0:T(8,128)S(1)}, u32[]{:S(2)}, u32[]{:S(2)}) collective-permute-start(f32[1024,128]{1,0:T(8,128)S(1)} %get-tuple-element.29), channel_id=1, source_target_pairs={{1,2},{2,1},{3,4},{4,3},{5,6},{6,5},{7,8},{8,7},{9,10},{10,9},{11,... | collective-permute-start | bytes 1572872 | tf_op jit(solution)/shard_map/ppermute | solution.py:668
  3.0 4.4 %collective-permute-start.1 = (f32[1024,128]{1,0:T(8,128)S(1)}, f32[1024,128]{1,0:T(8,128)S(1)}, u32[]{:S(2)}, u32[]{:S(2)}) collective-permute-start(f32[1024,128]{1,0:T(8,128)S(1)} %get-tuple-element.30), channel_id=1, source_target_pairs={{0,1},{1,0},{2,3},{3,2},{4,5},{5,4},{6,7},{7,6},{8,9},{9,8},{10,11... | collective-permute-start | bytes 1572872 | tf_op jit(solution)/shard_map/ppermute | solution.py:668
  7.3 3.1 %prepare.1 = (s32[6,128]{1,0:T(8,128)S(1)}, f32[16,128]{1,0:T(8,128)S(1)}, f32[6,128]{1,0:T(8,128)S(1)}, f32[6,128]{1,0:T(8,128)S(1)}, f32[6,40,128]{2,1,0:T(8,1...) custom-call(f32[50,40,128]{2,1,0:T(8,128)S(1)} %get-tuple-element.31, ...), custom_call_target="tpu_custom_call" | custom-call | tf_op jit(solution)/shard_map/prepare/pallas_call | solution.py:715
  10.5 11.2 %all_to_all.22 = f32[16,1,128]{2,1,0:T(1,128)S(1)} all-to-all(f32[16,1,128]{2,1,0:T(1,128)S(1)} %bitcast.11), channel_id=1, replica_groups=mesh['groups'=2,'mesh'=16] {'mesh'}, dimensions={0} | all-to-all | bytes 16384 | tf_op jit(solution)/shard_map/all_to_all | solution.py:792
  21.6 0.0 collective-permute-done.outer
  21.6 0.0 collective-permute-done.1.inner
  21.7 2.6 %wave.1 = (f32[50,40,128]{2,1,0:T(8,128)S(1)}, f32[16,128]{1,0:T(8,128)S(1)}) custom-call(f32[50,40,128]{2,1,0:T(8,128)S(1)} %get-tuple-element.31.spectra, f32[1024,128]{1,0:T(8,128)S(1)} %collective-permute-done.outer, f32[1024,128]{1,0:T(8,128)S(1)} %collective-permute-done.1.inner, f32[16,128]{1,0:T(8,128)S(1)} %bitcast.9, ...), custom_call_target="tpu_custom_call" | custom-call | tf_op jit(solution)/shard_map/wave/pallas_call | solution.py:715
  24.3 9.5 %all_to_all.23 = f32[16,1,128]{2,1,0:T(1,128)S(1)} all-to-all(f32[16,1,128]{2,1,0:T(1,128)S(1)} %bitcast.12), channel_id=1, replica_groups=mesh['groups'=2,'mesh'=16] {'mesh'}, dimensions={0} | all-to-all | bytes 16384 | tf_op jit(solution)/shard_map/all_to_all | solution.py:809
  33.8 2.5 %tracer.1 = (f32[2,16,1024]{2,1,0:T(8,128)}, f32[50,36,128]{2,1,0:T(8,128)}) custom-call(f32[1024,128]{1,0:T(8,128)S(1)} %collective-permute-done.outer, f32[1024,128]{1,0:T(8,128)S(1)} %collective-permute-done.1.inner, f32[16,128]{1,0:T(8,128)S(1)} %bitcast.10, f32[8,48,128]{2,1,0:T(8,128)S(1)} %get-tuple-element.48.fields, ...), custom_call_target="tpu_custom_call" | custom-call | tf_op jit(solution)/shard_map/tracer/pallas_call | solution.py:715
Async XLA Ops:
  2.3 19.4 %collective-permute-start = (f32[1024,128]{1,0:T(8,128)S(1)}, f32[1024,128]{1,0:T(8,128)S(1)}, u32[]{:S(2)}, u32[]{:S(2)}) collective-permute-start(f32[1024,128]{1,0:T(8,128)S(1)} %get-tuple-element.29), channel_id=1, source_target_pairs={{1,2},{2,1},{3,4},{4,3},{5,6},{6,5},{7,8},{8,7},{9,10},{10,9},{11,... | collective-permute-start | bytes 1572872 | tf_op jit(solution)/shard_map/ppermute | solution.py:668
  3.0 18.7 %collective-permute-start.1 = (f32[1024,128]{1,0:T(8,128)S(1)}, f32[1024,128]{1,0:T(8,128)S(1)}, u32[]{:S(2)}, u32[]{:S(2)}) collective-permute-start(f32[1024,128]{1,0:T(8,128)S(1)} %get-tuple-element.30), channel_id=1, source_target_pairs={{0,1},{1,0},{2,3},{3,2},{4,5},{5,4},{6,7},{7,6},{8,9},{9,8},{10,11... | collective-permute-start | bytes 1572872 | tf_op jit(solution)/shard_map/ppermute | solution.py:668

commit v21 on v14

--- a/solution.py
+++ b/solution.py
@@ -241,16 +241,13 @@
     freqs, padded, _ = spectra.shape
     step = step_rows // padded
 
-    def own_part(c, carry):
-        own = spectra[pl.ds(c * step, step)].reshape(step_rows, LANES)
-        own_change[pl.ds(pl.multiple_of(c * step_rows, 8), step_rows), :] = jnp.dot(
+    for c in range(freqs // step):
+        own = spectra[c * step : (c + 1) * step].reshape(step_rows, LANES)
+        own_change[c * step_rows : (c + 1) * step_rows, :] = jnp.dot(
             jnp.concatenate(split(own), axis=1),
             choice[0 : 2 * LANES, :],
             preferred_element_type=jnp.float32,
         )
-        return carry
-
-    lax.fori_loop(0, freqs // step, own_part, 0)
     tracer_count, layers, cells = tracers.shape
     blocks = cells // LANES
     edges = neighbors.shape[0]
@@ -361,8 +358,16 @@
     return [functools.partial(task, side, s) for s in range(edges) for side in range(2)]
 
 
+def chunk_sizes(pairs):
+    first = min(2, pairs)
+    left = pairs - first
+    parts = -(-left // 6)
+    sizes = [first] + [left * (k + 1) // parts - left * k // parts for k in range(parts)]
+    return [(sum(sizes[:k]), size) for k, size in enumerate(sizes)]
+
+
 def wave_kernel(
-    capacity, step_pairs, dirs, layers,
+    capacity, sizes, dirs, layers,
     spectra, outer, inner, table, node_slot, neighbors, cosine, sine, project, choice, ways, slots,
     own_change, fields, cell_neighbors, cell_inside, scale,
     spectra_new, rows_out, halo, tables, edge_change, halo_change,
@@ -409,8 +414,9 @@
     bands = [slice(r, r + 8) for r in range(0, stride, 8)]
 
     def gather(c, change):
-        for i in range(step_pairs):
-            g = c * step_pairs + i
+        start, count = sizes[c]
+        for i in range(count):
+            g = start + i
             parts = []
             for message in (outer, inner):
                 at = base + g * whole
@@ -423,76 +429,65 @@
             halos[at : at + dirs, :] = jnp.where(from_outer, x, y)
             at += stride
             halos[at : at + dirs, :] = pltpu.roll(jnp.where(from_outer, y, x), LANES // 2, 1)
-        mixed = jnp.concatenate(split(halos[...]), axis=1)
-        change[...] = jnp.dot(
+        rows = 2 * count * stride
+        mixed = jnp.concatenate(split(halos[0:rows, :]), axis=1)
+        change[0:rows, :] = jnp.dot(
             mixed, choice[2 * LANES : 4 * LANES, :], preferred_element_type=jnp.float32
         )
 
-    def advect(c, change, first_speed, first_slow, total):
+    def advect(c, change, total):
         total = list(total)
-        speeds = []
-        for i in range(step_pairs):
-            speeds += [first_speed * ratio**i, first_speed * ratio ** (i + pairs)]
-        slowness = []
-        for i in range(step_pairs):
-            slowness += [first_slow * ratio**-i, first_slow * ratio ** -(i + pairs)]
+        start, count = sizes[c]
+        order = [f for i in range(count) for f in (start + i, start + i + pairs)]
+        speeds = [ratio**f for f in order]
+        slowness = [ratio**-f for f in order]
         relative = [[drift * slow for drift in drifts] for slow in slowness]
         relative_sum = [sum(each[1:], each[0]) for each in relative]
         for k, band in enumerate(bands):
             along = [project[s, band, :] for s in range(edges)]
             along_sum = sum(along[1:], along[0])
-            for i in range(step_pairs):
-                g = c * step_pairs + i
-                for j, f in ((2 * i, g), (2 * i + 1, g + pairs)):
-                    own = spectra[f, band, :]
-                    at = j * stride + band.start
-                    own_at = slice(f * stride + band.start, f * stride + band.stop)
-                    flux = (along_sum + relative_sum[j]) * own
-                    for s in range(edges):
-                        down = jnp.minimum(along[s] + relative[j][s], 0.0)
-                        lanes = slice(s * LANES, (s + 1) * LANES)
-                        step = change[at : at + 8, lanes] + own_change[own_at, lanes]
-                        flux = flux + down * step
-                    value = own - speeds[j] * flux
-                    spectra_new[f, band, :] = value
-                    total[k] = total[k] + value
-        return first_speed * ratio**step_pairs, first_slow * ratio**-step_pairs, tuple(total)
+            for j, f in enumerate(order):
+                own = spectra[f, band, :]
+                at = j * stride + band.start
+                own_at = slice(f * stride + band.start, f * stride + band.stop)
+                flux = (along_sum + relative_sum[j]) * own
+                for s in range(edges):
+                    down = jnp.minimum(along[s] + relative[j][s], 0.0)
+                    lanes = slice(s * LANES, (s + 1) * LANES)
+                    step = change[at : at + 8, lanes] + own_change[own_at, lanes]
+                    flux = flux + down * step
+                value = own - speeds[j] * flux
+                spectra_new[f, band, :] = value
+                total[k] = total[k] + value
+        return tuple(total)
 
     zeros = tuple(jnp.zeros((8, LANES), jnp.float32) for _ in bands)
-    chunks = pairs // step_pairs
     buffers = (change_a, change_b)
-    carry = (1.0, 1.0, zeros)
+    total = zeros
     gather(0, change_a)
     tasks = halo_tasks(
         layers, outer, inner, fields, cell_neighbors, cell_inside, scale,
         halo, tables, edge_change, halo_change, near_cells,
     )
+    chunks = len(sizes)
     for c in range(chunks):
         if c + 1 < chunks:
             gather(c + 1, buffers[(c + 1) % 2])
         for task in tasks[c * len(tasks) // chunks : (c + 1) * len(tasks) // chunks]:
             task()
-        carry = advect(c, buffers[c % 2], *carry)
-    total = carry[2]
+        total = advect(c, buffers[c % 2], total)
     total = jnp.concatenate(total, axis=0)
     zero = jnp.zeros((stride, LANES), jnp.float32)
     cos_dir, sin_dir = ways[0], ways[1]
     mean = jnp.sum(total, axis=0, keepdims=True) * (1.0 / (freqs * dirs))
     step = jnp.exp((ways[2] - 2.0 * mean) * (1.0 / freqs))
-    run = 10 if freqs % 10 == 0 else 1
-
-    def grow(c, carry):
-        factor, weighted = carry
-        for i in range(run):
-            f = c * run + i
-            factor = factor * step
-            evolved = spectra_new[f] * factor
-            spectra_new[f] = evolved
-            kappa = (f + 1).astype(jnp.float32) * (1.0 / freqs)
-            weighted = weighted + kappa * evolved
-        return factor, weighted
-
-    _, weighted = lax.fori_loop(0, freqs // run, grow, (zero + 1.0, zero))
+    factor = zero + 1.0
+    weighted = zero
+    for f in range(freqs):
+        factor = factor * step
+        evolved = spectra_new[f] * factor
+        spectra_new[f] = evolved
+        weighted = weighted + ((f + 1) / freqs) * evolved
     stokes = jnp.concatenate(
         [
             jnp.sum(weighted * cos_dir, axis=0, keepdims=True),
@@ -791,7 +786,7 @@
     currents = lax.all_to_all(currents, "mesh", 0, 0, tiled=True)
 
     spectra_new, stokes_rows, halo, halo_tables, edge_change, halo_change = call(
-        functools.partial(wave_kernel, capacity, step_pairs, dirs, layers),
+        functools.partial(wave_kernel, capacity, chunk_sizes(freqs // 2), dirs, layers),
         "wave",
         (
             own_spectra, outer, inner, currents, own_slots, near,
@@ -808,9 +803,9 @@
         ),
         [
             pltpu.VMEM((8, LANES), f32),
-            pltpu.VMEM((step_rows, LANES), f32),
-            pltpu.VMEM((step_rows, edges * LANES), f32),
-            pltpu.VMEM((step_rows, edges * LANES), f32),
+            pltpu.VMEM((12 * stride, LANES), f32),
+            pltpu.VMEM((12 * stride, edges * LANES), f32),
+            pltpu.VMEM((12 * stride, edges * LANES), f32),
             pltpu.VMEM((2, 8, LANES), jnp.int32),
         ],
     )

time: 36.6 us -> 36.6 us (level)
  blocking collectives: 20.4 us -> 21.4 us
  Pallas kernels: 10.1 us -> 9.2 us
    all_to_all x1, blocking collectives: 9.23 us -> 10.2 us  [local(): stokes_all = lax.all_to_all(stokes_rows, 'mesh', 0, 0, tiled=True)]
    pallas_call x3, Pallas kernels: 8.5 us -> 7.58 us  [call(): pl.pallas_call(kernel, out_shape=outputs, in_specs=[whole_spec()] * len(i...]
  transfers between devices with their start and end apart: 2 -> 2, of which waited for: 0 -> 0; matrix products, arithmetic and copies ran while one was open for 0% -> 0% of each run, Pallas kernels for 9% -> 7%
where the time goes in v21:
time: 36.6 us; the launch traced here: 36.3 us
  blocking collectives  21.4 us (58%)
  Pallas kernels  9.2 us (25%)
  starting transfers between devices  5.06 us (14%)
  between operations  0.66 us (2%)
    all_to_all x1, blocking collectives, local(): currents = lax.all_to_all(currents, 'mesh', 0, 0, tiled=True)  11.2 us
    all_to_all x1, blocking collectives, local(): stokes_all = lax.all_to_all(stokes_rows, 'mesh', 0, 0, tiled=True)  10.2 us
    pallas_call x3, Pallas kernels, call(): pl.pallas_call(kernel, out_shape=outputs, in_specs=[whole_spec()] * len(i...  7.58 us
    ppermute x2, starting transfers between devices, swap(): return lax.ppermute(message, 'mesh', pairs)  5.06 us
    pallas_call x1, Pallas kernels, local(): pl.pallas_call(pack_kernel, out_shape=(shaped(peers, LANES), shaped(messa...  1.62 us
  transfers between devices with their start and end apart: 2, of which 0 were waited for; matrix products, arithmetic and copies ran while one was open for 0% of the time, Pallas kernels for 7%

profile of v21, /device:TPU:0, one launch (start us, length us, event | category | flops | bytes accessed | tf_op | source)
XLA Modules:
  0.0 36.3 jit_solution(2589938658692493864)
XLA Ops:
  0.6 1.6 %pack.1 = (f32[16,128]{1,0:T(8,128)S(1)}, f32[1024,128]{1,0:T(8,128)S(1)}, f32[1024,128]{1,0:T(8,128)S(1)}, f32[50,40,128]{2,1,0:T(8,128)S(1)}, s32[1,128]{1,0:T...) custom-call(f32[50,36,128]{2,1,0:T(8,128)} %spectra_in.1, ...), custom_call_target="tpu_custom_call" | custom-call | tf_op jit(solution)/shard_map/pack/pallas_call | solution.py:726
  2.3 0.7 %collective-permute-start = (f32[1024,128]{1,0:T(8,128)S(1)}, f32[1024,128]{1,0:T(8,128)S(1)}, u32[]{:S(2)}, u32[]{:S(2)}) collective-permute-start(f32[1024,128]{1,0:T(8,128)S(1)} %get-tuple-element.40), channel_id=1, source_target_pairs={{1,2},{2,1},{3,4},{4,3},{5,6},{6,5},{7,8},{8,7},{9,10},{10,9},{11,... | collective-permute-start | bytes 1572872 | tf_op jit(solution)/shard_map/ppermute | solution.py:662
  3.0 4.4 %collective-permute-start.1 = (f32[1024,128]{1,0:T(8,128)S(1)}, f32[1024,128]{1,0:T(8,128)S(1)}, u32[]{:S(2)}, u32[]{:S(2)}) collective-permute-start(f32[1024,128]{1,0:T(8,128)S(1)} %get-tuple-element.41), channel_id=1, source_target_pairs={{0,1},{1,0},{2,3},{3,2},{4,5},{5,4},{6,7},{7,6},{8,9},{9,8},{10,11... | collective-permute-start | bytes 1572872 | tf_op jit(solution)/shard_map/ppermute | solution.py:662
  7.3 2.4 %prepare.1 = (f32[6,128]{1,0:T(8,128)S(1)}, f32[6,128]{1,0:T(8,128)S(1)}, f32[6,40,128]{2,1,0:T(8,128)S(1)}, bf16[512,768]{1,0:T(8,128)(2,1)S(1)}, f32[3,40,128]...) custom-call(f32[50,40,128]{2,1,0:T(8,128)S(1)} %get-tuple-element.39, ...), custom_call_target="tpu_custom_call" | custom-call | tf_op jit(solution)/shard_map/prepare/pallas_call | solution.py:709
  9.7 11.2 %all_to_all.22 = f32[16,1,128]{2,1,0:T(1,128)S(1)} all-to-all(f32[16,1,128]{2,1,0:T(1,128)S(1)} %bitcast.11), channel_id=1, replica_groups=mesh['groups'=2,'mesh'=16] {'mesh'}, dimensions={0} | all-to-all | bytes 16384 | tf_op jit(solution)/shard_map/all_to_all | solution.py:786
  20.9 0.0 collective-permute-done.outer
  20.9 0.0 collective-permute-done.1.inner
  20.9 2.9 %wave.1 = (f32[50,40,128]{2,1,0:T(8,128)S(1)}, f32[16,128]{1,0:T(8,128)S(1)}, f32[4,48,128]{2,1,0:T(8,128)S(1)}, f32[2,3,8,128]{3,2,1,0:T(8,128)S(1)}, f32[2,48,...) custom-call(f32[50,40,128]{2,1,0:T(8,128)S(1)} %get-tuple-element.39.spectra, f32[1024,128]{1,0:T(8,128)S(1)} %collective-permute-done.outer, ...), custom_call_target="tpu_custom_call" | custom-call | tf_op jit(solution)/shard_map/wave/pallas_call | solution.py:709
  23.8 10.2 %all_to_all.23 = f32[16,1,128]{2,1,0:T(1,128)S(1)} all-to-all(f32[16,1,128]{2,1,0:T(1,128)S(1)} %bitcast.12), channel_id=1, replica_groups=mesh['groups'=2,'mesh'=16] {'mesh'}, dimensions={0} | all-to-all | bytes 16384 | tf_op jit(solution)/shard_map/all_to_all | solution.py:812
  34.0 2.3 %tracer.1 = (f32[2,16,1024]{2,1,0:T(8,128)}, f32[50,36,128]{2,1,0:T(8,128)}) custom-call(f32[4,48,128]{2,1,0:T(8,128)S(1)} %get-tuple-element.66.halo, f32[2,3,8,128]{3,2,1,0:T(8,128)S(1)} %get-tuple-element.67.halo_tables, f32[2,48,768]{2,1,0:T(8,128)S(1)} %get-tuple-element.68.edge_change, f32[2,48,768]{2,1,0:T(8,128)S(1)} %get-tuple-element.69.halo_change, ...), custom_call_target="tpu_custom_call" | custom-call | tf_op jit(solution)/shard_map/tracer/pallas_call | solution.py:709
Async XLA Ops:
  2.3 18.7 %collective-permute-start = (f32[1024,128]{1,0:T(8,128)S(1)}, f32[1024,128]{1,0:T(8,128)S(1)}, u32[]{:S(2)}, u32[]{:S(2)}) collective-permute-start(f32[1024,128]{1,0:T(8,128)S(1)} %get-tuple-element.40), channel_id=1, source_target_pairs={{1,2},{2,1},{3,4},{4,3},{5,6},{6,5},{7,8},{8,7},{9,10},{10,9},{11,... | collective-permute-start | bytes 1572872 | tf_op jit(solution)/shard_map/ppermute | solution.py:662
  3.0 18.0 %collective-permute-start.1 = (f32[1024,128]{1,0:T(8,128)S(1)}, f32[1024,128]{1,0:T(8,128)S(1)}, u32[]{:S(2)}, u32[]{:S(2)}) collective-permute-start(f32[1024,128]{1,0:T(8,128)S(1)} %get-tuple-element.41), channel_id=1, source_target_pairs={{0,1},{1,0},{2,3},{3,2},{4,5},{5,4},{6,7},{7,6},{8,9},{9,8},{10,11... | collective-permute-start | bytes 1572872 | tf_op jit(solution)/shard_map/ppermute | solution.py:662
